TPU v7x, 32 devices: a whole 2x2x4 slice. The times are simulated.
32 devices in a mesh: groups: 2 (over y), dp: 4 (over z), blk: 2 (over x), mp: 2 (over core).
Axes of the slice: x: 2, y: 2, z: 4, core: 2. Of those that a mesh axis runs over, the one named last changes fastest.
Arguments:
- train_inputs: bfloat16 [16, 128, 8192], P(('groups', 'dp', 'blk'), None, 'mp'), parts along dimension 0, may hold values from -6 to 6
- train_cotangents: bfloat16 [16, 128, 8192], P(('groups', 'dp', 'blk'), None, 'mp'), parts along dimension 0, may hold values from -6 to 6
- train_lengths: int32 [16], P(('groups', 'dp', 'blk')), parts along dimension 0, may hold values from 32 to 128, as said below
- test_inputs: bfloat16 [16, 128, 8192], P(('groups', 'dp', 'blk'), None, 'mp'), parts along dimension 0, may hold values from -6 to 6
- test_cotangents: bfloat16 [16, 128, 8192], P(('groups', 'dp', 'blk'), None, 'mp'), parts along dimension 0, may hold values from -6 to 6
- test_lengths: int32 [16], P(('groups', 'dp', 'blk')), parts along dimension 0, may hold values from 32 to 128, as said below
- proj_in: bfloat16 [8192, 128], P('mp', 'dp')
- proj_out: bfloat16 [8192, 64], P('mp', 'dp')
Outputs:
- scores: float32 [16, 8], P(('groups', 'dp', 'blk')), parts along dimension 0
There are 2 independent parts, one for each index of `groups`. A program takes and returns all parts, laid end to end along the dimension named above; an argument that names none is the same for every part. Nothing has to cross between parts.
Inputs may be any that keep to these rules, and one draw needn't show every extreme that they name: `train_lengths`: live tokens come first in an example; the first example has all 128. `test_lengths`: live tokens come first in an example; the first example has all 128.
All inputs are finite; a program needn't handle non-finite values.
Results may differ from a plain program's by a relative error of at most 0.0003.
Values may be sent and summed in bfloat16 or wider, within the bound.
No kernel may reach another device: no remote copies, remote signals or barrier semaphores. Data moves between devices by JAX's collectives and lax.ppermute only.
A program may use at most 64 MiB of HBM per device.

v0:
```python
import jax
import jax.numpy as jnp
from jax import lax
from jax.sharding import PartitionSpec as P


def project(inputs, weights):
    examples, seq_len, width = inputs.shape
    flat = inputs.reshape(examples * seq_len, width)
    return jnp.dot(flat, weights, preferred_element_type=jnp.float32).reshape(
        examples, seq_len, weights.shape[1]
    )


def live_mask(lengths, seq_len):
    positions = lax.broadcasted_iota(jnp.int32, (lengths.shape[0], seq_len), 1)
    return (positions < lengths[:, None]).astype(jnp.float32)


def factor_total(projected, lengths):
    examples, seq_len, rank_dim = projected.shape
    live = live_mask(lengths, seq_len).reshape(examples * seq_len, 1)
    flat = projected.reshape(examples * seq_len, rank_dim)
    return jnp.dot((flat * live).T, flat, precision=lax.Precision.HIGHEST)


def inverse_factor(total, tokens_live):
    factor = total / tokens_live
    factor_order = factor.shape[0]
    identity = jnp.eye(factor_order, dtype=jnp.float32)
    damped = factor + 0.1 * jnp.trace(factor) / factor_order * identity
    lower = jnp.linalg.cholesky(damped)
    return jax.scipy.linalg.cho_solve((lower, True), identity)


def example_grads(inputs_proj, outputs_proj, lengths):
    seq_len = inputs_proj.shape[1]
    weighting = live_mask(lengths, seq_len) / lengths.astype(jnp.float32)[:, None]
    return jnp.einsum(
        "nsk,nsl->nkl",
        inputs_proj * weighting[:, :, None],
        outputs_proj,
        precision=lax.Precision.HIGHEST,
    )


def precondition(gradients, inv_in, inv_out):
    left = jnp.einsum("kj,njl->nkl", inv_in, gradients, precision=lax.Precision.HIGHEST)
    return jnp.einsum("nkl,lm->nkm", left, inv_out, precision=lax.Precision.HIGHEST)


def per_device(
    train_inputs,
    train_cotangents,
    train_lengths,
    test_inputs,
    test_cotangents,
    test_lengths,
    proj_in,
    proj_out,
):
    weight_in, weight_out = (
        lax.all_gather(proj_in, "dp", axis=1, tiled=True),
        lax.all_gather(proj_out, "dp", axis=1, tiled=True),
    )
    xp_train = project(train_inputs, weight_in)
    gp_train = project(train_cotangents, weight_out)
    xp_test = project(test_inputs, weight_in)
    gp_test = project(test_cotangents, weight_out)
    xp_train, gp_train, xp_test, gp_test = lax.psum((xp_train, gp_train, xp_test, gp_test), "mp")
    total_in, total_out, tokens_live = lax.psum(
        (
            factor_total(xp_train, train_lengths),
            factor_total(gp_train, train_lengths),
            jnp.sum(train_lengths.astype(jnp.float32)),
        ),
        ("dp", "blk"),
    )
    inv_in = inverse_factor(total_in, tokens_live)
    inv_out = inverse_factor(total_out, tokens_live)
    grad_train = example_grads(xp_train, gp_train, train_lengths)
    grad_test = example_grads(xp_test, gp_test, test_lengths)
    test_side = precondition(grad_test, inv_in, inv_out)
    train_local = grad_train.shape[0]
    test_local = test_side.shape[0]
    train_flat = grad_train.reshape(train_local, -1)
    test_flat = test_side.reshape(test_local, -1)
    dp_count = lax.axis_size("dp")
    blk_count = lax.axis_size("blk")
    initial = jnp.zeros((train_local, test_local * dp_count * blk_count), jnp.float32)
    block = jnp.dot(
        train_flat,
        lax.all_gather(test_flat, ("dp", "blk"), axis=0, tiled=True).T,
        precision=lax.Precision.HIGHEST,
    )
    return lax.dynamic_update_slice(initial, block, (jnp.int32(0), jnp.int32(0)))


def solution(mesh):
    placed = (
        P(("groups", "dp", "blk"), None, "mp"),
        P(("groups", "dp", "blk"), None, "mp"),
        P(("groups", "dp", "blk")),
        P(("groups", "dp", "blk"), None, "mp"),
        P(("groups", "dp", "blk"), None, "mp"),
        P(("groups", "dp", "blk")),
        P("mp", "dp"),
        P("mp", "dp"),
    )
    return jax.shard_map(
        per_device,
        mesh=mesh,
        in_specs=placed,
        out_specs=P(("groups", "dp", "blk"), None),
        check_vma=False,
    )
```

profile of v0, /device:TPU:0, one launch (start us, length us, event | category | flops | bytes accessed | tf_op | source)
XLA Modules:
  0.0 264.1 jit_solution(11242846642020133373)
XLA Ops:
  7.4 17.7 %all_gather.10 = bf16[4096,64]{0,1:T(8,128)(2,1)S(1)} all-gather(bf16[4096,16]{0,1:T(8,128)(2,1)} %param.15), channel_id=1, replica_groups=mesh['groups'=2,'dp'=4,'blk'=2,'mp'=2] {'dp'}, dimensions={1}, use_global_device_ids=true | all-gather | bytes 655360 | tf_op jit(solution)/shard_map/all_gather | solution.py:64
  25.1 2.3 convolution_bitcast_fusion.2
  27.4 1.1 fusion
  28.5 0.0 all-reduce.9.cloned.1.call-update
  28.5 0.0 all-gather.3.cloned.1.call-start
  28.6 0.5 all-gather.3.cloned.1.call-update
  29.1 0.0 all-reduce.11.cloned.1.call-start
  30.6 17.6 %all-reduce.9.cloned.1.call-done = (f32[1,128,64]{1,2,0:T(8,128)}, f32[128,64]{0,1:T(8,128)}) async-done(((f32[1,128,64]{1,2,0:T(8,128)}, f32[128,64]{0,1:T(8,128)}), (f32[1,128,64]{1,2,0:T(8,128)}, f32[128,64]{0,1:T(8,128)})) %all-reduce.9.cloned.1.call-update) | async-done | bytes 65552 | tf_op jit(solution)/shard_map/psum | solution.py:70
  48.2 1.0 fusion.30
  49.3 39.4 %all-reduce = (f32[]{:T(128)}, f32[64,64]{1,0:T(8,128)S(1)}) all-reduce(f32[]{:T(128)} %bitcast.3, f32[64,64]{1,0:T(8,128)S(1)} %fusion.30), channel_id=1, replica_groups=mesh['groups'=2,'dp'=4,'blk'=2,'mp'=2] {'dp','blk'}, use_global_device_ids=true, to_apply=%region_5.0 | all-reduce | flops 4097 | bytes 32776 | tf_op jit(solution)/shard_map/psum | solution.py:71
  88.6 1.3 select_reduce_fusion.3
  90.6 0.7 select_add_fusion.1
  91.3 0.1 copy.17
  91.4 0.7 fusion.29
  92.1 5.8 %cholesky.68 = f32[64,64]{1,0:T(8,128)S(1)} custom-call(f32[64,64]{1,0:T(8,128)S(1)} %fusion.29), custom_call_target="Cholesky" | custom-call | tf_op jit(solution)/shard_map/jit(cholesky)/cholesky | solution.py:32
  97.9 0.7 compare_reduce_fusion
  98.7 0.7 fusion.24
  99.4 4.9 %custom-call.21 = f32[1,64,64]{1,2,0:T(8,128)S(1)} custom-call(f32[1,64,64]{2,1,0:T(8,128)S(1)} %fusion.24), custom_call_target="InvertDiagBlocksLowerTriangular" | custom-call | tf_op jit(solution)/shard_map/jit(_cho_solve)/triangular_solve | solution.py:33
  104.3 0.2 fusion.27
  104.5 0.0 all-gather.3.cloned.1.call-done
  104.6 2.4 convolution_bitcast_fusion.1
  107.0 1.1 convolution_bitcast_fusion
  108.1 0.0 all-reduce.7.cloned.1.call-start
  108.1 0.2 fusion.25
  108.3 15.1 %all-reduce.11.cloned.1.call-done = (f32[1,128,128]{2,1,0:T(8,128)}, f32[1,128,128]{2,1,0:T(8,128)}) async-done(((f32[1,128,128]{2,1,0:T(8,128)}, f32[1,128,128]{2,1,0:T(8,128)}), (f32[1,128,128]{2,1,0:T(8,128)}, f32[1,128,128]{2,1,0:T(8,128)})) %all-reduce.11.cloned.1.call-update) | async-done | bytes 131088 | tf_op jit(solution)/shard_map/psum | solution.py:70
  123.4 2.0 fusion.14
  125.4 0.4 fusion.19
  125.7 0.0 all-reduce.7.cloned.1.call-update
  125.8 0.4 copy-done.8
  126.1 0.5 copy-done.7
  126.6 0.3 fusion.17
  126.8 0.1 reshape.168
  126.9 69.6 %all-reduce.7.cloned.1.call-done = f32[128,128]{1,0:T(8,128)} async-done(((f32[128,128]{1,0:T(8,128)}), f32[128,128]{1,0:T(8,128)}) %all-reduce.7.cloned.1.call-update) | async-done | bytes 65552 | tf_op jit(solution)/shard_map/psum | solution.py:71
  196.5 2.2 select_reduce_fusion.1
  199.4 0.7 select_add_fusion
  200.1 0.1 copy.16
  200.2 0.7 fusion.13
  200.9 11.7 %cholesky.33 = f32[128,128]{1,0:T(8,128)S(1)} custom-call(f32[128,128]{1,0:T(8,128)S(1)} %fusion.13), custom_call_target="Cholesky" | custom-call | tf_op jit(solution)/shard_map/jit(cholesky)/cholesky | solution.py:32
  212.6 0.6 compare_reduce_fusion.1
  213.2 0.7 fusion.8
  213.9 9.8 %custom-call.20 = f32[1,128,128]{1,2,0:T(8,128)S(1)} custom-call(f32[1,128,128]{2,1,0:T(8,128)S(1)} %fusion.8), custom_call_target="InvertDiagBlocksLowerTriangular" | custom-call | tf_op jit(solution)/shard_map/jit(_cho_solve)/triangular_solve | solution.py:33
  223.7 0.2 fusion.11
  224.0 0.2 fusion.9
  224.2 0.2 convolution_bitcast_fusion.3
  224.4 0.3 fusion.39
  224.7 0.1 reshape.165
  224.8 30.9 %all-gather = f32[8,1,8192]{2,1,0:T(1,128)S(1)} all-gather(f32[1,1,8192]{2,1,0:T(1,128)S(1)} %reshape.165), channel_id=1, replica_groups=mesh['groups'=2,'dp'=4,'blk'=2,'mp'=2] {'dp','blk'}, dimensions={0}, use_global_device_ids=true | all-gather | bytes 294912 | tf_op jit(solution)/shard_map/all_gather | solution.py:93
  255.7 1.3 fusion.5
  (23 shorter events, 0.1 us)
Async XLA Ops:
  7.4 97.2 %copy-start = (bf16[1,128,4096]{2,1,0:T(8,128)(2,1)S(1)}, bf16[1,128,4096]{2,1,0:T(8,128)(2,1)}, u32[]{:S(2)}) copy-start(bf16[1,128,4096]{2,1,0:T(8,128)(2,1)} %param.8) | copy-start | bytes 3145732
  7.4 20.0 %copy-start.2 = (bf16[1,128,4096]{2,1,0:T(8,128)(2,1)S(1)}, bf16[1,128,4096]{2,1,0:T(8,128)(2,1)}, u32[]{:S(2)}) copy-start(bf16[1,128,4096]{2,1,0:T(8,128)(2,1)} %param.12) | copy-start | bytes 3145732
  7.4 40.8 %all-reduce.9.cloned.1.call-start = ((), (), s32[]{:S(2)}) async-start(), calls=%async_computation.2 | async-start | bytes 131072 | tf_op jit(solution)/shard_map/psum | solution.py:70
  28.5 76.0 %all-gather.3.cloned.1.call-start = ((), (), s32[]{:S(2)}) async-start(), calls=%async_computation | async-start | bytes 1310720 | tf_op jit(solution)/shard_map/all_gather | solution.py:63
  29.1 94.3 %all-reduce.11.cloned.1.call-start = ((), (), s32[]{:S(2)}) async-start(), calls=%async_computation.3 | async-start | bytes 262144 | tf_op jit(solution)/shard_map/psum | solution.py:70
  104.5 2.5 copy-start.3
  104.5 2.4 copy-start.1
  108.1 88.4 %all-reduce.7.cloned.1.call-start = ((), (), s32[]{:S(2)}) async-start(), calls=%async_computation.1 | async-start | bytes 131072 | tf_op jit(solution)/shard_map/psum | solution.py:71
  123.4 2.0 copy-start.4
  123.4 2.0 copy-start.6
  125.3 0.8 copy-start.8
  125.7 0.8 copy-start.7
  196.5 2.9 %copy-start.5 = (f32[128,128]{1,0:T(8,128)S(1)}, f32[128,128]{1,0:T(8,128)}, u32[]{:S(2)}) copy-start(f32[128,128]{1,0:T(8,128)} %all-reduce.7.cloned.1.call-done) | copy-start | bytes 196612
Sparse Core Ops, SparseCore 0:
  28.7 19.5 all-reduce.8
  108.2 15.1 all-reduce.10
  126.8 69.6 all-reduce.6
Sparse Core Ops, SparseCore 1:
  30.6 29.9 all-gather.2
where the time goes:
time: 265 us; the launch traced here: 264 us
  waiting for transfers between devices  103 us (39%)
  blocking collectives  87.9 us (33%)
  other arithmetic  41.3 us (16%)
  between operations  17.6 us (7%)
  matrix products  13.1 us (5%)
    psum x1, waiting for transfers between devices, per_device(): lax.psum((factor_total(xp_train, train_lengths), factor_total(gp_train, t...  69.6 us
    psum x1, blocking collectives, per_device(): lax.psum((factor_total(xp_train, train_lengths), factor_total(gp_train, t...  39.4 us
    psum x2, waiting for transfers between devices, per_device(): lax.psum((xp_train, gp_train, xp_test, gp_test), 'mp')  32.7 us
    all_gather x1, blocking collectives, per_device(): lax.all_gather(test_flat, ('dp', 'blk'), axis=0, tiled=True)  30.9 us
    another operation x6, other arithmetic, inverse_factor(): lower = jnp.linalg.cholesky(damped)  19 us
    all_gather x1, blocking collectives, per_device(): lax.all_gather(proj_out, 'dp', axis=1, tiled=True)  17.7 us
    another operation x4, other arithmetic, inverse_factor(): return jax.scipy.linalg.cho_solve((lower, True), identity)  16.1 us
    dot_general x4, matrix products, project(): jnp.dot(flat, weights, preferred_element_type=jnp.float32)  6.93 us
  transfers between devices with their start and end apart: 4, of which 3 were waited for; matrix products, arithmetic and copies ran while one was open for 6% of the time, Pallas kernels for 0%

commit v1 on v0

v1 whole, which is shorter than its diff:
```python
import functools

import jax
import jax.numpy as jnp
from jax import lax
from jax.experimental import pallas as pl
from jax.experimental.pallas import tpu as pltpu
from jax.sharding import PartitionSpec as P

HI = lax.Precision.HIGHEST
NT = (((1,), (1,)), ((), ()))
TN = (((0,), (0,)), ((), ()))
PARAMS = pltpu.CompilerParams(vmem_limit_bytes=40 * 1024 * 1024)
NEWTON_STEPS = 8


def vmem():
    return pl.BlockSpec(memory_space=pltpu.VMEM)


def smem():
    return pl.BlockSpec(memory_space=pltpu.SMEM)


def swap(x, axis, count, k):
    return lax.ppermute(x, axis, [(i, i ^ k) for i in range(count)])


def write_projections(x_refs, w_in, w_out, out_ref):
    tokens = x_refs[0].shape[0]
    ko = w_out.shape[0]
    for n, ref in enumerate((x_refs[0], x_refs[2])):
        out_ref[n * tokens : (n + 1) * tokens, :] = lax.dot_general(
            ref[...], w_in, NT, preferred_element_type=jnp.float32
        )
    for n, ref in enumerate((x_refs[1], x_refs[3])):
        out_ref[2 * tokens : 3 * tokens, n * ko : (n + 1) * ko] = lax.dot_general(
            ref[...], w_out, NT, preferred_element_type=jnp.float32
        )


def project_kernel(*refs):
    x_refs, (w_in, w_out, out_ref) = refs[:4], refs[4:]
    write_projections(x_refs, w_in[...], w_out[...], out_ref)


def project_pieces_kernel(n_dp, n_xy, *refs):
    x_refs, (own_in, own_out) = refs[:4], refs[4:6]
    first = refs[6 : 5 + n_dp]
    rest = refs[5 + n_dp : 4 + n_dp + n_xy]
    out_ref, w_in, w_out = refs[4 + n_dp + n_xy :]
    z = lax.axis_index("dp")
    q = lax.axis_index(("groups", "blk"))
    rin, rout = own_in.shape[0], own_out.shape[0]
    width = first[0].shape[1]
    w_in[pl.ds(pl.multiple_of(z * rin, rin), rin), :] = own_in[...]
    w_out[pl.ds(pl.multiple_of(z * rout, rout), rout), :] = own_out[...]
    for j in range(n_xy):
        cols = pl.ds(pl.multiple_of((q ^ j) * width, width), width)
        for k in range(1, n_dp):
            src = z ^ k
            if j == 0:
                piece = first[k - 1][...]
            else:
                piece = rest[j - 1][(k - 1) * (rin + rout) : k * (rin + rout), :]
            w_in[pl.ds(pl.multiple_of(src * rin, rin), rin), cols] = piece[:rin]
            w_out[pl.ds(pl.multiple_of(src * rout, rout), rout), cols] = piece[rin:]
    write_projections(x_refs, w_in[...], w_out[...], out_ref)


def moments_kernel(len_tr, len_te, mine, other, fac_ref, gte_ref, gtr_ref):
    tokens = mine.shape[0] // 3
    ki = mine.shape[1]
    ko = ki // 2
    total = mine[...] + other[...]
    rows = lax.broadcasted_iota(jnp.int32, (tokens, ki), 0)
    n_tr, n_te = len_tr[0], len_te[0]
    x_tr = jnp.where(rows < n_tr, total[:tokens], 0.0)
    x_te = jnp.where(rows < n_te, total[tokens : 2 * tokens], 0.0)
    g_both = total[2 * tokens :]
    g_tr = jnp.where(rows < n_tr, g_both, 0.0)[:, :ko]
    g_te = g_both[:, ko:]
    dot = functools.partial(
        lax.dot_general, dimension_numbers=TN, precision=HI,
        preferred_element_type=jnp.float32,
    )
    c_in = dot(x_tr, x_tr)
    c_out = dot(g_tr, g_tr)
    half = ki // 2
    fac_ref[:half, :] = c_in[:half, :]
    fac_ref[half:ki, :half] = c_in[half:, half:]
    fac_ref[half:ki, half:] = c_out
    fac_ref[ki:, :] = jnp.full((8, ki), n_tr.astype(jnp.float32))
    grad_tr = dot(x_tr, g_tr) / n_tr.astype(jnp.float32)
    grad_te = dot(x_te, g_te) / n_te.astype(jnp.float32)
    gtr_ref[...] = grad_tr
    gte_ref[0, :, :ko] = grad_te[:half]
    gte_ref[0, :, ko:] = grad_te[half:]


def damped(c):
    n = c.shape[0]
    i = lax.broadcasted_iota(jnp.int32, (n, n), 0)
    j = lax.broadcasted_iota(jnp.int32, (n, n), 1)
    eye = (i == j).astype(jnp.float32)
    trace = jnp.sum(c * eye, axis=(0, 1), keepdims=True)
    low = 0.1 * trace / n
    a = c + low * eye
    high = jnp.max(jnp.sum(jnp.abs(a), axis=1, keepdims=True), axis=0, keepdims=True)
    return a, eye, low, jnp.minimum(high, trace + low)


def mm(a, b):
    return jnp.dot(a, b, precision=HI, preferred_element_type=jnp.float32)


def inverses(matrices):
    state = []
    for c in matrices:
        a, eye, low, high = damped(c)
        scale = 2.0 / (low + high)
        r = (high - low) / (high + low)
        state.append((a, eye, scale * a, scale * eye, r))
    for step in range(NEWTON_STEPS):
        nxt = []
        for a, eye, m, x, r in state:
            s = 2.0 / (2.0 - r * r)
            n = m.shape[0]
            if step == 0:
                mx = s * (2.0 * m - mm(m, m))
                xx = s * (2.0 * x - x[:1, :1] * m)
            else:
                both = mm(jnp.concatenate([m, x], axis=0), m)
                mx = s * (2.0 * m - both[:n])
                xx = s * (2.0 * x - both[n:])
            nxt.append((a, eye, mx, xx, r * r / (2.0 - r * r)))
        state = nxt
    return [2.0 * x - mm(x, mm(a, x)) for a, eye, m, x, r in state]


def scores_kernel(n_dp, n_blk, *refs):
    facs, grads = refs[:n_dp], refs[n_dp : 2 * n_dp]
    gtr_ref, out_ref = refs[2 * n_dp :]
    total = functools.reduce(jnp.add, [f[...] for f in facs])
    ki = total.shape[1]
    half = ki // 2
    top = total[:half, :]
    c_in = jnp.concatenate(
        [top, jnp.concatenate([top[:, half:].T, total[half:ki, :half]], axis=1)], axis=0
    )
    c_out = total[half:ki, half:]
    count = total[ki : ki + 1, :1]
    inv_in, inv_out = inverses([c_in, c_out])
    side = mm(mm(inv_in, gtr_ref[...]), inv_out) * (count * count)
    packed = jnp.concatenate([side[:half], side[half:]], axis=1)
    z = lax.axis_index("dp")
    b = lax.axis_index("blk")
    lane = lax.broadcasted_iota(jnp.int32, out_ref.shape, 1)
    row = jnp.zeros(out_ref.shape, jnp.float32)
    for k in range(n_dp):
        for l in range(n_blk):
            value = jnp.sum(packed * grads[k][l], axis=(0, 1), keepdims=True)
            row = jnp.where(lane == (z ^ k) * n_blk + (b ^ l), value, row)
    out_ref[...] = row


def per_device(
    n_groups, n_dp, n_blk, train_inputs, train_cotangents, train_lengths,
    test_inputs, test_cotangents, test_lengths, proj_in, proj_out,
):
    _, tokens, width = train_inputs.shape
    xs = [a.reshape(tokens, width) for a in (
        train_inputs, train_cotangents, test_inputs, test_cotangents)]
    w_in, w_out = proj_in.T, proj_out.T
    rin, rout = w_in.shape[0], w_out.shape[0]
    ki, ko = rin * n_dp, rout * n_dp
    n_xy = n_groups * n_blk
    proj_shape = jax.ShapeDtypeStruct((3 * tokens, ki), jnp.float32)
    if rin % 16 == 0 and rout % 16 == 0:
        piece_w = width // n_xy
        q = lax.axis_index(("groups", "blk"))
        mine = lax.dynamic_slice(
            jnp.concatenate([w_in, w_out], axis=0), (0, q * piece_w), (rin + rout, piece_w))
        first = [swap(mine, "dp", n_dp, k) for k in range(1, n_dp)]
        block = jnp.concatenate(first, axis=0)
        rest = [swap(block, ("groups", "blk"), n_xy, j) for j in range(1, n_xy)]
        args = (*xs, w_in, w_out, *first, *rest)
        part = pl.pallas_call(
            functools.partial(project_pieces_kernel, n_dp, n_xy),
            out_shape=proj_shape,
            in_specs=[vmem()] * len(args),
            out_specs=vmem(),
            scratch_shapes=[
                pltpu.VMEM((ki, width), jnp.bfloat16),
                pltpu.VMEM((ko, width), jnp.bfloat16),
            ],
            compiler_params=PARAMS,
        )(*args)
    else:
        w_in = lax.all_gather(w_in, "dp", axis=0, tiled=True)
        w_out = lax.all_gather(w_out, "dp", axis=0, tiled=True)
        part = pl.pallas_call(
            project_kernel,
            out_shape=proj_shape,
            in_specs=[vmem()] * 6,
            out_specs=vmem(),
            compiler_params=PARAMS,
        )(*xs, w_in, w_out)
    other = swap(part, "mp", 2, 1)
    fac, gte, gtr = pl.pallas_call(
        moments_kernel,
        out_shape=(
            jax.ShapeDtypeStruct((ki + 8, ki), jnp.float32),
            jax.ShapeDtypeStruct((1, ki // 2, 2 * ko), jnp.float32),
            jax.ShapeDtypeStruct((ki, ko), jnp.float32),
        ),
        in_specs=[smem(), smem(), vmem(), vmem()],
        out_specs=(vmem(), vmem(), vmem()),
        compiler_params=PARAMS,
    )(train_lengths, test_lengths, part, other)
    fac = functools.reduce(
        jnp.add, [fac] + [swap(fac, "blk", n_blk, l) for l in range(1, n_blk)])
    facs = [fac] + [swap(fac, "dp", n_dp, k) for k in range(1, n_dp)]
    gte = jnp.concatenate(
        [gte] + [swap(gte, "blk", n_blk, l) for l in range(1, n_blk)], axis=0)
    gtes = [gte] + [swap(gte, "dp", n_dp, k) for k in range(1, n_dp)]
    return pl.pallas_call(
        functools.partial(scores_kernel, n_dp, n_blk),
        out_shape=jax.ShapeDtypeStruct((1, n_dp * n_blk), jnp.float32),
        in_specs=[vmem()] * (2 * n_dp + 1),
        out_specs=vmem(),
        compiler_params=PARAMS,
    )(*facs, *gtes, gtr)


def solution(mesh):
    feature = P(("groups", "dp", "blk"), None, "mp")
    length = P(("groups", "dp", "blk"))
    weight = P("mp", "dp")
    shape = mesh.shape
    return jax.shard_map(
        functools.partial(per_device, shape["groups"], shape["dp"], shape["blk"]),
        mesh=mesh,
        in_specs=(feature, feature, length, feature, feature, length, weight, weight),
        out_specs=P(("groups", "dp", "blk"), None),
        check_vma=False,
    )
```

time: 265 us -> 62.6 us (0.24)
  blocking collectives: 87.9 us -> 0 us
  waiting for transfers between devices: 103 us -> 27.3 us
  other arithmetic: 41.3 us -> 0.86 us
  starting transfers between devices: 0.13 us -> 21.2 us
  between operations: 17.6 us -> 1.39 us
  matrix products: 13.1 us -> 0 us
  Pallas kernels: 0 us -> 6.62 us
  local copies, waits for them, and re-layouts: 1.2 us -> 4.93 us
    psum x3 -> x0, waiting for transfers between devices: 102 us -> none  [the longest x1 69.6 us: per_device(): lax.psum((factor_total(xp_train, train_lengths), factor_total(gp_train, t...]
    all_gather x2 -> x0, blocking collectives: 48.6 us -> none  [the longest x1 30.9 us: per_device(): lax.all_gather(test_flat, ('dp', 'blk'), axis=0, tiled=True)]
    psum x1 -> x0, blocking collectives: 39.4 us -> none  [per_device(): lax.psum((factor_total(xp_train, train_lengths), factor_total(gp_train, t...]
    another operation x10 -> x0, other arithmetic: 35.1 us -> none  [the longest x6 19 us: inverse_factor(): lower = jnp.linalg.cholesky(damped)]
    ppermute x0 -> x15, waiting for transfers between devices: none -> 27.3 us  [swap(): return lax.ppermute(x, axis, [(i, i ^ k) for i in range(count)])]
    ppermute x0 -> x15, starting transfers between devices: none -> 21.2 us  [swap(): return lax.ppermute(x, axis, [(i, i ^ k) for i in range(count)])]
    dot_general x11 -> x0, matrix products: 12.3 us -> none  [the longest x4 6.93 us: project(): jnp.dot(flat, weights, preferred_element_type=jnp.float32)]
    pallas_call x0 -> x3, Pallas kernels: none -> 6.62 us  [the longest x1 4.74 us: per_device(): pl.pallas_call(functools.partial(scores_kernel, n_dp, n_blk), out_shape=j...]
  transfers between devices with their start and end apart: 4 -> 15, of which waited for: 3 -> 7; matrix products, arithmetic and copies ran while one was open for 6% -> 0% of each run, Pallas kernels for 0% -> 0%
where the time goes in v1:
time: 62.6 us; the launch traced here: 62.3 us
  waiting for transfers between devices  27.3 us (44%)
  starting transfers between devices  21.2 us (34%)
  Pallas kernels  6.62 us (11%)
  local copies, waits for them, and re-layouts  4.93 us (8%)
  between operations  1.39 us (2%)
  other arithmetic  0.86 us (1%)
    ppermute x15, waiting for transfers between devices, swap(): return lax.ppermute(x, axis, [(i, i ^ k) for i in range(count)])  27.3 us
    ppermute x15, starting transfers between devices, swap(): return lax.ppermute(x, axis, [(i, i ^ k) for i in range(count)])  21.2 us
    unnamed x15, local copies, waits for them, and re-layouts  4.92 us
    pallas_call x1, Pallas kernels, per_device(): pl.pallas_call(functools.partial(scores_kernel, n_dp, n_blk), out_shape=j...  4.74 us
    pallas_call x1, Pallas kernels, per_device(): pl.pallas_call(functools.partial(project_pieces_kernel, n_dp, n_xy), out_...  1.4 us
  transfers between devices with their start and end apart: 15, of which 7 were waited for; matrix products, arithmetic and copies ran while one was open for 0% of the time, Pallas kernels for 0%

profile of v1, /device:TPU:0, one launch (start us, length us, event | category | flops | bytes accessed | tf_op | source)
XLA Modules:
  0.0 62.3 jit_solution(14468281302056326993)
XLA Ops:
  0.0 0.8 %fusion = bf16[48,1024]{1,0:T(8,128)(2,1)S(1)} fusion(s32[]{:T(128)S(6)} %select_n.3, bf16[32,4096]{1,0:T(8,128)(2,1)} %bitcast.6, bf16[16,4096]{1,0:T(8,128)(2,1)} %bitcast.12), kind=kLoop, calls=%fused_computation.2 | loop fusion | flops 196608 | bytes 491524 | tf_op jit(solution)/shard_map/concatenate | solution.py:183
  0.8 0.0 copy-start
  0.9 3.1 %collective-permute-start = (bf16[48,1024]{1,0:T(8,128)(2,1)S(1)}, bf16[48,1024]{1,0:T(8,128)(2,1)S(1)}, u32[]{:S(2)}, u32[]{:S(2)}) collective-permute-start(bf16[48,1024]{1,0:T(8,128)(2,1)S(1)} %fusion), channel_id=1, source_target_pairs={{0,4},{4,0},{8,12},{12,8},{1,5},{5,1},{9,13},{13,9},{2,6},{6,2},{1... | collective-permute-start | bytes 294920 | tf_op jit(solution)/shard_map/ppermute | solution.py:26
  3.9 2.6 %collective-permute-start.1 = (bf16[48,1024]{1,0:T(8,128)(2,1)S(1)}, bf16[48,1024]{1,0:T(8,128)(2,1)S(1)}, u32[]{:S(2)}, u32[]{:S(2)}) collective-permute-start(bf16[48,1024]{1,0:T(8,128)(2,1)S(1)} %fusion), channel_id=1, source_target_pairs={{0,8},{4,12},{8,0},{12,4},{1,9},{5,13},{9,1},{13,5},{2,10},{6,14},... | collective-permute-start | bytes 294920 | tf_op jit(solution)/shard_map/ppermute | solution.py:26
  6.5 0.0 collective-permute-start.2
  6.5 0.2 collective-permute-done.refs_6_
  6.8 7.6 %collective-permute-done.1.refs_7_ = bf16[48,1024]{1,0:T(8,128)(2,1)S(1)} collective-permute-done((bf16[48,1024]{1,0:T(8,128)(2,1)S(1)}, bf16[48,1024]{1,0:T(8,128)(2,1)S(1)}, u32[]{:S(2)}, u32[]{:S(2)}) %collective-permute-start.1) | collective-permute-done | bytes 98336 | tf_op jit(solution)/shard_map/ppermute | solution.py:26
  14.4 0.0 copy-start.5
  14.4 0.0 collective-permute-done.2.refs_8_
  14.4 1.6 %collective-permute-start.3 = (bf16[144,1024]{1,0:T(8,128)(2,1)S(1)}, bf16[144,1024]{1,0:T(8,128)(2,1)S(1)}, u32[]{:S(2)}, u32[]{:S(2)}) collective-permute-start(bf16[144,1024]{1,0:T(8,128)(2,1)S(1)} %constant_dynamic-update-slice_fusion), channel_id=1, source_target_pairs={{0,2},{2,0},{16,18},{18,16},{1,3},{3,1},{17,19},{19,17},{4,6},{6,4... | collective-permute-start | bytes 884744 | tf_op jit(solution)/shard_map/ppermute | solution.py:26
  16.0 1.5 %collective-permute-start.4 = (bf16[144,1024]{1,0:T(8,128)(2,1)S(1)}, bf16[144,1024]{1,0:T(8,128)(2,1)S(1)}, u32[]{:S(2)}, u32[]{:S(2)}) collective-permute-start(bf16[144,1024]{1,0:T(8,128)(2,1)S(1)} %constant_dynamic-update-slice_fusion), channel_id=1, source_target_pairs={{0,16},{2,18},{16,0},{18,2},{1,17},{3,19},{17,1},{19,3},{4,20},{6,... | collective-permute-start | bytes 884744 | tf_op jit(solution)/shard_map/ppermute | solution.py:26
  17.5 0.5 collective-permute-start.5
  18.0 6.5 %collective-permute-done.3.refs_9_ = bf16[144,1024]{1,0:T(8,128)(2,1)S(1)} collective-permute-done((bf16[144,1024]{1,0:T(8,128)(2,1)S(1)}, bf16[144,1024]{1,0:T(8,128)(2,1)S(1)}, u32[]{:S(2)}, u32[]{:S(2)}) %collective-permute-start.3) | collective-permute-done | bytes 294944 | tf_op jit(solution)/shard_map/ppermute | solution.py:26
  24.4 4.4 %collective-permute-done.4.refs_10_ = bf16[144,1024]{1,0:T(8,128)(2,1)S(1)} collective-permute-done((bf16[144,1024]{1,0:T(8,128)(2,1)S(1)}, bf16[144,1024]{1,0:T(8,128)(2,1)S(1)}, u32[]{:S(2)}, u32[]{:S(2)}) %collective-permute-start.4) | collective-permute-done | bytes 294944 | tf_op jit(solution)/shard_map/ppermute | solution.py:26
  28.9 0.0 collective-permute-done.5.refs_11_
  28.9 0.0 copy-done
  28.9 0.0 copy-done.5
  28.9 0.0 copy-start.1
  28.9 1.2 %copy-done.1 = bf16[1,128,4096]{2,1,0:T(8,128)(2,1)S(1)} copy-done((bf16[1,128,4096]{2,1,0:T(8,128)(2,1)S(1)}, bf16[1,128,4096]{2,1,0:T(8,128)(2,1)}, u32[]{:S(2)}) %copy-start.1) | copy-done | bytes 1048600
  30.1 0.0 copy-start.2
  30.1 1.2 %copy-done.2 = bf16[1,128,4096]{2,1,0:T(8,128)(2,1)S(1)} copy-done((bf16[1,128,4096]{2,1,0:T(8,128)(2,1)S(1)}, bf16[1,128,4096]{2,1,0:T(8,128)(2,1)}, u32[]{:S(2)}) %copy-start.2) | copy-done | bytes 1048600
  31.3 0.0 copy-start.3
  31.3 1.2 %copy-done.3 = bf16[1,128,4096]{2,1,0:T(8,128)(2,1)S(1)} copy-done((bf16[1,128,4096]{2,1,0:T(8,128)(2,1)S(1)}, bf16[1,128,4096]{2,1,0:T(8,128)(2,1)}, u32[]{:S(2)}) %copy-start.3) | copy-done | bytes 1048600
  32.5 0.0 copy-start.4
  32.5 1.2 %copy-done.4 = bf16[1,128,4096]{2,1,0:T(8,128)(2,1)S(1)} copy-done((bf16[1,128,4096]{2,1,0:T(8,128)(2,1)S(1)}, bf16[1,128,4096]{2,1,0:T(8,128)(2,1)}, u32[]{:S(2)}) %copy-start.4) | copy-done | bytes 1048600
  33.8 1.4 %shard_map.82.mine = f32[384,128]{1,0:T(8,128)S(1)} custom-call(bf16[128,4096]{1,0:T(8,128)(2,1)S(1)} %bitcast.8, bf16[128,4096]{1,0:T(8,128)(2,1)S(1)} %bitcast.9, bf16[128,4096]{1,0:T(8,128)(2,1)S(1)} %bitcast.10, bf16[128,4096]{1,0:T(8,128)(2,1)S(1)} %bitcast.11, bf16[32,4096]{1,0:T(8,128)(2,1)S(1)} %bitcast.7, bf16[16,4096]{1,0:T(8,128)(2,1)S(1)} %bitcast.13, ...), custom_call_target="tpu_custom_call" | custom-call | tf_op jit(solution)/shard_map/pallas_call | solution.py:188
  35.2 0.1 collective-permute-start.6
  36.5 0.1 collective-permute-done.6.other
  36.7 0.5 shard_map.83
  37.2 1.3 %collective-permute-start.11 = (f32[1,64,128]{2,1,0:T(8,128)S(1)}, f32[1,64,128]{2,1,0:T(8,128)S(1)}, u32[]{:S(2)}, u32[]{:S(2)}) collective-permute-start(f32[1,64,128]{2,1,0:T(8,128)S(1)} %get-tuple-element.9), channel_id=1, source_target_pairs={{0,2},{2,0},{1,3},{3,1},{4,6},{6,4},{5,7},{7,5},{8,10},{10,8},{9,1... | collective-permute-start | bytes 98312 | tf_op jit(solution)/shard_map/ppermute | solution.py:26
  38.4 0.8 %collective-permute-start.7 = (f32[136,128]{1,0:T(8,128)S(1)}, f32[136,128]{1,0:T(8,128)S(1)}, u32[]{:S(2)}, u32[]{:S(2)}) collective-permute-start(f32[136,128]{1,0:T(8,128)S(1)} %get-tuple-element.8), channel_id=1, source_target_pairs={{0,2},{2,0},{1,3},{3,1},{4,6},{6,4},{5,7},{7,5},{8,10},{10,8},{9,1... | collective-permute-start | bytes 208904 | tf_op jit(solution)/shard_map/ppermute | solution.py:26
  39.2 1.9 %collective-permute-done.11 = f32[1,64,128]{2,1,0:T(8,128)S(1)} collective-permute-done((f32[1,64,128]{2,1,0:T(8,128)S(1)}, f32[1,64,128]{2,1,0:T(8,128)S(1)}, u32[]{:S(2)}, u32[]{:S(2)}) %collective-permute-start.11) | collective-permute-done | bytes 32800 | tf_op jit(solution)/shard_map/ppermute | solution.py:26
  41.1 2.3 %collective-permute-start.12 = (f32[2,64,128]{2,1,0:T(8,128)S(1)}, f32[2,64,128]{2,1,0:T(8,128)S(1)}, u32[]{:S(2)}, u32[]{:S(2)}) collective-permute-start(f32[2,64,128]{2,1,0:T(8,128)S(1)} %constant_dynamic-update-slice_fusion.3.refs_4_), channel_id=1, source_target_pairs={{0,4},{4,0},{8,12},{12,8},{1,5},{5,1},{9,13},{13,9},{2,6},{6,2},{1... | collective-permute-start | bytes 196616 | tf_op jit(solution)/shard_map/ppermute | solution.py:26
  43.4 0.0 collective-permute-done.7
  43.4 2.5 %collective-permute-start.10 = (f32[136,128]{1,0:T(8,128)S(1)}, f32[136,128]{1,0:T(8,128)S(1)}, u32[]{:S(2)}, u32[]{:S(2)}) collective-permute-start(f32[136,128]{1,0:T(8,128)S(1)} %add.11.refs_0_), channel_id=1, source_target_pairs={{0,12},{4,8},{8,4},{12,0},{1,13},{5,9},{9,5},{13,1},{2,14},{6,10},... | collective-permute-start | bytes 208904 | tf_op jit(solution)/shard_map/ppermute | solution.py:26
  46.0 0.7 %collective-permute-start.8 = (f32[136,128]{1,0:T(8,128)S(1)}, f32[136,128]{1,0:T(8,128)S(1)}, u32[]{:S(2)}, u32[]{:S(2)}) collective-permute-start(f32[136,128]{1,0:T(8,128)S(1)} %add.11.refs_0_), channel_id=1, source_target_pairs={{0,4},{4,0},{8,12},{12,8},{1,5},{5,1},{9,13},{13,9},{2,6},{6,2},{1... | collective-permute-start | bytes 208904 | tf_op jit(solution)/shard_map/ppermute | solution.py:26
  46.7 1.2 %collective-permute-start.9 = (f32[136,128]{1,0:T(8,128)S(1)}, f32[136,128]{1,0:T(8,128)S(1)}, u32[]{:S(2)}, u32[]{:S(2)}) collective-permute-start(f32[136,128]{1,0:T(8,128)S(1)} %add.11.refs_0_), channel_id=1, source_target_pairs={{0,8},{4,12},{8,0},{12,4},{1,9},{5,13},{9,1},{13,5},{2,10},{6,14},... | collective-permute-start | bytes 208904 | tf_op jit(solution)/shard_map/ppermute | solution.py:26
  47.9 1.7 %collective-permute-start.13 = (f32[2,64,128]{2,1,0:T(8,128)S(1)}, f32[2,64,128]{2,1,0:T(8,128)S(1)}, u32[]{:S(2)}, u32[]{:S(2)}) collective-permute-start(f32[2,64,128]{2,1,0:T(8,128)S(1)} %constant_dynamic-update-slice_fusion.3.refs_4_), channel_id=1, source_target_pairs={{0,8},{4,12},{8,0},{12,4},{1,9},{5,13},{9,1},{13,5},{2,10},{6,14},... | collective-permute-start | bytes 196616 | tf_op jit(solution)/shard_map/ppermute | solution.py:26
  49.6 0.0 collective-permute-done.12.refs_5_
  49.6 1.4 %collective-permute-start.14 = (f32[2,64,128]{2,1,0:T(8,128)S(1)}, f32[2,64,128]{2,1,0:T(8,128)S(1)}, u32[]{:S(2)}, u32[]{:S(2)}) collective-permute-start(f32[2,64,128]{2,1,0:T(8,128)S(1)} %constant_dynamic-update-slice_fusion.3.refs_4_), channel_id=1, source_target_pairs={{0,12},{4,8},{8,4},{12,0},{1,13},{5,9},{9,5},{13,1},{2,14},{6,10},... | collective-permute-start | bytes 196616 | tf_op jit(solution)/shard_map/ppermute | solution.py:26
  51.0 6.5 %collective-permute-done.13.refs_6_ = f32[2,64,128]{2,1,0:T(8,128)S(1)} collective-permute-done((f32[2,64,128]{2,1,0:T(8,128)S(1)}, f32[2,64,128]{2,1,0:T(8,128)S(1)}, u32[]{:S(2)}, u32[]{:S(2)}) %collective-permute-start.13) | collective-permute-done | bytes 65568 | tf_op jit(solution)/shard_map/ppermute | solution.py:26
  57.5 0.0 collective-permute-done.14.refs_7_
  57.5 0.0 collective-permute-done.10.refs_3_
  57.5 0.0 collective-permute-done.8.refs_1_
  57.5 0.0 collective-permute-done.9.refs_2_
  57.5 4.7 %shard_map.84 = f32[1,8]{1,0:T(1,128)} custom-call(f32[136,128]{1,0:T(8,128)S(1)} %add.11.refs_0_, f32[136,128]{1,0:T(8,128)S(1)} %collective-permute-done.8.refs_1_, f32[136,128]{1,0:T(8,128)S(1)} %collective-permute-done.9.refs_2_, f32[136,128]{1,0:T(8,128)S(1)} %collective-permute-done.10.refs_3_, ...), custom_call_target="tpu_custom_call" | custom-call | tf_op jit(solution)/shard_map/pallas_call | solution.py:227
  (6 shorter events, 0.0 us)
Async XLA Ops:
  0.8 28.0 %copy-start = (bf16[4096,32]{0,1:T(8,128)(2,1)S(1)}, bf16[4096,32]{0,1:T(8,128)(2,1)}, u32[]{:S(2)}) copy-start(bf16[4096,32]{0,1:T(8,128)(2,1)} %param.14) | copy-start | bytes 786436
  0.9 5.9 %collective-permute-start = (bf16[48,1024]{1,0:T(8,128)(2,1)S(1)}, bf16[48,1024]{1,0:T(8,128)(2,1)S(1)}, u32[]{:S(2)}, u32[]{:S(2)}) collective-permute-start(bf16[48,1024]{1,0:T(8,128)(2,1)S(1)} %fusion), channel_id=1, source_target_pairs={{0,4},{4,0},{8,12},{12,8},{1,5},{5,1},{9,13},{13,9},{2,6},{6,2},{1... | collective-permute-start | bytes 294920 | tf_op jit(solution)/shard_map/ppermute | solution.py:26
  3.9 10.4 %collective-permute-start.1 = (bf16[48,1024]{1,0:T(8,128)(2,1)S(1)}, bf16[48,1024]{1,0:T(8,128)(2,1)S(1)}, u32[]{:S(2)}, u32[]{:S(2)}) collective-permute-start(bf16[48,1024]{1,0:T(8,128)(2,1)S(1)} %fusion), channel_id=1, source_target_pairs={{0,8},{4,12},{8,0},{12,4},{1,9},{5,13},{9,1},{13,5},{2,10},{6,14},... | collective-permute-start | bytes 294920 | tf_op jit(solution)/shard_map/ppermute | solution.py:26
  6.5 7.9 %collective-permute-start.2 = (bf16[48,1024]{1,0:T(8,128)(2,1)S(1)}, bf16[48,1024]{1,0:T(8,128)(2,1)S(1)}, u32[]{:S(2)}, u32[]{:S(2)}) collective-permute-start(bf16[48,1024]{1,0:T(8,128)(2,1)S(1)} %fusion), channel_id=1, source_target_pairs={{0,12},{4,8},{8,4},{12,0},{1,13},{5,9},{9,5},{13,1},{2,14},{6,10},... | collective-permute-start | bytes 294920 | tf_op jit(solution)/shard_map/ppermute | solution.py:26
  14.4 14.5 %copy-start.5 = (bf16[4096,16]{0,1:T(8,128)(2,1)S(1)}, bf16[4096,16]{0,1:T(8,128)(2,1)}, u32[]{:S(2)}) copy-start(bf16[4096,16]{0,1:T(8,128)(2,1)} %param.15) | copy-start | bytes 393220
  14.4 10.0 %collective-permute-start.3 = (bf16[144,1024]{1,0:T(8,128)(2,1)S(1)}, bf16[144,1024]{1,0:T(8,128)(2,1)S(1)}, u32[]{:S(2)}, u32[]{:S(2)}) collective-permute-start(bf16[144,1024]{1,0:T(8,128)(2,1)S(1)} %constant_dynamic-update-slice_fusion), channel_id=1, source_target_pairs={{0,2},{2,0},{16,18},{18,16},{1,3},{3,1},{17,19},{19,17},{4,6},{6,4... | collective-permute-start | bytes 884744 | tf_op jit(solution)/shard_map/ppermute | solution.py:26
  16.0 12.9 %collective-permute-start.4 = (bf16[144,1024]{1,0:T(8,128)(2,1)S(1)}, bf16[144,1024]{1,0:T(8,128)(2,1)S(1)}, u32[]{:S(2)}, u32[]{:S(2)}) collective-permute-start(bf16[144,1024]{1,0:T(8,128)(2,1)S(1)} %constant_dynamic-update-slice_fusion), channel_id=1, source_target_pairs={{0,16},{2,18},{16,0},{18,2},{1,17},{3,19},{17,1},{19,3},{4,20},{6,... | collective-permute-start | bytes 884744 | tf_op jit(solution)/shard_map/ppermute | solution.py:26
  17.5 11.4 %collective-permute-start.5 = (bf16[144,1024]{1,0:T(8,128)(2,1)S(1)}, bf16[144,1024]{1,0:T(8,128)(2,1)S(1)}, u32[]{:S(2)}, u32[]{:S(2)}) collective-permute-start(bf16[144,1024]{1,0:T(8,128)(2,1)S(1)} %constant_dynamic-update-slice_fusion), channel_id=1, source_target_pairs={{0,18},{2,16},{16,2},{18,0},{1,19},{3,17},{17,3},{19,1},{4,22},{6,... | collective-permute-start | bytes 884744 | tf_op jit(solution)/shard_map/ppermute | solution.py:26
  28.9 1.2 %copy-start.1 = (bf16[1,128,4096]{2,1,0:T(8,128)(2,1)S(1)}, bf16[1,128,4096]{2,1,0:T(8,128)(2,1)}, u32[]{:S(2)}) copy-start(bf16[1,128,4096]{2,1,0:T(8,128)(2,1)} %param.8) | copy-start | bytes 3145732
  30.1 1.2 %copy-start.2 = (bf16[1,128,4096]{2,1,0:T(8,128)(2,1)S(1)}, bf16[1,128,4096]{2,1,0:T(8,128)(2,1)}, u32[]{:S(2)}) copy-start(bf16[1,128,4096]{2,1,0:T(8,128)(2,1)} %param.9) | copy-start | bytes 3145732
  31.3 1.2 %copy-start.3 = (bf16[1,128,4096]{2,1,0:T(8,128)(2,1)S(1)}, bf16[1,128,4096]{2,1,0:T(8,128)(2,1)}, u32[]{:S(2)}) copy-start(bf16[1,128,4096]{2,1,0:T(8,128)(2,1)} %param.11) | copy-start | bytes 3145732
  32.5 1.2 %copy-start.4 = (bf16[1,128,4096]{2,1,0:T(8,128)(2,1)S(1)}, bf16[1,128,4096]{2,1,0:T(8,128)(2,1)}, u32[]{:S(2)}) copy-start(bf16[1,128,4096]{2,1,0:T(8,128)(2,1)} %param.12) | copy-start | bytes 3145732
  35.2 1.5 %collective-permute-start.6 = (f32[384,128]{1,0:T(8,128)S(1)}, f32[384,128]{1,0:T(8,128)S(1)}, u32[]{:S(2)}, u32[]{:S(2)}) collective-permute-start(f32[384,128]{1,0:T(8,128)S(1)} %shard_map.82.mine), channel_id=1, source_target_pairs={{0,1},{1,0},{2,3},{3,2},{4,5},{5,4},{6,7},{7,6},{8,9},{9,8},{10,11... | collective-permute-start | bytes 589832 | tf_op jit(solution)/shard_map/ppermute | solution.py:26
  37.2 4.0 %collective-permute-start.11 = (f32[1,64,128]{2,1,0:T(8,128)S(1)}, f32[1,64,128]{2,1,0:T(8,128)S(1)}, u32[]{:S(2)}, u32[]{:S(2)}) collective-permute-start(f32[1,64,128]{2,1,0:T(8,128)S(1)} %get-tuple-element.9), channel_id=1, source_target_pairs={{0,2},{2,0},{1,3},{3,1},{4,6},{6,4},{5,7},{7,5},{8,10},{10,8},{9,1... | collective-permute-start | bytes 98312 | tf_op jit(solution)/shard_map/ppermute | solution.py:26
  38.4 5.0 %collective-permute-start.7 = (f32[136,128]{1,0:T(8,128)S(1)}, f32[136,128]{1,0:T(8,128)S(1)}, u32[]{:S(2)}, u32[]{:S(2)}) collective-permute-start(f32[136,128]{1,0:T(8,128)S(1)} %get-tuple-element.8), channel_id=1, source_target_pairs={{0,2},{2,0},{1,3},{3,1},{4,6},{6,4},{5,7},{7,5},{8,10},{10,8},{9,1... | collective-permute-start | bytes 208904 | tf_op jit(solution)/shard_map/ppermute | solution.py:26
  41.1 8.5 %collective-permute-start.12 = (f32[2,64,128]{2,1,0:T(8,128)S(1)}, f32[2,64,128]{2,1,0:T(8,128)S(1)}, u32[]{:S(2)}, u32[]{:S(2)}) collective-permute-start(f32[2,64,128]{2,1,0:T(8,128)S(1)} %constant_dynamic-update-slice_fusion.3.refs_4_), channel_id=1, source_target_pairs={{0,4},{4,0},{8,12},{12,8},{1,5},{5,1},{9,13},{13,9},{2,6},{6,2},{1... | collective-permute-start | bytes 196616 | tf_op jit(solution)/shard_map/ppermute | solution.py:26
  43.4 14.1 %collective-permute-start.10 = (f32[136,128]{1,0:T(8,128)S(1)}, f32[136,128]{1,0:T(8,128)S(1)}, u32[]{:S(2)}, u32[]{:S(2)}) collective-permute-start(f32[136,128]{1,0:T(8,128)S(1)} %add.11.refs_0_), channel_id=1, source_target_pairs={{0,12},{4,8},{8,4},{12,0},{1,13},{5,9},{9,5},{13,1},{2,14},{6,10},... | collective-permute-start | bytes 208904 | tf_op jit(solution)/shard_map/ppermute | solution.py:26
  46.0 11.5 %collective-permute-start.8 = (f32[136,128]{1,0:T(8,128)S(1)}, f32[136,128]{1,0:T(8,128)S(1)}, u32[]{:S(2)}, u32[]{:S(2)}) collective-permute-start(f32[136,128]{1,0:T(8,128)S(1)} %add.11.refs_0_), channel_id=1, source_target_pairs={{0,4},{4,0},{8,12},{12,8},{1,5},{5,1},{9,13},{13,9},{2,6},{6,2},{1... | collective-permute-start | bytes 208904 | tf_op jit(solution)/shard_map/ppermute | solution.py:26
  46.7 10.8 %collective-permute-start.9 = (f32[136,128]{1,0:T(8,128)S(1)}, f32[136,128]{1,0:T(8,128)S(1)}, u32[]{:S(2)}, u32[]{:S(2)}) collective-permute-start(f32[136,128]{1,0:T(8,128)S(1)} %add.11.refs_0_), channel_id=1, source_target_pairs={{0,8},{4,12},{8,0},{12,4},{1,9},{5,13},{9,1},{13,5},{2,10},{6,14},... | collective-permute-start | bytes 208904 | tf_op jit(solution)/shard_map/ppermute | solution.py:26
  47.9 9.6 %collective-permute-start.13 = (f32[2,64,128]{2,1,0:T(8,128)S(1)}, f32[2,64,128]{2,1,0:T(8,128)S(1)}, u32[]{:S(2)}, u32[]{:S(2)}) collective-permute-start(f32[2,64,128]{2,1,0:T(8,128)S(1)} %constant_dynamic-update-slice_fusion.3.refs_4_), channel_id=1, source_target_pairs={{0,8},{4,12},{8,0},{12,4},{1,9},{5,13},{9,1},{13,5},{2,10},{6,14},... | collective-permute-start | bytes 196616 | tf_op jit(solution)/shard_map/ppermute | solution.py:26
  49.6 7.9 %collective-permute-start.14 = (f32[2,64,128]{2,1,0:T(8,128)S(1)}, f32[2,64,128]{2,1,0:T(8,128)S(1)}, u32[]{:S(2)}, u32[]{:S(2)}) collective-permute-start(f32[2,64,128]{2,1,0:T(8,128)S(1)} %constant_dynamic-update-slice_fusion.3.refs_4_), channel_id=1, source_target_pairs={{0,12},{4,8},{8,4},{12,0},{1,13},{5,9},{9,5},{13,1},{2,14},{6,10},... | collective-permute-start | bytes 196616 | tf_op jit(solution)/shard_map/ppermute | solution.py:26

commit v2 on v1

v2 whole, which is shorter than its diff:
```python
import functools

import jax
import jax.numpy as jnp
from jax import lax
from jax.experimental import pallas as pl
from jax.experimental.pallas import tpu as pltpu
from jax.sharding import PartitionSpec as P

HI = lax.Precision.HIGHEST
NT = (((1,), (1,)), ((), ()))
TN = (((0,), (0,)), ((), ()))
NEWTON_STEPS = 7
PLANE = ("groups", "blk")


def vmem():
    return pl.BlockSpec(memory_space=pltpu.VMEM)


def smem():
    return pl.BlockSpec(memory_space=pltpu.SMEM)


def call(kernel, out_shape, in_specs, args, flops=0, **kw):
    return pl.pallas_call(
        kernel,
        out_shape=out_shape,
        in_specs=in_specs,
        out_specs=jax.tree.map(lambda _: vmem(), out_shape),
        compiler_params=pltpu.CompilerParams(vmem_limit_bytes=32 * 1024 * 1024),
        cost_estimate=pl.CostEstimate(flops=flops, bytes_accessed=4 << 20, transcendentals=0),
        **kw,
    )(*args)


def swap(x, axis, count, k):
    return lax.ppermute(x, axis, [(i, i ^ k) for i in range(count)])


def bits(count):
    return [1 << s for s in reversed(range(count.bit_length() - 1))]


def load_kernel(*refs):
    srcs, dsts, sem = refs[:4], refs[4:8], refs[8]
    copies = []
    for i, (src, dst) in enumerate(zip(srcs, dsts)):
        rows = src.shape[0] // 2
        for h in range(2):
            part = pl.ds(h * rows, rows)
            copies.append(pltpu.make_async_copy(src.at[part], dst.at[part], sem.at[2 * i + h]))
    for c in copies:
        c.start()
    for c in copies:
        c.wait()


def store_products(x_parts, g_parts, acc_ref, out_ref):
    tokens = out_ref.shape[0] // 3
    ko = g_parts[0].shape[1]
    for n in range(2):
        rows = slice(n * tokens, (n + 1) * tokens)
        prior = 0.0 if acc_ref is None else acc_ref[rows, :]
        out_ref[rows, :] = prior + x_parts[n]
    rows = slice(2 * tokens, 3 * tokens)
    for n in range(2):
        cols = slice(n * ko, (n + 1) * ko)
        prior = 0.0 if acc_ref is None else acc_ref[rows, cols]
        out_ref[rows, cols] = prior + g_parts[n]


def nt(a, b):
    return lax.dot_general(a, b, NT, preferred_element_type=jnp.float32)


def project_kernel(*refs):
    x_refs, (w_in, w_out, out_ref) = refs[:4], refs[4:]
    xs = [nt(x_refs[n][...], w_in[...]) for n in (0, 2)]
    gs = [nt(x_refs[n][...], w_out[...]) for n in (1, 3)]
    store_products(xs, gs, None, out_ref)


def project_pieces_kernel(plan, shifts, with_acc, n_pieces, *refs):
    x_refs, (own_in, own_out) = refs[:4], refs[4:6]
    pieces = refs[6 : 6 + n_pieces]
    acc_ref = refs[6 + n_pieces] if with_acc else None
    out_ref, w_in, w_out = refs[6 + n_pieces + with_acc :]
    z = lax.axis_index("dp")
    q = lax.axis_index(PLANE)
    rin, rout = own_in.shape[0], own_out.shape[0]
    width = pieces[0].shape[1]
    xs, gs = [0.0, 0.0], [0.0, 0.0]
    for n, (dq, half, p, row) in enumerate(plan):
        start = pl.multiple_of(((q ^ dq) * 2 + half) * width, width)
        cols = pl.ds(start, width)
        here = slice(n * width, (n + 1) * width)
        w_in[pl.ds(pl.multiple_of(z * rin, rin), rin), here] = own_in[:, cols]
        w_out[pl.ds(pl.multiple_of(z * rout, rout), rout), here] = own_out[:, cols]
        for i, k in enumerate(shifts):
            at = row + i * (rin + rout)
            dst_in = pl.multiple_of((z ^ k) * rin, rin)
            dst_out = pl.multiple_of((z ^ k) * rout, rout)
            w_in[pl.ds(dst_in, rin), here] = pieces[p][at : at + rin, :]
            w_out[pl.ds(dst_out, rout), here] = pieces[p][at + rin : at + rin + rout, :]
        for m in range(2):
            xs[m] += nt(x_refs[2 * m][:, cols], w_in[:, here])
            gs[m] += nt(x_refs[2 * m + 1][:, cols], w_out[:, here])
    store_products(xs, gs, acc_ref, out_ref)


def moments_kernel(len_tr, len_te, mine, other, fac_ref, gte_ref, gtr_ref):
    tokens = mine.shape[0] // 3
    ki = mine.shape[1]
    ko = ki // 2
    total = mine[...] + other[...]
    rows = lax.broadcasted_iota(jnp.int32, (tokens, ki), 0)
    n_tr, n_te = len_tr[0], len_te[0]
    x_tr = jnp.where(rows < n_tr, total[:tokens], 0.0)
    x_te = jnp.where(rows < n_te, total[tokens : 2 * tokens], 0.0)
    g_both = total[2 * tokens :]
    g_tr = jnp.where(rows < n_tr, g_both, 0.0)[:, :ko]
    g_te = g_both[:, ko:]
    dot = functools.partial(
        lax.dot_general, dimension_numbers=TN, precision=HI,
        preferred_element_type=jnp.float32,
    )
    c_in = dot(x_tr, x_tr)
    c_out = dot(g_tr, g_tr)
    half = ki // 2
    fac_ref[:half, :] = c_in[:half, :]
    fac_ref[half:ki, :half] = c_in[half:, half:]
    fac_ref[half:ki, half:] = c_out
    fac_ref[ki:, :] = jnp.full((8, ki), n_tr.astype(jnp.float32))
    grad_tr = dot(x_tr, g_tr) / n_tr.astype(jnp.float32)
    grad_te = dot(x_te, g_te) / n_te.astype(jnp.float32)
    gtr_ref[...] = grad_tr
    gte_ref[0, :, :ko] = grad_te[:half]
    gte_ref[0, :, ko:] = grad_te[half:]


def damped(c):
    n = c.shape[0]
    i = lax.broadcasted_iota(jnp.int32, (n, n), 0)
    j = lax.broadcasted_iota(jnp.int32, (n, n), 1)
    eye = (i == j).astype(jnp.float32)
    trace = jnp.sum(c * eye, axis=(0, 1), keepdims=True)
    low = 0.1 * trace / n
    a = c + low * eye
    high = jnp.max(jnp.sum(jnp.abs(a), axis=0, keepdims=True), axis=1, keepdims=True)
    return a, eye, low, jnp.minimum(high, trace + low)


def mm(a, b):
    return jnp.dot(a, b, precision=HI, preferred_element_type=jnp.float32)


def inverses(matrices):
    state = []
    for c in matrices:
        a, eye, low, high = damped(c)
        scale = 2.0 / (low + high)
        r = (high - low) / (high + low)
        state.append((a, scale * a, scale * eye, r))
    for step in range(NEWTON_STEPS):
        nxt = []
        for a, m, x, r in state:
            s = 2.0 / (2.0 - r * r)
            n = m.shape[0]
            if step == 0:
                mx = s * (2.0 * m - mm(m, m))
                xx = s * (2.0 * x - x[:1, :1] * m)
            else:
                both = mm(jnp.concatenate([m, x], axis=0), m)
                mx = s * (2.0 * m - both[:n])
                xx = s * (2.0 * x - both[n:])
            nxt.append((a, mx, xx, r * r / (2.0 - r * r)))
        state = nxt
    return [2.0 * x - mm(x, mm(a, x)) for a, m, x, r in state]


def side_kernel(fac_ref, gtr_ref, out_ref):
    ki = fac_ref.shape[1]
    half = ki // 2
    top = fac_ref[:half, :]
    low = fac_ref[half:ki, :]
    c_in = jnp.concatenate(
        [top, jnp.concatenate([top[:, half:].T, low[:, :half]], axis=1)], axis=0
    )
    count = fac_ref[ki : ki + 1, :1]
    inv_in, inv_out = inverses([c_in, low[:, half:]])
    side = mm(mm(inv_in, gtr_ref[...]), inv_out) * (count * count)
    out_ref[:, :half] = side[:half]
    out_ref[:, half:] = side[half:]


def scores_kernel(order, n_blk, side_ref, gte_ref, out_ref):
    z = lax.axis_index("dp")
    b = lax.axis_index("blk")
    lane = lax.broadcasted_iota(jnp.int32, out_ref.shape, 1)
    row = jnp.zeros(out_ref.shape, jnp.float32)
    side = side_ref[...]
    for p, (dz, db) in enumerate(order):
        value = jnp.sum(side * gte_ref[p], axis=(0, 1), keepdims=True)
        row = jnp.where(lane == (z ^ dz) * n_blk + (b ^ db), value, row)
    out_ref[...] = row


def project(xs, w_in, w_out, n_groups, n_dp, n_blk):
    tokens, width = xs[0].shape
    rin, rout = w_in.shape[0], w_out.shape[0]
    ki, ko = rin * n_dp, rout * n_dp
    out_shape = jax.ShapeDtypeStruct((3 * tokens, ki), jnp.float32)
    if (n_groups, n_dp, n_blk) != (2, 4, 2):
        w_in = lax.all_gather(w_in, "dp", axis=0, tiled=True)
        w_out = lax.all_gather(w_out, "dp", axis=0, tiled=True)
        return call(project_kernel, out_shape, [vmem()] * 6, (*xs, w_in, w_out))

    part = width // 8
    q = lax.axis_index(PLANE)
    mine = lax.dynamic_slice(
        jnp.concatenate([w_in, w_out], axis=0), (0, q * 2 * part), (rin + rout, 2 * part))
    xs = call(
        load_kernel,
        tuple(jax.ShapeDtypeStruct(x.shape, x.dtype) for x in xs),
        [pl.BlockSpec(memory_space=pltpu.HBM)] * 4,
        xs,
        flops=1 << 30,
        scratch_shapes=[pltpu.SemaphoreType.DMA((8,))],
    )
    halves = [mine[:, :part], mine[:, part:]]
    far = [swap(h, "dp", n_dp, 2) for h in halves]
    near = [swap(jnp.concatenate([h, f], axis=0), "dp", n_dp, 1) for h, f in zip(halves, far)]
    za, zb = [jnp.concatenate([f, n], axis=0) for f, n in zip(far, near)]
    shifts = (2, 1, 3)

    def accumulate(plan, pieces, acc):
        args = (*xs, w_in, w_out, *pieces) + (() if acc is None else (acc,))
        return call(
            functools.partial(
                project_pieces_kernel, plan, shifts, acc is not None, len(pieces)),
            out_shape,
            [vmem()] * len(args),
            args,
            flops=1 << 30,
            scratch_shapes=[
                pltpu.VMEM((ki, part * len(plan)), jnp.bfloat16),
                pltpu.VMEM((ko, part * len(plan)), jnp.bfloat16),
            ],
        )

    xa = swap(za, PLANE, 4, 1)
    yb = swap(zb, PLANE, 4, 2)
    acc = accumulate(((0, 0, 0, 0), (0, 1, 1, 0)), (za, zb), None)
    ya_da = swap(jnp.concatenate([za, xa], axis=0), PLANE, 4, 2)
    xb_db = swap(jnp.concatenate([zb, yb], axis=0), PLANE, 4, 1)
    acc = accumulate(((1, 0, 0, 0), (2, 1, 1, 0)), (xa, yb), acc)
    rows = za.shape[0]
    return accumulate(
        ((2, 0, 0, 0), (3, 0, 0, rows), (1, 1, 1, 0), (3, 1, 1, rows)), (ya_da, xb_db), acc)


def per_device(
    n_groups, n_dp, n_blk, train_inputs, train_cotangents, train_lengths,
    test_inputs, test_cotangents, test_lengths, proj_in, proj_out,
):
    _, tokens, width = train_inputs.shape
    xs = [a.reshape(tokens, width) for a in (
        train_inputs, train_cotangents, test_inputs, test_cotangents)]
    part = project(xs, proj_in.T, proj_out.T, n_groups, n_dp, n_blk)
    ki = part.shape[1]
    ko = ki // 2
    other = swap(part, "mp", 2, 1)
    fac, gte, gtr = call(
        moments_kernel,
        (
            jax.ShapeDtypeStruct((ki + 8, ki), jnp.float32),
            jax.ShapeDtypeStruct((1, ki // 2, ki), jnp.float32),
            jax.ShapeDtypeStruct((ki, ko), jnp.float32),
        ),
        [smem(), smem(), vmem(), vmem()],
        (train_lengths, test_lengths, part, other),
    )
    order = [(0, 0)]
    for axis, count in (("blk", n_blk), ("dp", n_dp)):
        for k in bits(count):
            fac = fac + swap(fac, axis, count, k)
            gte = jnp.concatenate([gte, swap(gte, axis, count, k)], axis=0)
            order += [(dz ^ k, db) if axis == "dp" else (dz, db ^ k) for dz, db in order]
    side = call(
        side_kernel,
        jax.ShapeDtypeStruct((ki // 2, ki), jnp.float32),
        [vmem()] * 2,
        (fac, gtr),
        flops=4 << 30,
    )
    return call(
        functools.partial(scores_kernel, order, n_blk),
        jax.ShapeDtypeStruct((1, n_dp * n_blk), jnp.float32),
        [vmem()] * 2,
        (side, gte),
    )


def solution(mesh):
    feature = P(("groups", "dp", "blk"), None, "mp")
    length = P(("groups", "dp", "blk"))
    weight = P("mp", "dp")
    shape = mesh.shape
    return jax.shard_map(
        functools.partial(per_device, shape["groups"], shape["dp"], shape["blk"]),
        mesh=mesh,
        in_specs=(feature, feature, length, feature, feature, length, weight, weight),
        out_specs=P(("groups", "dp", "blk"), None),
        check_vma=False,
    )
```

time: 62.6 us -> 52.5 us (0.84)
  waiting for transfers between devices: 27.3 us -> 14.5 us
  starting transfers between devices: 21.2 us -> 24.7 us
  local copies, waits for them, and re-layouts: 4.93 us -> 3.09 us
    ppermute x15, waiting for transfers between devices: 27.3 us -> 14.5 us  [swap(): return lax.ppermute(x, axis, [(i, i ^ k) for i in range(count)])]
    ppermute x15, starting transfers between devices: 21.2 us -> 24.7 us  [swap(): return lax.ppermute(x, axis, [(i, i ^ k) for i in range(count)])]
    unnamed x15 -> x14, local copies, waits for them, and re-layouts: 4.92 us -> 3.07 us
    pallas_call x3 -> x7, Pallas kernels: 6.62 us -> 7.16 us  [call(): pl.pallas_call(kernel, out_shape=out_shape, in_specs=in_specs, out_specs=...]
  transfers between devices with their start and end apart: 15 -> 15, of which waited for: 7 -> 12; matrix products, arithmetic and copies ran while one was open for 0% -> 0% of each run, Pallas kernels for 0% -> 10%
where the time goes in v2:
time: 52.5 us; the launch traced here: 51.8 us
  starting transfers between devices  24.7 us (47%)
  waiting for transfers between devices  14.5 us (28%)
  Pallas kernels  7.16 us (14%)
  local copies, waits for them, and re-layouts  3.09 us (6%)
  between operations  1.39 us (3%)
  other arithmetic  0.97 us (2%)
    ppermute x15, starting transfers between devices, swap(): return lax.ppermute(x, axis, [(i, i ^ k) for i in range(count)])  24.7 us
    ppermute x15, waiting for transfers between devices, swap(): return lax.ppermute(x, axis, [(i, i ^ k) for i in range(count)])  14.5 us
    pallas_call x7, Pallas kernels, call(): pl.pallas_call(kernel, out_shape=out_shape, in_specs=in_specs, out_specs=...  7.16 us
    unnamed x14, local copies, waits for them, and re-layouts  3.07 us
  transfers between devices with their start and end apart: 15, of which 12 were waited for; matrix products, arithmetic and copies ran while one was open for 0% of the time, Pallas kernels for 10%

profile of v2, /device:TPU:0, one launch (start us, length us, event | category | flops | bytes accessed | tf_op | source)
XLA Modules:
  0.0 51.8 jit_solution(13002384887981856265)
XLA Ops:
  0.0 0.8 %fusion = bf16[48,1024]{1,0:T(8,128)(2,1)S(1)} fusion(s32[]{:T(128)S(6)} %select_n.3, bf16[32,4096]{1,0:T(8,128)(2,1)} %bitcast.6, bf16[16,4096]{1,0:T(8,128)(2,1)} %bitcast.10), kind=kLoop, calls=%fused_computation.6 | loop fusion | flops 196608 | bytes 491524 | tf_op jit(solution)/shard_map/concatenate | solution.py:222
  0.9 4.1 %collective-permute-start = (bf16[48,512]{1,0:T(8,128)(2,1)S(1)}, bf16[48,512]{1,0:T(8,128)(2,1)S(1)}, u32[]{:S(2)}, u32[]{:S(2)}) collective-permute-start(bf16[48,512]{1,0:T(8,128)(2,1)S(1)} %get-tuple-element.20), channel_id=1, source_target_pairs={{0,8},{4,12},{8,0},{12,4},{1,9},{5,13},{9,1},{13,5},{2,10},{6,14},... | collective-permute-start | bytes 147464 | tf_op jit(solution)/shard_map/ppermute | solution.py:38
  5.0 0.0 copy-start.2
  5.0 0.0 copy-start.3
  5.0 0.1 collective-permute-start.4
  5.1 2.5 %collective-permute-done = bf16[48,512]{1,0:T(8,128)(2,1)S(1)} collective-permute-done((bf16[48,512]{1,0:T(8,128)(2,1)S(1)}, bf16[48,512]{1,0:T(8,128)(2,1)S(1)}, u32[]{:S(2)}, u32[]{:S(2)}) %collective-permute-start) | collective-permute-done | bytes 49184 | tf_op jit(solution)/shard_map/ppermute | solution.py:38
  7.6 2.1 %collective-permute-start.1 = (bf16[96,512]{1,0:T(8,128)(2,1)S(1)}, bf16[96,512]{1,0:T(8,128)(2,1)S(1)}, u32[]{:S(2)}, u32[]{:S(2)}) collective-permute-start(bf16[96,512]{1,0:T(8,128)(2,1)S(1)} %pad_maximum_fusion.4), channel_id=1, source_target_pairs={{0,4},{4,0},{8,12},{12,8},{1,5},{5,1},{9,13},{13,9},{2,6},{6,2},{1... | collective-permute-start | bytes 294920 | tf_op jit(solution)/shard_map/ppermute | solution.py:38
  9.6 0.4 collective-permute-done.4
  10.1 1.5 %collective-permute-start.5 = (bf16[96,512]{1,0:T(8,128)(2,1)S(1)}, bf16[96,512]{1,0:T(8,128)(2,1)S(1)}, u32[]{:S(2)}, u32[]{:S(2)}) collective-permute-start(bf16[96,512]{1,0:T(8,128)(2,1)S(1)} %pad_maximum_fusion.5), channel_id=1, source_target_pairs={{0,4},{4,0},{8,12},{12,8},{1,5},{5,1},{9,13},{13,9},{2,6},{6,2},{1... | collective-permute-start | bytes 294920 | tf_op jit(solution)/shard_map/ppermute | solution.py:38
  11.6 1.5 %collective-permute-done.1 = bf16[96,512]{1,0:T(8,128)(2,1)S(1)} collective-permute-done((bf16[96,512]{1,0:T(8,128)(2,1)S(1)}, bf16[96,512]{1,0:T(8,128)(2,1)S(1)}, u32[]{:S(2)}, u32[]{:S(2)}) %collective-permute-start.1) | collective-permute-done | bytes 98336 | tf_op jit(solution)/shard_map/ppermute | solution.py:38
  13.1 1.6 %collective-permute-start.2 = (bf16[144,512]{1,0:T(8,128)(2,1)S(1)}, bf16[144,512]{1,0:T(8,128)(2,1)S(1)}, u32[]{:S(2)}, u32[]{:S(2)}) collective-permute-start(bf16[144,512]{1,0:T(8,128)(2,1)S(1)} %constant_dynamic-update-slice_fusion.refs_6_), channel_id=1, source_target_pairs={{0,2},{2,0},{16,18},{18,16},{1,3},{3,1},{17,19},{19,17},{4,6},{6,4... | collective-permute-start | bytes 442376 | tf_op jit(solution)/shard_map/ppermute | solution.py:38
  14.7 0.1 collective-permute-done.5
  14.8 1.6 %collective-permute-start.6 = (bf16[144,512]{1,0:T(8,128)(2,1)S(1)}, bf16[144,512]{1,0:T(8,128)(2,1)S(1)}, u32[]{:S(2)}, u32[]{:S(2)}) collective-permute-start(bf16[144,512]{1,0:T(8,128)(2,1)S(1)} %constant_dynamic-update-slice_fusion.2.refs_7_), channel_id=1, source_target_pairs={{0,16},{2,18},{16,0},{18,2},{1,17},{3,19},{17,1},{19,3},{4,20},{6,... | collective-permute-start | bytes 442376 | tf_op jit(solution)/shard_map/ppermute | solution.py:38
  16.4 2.0 %collective-permute-done.2.refs_6_ = bf16[144,512]{1,0:T(8,128)(2,1)S(1)} collective-permute-done((bf16[144,512]{1,0:T(8,128)(2,1)S(1)}, bf16[144,512]{1,0:T(8,128)(2,1)S(1)}, u32[]{:S(2)}, u32[]{:S(2)}) %collective-permute-start.2) | collective-permute-done | bytes 147488 | tf_op jit(solution)/shard_map/ppermute | solution.py:38
  18.4 1.6 %collective-permute-start.3 = (bf16[288,512]{1,0:T(8,128)(2,1)S(1)}, bf16[288,512]{1,0:T(8,128)(2,1)S(1)}, u32[]{:S(2)}, u32[]{:S(2)}) collective-permute-start(bf16[288,512]{1,0:T(8,128)(2,1)S(1)} %pad_maximum_fusion), channel_id=1, source_target_pairs={{0,16},{2,18},{16,0},{18,2},{1,17},{3,19},{17,1},{19,3},{4,20},{6,... | collective-permute-start | bytes 884744 | tf_op jit(solution)/shard_map/ppermute | solution.py:38
  20.0 1.4 %collective-permute-done.6.refs_7_ = bf16[144,512]{1,0:T(8,128)(2,1)S(1)} collective-permute-done((bf16[144,512]{1,0:T(8,128)(2,1)S(1)}, bf16[144,512]{1,0:T(8,128)(2,1)S(1)}, u32[]{:S(2)}, u32[]{:S(2)}) %collective-permute-start.6) | collective-permute-done | bytes 147488 | tf_op jit(solution)/shard_map/ppermute | solution.py:38
  21.4 1.8 %collective-permute-start.7 = (bf16[288,512]{1,0:T(8,128)(2,1)S(1)}, bf16[288,512]{1,0:T(8,128)(2,1)S(1)}, u32[]{:S(2)}, u32[]{:S(2)}) collective-permute-start(bf16[288,512]{1,0:T(8,128)(2,1)S(1)} %pad_maximum_fusion.1), channel_id=1, source_target_pairs={{0,2},{2,0},{16,18},{18,16},{1,3},{3,1},{17,19},{19,17},{4,6},{6,4... | collective-permute-start | bytes 884744 | tf_op jit(solution)/shard_map/ppermute | solution.py:38
  23.2 0.0 copy-done.2
  23.2 0.0 copy-done.3
  23.2 0.0 copy-start.4
  23.2 1.2 %copy-done.4 = bf16[1,128,4096]{2,1,0:T(8,128)(2,1)S(1)} copy-done((bf16[1,128,4096]{2,1,0:T(8,128)(2,1)S(1)}, bf16[1,128,4096]{2,1,0:T(8,128)(2,1)}, u32[]{:S(2)}) %copy-start.4) | copy-done | bytes 1048600
  24.4 0.0 copy-start.5
  24.4 1.2 %copy-done.5 = bf16[1,128,4096]{2,1,0:T(8,128)(2,1)S(1)} copy-done((bf16[1,128,4096]{2,1,0:T(8,128)(2,1)S(1)}, bf16[1,128,4096]{2,1,0:T(8,128)(2,1)}, u32[]{:S(2)}) %copy-start.5) | copy-done | bytes 1048600
  25.6 0.4 shard_map.82
  26.0 0.6 %copy-done = bf16[4096,32]{0,1:T(8,128)(2,1)S(1)} copy-done((bf16[4096,32]{0,1:T(8,128)(2,1)S(1)}, bf16[4096,32]{0,1:T(8,128)(2,1)}, u32[]{:S(2)}) %copy-start) | copy-done | bytes 262168
  26.6 0.0 copy-done.1
  26.6 0.5 %shard_map.83.refs_8_ = f32[384,128]{1,0:T(8,128)S(1)} custom-call(bf16[128,4096]{1,0:T(8,128)(2,1)S(1)} %get-tuple-element.12.refs_0_, bf16[128,4096]{1,0:T(8,128)(2,1)S(1)} %get-tuple-element.13.refs_1_, bf16[128,4096]{1,0:T(8,128)(2,1)S(1)} %get-tuple-element.14.refs_2_, bf16[128,4096]{1,0:T(8,128)(2,1)S(1)} %get-tuple-element.15.refs_3_, ...), custom_call_target="tpu_custom_call" | custom-call | flops 1073741824 | bytes 4194304 | tf_op jit(solution)/shard_map/pallas_call | solution.py:26
  27.1 0.5 %shard_map.84.refs_8_ = f32[384,128]{1,0:T(8,128)S(1)} custom-call(bf16[128,4096]{1,0:T(8,128)(2,1)S(1)} %get-tuple-element.12.refs_0_, bf16[128,4096]{1,0:T(8,128)(2,1)S(1)} %get-tuple-element.13.refs_1_, bf16[128,4096]{1,0:T(8,128)(2,1)S(1)} %get-tuple-element.14.refs_2_, bf16[128,4096]{1,0:T(8,128)(2,1)S(1)} %get-tuple-element.15.refs_3_, ...), custom_call_target="tpu_custom_call" | custom-call | flops 1073741824 | bytes 4194304 | tf_op jit(solution)/shard_map/pallas_call | solution.py:26
  27.7 0.0 collective-permute-done.3.refs_6_
  27.7 0.5 collective-permute-done.7.refs_7_
  28.2 0.8 %shard_map.85.mine = f32[384,128]{1,0:T(8,128)S(1)} custom-call(bf16[128,4096]{1,0:T(8,128)(2,1)S(1)} %get-tuple-element.12.refs_0_, bf16[128,4096]{1,0:T(8,128)(2,1)S(1)} %get-tuple-element.13.refs_1_, bf16[128,4096]{1,0:T(8,128)(2,1)S(1)} %get-tuple-element.14.refs_2_, bf16[128,4096]{1,0:T(8,128)(2,1)S(1)} %get-tuple-element.15.refs_3_, ...), custom_call_target="tpu_custom_call" | custom-call | flops 1073741824 | bytes 4194304 | tf_op jit(solution)/shard_map/pallas_call | solution.py:26
  29.0 0.1 collective-permute-start.8
  30.4 0.1 collective-permute-done.8.other
  30.5 0.5 shard_map.86
  31.0 1.8 %collective-permute-start.9 = (f32[136,128]{1,0:T(8,128)S(1)}, f32[136,128]{1,0:T(8,128)S(1)}, u32[]{:S(2)}, u32[]{:S(2)}) collective-permute-start(f32[136,128]{1,0:T(8,128)S(1)} %get-tuple-element.16), channel_id=1, source_target_pairs={{0,2},{2,0},{1,3},{3,1},{4,6},{6,4},{5,7},{7,5},{8,10},{10,8},{9,1... | collective-permute-start | bytes 208904 | tf_op jit(solution)/shard_map/ppermute | solution.py:38
  32.8 0.3 collective-permute-start.12
  33.1 2.5 %collective-permute-done.9 = f32[136,128]{1,0:T(8,128)S(1)} collective-permute-done((f32[136,128]{1,0:T(8,128)S(1)}, f32[136,128]{1,0:T(8,128)S(1)}, u32[]{:S(2)}, u32[]{:S(2)}) %collective-permute-start.9) | collective-permute-done | bytes 69664 | tf_op jit(solution)/shard_map/ppermute | solution.py:38
  35.6 3.6 %collective-permute-start.10 = (f32[136,128]{1,0:T(8,128)S(1)}, f32[136,128]{1,0:T(8,128)S(1)}, u32[]{:S(2)}, u32[]{:S(2)}) collective-permute-start(f32[136,128]{1,0:T(8,128)S(1)} %add.17), channel_id=1, source_target_pairs={{0,8},{4,12},{8,0},{12,4},{1,9},{5,13},{9,1},{13,5},{2,10},{6,14},... | collective-permute-start | bytes 208904 | tf_op jit(solution)/shard_map/ppermute | solution.py:38
  39.2 0.0 collective-permute-done.12
  39.2 0.5 collective-permute-start.13
  39.7 2.8 %collective-permute-done.10 = f32[136,128]{1,0:T(8,128)S(1)} collective-permute-done((f32[136,128]{1,0:T(8,128)S(1)}, f32[136,128]{1,0:T(8,128)S(1)}, u32[]{:S(2)}, u32[]{:S(2)}) %collective-permute-start.10) | collective-permute-done | bytes 69664 | tf_op jit(solution)/shard_map/ppermute | solution.py:38
  42.5 2.3 %collective-permute-start.11 = (f32[136,128]{1,0:T(8,128)S(1)}, f32[136,128]{1,0:T(8,128)S(1)}, u32[]{:S(2)}, u32[]{:S(2)}) collective-permute-start(f32[136,128]{1,0:T(8,128)S(1)} %add.18), channel_id=1, source_target_pairs={{0,4},{4,0},{8,12},{12,8},{1,5},{5,1},{9,13},{13,9},{2,6},{6,2},{1... | collective-permute-start | bytes 208904 | tf_op jit(solution)/shard_map/ppermute | solution.py:38
  44.7 0.3 collective-permute-done.13
  45.1 1.9 %collective-permute-start.14 = (f32[4,64,128]{2,1,0:T(8,128)S(1)}, f32[4,64,128]{2,1,0:T(8,128)S(1)}, u32[]{:S(2)}, u32[]{:S(2)}) collective-permute-start(f32[4,64,128]{2,1,0:T(8,128)S(1)} %pad_maximum_fusion.3), channel_id=1, source_target_pairs={{0,4},{4,0},{8,12},{12,8},{1,5},{5,1},{9,13},{13,9},{2,6},{6,2},{1... | collective-permute-start | bytes 393224 | tf_op jit(solution)/shard_map/ppermute | solution.py:38
  47.0 0.3 collective-permute-done.11
  47.3 3.8 %shard_map.87.side_ref = f32[64,128]{1,0:T(8,128)S(1)} custom-call(f32[136,128]{1,0:T(8,128)S(1)} %add.19.fac_ref, f32[128,64]{1,0:T(8,128)S(1)} %get-tuple-element.17.gtr_ref), custom_call_target="tpu_custom_call" | custom-call | flops 4294967296 | bytes 4194304 | tf_op jit(solution)/shard_map/pallas_call | solution.py:26
  51.1 0.0 collective-permute-done.14
  51.1 0.7 %shard_map.88 = f32[1,8]{1,0:T(1,128)} custom-call(f32[64,128]{1,0:T(8,128)S(1)} %shard_map.87.side_ref, f32[8,64,128]{2,1,0:T(8,128)S(1)} %pad_maximum_fusion.2.gte_ref), custom_call_target="tpu_custom_call" | custom-call | bytes 4194304 | tf_op jit(solution)/shard_map/pallas_call | solution.py:26
  (17 shorter events, 0.2 us)
Async XLA Ops:
  0.9 6.7 %collective-permute-start = (bf16[48,512]{1,0:T(8,128)(2,1)S(1)}, bf16[48,512]{1,0:T(8,128)(2,1)S(1)}, u32[]{:S(2)}, u32[]{:S(2)}) collective-permute-start(bf16[48,512]{1,0:T(8,128)(2,1)S(1)} %get-tuple-element.20), channel_id=1, source_target_pairs={{0,8},{4,12},{8,0},{12,4},{1,9},{5,13},{9,1},{13,5},{2,10},{6,14},... | collective-permute-start | bytes 147464 | tf_op jit(solution)/shard_map/ppermute | solution.py:38
  5.0 18.2 %copy-start.2 = (bf16[1,128,4096]{2,1,0:T(8,128)(2,1)S(1)}, bf16[1,128,4096]{2,1,0:T(8,128)(2,1)}, u32[]{:S(2)}) copy-start(bf16[1,128,4096]{2,1,0:T(8,128)(2,1)} %param.8) | copy-start | bytes 3145732
  5.0 18.2 %copy-start.3 = (bf16[1,128,4096]{2,1,0:T(8,128)(2,1)S(1)}, bf16[1,128,4096]{2,1,0:T(8,128)(2,1)}, u32[]{:S(2)}) copy-start(bf16[1,128,4096]{2,1,0:T(8,128)(2,1)} %param.9) | copy-start | bytes 3145732
  5.0 5.1 %collective-permute-start.4 = (bf16[48,512]{1,0:T(8,128)(2,1)S(1)}, bf16[48,512]{1,0:T(8,128)(2,1)S(1)}, u32[]{:S(2)}, u32[]{:S(2)}) collective-permute-start(bf16[48,512]{1,0:T(8,128)(2,1)S(1)} %get-tuple-element.19), channel_id=1, source_target_pairs={{0,8},{4,12},{8,0},{12,4},{1,9},{5,13},{9,1},{13,5},{2,10},{6,14},... | collective-permute-start | bytes 147464 | tf_op jit(solution)/shard_map/ppermute | solution.py:38
  7.6 5.5 %collective-permute-start.1 = (bf16[96,512]{1,0:T(8,128)(2,1)S(1)}, bf16[96,512]{1,0:T(8,128)(2,1)S(1)}, u32[]{:S(2)}, u32[]{:S(2)}) collective-permute-start(bf16[96,512]{1,0:T(8,128)(2,1)S(1)} %pad_maximum_fusion.4), channel_id=1, source_target_pairs={{0,4},{4,0},{8,12},{12,8},{1,5},{5,1},{9,13},{13,9},{2,6},{6,2},{1... | collective-permute-start | bytes 294920 | tf_op jit(solution)/shard_map/ppermute | solution.py:38
  10.1 4.7 %collective-permute-start.5 = (bf16[96,512]{1,0:T(8,128)(2,1)S(1)}, bf16[96,512]{1,0:T(8,128)(2,1)S(1)}, u32[]{:S(2)}, u32[]{:S(2)}) collective-permute-start(bf16[96,512]{1,0:T(8,128)(2,1)S(1)} %pad_maximum_fusion.5), channel_id=1, source_target_pairs={{0,4},{4,0},{8,12},{12,8},{1,5},{5,1},{9,13},{13,9},{2,6},{6,2},{1... | collective-permute-start | bytes 294920 | tf_op jit(solution)/shard_map/ppermute | solution.py:38
  13.1 5.2 %collective-permute-start.2 = (bf16[144,512]{1,0:T(8,128)(2,1)S(1)}, bf16[144,512]{1,0:T(8,128)(2,1)S(1)}, u32[]{:S(2)}, u32[]{:S(2)}) collective-permute-start(bf16[144,512]{1,0:T(8,128)(2,1)S(1)} %constant_dynamic-update-slice_fusion.refs_6_), channel_id=1, source_target_pairs={{0,2},{2,0},{16,18},{18,16},{1,3},{3,1},{17,19},{19,17},{4,6},{6,4... | collective-permute-start | bytes 442376 | tf_op jit(solution)/shard_map/ppermute | solution.py:38
  14.8 6.6 %collective-permute-start.6 = (bf16[144,512]{1,0:T(8,128)(2,1)S(1)}, bf16[144,512]{1,0:T(8,128)(2,1)S(1)}, u32[]{:S(2)}, u32[]{:S(2)}) collective-permute-start(bf16[144,512]{1,0:T(8,128)(2,1)S(1)} %constant_dynamic-update-slice_fusion.2.refs_7_), channel_id=1, source_target_pairs={{0,16},{2,18},{16,0},{18,2},{1,17},{3,19},{17,1},{19,3},{4,20},{6,... | collective-permute-start | bytes 442376 | tf_op jit(solution)/shard_map/ppermute | solution.py:38
  18.4 9.3 %collective-permute-start.3 = (bf16[288,512]{1,0:T(8,128)(2,1)S(1)}, bf16[288,512]{1,0:T(8,128)(2,1)S(1)}, u32[]{:S(2)}, u32[]{:S(2)}) collective-permute-start(bf16[288,512]{1,0:T(8,128)(2,1)S(1)} %pad_maximum_fusion), channel_id=1, source_target_pairs={{0,16},{2,18},{16,0},{18,2},{1,17},{3,19},{17,1},{19,3},{4,20},{6,... | collective-permute-start | bytes 884744 | tf_op jit(solution)/shard_map/ppermute | solution.py:38
  21.4 6.8 %collective-permute-start.7 = (bf16[288,512]{1,0:T(8,128)(2,1)S(1)}, bf16[288,512]{1,0:T(8,128)(2,1)S(1)}, u32[]{:S(2)}, u32[]{:S(2)}) collective-permute-start(bf16[288,512]{1,0:T(8,128)(2,1)S(1)} %pad_maximum_fusion.1), channel_id=1, source_target_pairs={{0,2},{2,0},{16,18},{18,16},{1,3},{3,1},{17,19},{19,17},{4,6},{6,4... | collective-permute-start | bytes 884744 | tf_op jit(solution)/shard_map/ppermute | solution.py:38
  23.2 1.2 %copy-start.4 = (bf16[1,128,4096]{2,1,0:T(8,128)(2,1)S(1)}, bf16[1,128,4096]{2,1,0:T(8,128)(2,1)}, u32[]{:S(2)}) copy-start(bf16[1,128,4096]{2,1,0:T(8,128)(2,1)} %param.11) | copy-start | bytes 3145732
  24.4 1.2 %copy-start.5 = (bf16[1,128,4096]{2,1,0:T(8,128)(2,1)S(1)}, bf16[1,128,4096]{2,1,0:T(8,128)(2,1)}, u32[]{:S(2)}) copy-start(bf16[1,128,4096]{2,1,0:T(8,128)(2,1)} %param.12) | copy-start | bytes 3145732
  25.6 0.9 %copy-start = (bf16[4096,32]{0,1:T(8,128)(2,1)S(1)}, bf16[4096,32]{0,1:T(8,128)(2,1)}, u32[]{:S(2)}) copy-start(bf16[4096,32]{0,1:T(8,128)(2,1)} %param.14) | copy-start | bytes 786436
  25.6 1.0 %copy-start.1 = (bf16[4096,16]{0,1:T(8,128)(2,1)S(1)}, bf16[4096,16]{0,1:T(8,128)(2,1)}, u32[]{:S(2)}) copy-start(bf16[4096,16]{0,1:T(8,128)(2,1)} %param.15) | copy-start | bytes 393220
  29.0 1.5 %collective-permute-start.8 = (f32[384,128]{1,0:T(8,128)S(1)}, f32[384,128]{1,0:T(8,128)S(1)}, u32[]{:S(2)}, u32[]{:S(2)}) collective-permute-start(f32[384,128]{1,0:T(8,128)S(1)} %shard_map.85.mine), channel_id=1, source_target_pairs={{0,1},{1,0},{2,3},{3,2},{4,5},{5,4},{6,7},{7,6},{8,9},{9,8},{10,11... | collective-permute-start | bytes 589832 | tf_op jit(solution)/shard_map/ppermute | solution.py:38
  31.0 4.6 %collective-permute-start.9 = (f32[136,128]{1,0:T(8,128)S(1)}, f32[136,128]{1,0:T(8,128)S(1)}, u32[]{:S(2)}, u32[]{:S(2)}) collective-permute-start(f32[136,128]{1,0:T(8,128)S(1)} %get-tuple-element.16), channel_id=1, source_target_pairs={{0,2},{2,0},{1,3},{3,1},{4,6},{6,4},{5,7},{7,5},{8,10},{10,8},{9,1... | collective-permute-start | bytes 208904 | tf_op jit(solution)/shard_map/ppermute | solution.py:38
  32.8 6.4 %collective-permute-start.12 = (f32[1,64,128]{2,1,0:T(8,128)S(1)}, f32[1,64,128]{2,1,0:T(8,128)S(1)}, u32[]{:S(2)}, u32[]{:S(2)}) collective-permute-start(f32[1,64,128]{2,1,0:T(8,128)S(1)} %get-tuple-element.18), channel_id=1, source_target_pairs={{0,2},{2,0},{1,3},{3,1},{4,6},{6,4},{5,7},{7,5},{8,10},{10,8},{9,1... | collective-permute-start | bytes 98312 | tf_op jit(solution)/shard_map/ppermute | solution.py:38
  35.6 6.8 %collective-permute-start.10 = (f32[136,128]{1,0:T(8,128)S(1)}, f32[136,128]{1,0:T(8,128)S(1)}, u32[]{:S(2)}, u32[]{:S(2)}) collective-permute-start(f32[136,128]{1,0:T(8,128)S(1)} %add.17), channel_id=1, source_target_pairs={{0,8},{4,12},{8,0},{12,4},{1,9},{5,13},{9,1},{13,5},{2,10},{6,14},... | collective-permute-start | bytes 208904 | tf_op jit(solution)/shard_map/ppermute | solution.py:38
  39.2 5.9 %collective-permute-start.13 = (f32[2,64,128]{2,1,0:T(8,128)S(1)}, f32[2,64,128]{2,1,0:T(8,128)S(1)}, u32[]{:S(2)}, u32[]{:S(2)}) collective-permute-start(f32[2,64,128]{2,1,0:T(8,128)S(1)} %pad_maximum_fusion.6), channel_id=1, source_target_pairs={{0,8},{4,12},{8,0},{12,4},{1,9},{5,13},{9,1},{13,5},{2,10},{6,14},... | collective-permute-start | bytes 196616 | tf_op jit(solution)/shard_map/ppermute | solution.py:38
  42.5 4.8 %collective-permute-start.11 = (f32[136,128]{1,0:T(8,128)S(1)}, f32[136,128]{1,0:T(8,128)S(1)}, u32[]{:S(2)}, u32[]{:S(2)}) collective-permute-start(f32[136,128]{1,0:T(8,128)S(1)} %add.18), channel_id=1, source_target_pairs={{0,4},{4,0},{8,12},{12,8},{1,5},{5,1},{9,13},{13,9},{2,6},{6,2},{1... | collective-permute-start | bytes 208904 | tf_op jit(solution)/shard_map/ppermute | solution.py:38
  45.1 6.0 %collective-permute-start.14 = (f32[4,64,128]{2,1,0:T(8,128)S(1)}, f32[4,64,128]{2,1,0:T(8,128)S(1)}, u32[]{:S(2)}, u32[]{:S(2)}) collective-permute-start(f32[4,64,128]{2,1,0:T(8,128)S(1)} %pad_maximum_fusion.3), channel_id=1, source_target_pairs={{0,4},{4,0},{8,12},{12,8},{1,5},{5,1},{9,13},{13,9},{2,6},{6,2},{1... | collective-permute-start | bytes 393224 | tf_op jit(solution)/shard_map/ppermute | solution.py:38

commit v3 on v2

--- a/solution.py
+++ b/solution.py
@@ -42,8 +42,8 @@
     return [1 << s for s in reversed(range(count.bit_length() - 1))]
 
 
-def load_kernel(*refs):
-    srcs, dsts, sem = refs[:4], refs[4:8], refs[8]
+def load_kernel(n, *refs):
+    srcs, dsts, token, sem = refs[:n], refs[n : 2 * n], refs[2 * n], refs[2 * n + 1]
     copies = []
     for i, (src, dst) in enumerate(zip(srcs, dsts)):
         rows = src.shape[0] // 2
@@ -52,6 +52,7 @@
             copies.append(pltpu.make_async_copy(src.at[part], dst.at[part], sem.at[2 * i + h]))
     for c in copies:
         c.start()
+    token[...] = jnp.zeros_like(token)
     for c in copies:
         c.wait()
 
@@ -81,7 +82,7 @@
     store_products(xs, gs, None, out_ref)
 
 
-def project_pieces_kernel(plan, shifts, with_acc, n_pieces, *refs):
+def project_pieces_kernel(plan, with_acc, n_pieces, *refs):
     x_refs, (own_in, own_out) = refs[:4], refs[4:6]
     pieces = refs[6 : 6 + n_pieces]
     acc_ref = refs[6 + n_pieces] if with_acc else None
@@ -89,20 +90,21 @@
     z = lax.axis_index("dp")
     q = lax.axis_index(PLANE)
     rin, rout = own_in.shape[0], own_out.shape[0]
-    width = pieces[0].shape[1]
+    quarter = own_in.shape[1] // 4
     xs, gs = [0.0, 0.0], [0.0, 0.0]
-    for n, (dq, half, p, row) in enumerate(plan):
-        start = pl.multiple_of(((q ^ dq) * 2 + half) * width, width)
+    at = 0
+    for dq, col, width, rows in plan:
+        start = pl.multiple_of((q ^ dq) * quarter + col, 128)
         cols = pl.ds(start, width)
-        here = slice(n * width, (n + 1) * width)
+        here = slice(at, at + width)
+        at += width
         w_in[pl.ds(pl.multiple_of(z * rin, rin), rin), here] = own_in[:, cols]
         w_out[pl.ds(pl.multiple_of(z * rout, rout), rout), here] = own_out[:, cols]
-        for i, k in enumerate(shifts):
-            at = row + i * (rin + rout)
+        for p, row, k in rows:
             dst_in = pl.multiple_of((z ^ k) * rin, rin)
             dst_out = pl.multiple_of((z ^ k) * rout, rout)
-            w_in[pl.ds(dst_in, rin), here] = pieces[p][at : at + rin, :]
-            w_out[pl.ds(dst_out, rout), here] = pieces[p][at + rin : at + rin + rout, :]
+            w_in[pl.ds(dst_in, rin), here] = pieces[p][row : row + rin, :]
+            w_out[pl.ds(dst_out, rout), here] = pieces[p][row + rin : row + rin + rout, :]
         for m in range(2):
             xs[m] += nt(x_refs[2 * m][:, cols], w_in[:, here])
             gs[m] += nt(x_refs[2 * m + 1][:, cols], w_out[:, here])
@@ -217,47 +219,61 @@
         return call(project_kernel, out_shape, [vmem()] * 6, (*xs, w_in, w_out))
 
     part = width // 8
+    shard = rin + rout
     q = lax.axis_index(PLANE)
-    mine = lax.dynamic_slice(
-        jnp.concatenate([w_in, w_out], axis=0), (0, q * 2 * part), (rin + rout, 2 * part))
-    xs = call(
-        load_kernel,
-        tuple(jax.ShapeDtypeStruct(x.shape, x.dtype) for x in xs),
-        [pl.BlockSpec(memory_space=pltpu.HBM)] * 4,
-        xs,
+    whole = jnp.concatenate([w_in, w_out], axis=0)
+    mine = lax.dynamic_slice(whole, (0, q * 2 * part), (shard, 2 * part))
+    opposite = lax.dynamic_slice(whole, (0, (q ^ 3) * 2 * part), (shard, 2 * part))
+    *xs, w_in, w_out, token = call(
+        functools.partial(load_kernel, 6),
+        tuple(pltpu.VMEM(x.shape, x.dtype) for x in (*xs, w_in, w_out))
+        + (jax.ShapeDtypeStruct((1, part), jnp.bfloat16),),
+        [pl.BlockSpec(memory_space=pltpu.HBM)] * 6,
+        [pltpu.with_memory_space_constraint(x, pltpu.HBM) for x in (*xs, w_in, w_out)],
         flops=1 << 30,
-        scratch_shapes=[pltpu.SemaphoreType.DMA((8,))],
+        scratch_shapes=[pltpu.SemaphoreType.DMA((12,))],
     )
     halves = [mine[:, :part], mine[:, part:]]
     far = [swap(h, "dp", n_dp, 2) for h in halves]
-    near = [swap(jnp.concatenate([h, f], axis=0), "dp", n_dp, 1) for h, f in zip(halves, far)]
+    far_op = swap(opposite, "dp", n_dp, 2)
+    doubled = [jnp.concatenate([h, f], axis=0) for h, f in zip(halves, far)]
+    near = [swap(doubled[0] + token, "dp", n_dp, 1), swap(doubled[1], "dp", n_dp, 1)]
+    near_op = swap(jnp.concatenate([opposite, far_op], axis=0), "dp", n_dp, 1)
     za, zb = [jnp.concatenate([f, n], axis=0) for f, n in zip(far, near)]
-    shifts = (2, 1, 3)
+    xa, ya = swap(za, PLANE, 4, 1), swap(za, PLANE, 4, 2)
+    xb, yb = swap(zb, PLANE, 4, 1), swap(zb, PLANE, 4, 2)
 
     def accumulate(plan, pieces, acc):
         args = (*xs, w_in, w_out, *pieces) + (() if acc is None else (acc,))
+        total = sum(width for _, _, width, _ in plan)
         return call(
-            functools.partial(
-                project_pieces_kernel, plan, shifts, acc is not None, len(pieces)),
+            functools.partial(project_pieces_kernel, plan, acc is not None, len(pieces)),
             out_shape,
             [vmem()] * len(args),
             args,
             flops=1 << 30,
             scratch_shapes=[
-                pltpu.VMEM((ki, part * len(plan)), jnp.bfloat16),
-                pltpu.VMEM((ko, part * len(plan)), jnp.bfloat16),
+                pltpu.VMEM((ki, total), jnp.bfloat16),
+                pltpu.VMEM((ko, total), jnp.bfloat16),
             ],
         )
 
-    xa = swap(za, PLANE, 4, 1)
-    yb = swap(zb, PLANE, 4, 2)
-    acc = accumulate(((0, 0, 0, 0), (0, 1, 1, 0)), (za, zb), None)
-    ya_da = swap(jnp.concatenate([za, xa], axis=0), PLANE, 4, 2)
-    xb_db = swap(jnp.concatenate([zb, yb], axis=0), PLANE, 4, 1)
-    acc = accumulate(((1, 0, 0, 0), (2, 1, 1, 0)), (xa, yb), acc)
-    rows = za.shape[0]
+    def stacked(p):
+        return tuple((p, i * shard, k) for i, k in enumerate((2, 1, 3)))
+
+    acc = accumulate(
+        ((0, 0, part, stacked(0)), (0, part, part, stacked(1))), (za, zb), None)
+    acc = accumulate(
+        ((1, 0, part, stacked(0)), (2, 0, part, stacked(1))), (xa, ya), acc)
     return accumulate(
-        ((2, 0, 0, 0), (3, 0, 0, rows), (1, 1, 1, 0), (3, 1, 1, rows)), (ya_da, xb_db), acc)
+        (
+            (1, part, part, stacked(0)),
+            (2, part, part, stacked(1)),
+            (3, 0, 2 * part, ((2, 0, 2), (3, 0, 1), (3, shard, 3))),
+        ),
+        (xb, yb, far_op, near_op),
+        acc,
+    )
 
 
 def per_device(

time: 52.5 us -> 55.2 us (1.051)
  other arithmetic: 0.97 us -> 4.34 us
  starting transfers between devices: 24.7 us -> 21.5 us
  Pallas kernels: 7.16 us -> 9.98 us
    ppermute x15 -> x17, starting transfers between devices: 24.7 us -> 21.5 us  [swap(): return lax.ppermute(x, axis, [(i, i ^ k) for i in range(count)])]
    pallas_call x7, Pallas kernels: 7.16 us -> 9.98 us  [call(): pl.pallas_call(kernel, out_shape=out_shape, in_specs=in_specs, out_specs=...]
    concatenate x5 -> x3, other arithmetic: 0.9 us -> 3.32 us  [the longest x1 1.53 us: project(): whole = jnp.concatenate([w_in, w_out], axis=0)]
    add x0 -> x1, other arithmetic: none -> 0.93 us  [project(): doubled[0] + token]
    slice x1, local copies, waits for them, and re-layouts: 0.01 us -> 0.65 us  [project(): halves = [mine[:, :part], mine[:, part:]]]
    unnamed x14 -> x6, local copies, waits for them, and re-layouts: 3.07 us -> 2.59 us
    ppermute x15 -> x17, waiting for transfers between devices: 14.5 us -> 14.2 us  [swap(): return lax.ppermute(x, axis, [(i, i ^ k) for i in range(count)])]
  transfers between devices with their start and end apart: 15 -> 17, of which waited for: 12 -> 9; matrix products, arithmetic and copies ran while one was open for 0% -> 8% of each run, Pallas kernels for 10% -> 13%
where the time goes in v3:
time: 55.2 us; the launch traced here: 54.7 us
  starting transfers between devices  21.5 us (39%)
  waiting for transfers between devices  14.2 us (26%)
  Pallas kernels  9.98 us (18%)
  other arithmetic  4.34 us (8%)
  local copies, waits for them, and re-layouts  3.25 us (6%)
  between operations  1.39 us (3%)
    ppermute x17, starting transfers between devices, swap(): return lax.ppermute(x, axis, [(i, i ^ k) for i in range(count)])  21.5 us
    ppermute x17, waiting for transfers between devices, swap(): return lax.ppermute(x, axis, [(i, i ^ k) for i in range(count)])  14.2 us
    pallas_call x7, Pallas kernels, call(): pl.pallas_call(kernel, out_shape=out_shape, in_specs=in_specs, out_specs=...  9.98 us
    unnamed x6, local copies, waits for them, and re-layouts  2.59 us
    concatenate x1, other arithmetic, project(): whole = jnp.concatenate([w_in, w_out], axis=0)  1.53 us
  transfers between devices with their start and end apart: 17, of which 9 were waited for; matrix products, arithmetic and copies ran while one was open for 8% of the time, Pallas kernels for 13%

profile of v3, /device:TPU:0, one launch (start us, length us, event | category | flops | bytes accessed | tf_op | source)
XLA Modules:
  0.0 54.7 jit_solution(7389584020826207804)
XLA Ops:
  0.0 1.5 %fusion = (bf16[48,1024]{1,0:T(8,128)(2,1)}, bf16[48,1024]{1,0:T(8,128)(2,1)S(1)}) fusion(s32[]{:T(128)S(6)} %select_n.7, bf16[32,4096]{1,0:T(8,128)(2,1)} %bitcast.6, bf16[16,4096]{1,0:T(8,128)(2,1)} %bitcast.12, s32[]{:T(128)S(6)} %select_n.6), kind=kLoop, calls=%fused_computation.7 | loop fusion | flops 393216 | bytes 589832 | tf_op jit(solution)/shard_map/concatenate | solution.py:224
  1.5 0.6 %fusion.2 = (bf16[48,512]{1,0:T(8,128)(2,1)}, bf16[48,512]{1,0:T(8,128)(2,1)}) fusion(bf16[48,1024]{1,0:T(8,128)(2,1)S(1)} %get-tuple-element.26), kind=kLoop, calls=%fused_computation.16 | loop fusion | bytes 196608 | tf_op jit(solution)/shard_map/slice | solution.py:236
  2.2 4.0 %collective-permute-start.6 = (bf16[48,512]{1,0:T(8,128)(2,1)}, bf16[48,512]{1,0:T(8,128)(2,1)}, u32[]{:S(2)}, u32[]{:S(2)}) collective-permute-start(bf16[48,512]{1,0:T(8,128)(2,1)} %get-tuple-element.27), channel_id=1, source_target_pairs={{0,8},{4,12},{8,0},{12,4},{1,9},{5,13},{9,1},{13,5},{2,10},{6,14},... | collective-permute-start | bytes 147464 | tf_op jit(solution)/shard_map/ppermute | solution.py:38
  6.2 0.0 collective-permute-start
  6.3 2.9 %collective-permute-start.4 = (bf16[48,1024]{1,0:T(8,128)(2,1)}, bf16[48,1024]{1,0:T(8,128)(2,1)}, u32[]{:S(2)}, u32[]{:S(2)}) collective-permute-start(bf16[48,1024]{1,0:T(8,128)(2,1)} %get-tuple-element.25), channel_id=1, source_target_pairs={{0,8},{4,12},{8,0},{12,4},{1,9},{5,13},{9,1},{13,5},{2,10},{6,14},... | collective-permute-start | bytes 294920 | tf_op jit(solution)/shard_map/ppermute | solution.py:38
  9.1 2.3 %shard_map.82 = (bf16[128,4096]{1,0:T(8,128)(2,1)S(1)}, bf16[128,4096]{1,0:T(8,128)(2,1)S(1)}, bf16[128,4096]{1,0:T(8,128)(2,1)S(1)}, bf16[128,4096]{1,0:T(8,128...) custom-call(bf16[128,4096]{1,0:T(8,128)(2,1)} %bitcast.8, ...), custom_call_target="tpu_custom_call" | custom-call | flops 1073741824 | bytes 4194304 | tf_op jit(solution)/shard_map/pallas_call | solution.py:26
  11.5 1.0 %copy-done = bf16[128,4096]{1,0:T(8,128)(2,1)} copy-done((bf16[128,4096]{1,0:T(8,128)(2,1)}, bf16[128,4096]{1,0:T(8,128)(2,1)S(1)}, u32[]{:S(2)}) %copy-start) | copy-done | bytes 1048600
  12.5 0.0 collective-permute-done.6
  12.5 0.9 %maximum_add_fusion = bf16[96,512]{1,0:T(8,128)(2,1)S(1)} fusion(bf16[48,512]{1,0:T(8,128)(2,1)} %collective-permute-done.6, bf16[48,512]{1,0:T(8,128)(2,1)} %get-tuple-element.27, bf16[512]{0:T(512)(128)(2,1)S(1)} %reduce), kind=kLoop, calls=%fused_computation.10 | loop fusion | flops 294912 | bytes 197632 | tf_op jit(solution)/shard_map/add | solution.py:240
  13.4 1.6 %collective-permute-start.7 = (bf16[96,512]{1,0:T(8,128)(2,1)S(1)}, bf16[96,512]{1,0:T(8,128)(2,1)S(1)}, u32[]{:S(2)}, u32[]{:S(2)}) collective-permute-start(bf16[96,512]{1,0:T(8,128)(2,1)S(1)} %maximum_add_fusion), channel_id=1, source_target_pairs={{0,4},{4,0},{8,12},{12,8},{1,5},{5,1},{9,13},{13,9},{2,6},{6,2},{1... | collective-permute-start | bytes 294920 | tf_op jit(solution)/shard_map/ppermute | solution.py:38
  15.1 0.0 collective-permute-done
  15.1 0.8 %pad_maximum_fusion.3 = bf16[96,512]{1,0:T(8,128)(2,1)S(1)} fusion(bf16[48,512]{1,0:T(8,128)(2,1)} %collective-permute-done, bf16[48,512]{1,0:T(8,128)(2,1)} %get-tuple-element.28), kind=kLoop, calls=%fused_computation.9 | loop fusion | flops 196608 | bytes 196608 | tf_op jit(solution)/shard_map/concatenate | solution.py:239
  15.9 0.5 collective-permute-start.1
  16.4 0.8 %constant_dynamic-update-slice_fusion.3 = bf16[144,512]{1,0:T(8,128)(2,1)S(1)} fusion(bf16[48,512]{1,0:T(8,128)(2,1)} %collective-permute-done.6), kind=kLoop, calls=%fused_computation.15 | loop fusion | bytes 98304
  17.2 0.8 %constant_dynamic-update-slice_fusion.1 = bf16[144,512]{1,0:T(8,128)(2,1)S(1)} fusion(bf16[48,512]{1,0:T(8,128)(2,1)} %collective-permute-done), kind=kLoop, calls=%fused_computation.13 | loop fusion | bytes 98304
  18.0 0.0 collective-permute-done.4.refs_8_
  18.0 1.0 %pad_maximum_fusion.1 = bf16[96,1024]{1,0:T(8,128)(2,1)S(1)} fusion(bf16[48,1024]{1,0:T(8,128)(2,1)} %collective-permute-done.4.refs_8_, bf16[48,1024]{1,0:T(8,128)(2,1)} %get-tuple-element.25), kind=kLoop, calls=%fused_computation.5 | loop fusion | flops 393216 | bytes 393216 | tf_op jit(solution)/shard_map/concatenate | solution.py:241
  19.0 1.6 %collective-permute-start.5 = (bf16[96,1024]{1,0:T(8,128)(2,1)S(1)}, bf16[96,1024]{1,0:T(8,128)(2,1)S(1)}, u32[]{:S(2)}, u32[]{:S(2)}) collective-permute-start(bf16[96,1024]{1,0:T(8,128)(2,1)S(1)} %pad_maximum_fusion.1), channel_id=1, source_target_pairs={{0,4},{4,0},{8,12},{12,8},{1,5},{5,1},{9,13},{13,9},{2,6},{6,2},{1... | collective-permute-start | bytes 589832 | tf_op jit(solution)/shard_map/ppermute | solution.py:38
  20.6 0.0 collective-permute-done.7
  20.6 1.6 %collective-permute-start.8 = (bf16[144,512]{1,0:T(8,128)(2,1)S(1)}, bf16[144,512]{1,0:T(8,128)(2,1)S(1)}, u32[]{:S(2)}, u32[]{:S(2)}) collective-permute-start(bf16[144,512]{1,0:T(8,128)(2,1)S(1)} %constant_dynamic-update-slice_fusion.2.refs_6_), channel_id=1, source_target_pairs={{0,2},{2,0},{16,18},{18,16},{1,3},{3,1},{17,19},{19,17},{4,6},{6,4... | collective-permute-start | bytes 442376 | tf_op jit(solution)/shard_map/ppermute | solution.py:38
  22.2 1.5 %collective-permute-start.9 = (bf16[144,512]{1,0:T(8,128)(2,1)S(1)}, bf16[144,512]{1,0:T(8,128)(2,1)S(1)}, u32[]{:S(2)}, u32[]{:S(2)}) collective-permute-start(bf16[144,512]{1,0:T(8,128)(2,1)S(1)} %constant_dynamic-update-slice_fusion.2.refs_6_), channel_id=1, source_target_pairs={{0,16},{2,18},{16,0},{18,2},{1,17},{3,19},{17,1},{19,3},{4,20},{6,... | collective-permute-start | bytes 442376 | tf_op jit(solution)/shard_map/ppermute | solution.py:38
  23.7 0.0 collective-permute-done.1
  23.7 0.6 %collective-permute-start.2 = (bf16[144,512]{1,0:T(8,128)(2,1)S(1)}, bf16[144,512]{1,0:T(8,128)(2,1)S(1)}, u32[]{:S(2)}, u32[]{:S(2)}) collective-permute-start(bf16[144,512]{1,0:T(8,128)(2,1)S(1)} %constant_dynamic-update-slice_fusion.refs_7_), channel_id=1, source_target_pairs={{0,2},{2,0},{16,18},{18,16},{1,3},{3,1},{17,19},{19,17},{4,6},{6,4... | collective-permute-start | bytes 442376 | tf_op jit(solution)/shard_map/ppermute | solution.py:38
  24.3 0.5 collective-permute-start.3
  24.8 0.5 shard_map.83.refs_8_
  25.4 1.8 %collective-permute-done.8.refs_6_ = bf16[144,512]{1,0:T(8,128)(2,1)S(1)} collective-permute-done((bf16[144,512]{1,0:T(8,128)(2,1)S(1)}, bf16[144,512]{1,0:T(8,128)(2,1)S(1)}, u32[]{:S(2)}, u32[]{:S(2)}) %collective-permute-start.8) | collective-permute-done | bytes 147488 | tf_op jit(solution)/shard_map/ppermute | solution.py:38
  27.1 0.3 collective-permute-done.9.refs_7_
  27.4 0.5 shard_map.84.refs_10_
  27.9 1.0 %collective-permute-done.2.refs_6_ = bf16[144,512]{1,0:T(8,128)(2,1)S(1)} collective-permute-done((bf16[144,512]{1,0:T(8,128)(2,1)S(1)}, bf16[144,512]{1,0:T(8,128)(2,1)S(1)}, u32[]{:S(2)}, u32[]{:S(2)}) %collective-permute-start.2) | collective-permute-done | bytes 147488 | tf_op jit(solution)/shard_map/ppermute | solution.py:38
  28.9 0.5 collective-permute-done.3.refs_7_
  29.5 1.7 %shard_map.85.mine = f32[384,128]{1,0:T(8,128)S(1)} custom-call(bf16[128,4096]{1,0:T(8,128)(2,1)S(1)} %get-tuple-element.15.refs_0_, bf16[128,4096]{1,0:T(8,128)(2,1)S(1)} %get-tuple-element.16.refs_1_, bf16[128,4096]{1,0:T(8,128)(2,1)S(1)} %get-tuple-element.17.refs_2_, bf16[128,4096]{1,0:T(8,128)(2,1)S(1)} %copy-done.1, ...), custom_call_target="tpu_custom_call" | custom-call | flops 1073741824 | bytes 4194304 | tf_op jit(solution)/shard_map/pallas_call | solution.py:26
  31.2 0.1 collective-permute-start.10
  32.5 0.1 collective-permute-done.10.other
  32.7 0.5 shard_map.86
  33.2 1.5 %collective-permute-start.11 = (f32[136,128]{1,0:T(8,128)S(1)}, f32[136,128]{1,0:T(8,128)S(1)}, u32[]{:S(2)}, u32[]{:S(2)}) collective-permute-start(f32[136,128]{1,0:T(8,128)S(1)} %get-tuple-element.22), channel_id=1, source_target_pairs={{0,2},{2,0},{1,3},{3,1},{4,6},{6,4},{5,7},{7,5},{8,10},{10,8},{9,1... | collective-permute-start | bytes 208904 | tf_op jit(solution)/shard_map/ppermute | solution.py:38
  34.7 0.5 collective-permute-start.14
  35.2 2.8 %collective-permute-done.11 = f32[136,128]{1,0:T(8,128)S(1)} collective-permute-done((f32[136,128]{1,0:T(8,128)S(1)}, f32[136,128]{1,0:T(8,128)S(1)}, u32[]{:S(2)}, u32[]{:S(2)}) %collective-permute-start.11) | collective-permute-done | bytes 69664 | tf_op jit(solution)/shard_map/ppermute | solution.py:38
  38.0 2.6 %collective-permute-start.12 = (f32[136,128]{1,0:T(8,128)S(1)}, f32[136,128]{1,0:T(8,128)S(1)}, u32[]{:S(2)}, u32[]{:S(2)}) collective-permute-start(f32[136,128]{1,0:T(8,128)S(1)} %add.34), channel_id=1, source_target_pairs={{0,8},{4,12},{8,0},{12,4},{1,9},{5,13},{9,1},{13,5},{2,10},{6,14},... | collective-permute-start | bytes 208904 | tf_op jit(solution)/shard_map/ppermute | solution.py:38
  40.6 0.0 collective-permute-done.14
  40.6 0.5 %collective-permute-start.15 = (f32[2,64,128]{2,1,0:T(8,128)S(1)}, f32[2,64,128]{2,1,0:T(8,128)S(1)}, u32[]{:S(2)}, u32[]{:S(2)}) collective-permute-start(f32[2,64,128]{2,1,0:T(8,128)S(1)} %pad_maximum_fusion.4), channel_id=1, source_target_pairs={{0,8},{4,12},{8,0},{12,4},{1,9},{5,13},{9,1},{13,5},{2,10},{6,14},... | collective-permute-start | bytes 196616 | tf_op jit(solution)/shard_map/ppermute | solution.py:38
  41.2 4.2 %collective-permute-done.12 = f32[136,128]{1,0:T(8,128)S(1)} collective-permute-done((f32[136,128]{1,0:T(8,128)S(1)}, f32[136,128]{1,0:T(8,128)S(1)}, u32[]{:S(2)}, u32[]{:S(2)}) %collective-permute-start.12) | collective-permute-done | bytes 69664 | tf_op jit(solution)/shard_map/ppermute | solution.py:38
  45.4 0.6 %collective-permute-start.13 = (f32[136,128]{1,0:T(8,128)S(1)}, f32[136,128]{1,0:T(8,128)S(1)}, u32[]{:S(2)}, u32[]{:S(2)}) collective-permute-start(f32[136,128]{1,0:T(8,128)S(1)} %add.35), channel_id=1, source_target_pairs={{0,4},{4,0},{8,12},{12,8},{1,5},{5,1},{9,13},{13,9},{2,6},{6,2},{1... | collective-permute-start | bytes 208904 | tf_op jit(solution)/shard_map/ppermute | solution.py:38
  46.0 0.8 %collective-permute-done.15 = f32[2,64,128]{2,1,0:T(8,128)S(1)} collective-permute-done((f32[2,64,128]{2,1,0:T(8,128)S(1)}, f32[2,64,128]{2,1,0:T(8,128)S(1)}, u32[]{:S(2)}, u32[]{:S(2)}) %collective-permute-start.15) | collective-permute-done | bytes 65568 | tf_op jit(solution)/shard_map/ppermute | solution.py:38
  46.8 0.8 %collective-permute-start.16 = (f32[4,64,128]{2,1,0:T(8,128)S(1)}, f32[4,64,128]{2,1,0:T(8,128)S(1)}, u32[]{:S(2)}, u32[]{:S(2)}) collective-permute-start(f32[4,64,128]{2,1,0:T(8,128)S(1)} %pad_maximum_fusion.2), channel_id=1, source_target_pairs={{0,4},{4,0},{8,12},{12,8},{1,5},{5,1},{9,13},{13,9},{2,6},{6,2},{1... | collective-permute-start | bytes 393224 | tf_op jit(solution)/shard_map/ppermute | solution.py:38
  47.6 2.7 %collective-permute-done.13 = f32[136,128]{1,0:T(8,128)S(1)} collective-permute-done((f32[136,128]{1,0:T(8,128)S(1)}, f32[136,128]{1,0:T(8,128)S(1)}, u32[]{:S(2)}, u32[]{:S(2)}) %collective-permute-start.13) | collective-permute-done | bytes 69664 | tf_op jit(solution)/shard_map/ppermute | solution.py:38
  50.3 3.8 %shard_map.87.side_ref = f32[64,128]{1,0:T(8,128)S(1)} custom-call(f32[136,128]{1,0:T(8,128)S(1)} %add.36.fac_ref, f32[128,64]{1,0:T(8,128)S(1)} %get-tuple-element.23.gtr_ref), custom_call_target="tpu_custom_call" | custom-call | flops 4294967296 | bytes 4194304 | tf_op jit(solution)/shard_map/pallas_call | solution.py:26
  54.1 0.0 collective-permute-done.16
  54.1 0.7 %shard_map.88 = f32[1,8]{1,0:T(1,128)} custom-call(f32[64,128]{1,0:T(8,128)S(1)} %shard_map.87.side_ref, f32[8,64,128]{2,1,0:T(8,128)S(1)} %pad_maximum_fusion.gte_ref), custom_call_target="tpu_custom_call" | custom-call | bytes 4194304 | tf_op jit(solution)/shard_map/pallas_call | solution.py:26
  (13 shorter events, 0.1 us)
Async XLA Ops:
  2.2 10.3 %collective-permute-start.6 = (bf16[48,512]{1,0:T(8,128)(2,1)}, bf16[48,512]{1,0:T(8,128)(2,1)}, u32[]{:S(2)}, u32[]{:S(2)}) collective-permute-start(bf16[48,512]{1,0:T(8,128)(2,1)} %get-tuple-element.27), channel_id=1, source_target_pairs={{0,8},{4,12},{8,0},{12,4},{1,9},{5,13},{9,1},{13,5},{2,10},{6,14},... | collective-permute-start | bytes 147464 | tf_op jit(solution)/shard_map/ppermute | solution.py:38
  6.2 8.9 %collective-permute-start = (bf16[48,512]{1,0:T(8,128)(2,1)}, bf16[48,512]{1,0:T(8,128)(2,1)}, u32[]{:S(2)}, u32[]{:S(2)}) collective-permute-start(bf16[48,512]{1,0:T(8,128)(2,1)} %get-tuple-element.28), channel_id=1, source_target_pairs={{0,8},{4,12},{8,0},{12,4},{1,9},{5,13},{9,1},{13,5},{2,10},{6,14},... | collective-permute-start | bytes 147464 | tf_op jit(solution)/shard_map/ppermute | solution.py:38
  6.3 11.8 %collective-permute-start.4 = (bf16[48,1024]{1,0:T(8,128)(2,1)}, bf16[48,1024]{1,0:T(8,128)(2,1)}, u32[]{:S(2)}, u32[]{:S(2)}) collective-permute-start(bf16[48,1024]{1,0:T(8,128)(2,1)} %get-tuple-element.25), channel_id=1, source_target_pairs={{0,8},{4,12},{8,0},{12,4},{1,9},{5,13},{9,1},{13,5},{2,10},{6,14},... | collective-permute-start | bytes 294920 | tf_op jit(solution)/shard_map/ppermute | solution.py:38
  11.5 1.0 %copy-start = (bf16[128,4096]{1,0:T(8,128)(2,1)}, bf16[128,4096]{1,0:T(8,128)(2,1)S(1)}, u32[]{:S(2)}) copy-start(bf16[128,4096]{1,0:T(8,128)(2,1)S(1)} %get-tuple-element.18.refs_3_) | copy-start | bytes 3145732
  12.5 12.3 %copy-start.1 = (bf16[128,4096]{1,0:T(8,128)(2,1)S(1)}, bf16[128,4096]{1,0:T(8,128)(2,1)}, u32[]{:S(2)}) copy-start(bf16[128,4096]{1,0:T(8,128)(2,1)} %copy-done) | copy-start | bytes 3145732
  13.4 7.2 %collective-permute-start.7 = (bf16[96,512]{1,0:T(8,128)(2,1)S(1)}, bf16[96,512]{1,0:T(8,128)(2,1)S(1)}, u32[]{:S(2)}, u32[]{:S(2)}) collective-permute-start(bf16[96,512]{1,0:T(8,128)(2,1)S(1)} %maximum_add_fusion), channel_id=1, source_target_pairs={{0,4},{4,0},{8,12},{12,8},{1,5},{5,1},{9,13},{13,9},{2,6},{6,2},{1... | collective-permute-start | bytes 294920 | tf_op jit(solution)/shard_map/ppermute | solution.py:38
  15.9 7.8 %collective-permute-start.1 = (bf16[96,512]{1,0:T(8,128)(2,1)S(1)}, bf16[96,512]{1,0:T(8,128)(2,1)S(1)}, u32[]{:S(2)}, u32[]{:S(2)}) collective-permute-start(bf16[96,512]{1,0:T(8,128)(2,1)S(1)} %pad_maximum_fusion.3), channel_id=1, source_target_pairs={{0,4},{4,0},{8,12},{12,8},{1,5},{5,1},{9,13},{13,9},{2,6},{6,2},{1... | collective-permute-start | bytes 294920 | tf_op jit(solution)/shard_map/ppermute | solution.py:38
  19.0 10.5 %collective-permute-start.5 = (bf16[96,1024]{1,0:T(8,128)(2,1)S(1)}, bf16[96,1024]{1,0:T(8,128)(2,1)S(1)}, u32[]{:S(2)}, u32[]{:S(2)}) collective-permute-start(bf16[96,1024]{1,0:T(8,128)(2,1)S(1)} %pad_maximum_fusion.1), channel_id=1, source_target_pairs={{0,4},{4,0},{8,12},{12,8},{1,5},{5,1},{9,13},{13,9},{2,6},{6,2},{1... | collective-permute-start | bytes 589832 | tf_op jit(solution)/shard_map/ppermute | solution.py:38
  20.6 6.5 %collective-permute-start.8 = (bf16[144,512]{1,0:T(8,128)(2,1)S(1)}, bf16[144,512]{1,0:T(8,128)(2,1)S(1)}, u32[]{:S(2)}, u32[]{:S(2)}) collective-permute-start(bf16[144,512]{1,0:T(8,128)(2,1)S(1)} %constant_dynamic-update-slice_fusion.2.refs_6_), channel_id=1, source_target_pairs={{0,2},{2,0},{16,18},{18,16},{1,3},{3,1},{17,19},{19,17},{4,6},{6,4... | collective-permute-start | bytes 442376 | tf_op jit(solution)/shard_map/ppermute | solution.py:38
  22.2 5.2 %collective-permute-start.9 = (bf16[144,512]{1,0:T(8,128)(2,1)S(1)}, bf16[144,512]{1,0:T(8,128)(2,1)S(1)}, u32[]{:S(2)}, u32[]{:S(2)}) collective-permute-start(bf16[144,512]{1,0:T(8,128)(2,1)S(1)} %constant_dynamic-update-slice_fusion.2.refs_6_), channel_id=1, source_target_pairs={{0,16},{2,18},{16,0},{18,2},{1,17},{3,19},{17,1},{19,3},{4,20},{6,... | collective-permute-start | bytes 442376 | tf_op jit(solution)/shard_map/ppermute | solution.py:38
  23.7 5.2 %collective-permute-start.2 = (bf16[144,512]{1,0:T(8,128)(2,1)S(1)}, bf16[144,512]{1,0:T(8,128)(2,1)S(1)}, u32[]{:S(2)}, u32[]{:S(2)}) collective-permute-start(bf16[144,512]{1,0:T(8,128)(2,1)S(1)} %constant_dynamic-update-slice_fusion.refs_7_), channel_id=1, source_target_pairs={{0,2},{2,0},{16,18},{18,16},{1,3},{3,1},{17,19},{19,17},{4,6},{6,4... | collective-permute-start | bytes 442376 | tf_op jit(solution)/shard_map/ppermute | solution.py:38
  24.3 5.1 %collective-permute-start.3 = (bf16[144,512]{1,0:T(8,128)(2,1)S(1)}, bf16[144,512]{1,0:T(8,128)(2,1)S(1)}, u32[]{:S(2)}, u32[]{:S(2)}) collective-permute-start(bf16[144,512]{1,0:T(8,128)(2,1)S(1)} %constant_dynamic-update-slice_fusion.refs_7_), channel_id=1, source_target_pairs={{0,16},{2,18},{16,0},{18,2},{1,17},{3,19},{17,1},{19,3},{4,20},{6,... | collective-permute-start | bytes 442376 | tf_op jit(solution)/shard_map/ppermute | solution.py:38
  31.2 1.5 %collective-permute-start.10 = (f32[384,128]{1,0:T(8,128)S(1)}, f32[384,128]{1,0:T(8,128)S(1)}, u32[]{:S(2)}, u32[]{:S(2)}) collective-permute-start(f32[384,128]{1,0:T(8,128)S(1)} %shard_map.85.mine), channel_id=1, source_target_pairs={{0,1},{1,0},{2,3},{3,2},{4,5},{5,4},{6,7},{7,6},{8,9},{9,8},{10,11... | collective-permute-start | bytes 589832 | tf_op jit(solution)/shard_map/ppermute | solution.py:38
  33.2 4.8 %collective-permute-start.11 = (f32[136,128]{1,0:T(8,128)S(1)}, f32[136,128]{1,0:T(8,128)S(1)}, u32[]{:S(2)}, u32[]{:S(2)}) collective-permute-start(f32[136,128]{1,0:T(8,128)S(1)} %get-tuple-element.22), channel_id=1, source_target_pairs={{0,2},{2,0},{1,3},{3,1},{4,6},{6,4},{5,7},{7,5},{8,10},{10,8},{9,1... | collective-permute-start | bytes 208904 | tf_op jit(solution)/shard_map/ppermute | solution.py:38
  34.7 5.9 %collective-permute-start.14 = (f32[1,64,128]{2,1,0:T(8,128)S(1)}, f32[1,64,128]{2,1,0:T(8,128)S(1)}, u32[]{:S(2)}, u32[]{:S(2)}) collective-permute-start(f32[1,64,128]{2,1,0:T(8,128)S(1)} %get-tuple-element.24), channel_id=1, source_target_pairs={{0,2},{2,0},{1,3},{3,1},{4,6},{6,4},{5,7},{7,5},{8,10},{10,8},{9,1... | collective-permute-start | bytes 98312 | tf_op jit(solution)/shard_map/ppermute | solution.py:38
  38.0 7.4 %collective-permute-start.12 = (f32[136,128]{1,0:T(8,128)S(1)}, f32[136,128]{1,0:T(8,128)S(1)}, u32[]{:S(2)}, u32[]{:S(2)}) collective-permute-start(f32[136,128]{1,0:T(8,128)S(1)} %add.34), channel_id=1, source_target_pairs={{0,8},{4,12},{8,0},{12,4},{1,9},{5,13},{9,1},{13,5},{2,10},{6,14},... | collective-permute-start | bytes 208904 | tf_op jit(solution)/shard_map/ppermute | solution.py:38
  40.6 6.2 %collective-permute-start.15 = (f32[2,64,128]{2,1,0:T(8,128)S(1)}, f32[2,64,128]{2,1,0:T(8,128)S(1)}, u32[]{:S(2)}, u32[]{:S(2)}) collective-permute-start(f32[2,64,128]{2,1,0:T(8,128)S(1)} %pad_maximum_fusion.4), channel_id=1, source_target_pairs={{0,8},{4,12},{8,0},{12,4},{1,9},{5,13},{9,1},{13,5},{2,10},{6,14},... | collective-permute-start | bytes 196616 | tf_op jit(solution)/shard_map/ppermute | solution.py:38
  45.4 4.9 %collective-permute-start.13 = (f32[136,128]{1,0:T(8,128)S(1)}, f32[136,128]{1,0:T(8,128)S(1)}, u32[]{:S(2)}, u32[]{:S(2)}) collective-permute-start(f32[136,128]{1,0:T(8,128)S(1)} %add.35), channel_id=1, source_target_pairs={{0,4},{4,0},{8,12},{12,8},{1,5},{5,1},{9,13},{13,9},{2,6},{6,2},{1... | collective-permute-start | bytes 208904 | tf_op jit(solution)/shard_map/ppermute | solution.py:38
  46.8 7.3 %collective-permute-start.16 = (f32[4,64,128]{2,1,0:T(8,128)S(1)}, f32[4,64,128]{2,1,0:T(8,128)S(1)}, u32[]{:S(2)}, u32[]{:S(2)}) collective-permute-start(f32[4,64,128]{2,1,0:T(8,128)S(1)} %pad_maximum_fusion.2), channel_id=1, source_target_pairs={{0,4},{4,0},{8,12},{12,8},{1,5},{5,1},{9,13},{13,9},{2,6},{6,2},{1... | collective-permute-start | bytes 393224 | tf_op jit(solution)/shard_map/ppermute | solution.py:38

commit v4 on v3

--- a/solution.py
+++ b/solution.py
@@ -28,7 +28,7 @@
         out_shape=out_shape,
         in_specs=in_specs,
         out_specs=jax.tree.map(lambda _: vmem(), out_shape),
-        compiler_params=pltpu.CompilerParams(vmem_limit_bytes=32 * 1024 * 1024),
+        compiler_params=pltpu.CompilerParams(vmem_limit_bytes=16 * 1024 * 1024),
         cost_estimate=pl.CostEstimate(flops=flops, bytes_accessed=4 << 20, transcendentals=0),
         **kw,
     )(*args)
@@ -43,7 +43,7 @@
 
 
 def load_kernel(n, *refs):
-    srcs, dsts, token, sem = refs[:n], refs[n : 2 * n], refs[2 * n], refs[2 * n + 1]
+    srcs, dsts, sem = refs[:n], refs[n + 1 : 2 * n + 1], refs[2 * n + 1]
     copies = []
     for i, (src, dst) in enumerate(zip(srcs, dsts)):
         rows = src.shape[0] // 2
@@ -52,7 +52,6 @@
             copies.append(pltpu.make_async_copy(src.at[part], dst.at[part], sem.at[2 * i + h]))
     for c in copies:
         c.start()
-    token[...] = jnp.zeros_like(token)
     for c in copies:
         c.wait()
 
@@ -224,24 +223,24 @@
     whole = jnp.concatenate([w_in, w_out], axis=0)
     mine = lax.dynamic_slice(whole, (0, q * 2 * part), (shard, 2 * part))
     opposite = lax.dynamic_slice(whole, (0, (q ^ 3) * 2 * part), (shard, 2 * part))
-    *xs, w_in, w_out, token = call(
-        functools.partial(load_kernel, 6),
-        tuple(pltpu.VMEM(x.shape, x.dtype) for x in (*xs, w_in, w_out))
-        + (jax.ShapeDtypeStruct((1, part), jnp.bfloat16),),
-        [pl.BlockSpec(memory_space=pltpu.HBM)] * 6,
-        [pltpu.with_memory_space_constraint(x, pltpu.HBM) for x in (*xs, w_in, w_out)],
-        flops=1 << 30,
-        scratch_shapes=[pltpu.SemaphoreType.DMA((12,))],
-    )
     halves = [mine[:, :part], mine[:, part:]]
     far = [swap(h, "dp", n_dp, 2) for h in halves]
     far_op = swap(opposite, "dp", n_dp, 2)
     doubled = [jnp.concatenate([h, f], axis=0) for h, f in zip(halves, far)]
-    near = [swap(doubled[0] + token, "dp", n_dp, 1), swap(doubled[1], "dp", n_dp, 1)]
+    near = [swap(d, "dp", n_dp, 1) for d in doubled]
     near_op = swap(jnp.concatenate([opposite, far_op], axis=0), "dp", n_dp, 1)
     za, zb = [jnp.concatenate([f, n], axis=0) for f, n in zip(far, near)]
     xa, ya = swap(za, PLANE, 4, 1), swap(za, PLANE, 4, 2)
     xb, yb = swap(zb, PLANE, 4, 1), swap(zb, PLANE, 4, 2)
+    operands = (*xs, w_in, w_out)
+    *xs, w_in, w_out = call(
+        functools.partial(load_kernel, 6),
+        tuple(pltpu.VMEM(x.shape, x.dtype) for x in operands),
+        [pl.BlockSpec(memory_space=pltpu.HBM)] * 6 + [pl.BlockSpec(memory_space=pl.ANY)],
+        [pltpu.with_memory_space_constraint(x, pltpu.HBM) for x in operands] + [zb],
+        flops=1 << 30,
+        scratch_shapes=[pltpu.SemaphoreType.DMA((12,))],
+    )
 
     def accumulate(plan, pieces, acc):
         args = (*xs, w_in, w_out, *pieces) + (() if acc is None else (acc,))

time: 55.2 us -> 52.3 us (0.947)
  waiting for transfers between devices: 14.2 us -> 18.7 us
  other arithmetic: 4.34 us -> 0.98 us
  local copies, waits for them, and re-layouts: 3.25 us -> 0.03 us
  Pallas kernels: 9.98 us -> 9.11 us
    ppermute x17, waiting for transfers between devices: 14.2 us -> 18.7 us  [swap(): return lax.ppermute(x, axis, [(i, i ^ k) for i in range(count)])]
    unnamed x6 -> x2, local copies, waits for them, and re-layouts: 2.59 us -> 0.01 us
    concatenate x1, other arithmetic: 0.95 us -> 0.01 us  [project(): near_op = swap(jnp.concatenate([opposite, far_op], axis=0), 'dp', n_dp, 1)]
    add x1 -> x0, other arithmetic: 0.93 us -> none  [project(): doubled[0] + token]
    pallas_call x7, Pallas kernels: 9.98 us -> 9.11 us  [call(): pl.pallas_call(kernel, out_shape=out_shape, in_specs=in_specs, out_specs=...]
    concatenate x1 -> x2, other arithmetic: 0.83 us -> 0.01 us  [project(): doubled = [jnp.concatenate([h, f], axis=0) for h, f in zip(halves, far)]]
    concatenate x1, other arithmetic: 1.53 us -> 0.89 us  [project(): whole = jnp.concatenate([w_in, w_out], axis=0)]
    slice x1, local copies, waits for them, and re-layouts: 0.65 us -> 0.01 us  [project(): halves = [mine[:, :part], mine[:, part:]]]
  transfers between devices with their start and end apart: 17 -> 17, of which waited for: 9 -> 10; matrix products, arithmetic and copies ran while one was open for 8% -> 0% of each run, Pallas kernels for 13% -> 14%
where the time goes in v4:
time: 52.3 us; the launch traced here: 52.1 us
  starting transfers between devices  21.8 us (42%)
  waiting for transfers between devices  18.7 us (36%)
  Pallas kernels  9.11 us (17%)
  between operations  1.41 us (3%)
  other arithmetic  0.98 us (2%)
    ppermute x17, starting transfers between devices, swap(): return lax.ppermute(x, axis, [(i, i ^ k) for i in range(count)])  21.8 us
    ppermute x17, waiting for transfers between devices, swap(): return lax.ppermute(x, axis, [(i, i ^ k) for i in range(count)])  18.7 us
    pallas_call x7, Pallas kernels, call(): pl.pallas_call(kernel, out_shape=out_shape, in_specs=in_specs, out_specs=...  9.11 us
  transfers between devices with their start and end apart: 17, of which 10 were waited for; matrix products, arithmetic and copies ran while one was open for 0% of the time, Pallas kernels for 14%

profile of v4, /device:TPU:0, one launch (start us, length us, event | category | flops | bytes accessed | tf_op | source)
XLA Modules:
  0.0 52.1 jit_solution(70007186853654205)
XLA Ops:
  0.0 0.9 %fusion = (bf16[48,1024]{1,0:T(8,128)(2,1)S(1)}, bf16[48,1024]{1,0:T(8,128)(2,1)S(1)}) fusion(s32[]{:T(128)S(6)} %select_n.7, bf16[32,4096]{1,0:T(8,128)(2,1)} %bitcast.6, bf16[16,4096]{1,0:T(8,128)(2,1)} %bitcast.12, s32[]{:T(128)S(6)} %select_n.6), kind=kLoop, calls=%fused_computation.7 | loop fusion | flops 393216 | bytes 589832 | tf_op jit(solution)/shard_map/concatenate | solution.py:223
  0.9 4.1 %collective-permute-start = (bf16[48,512]{1,0:T(8,128)(2,1)S(1)}, bf16[48,512]{1,0:T(8,128)(2,1)S(1)}, u32[]{:S(2)}, u32[]{:S(2)}) collective-permute-start(bf16[48,512]{1,0:T(8,128)(2,1)S(1)} %get-tuple-element.26), channel_id=1, source_target_pairs={{0,8},{4,12},{8,0},{12,4},{1,9},{5,13},{9,1},{13,5},{2,10},{6,14},... | collective-permute-start | bytes 147464 | tf_op jit(solution)/shard_map/ppermute | solution.py:38
  5.0 0.1 collective-permute-start.6
  5.1 2.8 %collective-permute-start.4 = (bf16[48,1024]{1,0:T(8,128)(2,1)S(1)}, bf16[48,1024]{1,0:T(8,128)(2,1)S(1)}, u32[]{:S(2)}, u32[]{:S(2)}) collective-permute-start(bf16[48,1024]{1,0:T(8,128)(2,1)S(1)} %get-tuple-element.23), channel_id=1, source_target_pairs={{0,8},{4,12},{8,0},{12,4},{1,9},{5,13},{9,1},{13,5},{2,10},{6,14},... | collective-permute-start | bytes 294920 | tf_op jit(solution)/shard_map/ppermute | solution.py:38
  7.9 0.0 collective-permute-done
  8.0 2.8 %collective-permute-start.1 = (bf16[96,512]{1,0:T(8,128)(2,1)S(1)}, bf16[96,512]{1,0:T(8,128)(2,1)S(1)}, u32[]{:S(2)}, u32[]{:S(2)}) collective-permute-start(bf16[96,512]{1,0:T(8,128)(2,1)S(1)} %pad_maximum_fusion.3), channel_id=1, source_target_pairs={{0,4},{4,0},{8,12},{12,8},{1,5},{5,1},{9,13},{13,9},{2,6},{6,2},{1... | collective-permute-start | bytes 294920 | tf_op jit(solution)/shard_map/ppermute | solution.py:38
  10.7 2.8 %collective-permute-done.6 = bf16[48,512]{1,0:T(8,128)(2,1)S(1)} collective-permute-done((bf16[48,512]{1,0:T(8,128)(2,1)S(1)}, bf16[48,512]{1,0:T(8,128)(2,1)S(1)}, u32[]{:S(2)}, u32[]{:S(2)}) %collective-permute-start.6) | collective-permute-done | bytes 49184 | tf_op jit(solution)/shard_map/ppermute | solution.py:38
  13.5 0.1 collective-permute-start.7
  13.7 1.2 %collective-permute-done.4.refs_8_ = bf16[48,1024]{1,0:T(8,128)(2,1)S(1)} collective-permute-done((bf16[48,1024]{1,0:T(8,128)(2,1)S(1)}, bf16[48,1024]{1,0:T(8,128)(2,1)S(1)}, u32[]{:S(2)}, u32[]{:S(2)}) %collective-permute-start.4) | collective-permute-done | bytes 98336 | tf_op jit(solution)/shard_map/ppermute | solution.py:38
  14.9 0.9 %collective-permute-start.5 = (bf16[96,1024]{1,0:T(8,128)(2,1)S(1)}, bf16[96,1024]{1,0:T(8,128)(2,1)S(1)}, u32[]{:S(2)}, u32[]{:S(2)}) collective-permute-start(bf16[96,1024]{1,0:T(8,128)(2,1)S(1)} %pad_maximum_fusion.1), channel_id=1, source_target_pairs={{0,4},{4,0},{8,12},{12,8},{1,5},{5,1},{9,13},{13,9},{2,6},{6,2},{1... | collective-permute-start | bytes 589832 | tf_op jit(solution)/shard_map/ppermute | solution.py:38
  15.8 3.6 %collective-permute-done.7 = bf16[96,512]{1,0:T(8,128)(2,1)S(1)} collective-permute-done((bf16[96,512]{1,0:T(8,128)(2,1)S(1)}, bf16[96,512]{1,0:T(8,128)(2,1)S(1)}, u32[]{:S(2)}, u32[]{:S(2)}) %collective-permute-start.7) | collective-permute-done | bytes 98336 | tf_op jit(solution)/shard_map/ppermute | solution.py:38
  19.4 1.6 %collective-permute-start.8 = (bf16[144,512]{1,0:T(8,128)(2,1)S(1)}, bf16[144,512]{1,0:T(8,128)(2,1)S(1)}, u32[]{:S(2)}, u32[]{:S(2)}) collective-permute-start(bf16[144,512]{1,0:T(8,128)(2,1)S(1)} %constant_dynamic-update-slice_fusion.2.refs_6_), channel_id=1, source_target_pairs={{0,2},{2,0},{16,18},{18,16},{1,3},{3,1},{17,19},{19,17},{4,6},{6,4... | collective-permute-start | bytes 442376 | tf_op jit(solution)/shard_map/ppermute | solution.py:38
  20.9 1.5 %collective-permute-start.9 = (bf16[144,512]{1,0:T(8,128)(2,1)S(1)}, bf16[144,512]{1,0:T(8,128)(2,1)S(1)}, u32[]{:S(2)}, u32[]{:S(2)}) collective-permute-start(bf16[144,512]{1,0:T(8,128)(2,1)S(1)} %constant_dynamic-update-slice_fusion.2.refs_6_), channel_id=1, source_target_pairs={{0,16},{2,18},{16,0},{18,2},{1,17},{3,19},{17,1},{19,3},{4,20},{6,... | collective-permute-start | bytes 442376 | tf_op jit(solution)/shard_map/ppermute | solution.py:38
  22.4 0.0 collective-permute-done.1
  22.5 0.6 %collective-permute-start.2 = (bf16[144,512]{1,0:T(8,128)(2,1)S(1)}, bf16[144,512]{1,0:T(8,128)(2,1)S(1)}, u32[]{:S(2)}, u32[]{:S(2)}) collective-permute-start(bf16[144,512]{1,0:T(8,128)(2,1)S(1)} %constant_dynamic-update-slice_fusion.refs_6_.refs_7_), channel_id=1, source_target_pairs={{0,2},{2,0},{16,18},{18,16},{1,3},{3,1},{17,19},{19,17},{4,6},{6,4... | collective-permute-start | bytes 442376 | tf_op jit(solution)/shard_map/ppermute | solution.py:38
  23.1 0.5 collective-permute-start.3
  23.6 2.3 %shard_map.82 = (bf16[128,4096]{1,0:T(8,128)(2,1)S(1)}, bf16[128,4096]{1,0:T(8,128)(2,1)S(1)}, bf16[128,4096]{1,0:T(8,128)(2,1)S(1)}, bf16[128,4096]{1,0:T(8,128...) custom-call(bf16[128,4096]{1,0:T(8,128)(2,1)} %bitcast.8, bf16[128,4096]{1,0:T(8,128)(2,1)} %bitcast.9, ...), custom_call_target="tpu_custom_call" | custom-call | flops 1073741824 | bytes 4194304 | tf_op jit(solution)/shard_map/pallas_call | solution.py:26
  25.9 0.6 %shard_map.83.refs_8_ = f32[384,128]{1,0:T(8,128)S(1)} custom-call(bf16[128,4096]{1,0:T(8,128)(2,1)S(1)} %get-tuple-element.14.refs_0_, bf16[128,4096]{1,0:T(8,128)(2,1)S(1)} %get-tuple-element.15.refs_1_, bf16[128,4096]{1,0:T(8,128)(2,1)S(1)} %get-tuple-element.16.refs_2_, bf16[128,4096]{1,0:T(8,128)(2,1)S(1)} %get-tuple-element.17.refs_3_, ...), custom_call_target="tpu_custom_call" | custom-call | flops 1073741824 | bytes 4194304 | tf_op jit(solution)/shard_map/pallas_call | solution.py:26
  26.4 0.0 collective-permute-done.8.refs_6_
  26.4 0.0 collective-permute-done.9.refs_7_
  26.4 0.5 %shard_map.84.refs_10_ = f32[384,128]{1,0:T(8,128)S(1)} custom-call(bf16[128,4096]{1,0:T(8,128)(2,1)S(1)} %get-tuple-element.14.refs_0_, bf16[128,4096]{1,0:T(8,128)(2,1)S(1)} %get-tuple-element.15.refs_1_, bf16[128,4096]{1,0:T(8,128)(2,1)S(1)} %get-tuple-element.16.refs_2_, bf16[128,4096]{1,0:T(8,128)(2,1)S(1)} %get-tuple-element.17.refs_3_, ...), custom_call_target="tpu_custom_call" | custom-call | flops 1073741824 | bytes 4194304 | tf_op jit(solution)/shard_map/pallas_call | solution.py:26
  27.0 0.7 %collective-permute-done.2.refs_6_ = bf16[144,512]{1,0:T(8,128)(2,1)S(1)} collective-permute-done((bf16[144,512]{1,0:T(8,128)(2,1)S(1)}, bf16[144,512]{1,0:T(8,128)(2,1)S(1)}, u32[]{:S(2)}, u32[]{:S(2)}) %collective-permute-start.2) | collective-permute-done | bytes 147488 | tf_op jit(solution)/shard_map/ppermute | solution.py:38
  27.7 0.5 %collective-permute-done.3.refs_7_ = bf16[144,512]{1,0:T(8,128)(2,1)S(1)} collective-permute-done((bf16[144,512]{1,0:T(8,128)(2,1)S(1)}, bf16[144,512]{1,0:T(8,128)(2,1)S(1)}, u32[]{:S(2)}, u32[]{:S(2)}) %collective-permute-start.3) | collective-permute-done | bytes 147488 | tf_op jit(solution)/shard_map/ppermute | solution.py:38
  28.2 0.0 collective-permute-done.5.refs_9_
  28.2 0.8 %shard_map.85.mine = f32[384,128]{1,0:T(8,128)S(1)} custom-call(bf16[128,4096]{1,0:T(8,128)(2,1)S(1)} %get-tuple-element.14.refs_0_, bf16[128,4096]{1,0:T(8,128)(2,1)S(1)} %get-tuple-element.15.refs_1_, bf16[128,4096]{1,0:T(8,128)(2,1)S(1)} %get-tuple-element.16.refs_2_, bf16[128,4096]{1,0:T(8,128)(2,1)S(1)} %get-tuple-element.17.refs_3_, ...), custom_call_target="tpu_custom_call" | custom-call | flops 1073741824 | bytes 4194304 | tf_op jit(solution)/shard_map/pallas_call | solution.py:26
  29.0 0.1 collective-permute-start.10
  30.4 0.1 collective-permute-done.10.other
  30.5 0.5 shard_map.86
  31.0 1.5 %collective-permute-start.11 = (f32[136,128]{1,0:T(8,128)S(1)}, f32[136,128]{1,0:T(8,128)S(1)}, u32[]{:S(2)}, u32[]{:S(2)}) collective-permute-start(f32[136,128]{1,0:T(8,128)S(1)} %get-tuple-element.20), channel_id=1, source_target_pairs={{0,2},{2,0},{1,3},{3,1},{4,6},{6,4},{5,7},{7,5},{8,10},{10,8},{9,1... | collective-permute-start | bytes 208904 | tf_op jit(solution)/shard_map/ppermute | solution.py:38
  32.5 0.5 %collective-permute-start.14 = (f32[1,64,128]{2,1,0:T(8,128)S(1)}, f32[1,64,128]{2,1,0:T(8,128)S(1)}, u32[]{:S(2)}, u32[]{:S(2)}) collective-permute-start(f32[1,64,128]{2,1,0:T(8,128)S(1)} %get-tuple-element.22), channel_id=1, source_target_pairs={{0,2},{2,0},{1,3},{3,1},{4,6},{6,4},{5,7},{7,5},{8,10},{10,8},{9,1... | collective-permute-start | bytes 98312 | tf_op jit(solution)/shard_map/ppermute | solution.py:38
  33.1 2.8 %collective-permute-done.11 = f32[136,128]{1,0:T(8,128)S(1)} collective-permute-done((f32[136,128]{1,0:T(8,128)S(1)}, f32[136,128]{1,0:T(8,128)S(1)}, u32[]{:S(2)}, u32[]{:S(2)}) %collective-permute-start.11) | collective-permute-done | bytes 69664 | tf_op jit(solution)/shard_map/ppermute | solution.py:38
  35.9 1.4 %collective-permute-start.12 = (f32[136,128]{1,0:T(8,128)S(1)}, f32[136,128]{1,0:T(8,128)S(1)}, u32[]{:S(2)}, u32[]{:S(2)}) collective-permute-start(f32[136,128]{1,0:T(8,128)S(1)} %add.21), channel_id=1, source_target_pairs={{0,8},{4,12},{8,0},{12,4},{1,9},{5,13},{9,1},{13,5},{2,10},{6,14},... | collective-permute-start | bytes 208904 | tf_op jit(solution)/shard_map/ppermute | solution.py:38
  37.3 0.0 collective-permute-done.14
  37.3 1.6 %collective-permute-start.15 = (f32[2,64,128]{2,1,0:T(8,128)S(1)}, f32[2,64,128]{2,1,0:T(8,128)S(1)}, u32[]{:S(2)}, u32[]{:S(2)}) collective-permute-start(f32[2,64,128]{2,1,0:T(8,128)S(1)} %pad_maximum_fusion.5), channel_id=1, source_target_pairs={{0,8},{4,12},{8,0},{12,4},{1,9},{5,13},{9,1},{13,5},{2,10},{6,14},... | collective-permute-start | bytes 196616 | tf_op jit(solution)/shard_map/ppermute | solution.py:38
  39.0 4.1 %collective-permute-done.12 = f32[136,128]{1,0:T(8,128)S(1)} collective-permute-done((f32[136,128]{1,0:T(8,128)S(1)}, f32[136,128]{1,0:T(8,128)S(1)}, u32[]{:S(2)}, u32[]{:S(2)}) %collective-permute-start.12) | collective-permute-done | bytes 69664 | tf_op jit(solution)/shard_map/ppermute | solution.py:38
  43.1 0.2 collective-permute-start.13
  43.3 0.5 collective-permute-done.15
  43.8 1.4 %collective-permute-start.16 = (f32[4,64,128]{2,1,0:T(8,128)S(1)}, f32[4,64,128]{2,1,0:T(8,128)S(1)}, u32[]{:S(2)}, u32[]{:S(2)}) collective-permute-start(f32[4,64,128]{2,1,0:T(8,128)S(1)} %pad_maximum_fusion.2), channel_id=1, source_target_pairs={{0,4},{4,0},{8,12},{12,8},{1,5},{5,1},{9,13},{13,9},{2,6},{6,2},{1... | collective-permute-start | bytes 393224 | tf_op jit(solution)/shard_map/ppermute | solution.py:38
  45.3 2.4 %collective-permute-done.13 = f32[136,128]{1,0:T(8,128)S(1)} collective-permute-done((f32[136,128]{1,0:T(8,128)S(1)}, f32[136,128]{1,0:T(8,128)S(1)}, u32[]{:S(2)}, u32[]{:S(2)}) %collective-permute-start.13) | collective-permute-done | bytes 69664 | tf_op jit(solution)/shard_map/ppermute | solution.py:38
  47.6 3.8 %shard_map.87.side_ref = f32[64,128]{1,0:T(8,128)S(1)} custom-call(f32[136,128]{1,0:T(8,128)S(1)} %add.23.fac_ref, f32[128,64]{1,0:T(8,128)S(1)} %get-tuple-element.21.gtr_ref), custom_call_target="tpu_custom_call" | custom-call | flops 4294967296 | bytes 4194304 | tf_op jit(solution)/shard_map/pallas_call | solution.py:26
  51.4 0.0 collective-permute-done.16
  51.4 0.7 %shard_map.88 = f32[1,8]{1,0:T(1,128)} custom-call(f32[64,128]{1,0:T(8,128)S(1)} %shard_map.87.side_ref, f32[8,64,128]{2,1,0:T(8,128)S(1)} %pad_maximum_fusion.gte_ref), custom_call_target="tpu_custom_call" | custom-call | bytes 4194304 | tf_op jit(solution)/shard_map/pallas_call | solution.py:26
  (14 shorter events, 0.1 us)
Async XLA Ops:
  0.9 7.0 %collective-permute-start = (bf16[48,512]{1,0:T(8,128)(2,1)S(1)}, bf16[48,512]{1,0:T(8,128)(2,1)S(1)}, u32[]{:S(2)}, u32[]{:S(2)}) collective-permute-start(bf16[48,512]{1,0:T(8,128)(2,1)S(1)} %get-tuple-element.26), channel_id=1, source_target_pairs={{0,8},{4,12},{8,0},{12,4},{1,9},{5,13},{9,1},{13,5},{2,10},{6,14},... | collective-permute-start | bytes 147464 | tf_op jit(solution)/shard_map/ppermute | solution.py:38
  5.0 8.5 %collective-permute-start.6 = (bf16[48,512]{1,0:T(8,128)(2,1)S(1)}, bf16[48,512]{1,0:T(8,128)(2,1)S(1)}, u32[]{:S(2)}, u32[]{:S(2)}) collective-permute-start(bf16[48,512]{1,0:T(8,128)(2,1)S(1)} %get-tuple-element.25), channel_id=1, source_target_pairs={{0,8},{4,12},{8,0},{12,4},{1,9},{5,13},{9,1},{13,5},{2,10},{6,14},... | collective-permute-start | bytes 147464 | tf_op jit(solution)/shard_map/ppermute | solution.py:38
  5.1 9.8 %collective-permute-start.4 = (bf16[48,1024]{1,0:T(8,128)(2,1)S(1)}, bf16[48,1024]{1,0:T(8,128)(2,1)S(1)}, u32[]{:S(2)}, u32[]{:S(2)}) collective-permute-start(bf16[48,1024]{1,0:T(8,128)(2,1)S(1)} %get-tuple-element.23), channel_id=1, source_target_pairs={{0,8},{4,12},{8,0},{12,4},{1,9},{5,13},{9,1},{13,5},{2,10},{6,14},... | collective-permute-start | bytes 294920 | tf_op jit(solution)/shard_map/ppermute | solution.py:38
  8.0 14.5 %collective-permute-start.1 = (bf16[96,512]{1,0:T(8,128)(2,1)S(1)}, bf16[96,512]{1,0:T(8,128)(2,1)S(1)}, u32[]{:S(2)}, u32[]{:S(2)}) collective-permute-start(bf16[96,512]{1,0:T(8,128)(2,1)S(1)} %pad_maximum_fusion.3), channel_id=1, source_target_pairs={{0,4},{4,0},{8,12},{12,8},{1,5},{5,1},{9,13},{13,9},{2,6},{6,2},{1... | collective-permute-start | bytes 294920 | tf_op jit(solution)/shard_map/ppermute | solution.py:38
  13.5 5.8 %collective-permute-start.7 = (bf16[96,512]{1,0:T(8,128)(2,1)S(1)}, bf16[96,512]{1,0:T(8,128)(2,1)S(1)}, u32[]{:S(2)}, u32[]{:S(2)}) collective-permute-start(bf16[96,512]{1,0:T(8,128)(2,1)S(1)} %pad_maximum_fusion.4), channel_id=1, source_target_pairs={{0,4},{4,0},{8,12},{12,8},{1,5},{5,1},{9,13},{13,9},{2,6},{6,2},{1... | collective-permute-start | bytes 294920 | tf_op jit(solution)/shard_map/ppermute | solution.py:38
  14.9 13.3 %collective-permute-start.5 = (bf16[96,1024]{1,0:T(8,128)(2,1)S(1)}, bf16[96,1024]{1,0:T(8,128)(2,1)S(1)}, u32[]{:S(2)}, u32[]{:S(2)}) collective-permute-start(bf16[96,1024]{1,0:T(8,128)(2,1)S(1)} %pad_maximum_fusion.1), channel_id=1, source_target_pairs={{0,4},{4,0},{8,12},{12,8},{1,5},{5,1},{9,13},{13,9},{2,6},{6,2},{1... | collective-permute-start | bytes 589832 | tf_op jit(solution)/shard_map/ppermute | solution.py:38
  19.4 7.1 %collective-permute-start.8 = (bf16[144,512]{1,0:T(8,128)(2,1)S(1)}, bf16[144,512]{1,0:T(8,128)(2,1)S(1)}, u32[]{:S(2)}, u32[]{:S(2)}) collective-permute-start(bf16[144,512]{1,0:T(8,128)(2,1)S(1)} %constant_dynamic-update-slice_fusion.2.refs_6_), channel_id=1, source_target_pairs={{0,2},{2,0},{16,18},{18,16},{1,3},{3,1},{17,19},{19,17},{4,6},{6,4... | collective-permute-start | bytes 442376 | tf_op jit(solution)/shard_map/ppermute | solution.py:38
  20.9 5.5 %collective-permute-start.9 = (bf16[144,512]{1,0:T(8,128)(2,1)S(1)}, bf16[144,512]{1,0:T(8,128)(2,1)S(1)}, u32[]{:S(2)}, u32[]{:S(2)}) collective-permute-start(bf16[144,512]{1,0:T(8,128)(2,1)S(1)} %constant_dynamic-update-slice_fusion.2.refs_6_), channel_id=1, source_target_pairs={{0,16},{2,18},{16,0},{18,2},{1,17},{3,19},{17,1},{19,3},{4,20},{6,... | collective-permute-start | bytes 442376 | tf_op jit(solution)/shard_map/ppermute | solution.py:38
  22.5 5.2 %collective-permute-start.2 = (bf16[144,512]{1,0:T(8,128)(2,1)S(1)}, bf16[144,512]{1,0:T(8,128)(2,1)S(1)}, u32[]{:S(2)}, u32[]{:S(2)}) collective-permute-start(bf16[144,512]{1,0:T(8,128)(2,1)S(1)} %constant_dynamic-update-slice_fusion.refs_6_.refs_7_), channel_id=1, source_target_pairs={{0,2},{2,0},{16,18},{18,16},{1,3},{3,1},{17,19},{19,17},{4,6},{6,4... | collective-permute-start | bytes 442376 | tf_op jit(solution)/shard_map/ppermute | solution.py:38
  23.1 5.1 %collective-permute-start.3 = (bf16[144,512]{1,0:T(8,128)(2,1)S(1)}, bf16[144,512]{1,0:T(8,128)(2,1)S(1)}, u32[]{:S(2)}, u32[]{:S(2)}) collective-permute-start(bf16[144,512]{1,0:T(8,128)(2,1)S(1)} %constant_dynamic-update-slice_fusion.refs_6_.refs_7_), channel_id=1, source_target_pairs={{0,16},{2,18},{16,0},{18,2},{1,17},{3,19},{17,1},{19,3},{4,20},{6,... | collective-permute-start | bytes 442376 | tf_op jit(solution)/shard_map/ppermute | solution.py:38
  29.0 1.5 %collective-permute-start.10 = (f32[384,128]{1,0:T(8,128)S(1)}, f32[384,128]{1,0:T(8,128)S(1)}, u32[]{:S(2)}, u32[]{:S(2)}) collective-permute-start(f32[384,128]{1,0:T(8,128)S(1)} %shard_map.85.mine), channel_id=1, source_target_pairs={{0,1},{1,0},{2,3},{3,2},{4,5},{5,4},{6,7},{7,6},{8,9},{9,8},{10,11... | collective-permute-start | bytes 589832 | tf_op jit(solution)/shard_map/ppermute | solution.py:38
  31.0 4.8 %collective-permute-start.11 = (f32[136,128]{1,0:T(8,128)S(1)}, f32[136,128]{1,0:T(8,128)S(1)}, u32[]{:S(2)}, u32[]{:S(2)}) collective-permute-start(f32[136,128]{1,0:T(8,128)S(1)} %get-tuple-element.20), channel_id=1, source_target_pairs={{0,2},{2,0},{1,3},{3,1},{4,6},{6,4},{5,7},{7,5},{8,10},{10,8},{9,1... | collective-permute-start | bytes 208904 | tf_op jit(solution)/shard_map/ppermute | solution.py:38
  32.5 4.8 %collective-permute-start.14 = (f32[1,64,128]{2,1,0:T(8,128)S(1)}, f32[1,64,128]{2,1,0:T(8,128)S(1)}, u32[]{:S(2)}, u32[]{:S(2)}) collective-permute-start(f32[1,64,128]{2,1,0:T(8,128)S(1)} %get-tuple-element.22), channel_id=1, source_target_pairs={{0,2},{2,0},{1,3},{3,1},{4,6},{6,4},{5,7},{7,5},{8,10},{10,8},{9,1... | collective-permute-start | bytes 98312 | tf_op jit(solution)/shard_map/ppermute | solution.py:38
  35.9 7.2 %collective-permute-start.12 = (f32[136,128]{1,0:T(8,128)S(1)}, f32[136,128]{1,0:T(8,128)S(1)}, u32[]{:S(2)}, u32[]{:S(2)}) collective-permute-start(f32[136,128]{1,0:T(8,128)S(1)} %add.21), channel_id=1, source_target_pairs={{0,8},{4,12},{8,0},{12,4},{1,9},{5,13},{9,1},{13,5},{2,10},{6,14},... | collective-permute-start | bytes 208904 | tf_op jit(solution)/shard_map/ppermute | solution.py:38
  37.3 6.5 %collective-permute-start.15 = (f32[2,64,128]{2,1,0:T(8,128)S(1)}, f32[2,64,128]{2,1,0:T(8,128)S(1)}, u32[]{:S(2)}, u32[]{:S(2)}) collective-permute-start(f32[2,64,128]{2,1,0:T(8,128)S(1)} %pad_maximum_fusion.5), channel_id=1, source_target_pairs={{0,8},{4,12},{8,0},{12,4},{1,9},{5,13},{9,1},{13,5},{2,10},{6,14},... | collective-permute-start | bytes 196616 | tf_op jit(solution)/shard_map/ppermute | solution.py:38
  43.1 4.5 %collective-permute-start.13 = (f32[136,128]{1,0:T(8,128)S(1)}, f32[136,128]{1,0:T(8,128)S(1)}, u32[]{:S(2)}, u32[]{:S(2)}) collective-permute-start(f32[136,128]{1,0:T(8,128)S(1)} %add.22), channel_id=1, source_target_pairs={{0,4},{4,0},{8,12},{12,8},{1,5},{5,1},{9,13},{13,9},{2,6},{6,2},{1... | collective-permute-start | bytes 208904 | tf_op jit(solution)/shard_map/ppermute | solution.py:38
  43.8 7.6 %collective-permute-start.16 = (f32[4,64,128]{2,1,0:T(8,128)S(1)}, f32[4,64,128]{2,1,0:T(8,128)S(1)}, u32[]{:S(2)}, u32[]{:S(2)}) collective-permute-start(f32[4,64,128]{2,1,0:T(8,128)S(1)} %pad_maximum_fusion.2), channel_id=1, source_target_pairs={{0,4},{4,0},{8,12},{12,8},{1,5},{5,1},{9,13},{13,9},{2,6},{6,2},{1... | collective-permute-start | bytes 393224 | tf_op jit(solution)/shard_map/ppermute | solution.py:38

commit v5 on v3

--- a/solution.py
+++ b/solution.py
@@ -22,14 +22,14 @@
     return pl.BlockSpec(memory_space=pltpu.SMEM)
 
 
-def call(kernel, out_shape, in_specs, args, flops=0, **kw):
+def call(kernel, out_shape, in_specs, args, flops=0, limit=16, **kw):
     return pl.pallas_call(
         kernel,
         out_shape=out_shape,
         in_specs=in_specs,
         out_specs=jax.tree.map(lambda _: vmem(), out_shape),
-        compiler_params=pltpu.CompilerParams(vmem_limit_bytes=32 * 1024 * 1024),
-        cost_estimate=pl.CostEstimate(flops=flops, bytes_accessed=4 << 20, transcendentals=0),
+        compiler_params=pltpu.CompilerParams(vmem_limit_bytes=limit * 1024 * 1024),
+        cost_estimate=pl.CostEstimate(flops=flops, bytes_accessed=1 << 16, transcendentals=0),
         **kw,
     )(*args)
 
@@ -43,7 +43,7 @@
 
 
 def load_kernel(n, *refs):
-    srcs, dsts, token, sem = refs[:n], refs[n : 2 * n], refs[2 * n], refs[2 * n + 1]
+    srcs, dsts, sem = refs[:n], refs[n : 2 * n], refs[2 * n]
     copies = []
     for i, (src, dst) in enumerate(zip(srcs, dsts)):
         rows = src.shape[0] // 2
@@ -52,9 +52,27 @@
             copies.append(pltpu.make_async_copy(src.at[part], dst.at[part], sem.at[2 * i + h]))
     for c in copies:
         c.start()
-    token[...] = jnp.zeros_like(token)
     for c in copies:
         c.wait()
+
+
+def stack_kernel(n, *refs):
+    at = 0
+    for src in refs[:n]:
+        refs[-1][at : at + src.shape[0], :] = src[...]
+        at += src.shape[0]
+
+
+def stack(parts, after=None):
+    rows = sum(p.shape[0] for p in parts)
+    extra = () if after is None else (after,)
+    return call(
+        functools.partial(stack_kernel, len(parts)),
+        pltpu.VMEM((rows, parts[0].shape[1]), parts[0].dtype),
+        [vmem()] * len(parts) + [pl.BlockSpec(memory_space=pl.ANY)] * len(extra),
+        (*parts, *extra),
+        limit=1,
+    )
 
 
 def store_products(x_parts, g_parts, acc_ref, out_ref):
@@ -224,23 +242,27 @@
     whole = jnp.concatenate([w_in, w_out], axis=0)
     mine = lax.dynamic_slice(whole, (0, q * 2 * part), (shard, 2 * part))
     opposite = lax.dynamic_slice(whole, (0, (q ^ 3) * 2 * part), (shard, 2 * part))
-    *xs, w_in, w_out, token = call(
+    operands = (*xs, w_in, w_out)
+    *xs, w_in, w_out = call(
         functools.partial(load_kernel, 6),
-        tuple(pltpu.VMEM(x.shape, x.dtype) for x in (*xs, w_in, w_out))
-        + (jax.ShapeDtypeStruct((1, part), jnp.bfloat16),),
+        tuple(pltpu.VMEM(x.shape, x.dtype) for x in operands),
         [pl.BlockSpec(memory_space=pltpu.HBM)] * 6,
-        [pltpu.with_memory_space_constraint(x, pltpu.HBM) for x in (*xs, w_in, w_out)],
+        [pltpu.with_memory_space_constraint(x, pltpu.HBM) for x in operands],
         flops=1 << 30,
         scratch_shapes=[pltpu.SemaphoreType.DMA((12,))],
     )
     halves = [mine[:, :part], mine[:, part:]]
     far = [swap(h, "dp", n_dp, 2) for h in halves]
     far_op = swap(opposite, "dp", n_dp, 2)
-    doubled = [jnp.concatenate([h, f], axis=0) for h, f in zip(halves, far)]
-    near = [swap(doubled[0] + token, "dp", n_dp, 1), swap(doubled[1], "dp", n_dp, 1)]
-    near_op = swap(jnp.concatenate([opposite, far_op], axis=0), "dp", n_dp, 1)
-    za, zb = [jnp.concatenate([f, n], axis=0) for f, n in zip(far, near)]
+    both_a = stack((halves[0], far[0]), w_out)
+    near_a = swap(both_a, "dp", n_dp, 1)
+    both_b = stack((halves[1], far[1]))
+    near_b = swap(both_b, "dp", n_dp, 1)
+    za = stack((far[0], near_a))
     xa, ya = swap(za, PLANE, 4, 1), swap(za, PLANE, 4, 2)
+    both_op = stack((opposite, far_op))
+    near_op = swap(both_op, "dp", n_dp, 1)
+    zb = stack((far[1], near_b))
     xb, yb = swap(zb, PLANE, 4, 1), swap(zb, PLANE, 4, 2)
 
     def accumulate(plan, pieces, acc):

time: 55.2 us -> 50.9 us (0.922)
  starting transfers between devices: 21.5 us -> 25.1 us
  other arithmetic: 4.34 us -> 0.95 us
  local copies, waits for them, and re-layouts: 3.25 us -> 0.01 us
  Pallas kernels: 9.98 us -> 9.15 us
    ppermute x17, starting transfers between devices: 21.5 us -> 25.1 us  [swap(): return lax.ppermute(x, axis, [(i, i ^ k) for i in range(count)])]
    unnamed x6 -> x0, local copies, waits for them, and re-layouts: 2.59 us -> none
    concatenate x2 -> x0, other arithmetic: 1.79 us -> none  [the longest x1 0.95 us: project(): near_op = swap(jnp.concatenate([opposite, far_op], axis=0), 'dp', n_dp, 1)]
    add x1 -> x0, other arithmetic: 0.93 us -> none  [project(): doubled[0] + token]
    pallas_call x7 -> x12, Pallas kernels: 9.98 us -> 9.15 us  [call(): pl.pallas_call(kernel, out_shape=out_shape, in_specs=in_specs, out_specs=...]
    concatenate x1, other arithmetic: 1.53 us -> 0.89 us  [project(): whole = jnp.concatenate([w_in, w_out], axis=0)]
    slice x1, local copies, waits for them, and re-layouts: 0.65 us -> 0.01 us  [project(): halves = [mine[:, :part], mine[:, part:]]]
  transfers between devices with their start and end apart: 17 -> 17, of which waited for: 9 -> 9; matrix products, arithmetic and copies ran while one was open for 8% -> 0% of each run, Pallas kernels for 13% -> 14%
where the time goes in v5:
time: 50.9 us; the launch traced here: 50.7 us
  starting transfers between devices  25.1 us (49%)
  waiting for transfers between devices  14.1 us (28%)
  Pallas kernels  9.15 us (18%)
  between operations  1.4 us (3%)
  other arithmetic  0.95 us (2%)
    ppermute x17, starting transfers between devices, swap(): return lax.ppermute(x, axis, [(i, i ^ k) for i in range(count)])  25.1 us
    ppermute x17, waiting for transfers between devices, swap(): return lax.ppermute(x, axis, [(i, i ^ k) for i in range(count)])  14.1 us
    pallas_call x12, Pallas kernels, call(): pl.pallas_call(kernel, out_shape=out_shape, in_specs=in_specs, out_specs=...  9.15 us
  transfers between devices with their start and end apart: 17, of which 9 were waited for; matrix products, arithmetic and copies ran while one was open for 0% of the time, Pallas kernels for 14%

profile of v5, /device:TPU:0, one launch (start us, length us, event | category | flops | bytes accessed | tf_op | source)
XLA Modules:
  0.0 50.7 jit_solution(12921193165809051505)
XLA Ops:
  0.0 0.9 %fusion = (bf16[48,1024]{1,0:T(8,128)(2,1)S(1)}, bf16[48,1024]{1,0:T(8,128)(2,1)S(1)}) fusion(s32[]{:T(128)S(6)} %select_n.7, bf16[32,4096]{1,0:T(8,128)(2,1)} %bitcast.6, bf16[16,4096]{1,0:T(8,128)(2,1)} %bitcast.12, s32[]{:T(128)S(6)} %select_n.6), kind=kLoop, calls=%fused_computation.6 | loop fusion | flops 393216 | bytes 589832 | tf_op jit(solution)/shard_map/concatenate | solution.py:242
  0.9 4.1 %collective-permute-start.6 = (bf16[48,512]{1,0:T(8,128)(2,1)S(1)}, bf16[48,512]{1,0:T(8,128)(2,1)S(1)}, u32[]{:S(2)}, u32[]{:S(2)}) collective-permute-start(bf16[48,512]{1,0:T(8,128)(2,1)S(1)} %get-tuple-element.25.refs_0_), channel_id=1, source_target_pairs={{0,8},{4,12},{8,0},{12,4},{1,9},{5,13},{9,1},{13,5},{2,10},{6,14},... | collective-permute-start | bytes 147464 | tf_op jit(solution)/shard_map/ppermute | solution.py:38
  5.0 0.1 collective-permute-start
  5.1 2.3 %shard_map.82 = (bf16[128,4096]{1,0:T(8,128)(2,1)S(1)}, bf16[128,4096]{1,0:T(8,128)(2,1)S(1)}, bf16[128,4096]{1,0:T(8,128)(2,1)S(1)}, bf16[128,4096]{1,0:T(8,128...) custom-call(bf16[128,4096]{1,0:T(8,128)(2,1)} %bitcast.8, bf16[128,4096]{1,0:T(8,128)(2,1)} %bitcast.9, ...), custom_call_target="tpu_custom_call" | custom-call | flops 1073741824 | bytes 65536 | tf_op jit(solution)/shard_map/pallas_call | solution.py:26
  7.4 0.2 collective-permute-done.6.refs_1_.refs_0_
  7.6 2.1 %collective-permute-start.7 = (bf16[96,512]{1,0:T(8,128)(2,1)S(1)}, bf16[96,512]{1,0:T(8,128)(2,1)S(1)}, u32[]{:S(2)}, u32[]{:S(2)}) collective-permute-start(bf16[96,512]{1,0:T(8,128)(2,1)S(1)} %shard_map.86), channel_id=1, source_target_pairs={{0,4},{4,0},{8,12},{12,8},{1,5},{5,1},{9,13},{13,9},{2,6},{6,2},{1... | collective-permute-start | bytes 294920 | tf_op jit(solution)/shard_map/ppermute | solution.py:38
  9.7 3.4 %collective-permute-start.4 = (bf16[48,1024]{1,0:T(8,128)(2,1)S(1)}, bf16[48,1024]{1,0:T(8,128)(2,1)S(1)}, u32[]{:S(2)}, u32[]{:S(2)}) collective-permute-start(bf16[48,1024]{1,0:T(8,128)(2,1)S(1)} %get-tuple-element.23.refs_0_), channel_id=1, source_target_pairs={{0,8},{4,12},{8,0},{12,4},{1,9},{5,13},{9,1},{13,5},{2,10},{6,14},... | collective-permute-start | bytes 294920 | tf_op jit(solution)/shard_map/ppermute | solution.py:38
  13.1 0.0 collective-permute-done.refs_1_.refs_0_
  13.1 0.1 collective-permute-start.1
  13.3 0.0 collective-permute-done.7.refs_1_
  13.3 1.6 %collective-permute-start.8 = (bf16[144,512]{1,0:T(8,128)(2,1)S(1)}, bf16[144,512]{1,0:T(8,128)(2,1)S(1)}, u32[]{:S(2)}, u32[]{:S(2)}) collective-permute-start(bf16[144,512]{1,0:T(8,128)(2,1)S(1)} %shard_map.87.refs_6_), channel_id=1, source_target_pairs={{0,2},{2,0},{16,18},{18,16},{1,3},{3,1},{17,19},{19,17},{4,6},{6,4... | collective-permute-start | bytes 442376 | tf_op jit(solution)/shard_map/ppermute | solution.py:38
  14.9 1.5 %collective-permute-start.9 = (bf16[144,512]{1,0:T(8,128)(2,1)S(1)}, bf16[144,512]{1,0:T(8,128)(2,1)S(1)}, u32[]{:S(2)}, u32[]{:S(2)}) collective-permute-start(bf16[144,512]{1,0:T(8,128)(2,1)S(1)} %shard_map.87.refs_6_), channel_id=1, source_target_pairs={{0,16},{2,18},{16,0},{18,2},{1,17},{3,19},{17,1},{19,3},{4,20},{6,... | collective-permute-start | bytes 442376 | tf_op jit(solution)/shard_map/ppermute | solution.py:38
  16.4 1.0 %collective-permute-done.4.refs_1_.refs_8_ = bf16[48,1024]{1,0:T(8,128)(2,1)S(1)} collective-permute-done((bf16[48,1024]{1,0:T(8,128)(2,1)S(1)}, bf16[48,1024]{1,0:T(8,128)(2,1)S(1)}, u32[]{:S(2)}, u32[]{:S(2)}) %collective-permute-start.4) | collective-permute-done | bytes 98336 | tf_op jit(solution)/shard_map/ppermute | solution.py:38
  17.4 1.5 %collective-permute-start.5 = (bf16[96,1024]{1,0:T(8,128)(2,1)S(1)}, bf16[96,1024]{1,0:T(8,128)(2,1)S(1)}, u32[]{:S(2)}, u32[]{:S(2)}) collective-permute-start(bf16[96,1024]{1,0:T(8,128)(2,1)S(1)} %shard_map.85), channel_id=1, source_target_pairs={{0,4},{4,0},{8,12},{12,8},{1,5},{5,1},{9,13},{13,9},{2,6},{6,2},{1... | collective-permute-start | bytes 589832 | tf_op jit(solution)/shard_map/ppermute | solution.py:38
  18.9 0.0 collective-permute-done.1.refs_1_
  18.9 1.6 %collective-permute-start.2 = (bf16[144,512]{1,0:T(8,128)(2,1)S(1)}, bf16[144,512]{1,0:T(8,128)(2,1)S(1)}, u32[]{:S(2)}, u32[]{:S(2)}) collective-permute-start(bf16[144,512]{1,0:T(8,128)(2,1)S(1)} %shard_map.84.refs_7_), channel_id=1, source_target_pairs={{0,2},{2,0},{16,18},{18,16},{1,3},{3,1},{17,19},{19,17},{4,6},{6,4... | collective-permute-start | bytes 442376 | tf_op jit(solution)/shard_map/ppermute | solution.py:38
  20.5 1.5 %collective-permute-start.3 = (bf16[144,512]{1,0:T(8,128)(2,1)S(1)}, bf16[144,512]{1,0:T(8,128)(2,1)S(1)}, u32[]{:S(2)}, u32[]{:S(2)}) collective-permute-start(bf16[144,512]{1,0:T(8,128)(2,1)S(1)} %shard_map.84.refs_7_), channel_id=1, source_target_pairs={{0,16},{2,18},{16,0},{18,2},{1,17},{3,19},{17,1},{19,3},{4,20},{6,... | collective-permute-start | bytes 442376 | tf_op jit(solution)/shard_map/ppermute | solution.py:38
  22.0 0.5 %shard_map.88.refs_8_ = f32[384,128]{1,0:T(8,128)S(1)} custom-call(bf16[128,4096]{1,0:T(8,128)(2,1)S(1)} %get-tuple-element.14.refs_0_, bf16[128,4096]{1,0:T(8,128)(2,1)S(1)} %get-tuple-element.15.refs_1_, bf16[128,4096]{1,0:T(8,128)(2,1)S(1)} %get-tuple-element.16.refs_2_, bf16[128,4096]{1,0:T(8,128)(2,1)S(1)} %get-tuple-element.17.refs_3_, ...), custom_call_target="tpu_custom_call" | custom-call | flops 1073741824 | bytes 65536 | tf_op jit(solution)/shard_map/pallas_call | solution.py:26
  22.6 0.0 collective-permute-done.8.refs_6_
  22.6 0.0 collective-permute-done.9.refs_7_
  22.6 0.5 %shard_map.89.refs_10_ = f32[384,128]{1,0:T(8,128)S(1)} custom-call(bf16[128,4096]{1,0:T(8,128)(2,1)S(1)} %get-tuple-element.14.refs_0_, bf16[128,4096]{1,0:T(8,128)(2,1)S(1)} %get-tuple-element.15.refs_1_, bf16[128,4096]{1,0:T(8,128)(2,1)S(1)} %get-tuple-element.16.refs_2_, bf16[128,4096]{1,0:T(8,128)(2,1)S(1)} %get-tuple-element.17.refs_3_, ...), custom_call_target="tpu_custom_call" | custom-call | flops 1073741824 | bytes 65536 | tf_op jit(solution)/shard_map/pallas_call | solution.py:26
  23.1 1.0 %collective-permute-done.2.refs_6_ = bf16[144,512]{1,0:T(8,128)(2,1)S(1)} collective-permute-done((bf16[144,512]{1,0:T(8,128)(2,1)S(1)}, bf16[144,512]{1,0:T(8,128)(2,1)S(1)}, u32[]{:S(2)}, u32[]{:S(2)}) %collective-permute-start.2) | collective-permute-done | bytes 147488 | tf_op jit(solution)/shard_map/ppermute | solution.py:38
  24.2 1.5 %collective-permute-done.3.refs_7_ = bf16[144,512]{1,0:T(8,128)(2,1)S(1)} collective-permute-done((bf16[144,512]{1,0:T(8,128)(2,1)S(1)}, bf16[144,512]{1,0:T(8,128)(2,1)S(1)}, u32[]{:S(2)}, u32[]{:S(2)}) %collective-permute-start.3) | collective-permute-done | bytes 147488 | tf_op jit(solution)/shard_map/ppermute | solution.py:38
  25.7 0.0 collective-permute-done.5.refs_9_
  25.7 0.8 %shard_map.90.mine = f32[384,128]{1,0:T(8,128)S(1)} custom-call(bf16[128,4096]{1,0:T(8,128)(2,1)S(1)} %get-tuple-element.14.refs_0_, bf16[128,4096]{1,0:T(8,128)(2,1)S(1)} %get-tuple-element.15.refs_1_, bf16[128,4096]{1,0:T(8,128)(2,1)S(1)} %get-tuple-element.16.refs_2_, bf16[128,4096]{1,0:T(8,128)(2,1)S(1)} %get-tuple-element.17.refs_3_, ...), custom_call_target="tpu_custom_call" | custom-call | flops 1073741824 | bytes 65536 | tf_op jit(solution)/shard_map/pallas_call | solution.py:26
  26.5 0.1 collective-permute-start.10
  27.9 0.1 collective-permute-done.10.other
  28.0 0.5 shard_map.91
  28.5 0.6 %collective-permute-start.11 = (f32[136,128]{1,0:T(8,128)S(1)}, f32[136,128]{1,0:T(8,128)S(1)}, u32[]{:S(2)}, u32[]{:S(2)}) collective-permute-start(f32[136,128]{1,0:T(8,128)S(1)} %get-tuple-element.20), channel_id=1, source_target_pairs={{0,2},{2,0},{1,3},{3,1},{4,6},{6,4},{5,7},{7,5},{8,10},{10,8},{9,1... | collective-permute-start | bytes 208904 | tf_op jit(solution)/shard_map/ppermute | solution.py:38
  29.0 1.5 %collective-permute-start.14 = (f32[1,64,128]{2,1,0:T(8,128)S(1)}, f32[1,64,128]{2,1,0:T(8,128)S(1)}, u32[]{:S(2)}, u32[]{:S(2)}) collective-permute-start(f32[1,64,128]{2,1,0:T(8,128)S(1)} %get-tuple-element.22), channel_id=1, source_target_pairs={{0,2},{2,0},{1,3},{3,1},{4,6},{6,4},{5,7},{7,5},{8,10},{10,8},{9,1... | collective-permute-start | bytes 98312 | tf_op jit(solution)/shard_map/ppermute | solution.py:38
  30.5 2.8 %collective-permute-done.11 = f32[136,128]{1,0:T(8,128)S(1)} collective-permute-done((f32[136,128]{1,0:T(8,128)S(1)}, f32[136,128]{1,0:T(8,128)S(1)}, u32[]{:S(2)}, u32[]{:S(2)}) %collective-permute-start.11) | collective-permute-done | bytes 69664 | tf_op jit(solution)/shard_map/ppermute | solution.py:38
  33.3 4.2 %collective-permute-start.12 = (f32[136,128]{1,0:T(8,128)S(1)}, f32[136,128]{1,0:T(8,128)S(1)}, u32[]{:S(2)}, u32[]{:S(2)}) collective-permute-start(f32[136,128]{1,0:T(8,128)S(1)} %add.21), channel_id=1, source_target_pairs={{0,8},{4,12},{8,0},{12,4},{1,9},{5,13},{9,1},{13,5},{2,10},{6,14},... | collective-permute-start | bytes 208904 | tf_op jit(solution)/shard_map/ppermute | solution.py:38
  37.6 0.0 collective-permute-done.14
  37.6 0.5 %collective-permute-start.15 = (f32[2,64,128]{2,1,0:T(8,128)S(1)}, f32[2,64,128]{2,1,0:T(8,128)S(1)}, u32[]{:S(2)}, u32[]{:S(2)}) collective-permute-start(f32[2,64,128]{2,1,0:T(8,128)S(1)} %pad_maximum_fusion.2), channel_id=1, source_target_pairs={{0,8},{4,12},{8,0},{12,4},{1,9},{5,13},{9,1},{13,5},{2,10},{6,14},... | collective-permute-start | bytes 196616 | tf_op jit(solution)/shard_map/ppermute | solution.py:38
  38.1 3.2 %collective-permute-done.12 = f32[136,128]{1,0:T(8,128)S(1)} collective-permute-done((f32[136,128]{1,0:T(8,128)S(1)}, f32[136,128]{1,0:T(8,128)S(1)}, u32[]{:S(2)}, u32[]{:S(2)}) %collective-permute-start.12) | collective-permute-done | bytes 69664 | tf_op jit(solution)/shard_map/ppermute | solution.py:38
  41.4 0.1 collective-permute-start.13
  41.4 1.5 %collective-permute-done.15 = f32[2,64,128]{2,1,0:T(8,128)S(1)} collective-permute-done((f32[2,64,128]{2,1,0:T(8,128)S(1)}, f32[2,64,128]{2,1,0:T(8,128)S(1)}, u32[]{:S(2)}, u32[]{:S(2)}) %collective-permute-start.15) | collective-permute-done | bytes 65568 | tf_op jit(solution)/shard_map/ppermute | solution.py:38
  43.0 0.6 %collective-permute-start.16 = (f32[4,64,128]{2,1,0:T(8,128)S(1)}, f32[4,64,128]{2,1,0:T(8,128)S(1)}, u32[]{:S(2)}, u32[]{:S(2)}) collective-permute-start(f32[4,64,128]{2,1,0:T(8,128)S(1)} %pad_maximum_fusion.1), channel_id=1, source_target_pairs={{0,4},{4,0},{8,12},{12,8},{1,5},{5,1},{9,13},{13,9},{2,6},{6,2},{1... | collective-permute-start | bytes 393224 | tf_op jit(solution)/shard_map/ppermute | solution.py:38
  43.5 2.7 %collective-permute-done.13 = f32[136,128]{1,0:T(8,128)S(1)} collective-permute-done((f32[136,128]{1,0:T(8,128)S(1)}, f32[136,128]{1,0:T(8,128)S(1)}, u32[]{:S(2)}, u32[]{:S(2)}) %collective-permute-start.13) | collective-permute-done | bytes 69664 | tf_op jit(solution)/shard_map/ppermute | solution.py:38
  46.3 3.8 %shard_map.92.side_ref = f32[64,128]{1,0:T(8,128)S(1)} custom-call(f32[136,128]{1,0:T(8,128)S(1)} %add.23.fac_ref, f32[128,64]{1,0:T(8,128)S(1)} %get-tuple-element.21.gtr_ref), custom_call_target="tpu_custom_call" | custom-call | flops 4294967296 | bytes 65536 | tf_op jit(solution)/shard_map/pallas_call | solution.py:26
  50.0 0.0 collective-permute-done.16
  50.1 0.7 %shard_map.93 = f32[1,8]{1,0:T(1,128)} custom-call(f32[64,128]{1,0:T(8,128)S(1)} %shard_map.92.side_ref, f32[8,64,128]{2,1,0:T(8,128)S(1)} %pad_maximum_fusion.gte_ref), custom_call_target="tpu_custom_call" | custom-call | bytes 65536 | tf_op jit(solution)/shard_map/pallas_call | solution.py:26
  (12 shorter events, 0.1 us)
Async XLA Ops:
  0.9 6.7 %collective-permute-start.6 = (bf16[48,512]{1,0:T(8,128)(2,1)S(1)}, bf16[48,512]{1,0:T(8,128)(2,1)S(1)}, u32[]{:S(2)}, u32[]{:S(2)}) collective-permute-start(bf16[48,512]{1,0:T(8,128)(2,1)S(1)} %get-tuple-element.25.refs_0_), channel_id=1, source_target_pairs={{0,8},{4,12},{8,0},{12,4},{1,9},{5,13},{9,1},{13,5},{2,10},{6,14},... | collective-permute-start | bytes 147464 | tf_op jit(solution)/shard_map/ppermute | solution.py:38
  5.0 8.1 %collective-permute-start = (bf16[48,512]{1,0:T(8,128)(2,1)S(1)}, bf16[48,512]{1,0:T(8,128)(2,1)S(1)}, u32[]{:S(2)}, u32[]{:S(2)}) collective-permute-start(bf16[48,512]{1,0:T(8,128)(2,1)S(1)} %get-tuple-element.26.refs_0_), channel_id=1, source_target_pairs={{0,8},{4,12},{8,0},{12,4},{1,9},{5,13},{9,1},{13,5},{2,10},{6,14},... | collective-permute-start | bytes 147464 | tf_op jit(solution)/shard_map/ppermute | solution.py:38
  7.6 5.7 %collective-permute-start.7 = (bf16[96,512]{1,0:T(8,128)(2,1)S(1)}, bf16[96,512]{1,0:T(8,128)(2,1)S(1)}, u32[]{:S(2)}, u32[]{:S(2)}) collective-permute-start(bf16[96,512]{1,0:T(8,128)(2,1)S(1)} %shard_map.86), channel_id=1, source_target_pairs={{0,4},{4,0},{8,12},{12,8},{1,5},{5,1},{9,13},{13,9},{2,6},{6,2},{1... | collective-permute-start | bytes 294920 | tf_op jit(solution)/shard_map/ppermute | solution.py:38
  9.7 7.7 %collective-permute-start.4 = (bf16[48,1024]{1,0:T(8,128)(2,1)S(1)}, bf16[48,1024]{1,0:T(8,128)(2,1)S(1)}, u32[]{:S(2)}, u32[]{:S(2)}) collective-permute-start(bf16[48,1024]{1,0:T(8,128)(2,1)S(1)} %get-tuple-element.23.refs_0_), channel_id=1, source_target_pairs={{0,8},{4,12},{8,0},{12,4},{1,9},{5,13},{9,1},{13,5},{2,10},{6,14},... | collective-permute-start | bytes 294920 | tf_op jit(solution)/shard_map/ppermute | solution.py:38
  13.1 5.8 %collective-permute-start.1 = (bf16[96,512]{1,0:T(8,128)(2,1)S(1)}, bf16[96,512]{1,0:T(8,128)(2,1)S(1)}, u32[]{:S(2)}, u32[]{:S(2)}) collective-permute-start(bf16[96,512]{1,0:T(8,128)(2,1)S(1)} %shard_map.83), channel_id=1, source_target_pairs={{0,4},{4,0},{8,12},{12,8},{1,5},{5,1},{9,13},{13,9},{2,6},{6,2},{1... | collective-permute-start | bytes 294920 | tf_op jit(solution)/shard_map/ppermute | solution.py:38
  13.3 9.3 %collective-permute-start.8 = (bf16[144,512]{1,0:T(8,128)(2,1)S(1)}, bf16[144,512]{1,0:T(8,128)(2,1)S(1)}, u32[]{:S(2)}, u32[]{:S(2)}) collective-permute-start(bf16[144,512]{1,0:T(8,128)(2,1)S(1)} %shard_map.87.refs_6_), channel_id=1, source_target_pairs={{0,2},{2,0},{16,18},{18,16},{1,3},{3,1},{17,19},{19,17},{4,6},{6,4... | collective-permute-start | bytes 442376 | tf_op jit(solution)/shard_map/ppermute | solution.py:38
  14.9 7.7 %collective-permute-start.9 = (bf16[144,512]{1,0:T(8,128)(2,1)S(1)}, bf16[144,512]{1,0:T(8,128)(2,1)S(1)}, u32[]{:S(2)}, u32[]{:S(2)}) collective-permute-start(bf16[144,512]{1,0:T(8,128)(2,1)S(1)} %shard_map.87.refs_6_), channel_id=1, source_target_pairs={{0,16},{2,18},{16,0},{18,2},{1,17},{3,19},{17,1},{19,3},{4,20},{6,... | collective-permute-start | bytes 442376 | tf_op jit(solution)/shard_map/ppermute | solution.py:38
  17.4 8.3 %collective-permute-start.5 = (bf16[96,1024]{1,0:T(8,128)(2,1)S(1)}, bf16[96,1024]{1,0:T(8,128)(2,1)S(1)}, u32[]{:S(2)}, u32[]{:S(2)}) collective-permute-start(bf16[96,1024]{1,0:T(8,128)(2,1)S(1)} %shard_map.85), channel_id=1, source_target_pairs={{0,4},{4,0},{8,12},{12,8},{1,5},{5,1},{9,13},{13,9},{2,6},{6,2},{1... | collective-permute-start | bytes 589832 | tf_op jit(solution)/shard_map/ppermute | solution.py:38
  18.9 5.2 %collective-permute-start.2 = (bf16[144,512]{1,0:T(8,128)(2,1)S(1)}, bf16[144,512]{1,0:T(8,128)(2,1)S(1)}, u32[]{:S(2)}, u32[]{:S(2)}) collective-permute-start(bf16[144,512]{1,0:T(8,128)(2,1)S(1)} %shard_map.84.refs_7_), channel_id=1, source_target_pairs={{0,2},{2,0},{16,18},{18,16},{1,3},{3,1},{17,19},{19,17},{4,6},{6,4... | collective-permute-start | bytes 442376 | tf_op jit(solution)/shard_map/ppermute | solution.py:38
  20.5 5.1 %collective-permute-start.3 = (bf16[144,512]{1,0:T(8,128)(2,1)S(1)}, bf16[144,512]{1,0:T(8,128)(2,1)S(1)}, u32[]{:S(2)}, u32[]{:S(2)}) collective-permute-start(bf16[144,512]{1,0:T(8,128)(2,1)S(1)} %shard_map.84.refs_7_), channel_id=1, source_target_pairs={{0,16},{2,18},{16,0},{18,2},{1,17},{3,19},{17,1},{19,3},{4,20},{6,... | collective-permute-start | bytes 442376 | tf_op jit(solution)/shard_map/ppermute | solution.py:38
  26.5 1.5 %collective-permute-start.10 = (f32[384,128]{1,0:T(8,128)S(1)}, f32[384,128]{1,0:T(8,128)S(1)}, u32[]{:S(2)}, u32[]{:S(2)}) collective-permute-start(f32[384,128]{1,0:T(8,128)S(1)} %shard_map.90.mine), channel_id=1, source_target_pairs={{0,1},{1,0},{2,3},{3,2},{4,5},{5,4},{6,7},{7,6},{8,9},{9,8},{10,11... | collective-permute-start | bytes 589832 | tf_op jit(solution)/shard_map/ppermute | solution.py:38
  28.5 4.9 %collective-permute-start.11 = (f32[136,128]{1,0:T(8,128)S(1)}, f32[136,128]{1,0:T(8,128)S(1)}, u32[]{:S(2)}, u32[]{:S(2)}) collective-permute-start(f32[136,128]{1,0:T(8,128)S(1)} %get-tuple-element.20), channel_id=1, source_target_pairs={{0,2},{2,0},{1,3},{3,1},{4,6},{6,4},{5,7},{7,5},{8,10},{10,8},{9,1... | collective-permute-start | bytes 208904 | tf_op jit(solution)/shard_map/ppermute | solution.py:38
  29.0 8.5 %collective-permute-start.14 = (f32[1,64,128]{2,1,0:T(8,128)S(1)}, f32[1,64,128]{2,1,0:T(8,128)S(1)}, u32[]{:S(2)}, u32[]{:S(2)}) collective-permute-start(f32[1,64,128]{2,1,0:T(8,128)S(1)} %get-tuple-element.22), channel_id=1, source_target_pairs={{0,2},{2,0},{1,3},{3,1},{4,6},{6,4},{5,7},{7,5},{8,10},{10,8},{9,1... | collective-permute-start | bytes 98312 | tf_op jit(solution)/shard_map/ppermute | solution.py:38
  33.3 8.0 %collective-permute-start.12 = (f32[136,128]{1,0:T(8,128)S(1)}, f32[136,128]{1,0:T(8,128)S(1)}, u32[]{:S(2)}, u32[]{:S(2)}) collective-permute-start(f32[136,128]{1,0:T(8,128)S(1)} %add.21), channel_id=1, source_target_pairs={{0,8},{4,12},{8,0},{12,4},{1,9},{5,13},{9,1},{13,5},{2,10},{6,14},... | collective-permute-start | bytes 208904 | tf_op jit(solution)/shard_map/ppermute | solution.py:38
  37.6 5.4 %collective-permute-start.15 = (f32[2,64,128]{2,1,0:T(8,128)S(1)}, f32[2,64,128]{2,1,0:T(8,128)S(1)}, u32[]{:S(2)}, u32[]{:S(2)}) collective-permute-start(f32[2,64,128]{2,1,0:T(8,128)S(1)} %pad_maximum_fusion.2), channel_id=1, source_target_pairs={{0,8},{4,12},{8,0},{12,4},{1,9},{5,13},{9,1},{13,5},{2,10},{6,14},... | collective-permute-start | bytes 196616 | tf_op jit(solution)/shard_map/ppermute | solution.py:38
  41.4 4.9 %collective-permute-start.13 = (f32[136,128]{1,0:T(8,128)S(1)}, f32[136,128]{1,0:T(8,128)S(1)}, u32[]{:S(2)}, u32[]{:S(2)}) collective-permute-start(f32[136,128]{1,0:T(8,128)S(1)} %add.22), channel_id=1, source_target_pairs={{0,4},{4,0},{8,12},{12,8},{1,5},{5,1},{9,13},{13,9},{2,6},{6,2},{1... | collective-permute-start | bytes 208904 | tf_op jit(solution)/shard_map/ppermute | solution.py:38
  43.0 7.1 %collective-permute-start.16 = (f32[4,64,128]{2,1,0:T(8,128)S(1)}, f32[4,64,128]{2,1,0:T(8,128)S(1)}, u32[]{:S(2)}, u32[]{:S(2)}) collective-permute-start(f32[4,64,128]{2,1,0:T(8,128)S(1)} %pad_maximum_fusion.1), channel_id=1, source_target_pairs={{0,4},{4,0},{8,12},{12,8},{1,5},{5,1},{9,13},{13,9},{2,6},{6,2},{1... | collective-permute-start | bytes 393224 | tf_op jit(solution)/shard_map/ppermute | solution.py:38

commit v6 on v5

--- a/solution.py
+++ b/solution.py
@@ -220,9 +220,10 @@
     lane = lax.broadcasted_iota(jnp.int32, out_ref.shape, 1)
     row = jnp.zeros(out_ref.shape, jnp.float32)
     side = side_ref[...]
+    sums = [jnp.sum(side * gte_ref[p], axis=0, keepdims=True) for p in range(len(order))]
+    values = jnp.sum(jnp.concatenate(sums, axis=0), axis=1, keepdims=True)
     for p, (dz, db) in enumerate(order):
-        value = jnp.sum(side * gte_ref[p], axis=(0, 1), keepdims=True)
-        row = jnp.where(lane == (z ^ dz) * n_blk + (b ^ db), value, row)
+        row = jnp.where(lane == (z ^ dz) * n_blk + (b ^ db), values[p : p + 1, :], row)
     out_ref[...] = row
 
 
@@ -320,11 +321,13 @@
         (train_lengths, test_lengths, part, other),
     )
     order = [(0, 0)]
+    for axis, count in (("dp", n_dp), ("blk", n_blk)):
+        for k in bits(count):
+            gte = jnp.concatenate([gte, swap(gte, axis, count, k)], axis=0)
+            order += [(dz ^ k, db) if axis == "dp" else (dz, db ^ k) for dz, db in order]
     for axis, count in (("blk", n_blk), ("dp", n_dp)):
         for k in bits(count):
             fac = fac + swap(fac, axis, count, k)
-            gte = jnp.concatenate([gte, swap(gte, axis, count, k)], axis=0)
-            order += [(dz ^ k, db) if axis == "dp" else (dz, db ^ k) for dz, db in order]
     side = call(
         side_kernel,
         jax.ShapeDtypeStruct((ki // 2, ki), jnp.float32),

time: 50.9 us -> 49.2 us (0.967)
  waiting for transfers between devices: 14.1 us -> 9.45 us
  starting transfers between devices: 25.1 us -> 28.1 us
    ppermute x17, waiting for transfers between devices: 14.1 us -> 9.45 us  [swap(): return lax.ppermute(x, axis, [(i, i ^ k) for i in range(count)])]
    ppermute x17, starting transfers between devices: 25.1 us -> 28.1 us  [swap(): return lax.ppermute(x, axis, [(i, i ^ k) for i in range(count)])]
  transfers between devices with their start and end apart: 17 -> 17, of which waited for: 9 -> 8; matrix products, arithmetic and copies ran while one was open for 0% -> 0% of each run, Pallas kernels for 14% -> 15%
where the time goes in v6:
time: 49.2 us; the launch traced here: 49 us
  starting transfers between devices  28.1 us (57%)
  waiting for transfers between devices  9.45 us (19%)
  Pallas kernels  9.14 us (19%)
  between operations  1.4 us (3%)
  other arithmetic  0.95 us (2%)
    ppermute x17, starting transfers between devices, swap(): return lax.ppermute(x, axis, [(i, i ^ k) for i in range(count)])  28.1 us
    ppermute x17, waiting for transfers between devices, swap(): return lax.ppermute(x, axis, [(i, i ^ k) for i in range(count)])  9.45 us
    pallas_call x12, Pallas kernels, call(): pl.pallas_call(kernel, out_shape=out_shape, in_specs=in_specs, out_specs=...  9.14 us
  transfers between devices with their start and end apart: 17, of which 8 were waited for; matrix products, arithmetic and copies ran while one was open for 0% of the time, Pallas kernels for 15%

profile of v6, /device:TPU:0, one launch (start us, length us, event | category | flops | bytes accessed | tf_op | source)
XLA Modules:
  0.0 49.0 jit_solution(16245963104905549210)
XLA Ops:
  0.0 0.9 %fusion = (bf16[48,1024]{1,0:T(8,128)(2,1)S(1)}, bf16[48,1024]{1,0:T(8,128)(2,1)S(1)}) fusion(s32[]{:T(128)S(6)} %select_n.7, bf16[32,4096]{1,0:T(8,128)(2,1)} %bitcast.6, bf16[16,4096]{1,0:T(8,128)(2,1)} %bitcast.12, s32[]{:T(128)S(6)} %select_n.6), kind=kLoop, calls=%fused_computation.6 | loop fusion | flops 393216 | bytes 589832 | tf_op jit(solution)/shard_map/concatenate | solution.py:243
  0.9 4.1 %collective-permute-start.6 = (bf16[48,512]{1,0:T(8,128)(2,1)S(1)}, bf16[48,512]{1,0:T(8,128)(2,1)S(1)}, u32[]{:S(2)}, u32[]{:S(2)}) collective-permute-start(bf16[48,512]{1,0:T(8,128)(2,1)S(1)} %get-tuple-element.25.refs_0_), channel_id=1, source_target_pairs={{0,8},{4,12},{8,0},{12,4},{1,9},{5,13},{9,1},{13,5},{2,10},{6,14},... | collective-permute-start | bytes 147464 | tf_op jit(solution)/shard_map/ppermute | solution.py:38
  5.0 0.1 collective-permute-start
  5.1 2.3 %shard_map.82 = (bf16[128,4096]{1,0:T(8,128)(2,1)S(1)}, bf16[128,4096]{1,0:T(8,128)(2,1)S(1)}, bf16[128,4096]{1,0:T(8,128)(2,1)S(1)}, bf16[128,4096]{1,0:T(8,128...) custom-call(bf16[128,4096]{1,0:T(8,128)(2,1)} %bitcast.8, bf16[128,4096]{1,0:T(8,128)(2,1)} %bitcast.9, ...), custom_call_target="tpu_custom_call" | custom-call | flops 1073741824 | bytes 65536 | tf_op jit(solution)/shard_map/pallas_call | solution.py:26
  7.4 0.2 collective-permute-done.6.refs_1_.refs_0_
  7.6 2.1 %collective-permute-start.7 = (bf16[96,512]{1,0:T(8,128)(2,1)S(1)}, bf16[96,512]{1,0:T(8,128)(2,1)S(1)}, u32[]{:S(2)}, u32[]{:S(2)}) collective-permute-start(bf16[96,512]{1,0:T(8,128)(2,1)S(1)} %shard_map.86), channel_id=1, source_target_pairs={{0,4},{4,0},{8,12},{12,8},{1,5},{5,1},{9,13},{13,9},{2,6},{6,2},{1... | collective-permute-start | bytes 294920 | tf_op jit(solution)/shard_map/ppermute | solution.py:38
  9.7 3.4 %collective-permute-start.4 = (bf16[48,1024]{1,0:T(8,128)(2,1)S(1)}, bf16[48,1024]{1,0:T(8,128)(2,1)S(1)}, u32[]{:S(2)}, u32[]{:S(2)}) collective-permute-start(bf16[48,1024]{1,0:T(8,128)(2,1)S(1)} %get-tuple-element.23.refs_0_), channel_id=1, source_target_pairs={{0,8},{4,12},{8,0},{12,4},{1,9},{5,13},{9,1},{13,5},{2,10},{6,14},... | collective-permute-start | bytes 294920 | tf_op jit(solution)/shard_map/ppermute | solution.py:38
  13.1 0.0 collective-permute-done.refs_1_.refs_0_
  13.1 0.1 collective-permute-start.1
  13.3 0.0 collective-permute-done.7.refs_1_
  13.3 1.6 %collective-permute-start.8 = (bf16[144,512]{1,0:T(8,128)(2,1)S(1)}, bf16[144,512]{1,0:T(8,128)(2,1)S(1)}, u32[]{:S(2)}, u32[]{:S(2)}) collective-permute-start(bf16[144,512]{1,0:T(8,128)(2,1)S(1)} %shard_map.87.refs_6_), channel_id=1, source_target_pairs={{0,2},{2,0},{16,18},{18,16},{1,3},{3,1},{17,19},{19,17},{4,6},{6,4... | collective-permute-start | bytes 442376 | tf_op jit(solution)/shard_map/ppermute | solution.py:38
  14.9 1.5 %collective-permute-start.9 = (bf16[144,512]{1,0:T(8,128)(2,1)S(1)}, bf16[144,512]{1,0:T(8,128)(2,1)S(1)}, u32[]{:S(2)}, u32[]{:S(2)}) collective-permute-start(bf16[144,512]{1,0:T(8,128)(2,1)S(1)} %shard_map.87.refs_6_), channel_id=1, source_target_pairs={{0,16},{2,18},{16,0},{18,2},{1,17},{3,19},{17,1},{19,3},{4,20},{6,... | collective-permute-start | bytes 442376 | tf_op jit(solution)/shard_map/ppermute | solution.py:38
  16.4 1.0 %collective-permute-done.4.refs_1_.refs_8_ = bf16[48,1024]{1,0:T(8,128)(2,1)S(1)} collective-permute-done((bf16[48,1024]{1,0:T(8,128)(2,1)S(1)}, bf16[48,1024]{1,0:T(8,128)(2,1)S(1)}, u32[]{:S(2)}, u32[]{:S(2)}) %collective-permute-start.4) | collective-permute-done | bytes 98336 | tf_op jit(solution)/shard_map/ppermute | solution.py:38
  17.4 1.5 %collective-permute-start.5 = (bf16[96,1024]{1,0:T(8,128)(2,1)S(1)}, bf16[96,1024]{1,0:T(8,128)(2,1)S(1)}, u32[]{:S(2)}, u32[]{:S(2)}) collective-permute-start(bf16[96,1024]{1,0:T(8,128)(2,1)S(1)} %shard_map.85), channel_id=1, source_target_pairs={{0,4},{4,0},{8,12},{12,8},{1,5},{5,1},{9,13},{13,9},{2,6},{6,2},{1... | collective-permute-start | bytes 589832 | tf_op jit(solution)/shard_map/ppermute | solution.py:38
  18.9 0.0 collective-permute-done.1.refs_1_
  18.9 1.6 %collective-permute-start.2 = (bf16[144,512]{1,0:T(8,128)(2,1)S(1)}, bf16[144,512]{1,0:T(8,128)(2,1)S(1)}, u32[]{:S(2)}, u32[]{:S(2)}) collective-permute-start(bf16[144,512]{1,0:T(8,128)(2,1)S(1)} %shard_map.84.refs_7_), channel_id=1, source_target_pairs={{0,2},{2,0},{16,18},{18,16},{1,3},{3,1},{17,19},{19,17},{4,6},{6,4... | collective-permute-start | bytes 442376 | tf_op jit(solution)/shard_map/ppermute | solution.py:38
  20.5 1.5 %collective-permute-start.3 = (bf16[144,512]{1,0:T(8,128)(2,1)S(1)}, bf16[144,512]{1,0:T(8,128)(2,1)S(1)}, u32[]{:S(2)}, u32[]{:S(2)}) collective-permute-start(bf16[144,512]{1,0:T(8,128)(2,1)S(1)} %shard_map.84.refs_7_), channel_id=1, source_target_pairs={{0,16},{2,18},{16,0},{18,2},{1,17},{3,19},{17,1},{19,3},{4,20},{6,... | collective-permute-start | bytes 442376 | tf_op jit(solution)/shard_map/ppermute | solution.py:38
  22.0 0.5 %shard_map.88.refs_8_ = f32[384,128]{1,0:T(8,128)S(1)} custom-call(bf16[128,4096]{1,0:T(8,128)(2,1)S(1)} %get-tuple-element.14.refs_0_, bf16[128,4096]{1,0:T(8,128)(2,1)S(1)} %get-tuple-element.15.refs_1_, bf16[128,4096]{1,0:T(8,128)(2,1)S(1)} %get-tuple-element.16.refs_2_, bf16[128,4096]{1,0:T(8,128)(2,1)S(1)} %get-tuple-element.17.refs_3_, ...), custom_call_target="tpu_custom_call" | custom-call | flops 1073741824 | bytes 65536 | tf_op jit(solution)/shard_map/pallas_call | solution.py:26
  22.6 0.0 collective-permute-done.8.refs_6_
  22.6 0.0 collective-permute-done.9.refs_7_
  22.6 0.5 %shard_map.89.refs_10_ = f32[384,128]{1,0:T(8,128)S(1)} custom-call(bf16[128,4096]{1,0:T(8,128)(2,1)S(1)} %get-tuple-element.14.refs_0_, bf16[128,4096]{1,0:T(8,128)(2,1)S(1)} %get-tuple-element.15.refs_1_, bf16[128,4096]{1,0:T(8,128)(2,1)S(1)} %get-tuple-element.16.refs_2_, bf16[128,4096]{1,0:T(8,128)(2,1)S(1)} %get-tuple-element.17.refs_3_, ...), custom_call_target="tpu_custom_call" | custom-call | flops 1073741824 | bytes 65536 | tf_op jit(solution)/shard_map/pallas_call | solution.py:26
  23.1 1.0 %collective-permute-done.2.refs_6_ = bf16[144,512]{1,0:T(8,128)(2,1)S(1)} collective-permute-done((bf16[144,512]{1,0:T(8,128)(2,1)S(1)}, bf16[144,512]{1,0:T(8,128)(2,1)S(1)}, u32[]{:S(2)}, u32[]{:S(2)}) %collective-permute-start.2) | collective-permute-done | bytes 147488 | tf_op jit(solution)/shard_map/ppermute | solution.py:38
  24.2 1.5 %collective-permute-done.3.refs_7_ = bf16[144,512]{1,0:T(8,128)(2,1)S(1)} collective-permute-done((bf16[144,512]{1,0:T(8,128)(2,1)S(1)}, bf16[144,512]{1,0:T(8,128)(2,1)S(1)}, u32[]{:S(2)}, u32[]{:S(2)}) %collective-permute-start.3) | collective-permute-done | bytes 147488 | tf_op jit(solution)/shard_map/ppermute | solution.py:38
  25.7 0.0 collective-permute-done.5.refs_9_
  25.7 0.8 %shard_map.90.mine = f32[384,128]{1,0:T(8,128)S(1)} custom-call(bf16[128,4096]{1,0:T(8,128)(2,1)S(1)} %get-tuple-element.14.refs_0_, bf16[128,4096]{1,0:T(8,128)(2,1)S(1)} %get-tuple-element.15.refs_1_, bf16[128,4096]{1,0:T(8,128)(2,1)S(1)} %get-tuple-element.16.refs_2_, bf16[128,4096]{1,0:T(8,128)(2,1)S(1)} %get-tuple-element.17.refs_3_, ...), custom_call_target="tpu_custom_call" | custom-call | flops 1073741824 | bytes 65536 | tf_op jit(solution)/shard_map/pallas_call | solution.py:26
  26.5 0.1 collective-permute-start.10
  27.9 0.1 collective-permute-done.10.other
  28.0 0.5 shard_map.91
  28.5 0.6 %collective-permute-start.11 = (f32[136,128]{1,0:T(8,128)S(1)}, f32[136,128]{1,0:T(8,128)S(1)}, u32[]{:S(2)}, u32[]{:S(2)}) collective-permute-start(f32[136,128]{1,0:T(8,128)S(1)} %get-tuple-element.20), channel_id=1, source_target_pairs={{0,2},{2,0},{1,3},{3,1},{4,6},{6,4},{5,7},{7,5},{8,10},{10,8},{9,1... | collective-permute-start | bytes 208904 | tf_op jit(solution)/shard_map/ppermute | solution.py:38
  29.0 5.1 %collective-permute-start.14 = (f32[1,64,128]{2,1,0:T(8,128)S(1)}, f32[1,64,128]{2,1,0:T(8,128)S(1)}, u32[]{:S(2)}, u32[]{:S(2)}) collective-permute-start(f32[1,64,128]{2,1,0:T(8,128)S(1)} %get-tuple-element.22), channel_id=1, source_target_pairs={{0,8},{4,12},{8,0},{12,4},{1,9},{5,13},{9,1},{13,5},{2,10},{6,14},... | collective-permute-start | bytes 98312 | tf_op jit(solution)/shard_map/ppermute | solution.py:38
  34.2 0.0 collective-permute-done.11
  34.2 3.0 %collective-permute-start.12 = (f32[136,128]{1,0:T(8,128)S(1)}, f32[136,128]{1,0:T(8,128)S(1)}, u32[]{:S(2)}, u32[]{:S(2)}) collective-permute-start(f32[136,128]{1,0:T(8,128)S(1)} %add.21), channel_id=1, source_target_pairs={{0,8},{4,12},{8,0},{12,4},{1,9},{5,13},{9,1},{13,5},{2,10},{6,14},... | collective-permute-start | bytes 208904 | tf_op jit(solution)/shard_map/ppermute | solution.py:38
  37.2 0.0 collective-permute-done.14
  37.2 0.1 collective-permute-start.15
  37.3 2.9 %collective-permute-done.12 = f32[136,128]{1,0:T(8,128)S(1)} collective-permute-done((f32[136,128]{1,0:T(8,128)S(1)}, f32[136,128]{1,0:T(8,128)S(1)}, u32[]{:S(2)}, u32[]{:S(2)}) %collective-permute-start.12) | collective-permute-done | bytes 69664 | tf_op jit(solution)/shard_map/ppermute | solution.py:38
  40.2 0.1 collective-permute-start.13
  40.3 1.3 %collective-permute-done.15 = f32[2,64,128]{2,1,0:T(8,128)S(1)} collective-permute-done((f32[2,64,128]{2,1,0:T(8,128)S(1)}, f32[2,64,128]{2,1,0:T(8,128)S(1)}, u32[]{:S(2)}, u32[]{:S(2)}) %collective-permute-start.15) | collective-permute-done | bytes 65568 | tf_op jit(solution)/shard_map/ppermute | solution.py:38
  41.6 1.6 %collective-permute-start.16 = (f32[4,64,128]{2,1,0:T(8,128)S(1)}, f32[4,64,128]{2,1,0:T(8,128)S(1)}, u32[]{:S(2)}, u32[]{:S(2)}) collective-permute-start(f32[4,64,128]{2,1,0:T(8,128)S(1)} %pad_maximum_fusion.1), channel_id=1, source_target_pairs={{0,2},{2,0},{1,3},{3,1},{4,6},{6,4},{5,7},{7,5},{8,10},{10,8},{9,1... | collective-permute-start | bytes 393224 | tf_op jit(solution)/shard_map/ppermute | solution.py:38
  43.1 1.4 %collective-permute-done.13 = f32[136,128]{1,0:T(8,128)S(1)} collective-permute-done((f32[136,128]{1,0:T(8,128)S(1)}, f32[136,128]{1,0:T(8,128)S(1)}, u32[]{:S(2)}, u32[]{:S(2)}) %collective-permute-start.13) | collective-permute-done | bytes 69664 | tf_op jit(solution)/shard_map/ppermute | solution.py:38
  44.6 3.8 %shard_map.92.side_ref = f32[64,128]{1,0:T(8,128)S(1)} custom-call(f32[136,128]{1,0:T(8,128)S(1)} %add.23.fac_ref, f32[128,64]{1,0:T(8,128)S(1)} %get-tuple-element.21.gtr_ref), custom_call_target="tpu_custom_call" | custom-call | flops 4294967296 | bytes 65536 | tf_op jit(solution)/shard_map/pallas_call | solution.py:26
  48.3 0.0 collective-permute-done.16
  48.4 0.6 %shard_map.93 = f32[1,8]{1,0:T(1,128)} custom-call(f32[64,128]{1,0:T(8,128)S(1)} %shard_map.92.side_ref, f32[8,64,128]{2,1,0:T(8,128)S(1)} %pad_maximum_fusion.gte_ref), custom_call_target="tpu_custom_call" | custom-call | bytes 65536 | tf_op jit(solution)/shard_map/pallas_call | solution.py:26
  (12 shorter events, 0.1 us)
Async XLA Ops:
  0.9 6.7 %collective-permute-start.6 = (bf16[48,512]{1,0:T(8,128)(2,1)S(1)}, bf16[48,512]{1,0:T(8,128)(2,1)S(1)}, u32[]{:S(2)}, u32[]{:S(2)}) collective-permute-start(bf16[48,512]{1,0:T(8,128)(2,1)S(1)} %get-tuple-element.25.refs_0_), channel_id=1, source_target_pairs={{0,8},{4,12},{8,0},{12,4},{1,9},{5,13},{9,1},{13,5},{2,10},{6,14},... | collective-permute-start | bytes 147464 | tf_op jit(solution)/shard_map/ppermute | solution.py:38
  5.0 8.1 %collective-permute-start = (bf16[48,512]{1,0:T(8,128)(2,1)S(1)}, bf16[48,512]{1,0:T(8,128)(2,1)S(1)}, u32[]{:S(2)}, u32[]{:S(2)}) collective-permute-start(bf16[48,512]{1,0:T(8,128)(2,1)S(1)} %get-tuple-element.26.refs_0_), channel_id=1, source_target_pairs={{0,8},{4,12},{8,0},{12,4},{1,9},{5,13},{9,1},{13,5},{2,10},{6,14},... | collective-permute-start | bytes 147464 | tf_op jit(solution)/shard_map/ppermute | solution.py:38
  7.6 5.7 %collective-permute-start.7 = (bf16[96,512]{1,0:T(8,128)(2,1)S(1)}, bf16[96,512]{1,0:T(8,128)(2,1)S(1)}, u32[]{:S(2)}, u32[]{:S(2)}) collective-permute-start(bf16[96,512]{1,0:T(8,128)(2,1)S(1)} %shard_map.86), channel_id=1, source_target_pairs={{0,4},{4,0},{8,12},{12,8},{1,5},{5,1},{9,13},{13,9},{2,6},{6,2},{1... | collective-permute-start | bytes 294920 | tf_op jit(solution)/shard_map/ppermute | solution.py:38
  9.7 7.7 %collective-permute-start.4 = (bf16[48,1024]{1,0:T(8,128)(2,1)S(1)}, bf16[48,1024]{1,0:T(8,128)(2,1)S(1)}, u32[]{:S(2)}, u32[]{:S(2)}) collective-permute-start(bf16[48,1024]{1,0:T(8,128)(2,1)S(1)} %get-tuple-element.23.refs_0_), channel_id=1, source_target_pairs={{0,8},{4,12},{8,0},{12,4},{1,9},{5,13},{9,1},{13,5},{2,10},{6,14},... | collective-permute-start | bytes 294920 | tf_op jit(solution)/shard_map/ppermute | solution.py:38
  13.1 5.8 %collective-permute-start.1 = (bf16[96,512]{1,0:T(8,128)(2,1)S(1)}, bf16[96,512]{1,0:T(8,128)(2,1)S(1)}, u32[]{:S(2)}, u32[]{:S(2)}) collective-permute-start(bf16[96,512]{1,0:T(8,128)(2,1)S(1)} %shard_map.83), channel_id=1, source_target_pairs={{0,4},{4,0},{8,12},{12,8},{1,5},{5,1},{9,13},{13,9},{2,6},{6,2},{1... | collective-permute-start | bytes 294920 | tf_op jit(solution)/shard_map/ppermute | solution.py:38
  13.3 9.3 %collective-permute-start.8 = (bf16[144,512]{1,0:T(8,128)(2,1)S(1)}, bf16[144,512]{1,0:T(8,128)(2,1)S(1)}, u32[]{:S(2)}, u32[]{:S(2)}) collective-permute-start(bf16[144,512]{1,0:T(8,128)(2,1)S(1)} %shard_map.87.refs_6_), channel_id=1, source_target_pairs={{0,2},{2,0},{16,18},{18,16},{1,3},{3,1},{17,19},{19,17},{4,6},{6,4... | collective-permute-start | bytes 442376 | tf_op jit(solution)/shard_map/ppermute | solution.py:38
  14.9 7.7 %collective-permute-start.9 = (bf16[144,512]{1,0:T(8,128)(2,1)S(1)}, bf16[144,512]{1,0:T(8,128)(2,1)S(1)}, u32[]{:S(2)}, u32[]{:S(2)}) collective-permute-start(bf16[144,512]{1,0:T(8,128)(2,1)S(1)} %shard_map.87.refs_6_), channel_id=1, source_target_pairs={{0,16},{2,18},{16,0},{18,2},{1,17},{3,19},{17,1},{19,3},{4,20},{6,... | collective-permute-start | bytes 442376 | tf_op jit(solution)/shard_map/ppermute | solution.py:38
  17.4 8.3 %collective-permute-start.5 = (bf16[96,1024]{1,0:T(8,128)(2,1)S(1)}, bf16[96,1024]{1,0:T(8,128)(2,1)S(1)}, u32[]{:S(2)}, u32[]{:S(2)}) collective-permute-start(bf16[96,1024]{1,0:T(8,128)(2,1)S(1)} %shard_map.85), channel_id=1, source_target_pairs={{0,4},{4,0},{8,12},{12,8},{1,5},{5,1},{9,13},{13,9},{2,6},{6,2},{1... | collective-permute-start | bytes 589832 | tf_op jit(solution)/shard_map/ppermute | solution.py:38
  18.9 5.2 %collective-permute-start.2 = (bf16[144,512]{1,0:T(8,128)(2,1)S(1)}, bf16[144,512]{1,0:T(8,128)(2,1)S(1)}, u32[]{:S(2)}, u32[]{:S(2)}) collective-permute-start(bf16[144,512]{1,0:T(8,128)(2,1)S(1)} %shard_map.84.refs_7_), channel_id=1, source_target_pairs={{0,2},{2,0},{16,18},{18,16},{1,3},{3,1},{17,19},{19,17},{4,6},{6,4... | collective-permute-start | bytes 442376 | tf_op jit(solution)/shard_map/ppermute | solution.py:38
  20.5 5.1 %collective-permute-start.3 = (bf16[144,512]{1,0:T(8,128)(2,1)S(1)}, bf16[144,512]{1,0:T(8,128)(2,1)S(1)}, u32[]{:S(2)}, u32[]{:S(2)}) collective-permute-start(bf16[144,512]{1,0:T(8,128)(2,1)S(1)} %shard_map.84.refs_7_), channel_id=1, source_target_pairs={{0,16},{2,18},{16,0},{18,2},{1,17},{3,19},{17,1},{19,3},{4,20},{6,... | collective-permute-start | bytes 442376 | tf_op jit(solution)/shard_map/ppermute | solution.py:38
  26.5 1.5 %collective-permute-start.10 = (f32[384,128]{1,0:T(8,128)S(1)}, f32[384,128]{1,0:T(8,128)S(1)}, u32[]{:S(2)}, u32[]{:S(2)}) collective-permute-start(f32[384,128]{1,0:T(8,128)S(1)} %shard_map.90.mine), channel_id=1, source_target_pairs={{0,1},{1,0},{2,3},{3,2},{4,5},{5,4},{6,7},{7,6},{8,9},{9,8},{10,11... | collective-permute-start | bytes 589832 | tf_op jit(solution)/shard_map/ppermute | solution.py:38
  28.5 5.7 %collective-permute-start.11 = (f32[136,128]{1,0:T(8,128)S(1)}, f32[136,128]{1,0:T(8,128)S(1)}, u32[]{:S(2)}, u32[]{:S(2)}) collective-permute-start(f32[136,128]{1,0:T(8,128)S(1)} %get-tuple-element.20), channel_id=1, source_target_pairs={{0,2},{2,0},{1,3},{3,1},{4,6},{6,4},{5,7},{7,5},{8,10},{10,8},{9,1... | collective-permute-start | bytes 208904 | tf_op jit(solution)/shard_map/ppermute | solution.py:38
  29.0 8.2 %collective-permute-start.14 = (f32[1,64,128]{2,1,0:T(8,128)S(1)}, f32[1,64,128]{2,1,0:T(8,128)S(1)}, u32[]{:S(2)}, u32[]{:S(2)}) collective-permute-start(f32[1,64,128]{2,1,0:T(8,128)S(1)} %get-tuple-element.22), channel_id=1, source_target_pairs={{0,8},{4,12},{8,0},{12,4},{1,9},{5,13},{9,1},{13,5},{2,10},{6,14},... | collective-permute-start | bytes 98312 | tf_op jit(solution)/shard_map/ppermute | solution.py:38
  34.2 6.0 %collective-permute-start.12 = (f32[136,128]{1,0:T(8,128)S(1)}, f32[136,128]{1,0:T(8,128)S(1)}, u32[]{:S(2)}, u32[]{:S(2)}) collective-permute-start(f32[136,128]{1,0:T(8,128)S(1)} %add.21), channel_id=1, source_target_pairs={{0,8},{4,12},{8,0},{12,4},{1,9},{5,13},{9,1},{13,5},{2,10},{6,14},... | collective-permute-start | bytes 208904 | tf_op jit(solution)/shard_map/ppermute | solution.py:38
  37.2 4.3 %collective-permute-start.15 = (f32[2,64,128]{2,1,0:T(8,128)S(1)}, f32[2,64,128]{2,1,0:T(8,128)S(1)}, u32[]{:S(2)}, u32[]{:S(2)}) collective-permute-start(f32[2,64,128]{2,1,0:T(8,128)S(1)} %pad_maximum_fusion.2), channel_id=1, source_target_pairs={{0,4},{4,0},{8,12},{12,8},{1,5},{5,1},{9,13},{13,9},{2,6},{6,2},{1... | collective-permute-start | bytes 196616 | tf_op jit(solution)/shard_map/ppermute | solution.py:38
  40.2 4.4 %collective-permute-start.13 = (f32[136,128]{1,0:T(8,128)S(1)}, f32[136,128]{1,0:T(8,128)S(1)}, u32[]{:S(2)}, u32[]{:S(2)}) collective-permute-start(f32[136,128]{1,0:T(8,128)S(1)} %add.22), channel_id=1, source_target_pairs={{0,4},{4,0},{8,12},{12,8},{1,5},{5,1},{9,13},{13,9},{2,6},{6,2},{1... | collective-permute-start | bytes 208904 | tf_op jit(solution)/shard_map/ppermute | solution.py:38
  41.6 6.8 %collective-permute-start.16 = (f32[4,64,128]{2,1,0:T(8,128)S(1)}, f32[4,64,128]{2,1,0:T(8,128)S(1)}, u32[]{:S(2)}, u32[]{:S(2)}) collective-permute-start(f32[4,64,128]{2,1,0:T(8,128)S(1)} %pad_maximum_fusion.1), channel_id=1, source_target_pairs={{0,2},{2,0},{1,3},{3,1},{4,6},{6,4},{5,7},{7,5},{8,10},{10,8},{9,1... | collective-permute-start | bytes 393224 | tf_op jit(solution)/shard_map/ppermute | solution.py:38

commit v7 on v6

--- a/solution.py
+++ b/solution.py
@@ -36,6 +36,11 @@
 
 def swap(x, axis, count, k):
     return lax.ppermute(x, axis, [(i, i ^ k) for i in range(count)])
+
+
+def swap_on(x, axis, count, k, core):
+    pairs = [(2 * i + core, 2 * (i ^ k) + core) for i in range(count)]
+    return lax.ppermute(x, (axis, "mp"), pairs)
 
 
 def bits(count):
@@ -199,28 +204,33 @@
     return [2.0 * x - mm(x, mm(a, x)) for a, m, x, r in state]
 
 
-def side_kernel(fac_ref, gtr_ref, out_ref):
+def side_kernel(fac_ref, other_ref, gtr_ref, out_ref):
     ki = fac_ref.shape[1]
     half = ki // 2
-    top = fac_ref[:half, :]
-    low = fac_ref[half:ki, :]
+    total = jnp.where(lax.axis_index("mp") == 0, fac_ref[...], other_ref[...])
+    top = total[:half]
+    low = total[half:ki]
     c_in = jnp.concatenate(
         [top, jnp.concatenate([top[:, half:].T, low[:, :half]], axis=1)], axis=0
     )
-    count = fac_ref[ki : ki + 1, :1]
+    count = total[ki : ki + 1, :1]
     inv_in, inv_out = inverses([c_in, low[:, half:]])
     side = mm(mm(inv_in, gtr_ref[...]), inv_out) * (count * count)
     out_ref[:, :half] = side[:half]
     out_ref[:, half:] = side[half:]
 
 
-def scores_kernel(order, n_blk, side_ref, gte_ref, out_ref):
+def scores_kernel(order, n_blk, side_ref, gte_ref, other_ref, out_ref):
     z = lax.axis_index("dp")
     b = lax.axis_index("blk")
     lane = lax.broadcasted_iota(jnp.int32, out_ref.shape, 1)
     row = jnp.zeros(out_ref.shape, jnp.float32)
     side = side_ref[...]
-    sums = [jnp.sum(side * gte_ref[p], axis=0, keepdims=True) for p in range(len(order))]
+    own = lax.axis_index("mp") == 1
+    sums = [
+        jnp.sum(side * jnp.where(own, gte_ref[p], other_ref[p]), axis=0, keepdims=True)
+        for p in range(len(order))
+    ]
     values = jnp.sum(jnp.concatenate(sums, axis=0), axis=1, keepdims=True)
     for p, (dz, db) in enumerate(order):
         row = jnp.where(lane == (z ^ dz) * n_blk + (b ^ db), values[p : p + 1, :], row)
@@ -323,23 +333,25 @@
     order = [(0, 0)]
     for axis, count in (("dp", n_dp), ("blk", n_blk)):
         for k in bits(count):
-            gte = jnp.concatenate([gte, swap(gte, axis, count, k)], axis=0)
+            gte = jnp.concatenate([gte, swap_on(gte, axis, count, k, 1)], axis=0)
             order += [(dz ^ k, db) if axis == "dp" else (dz, db ^ k) for dz, db in order]
     for axis, count in (("blk", n_blk), ("dp", n_dp)):
         for k in bits(count):
-            fac = fac + swap(fac, axis, count, k)
+            fac = fac + swap_on(fac, axis, count, k, 0)
+    fac_other = lax.ppermute(fac, "mp", [(0, 1)])
+    gte_other = lax.ppermute(gte, "mp", [(1, 0)])
     side = call(
         side_kernel,
         jax.ShapeDtypeStruct((ki // 2, ki), jnp.float32),
-        [vmem()] * 2,
-        (fac, gtr),
+        [vmem()] * 3,
+        (fac, fac_other, gtr),
         flops=4 << 30,
     )
     return call(
         functools.partial(scores_kernel, order, n_blk),
         jax.ShapeDtypeStruct((1, n_dp * n_blk), jnp.float32),
-        [vmem()] * 2,
-        (side, gte),
+        [vmem()] * 3,
+        (side, gte, gte_other),
     )
 
 

time: 49.2 us -> 58.5 us (1.19); the launches traced: 49 us -> 57.5 us
  starting transfers between devices: 28.1 us -> 32.9 us
  waiting for transfers between devices: 9.45 us -> 12.9 us
    ppermute x0 -> x8, starting transfers between devices: none -> 15.3 us  [the longest x6 12.7 us: swap_on(): return lax.ppermute(x, (axis, 'mp'), pairs)]
    ppermute x17 -> x11, starting transfers between devices: 28.1 us -> 17.6 us  [swap(): return lax.ppermute(x, axis, [(i, i ^ k) for i in range(count)])]
    ppermute x0 -> x8, waiting for transfers between devices: none -> 9.07 us  [the longest x6 9.06 us: swap_on(): return lax.ppermute(x, (axis, 'mp'), pairs)]
    ppermute x17 -> x11, waiting for transfers between devices: 9.45 us -> 3.86 us  [swap(): return lax.ppermute(x, axis, [(i, i ^ k) for i in range(count)])]
  transfers between devices with their start and end apart: 17 -> 19, of which waited for: 8 -> 8; matrix products, arithmetic and copies ran while one was open for 0% -> 0% of each run, Pallas kernels for 15% -> 13%
where the time goes in v7:
time: 58.5 us; the launch traced here: 57.5 us
  starting transfers between devices  32.9 us (56%)
  waiting for transfers between devices  12.9 us (22%)
  Pallas kernels  9.16 us (16%)
  between operations  1.52 us (3%)
  other arithmetic  0.93 us (2%)
    ppermute x11, starting transfers between devices, swap(): return lax.ppermute(x, axis, [(i, i ^ k) for i in range(count)])  17.6 us
    ppermute x6, starting transfers between devices, swap_on(): return lax.ppermute(x, (axis, 'mp'), pairs)  12.7 us
    pallas_call x12, Pallas kernels, call(): pl.pallas_call(kernel, out_shape=out_shape, in_specs=in_specs, out_specs=...  9.16 us
    ppermute x6, waiting for transfers between devices, swap_on(): return lax.ppermute(x, (axis, 'mp'), pairs)  9.06 us
    ppermute x11, waiting for transfers between devices, swap(): return lax.ppermute(x, axis, [(i, i ^ k) for i in range(count)])  3.86 us
    ppermute x1, starting transfers between devices, per_device(): fac_other = lax.ppermute(fac, 'mp', [(0, 1)])  1.29 us
    ppermute x1, starting transfers between devices, per_device(): gte_other = lax.ppermute(gte, 'mp', [(1, 0)])  1.29 us
  transfers between devices with their start and end apart: 19, of which 8 were waited for; matrix products, arithmetic and copies ran while one was open for 0% of the time, Pallas kernels for 13%

profile of v7, /device:TPU:0, one launch (start us, length us, event | category | flops | bytes accessed | tf_op | source)
XLA Modules:
  0.0 57.5 jit_solution(11701228077154386483)
XLA Ops:
  0.0 0.9 %fusion = (bf16[48,1024]{1,0:T(8,128)(2,1)S(1)}, bf16[48,1024]{1,0:T(8,128)(2,1)S(1)}) fusion(s32[]{:T(128)S(6)} %select_n.7, bf16[32,4096]{1,0:T(8,128)(2,1)} %bitcast.6, bf16[16,4096]{1,0:T(8,128)(2,1)} %bitcast.12, s32[]{:T(128)S(6)} %select_n.6), kind=kLoop, calls=%fused_computation.5 | loop fusion | flops 393216 | bytes 589832 | tf_op jit(solution)/shard_map/concatenate | solution.py:253
  0.9 4.1 %collective-permute-start.6 = (bf16[48,512]{1,0:T(8,128)(2,1)S(1)}, bf16[48,512]{1,0:T(8,128)(2,1)S(1)}, u32[]{:S(2)}, u32[]{:S(2)}) collective-permute-start(bf16[48,512]{1,0:T(8,128)(2,1)S(1)} %get-tuple-element.25.refs_0_), channel_id=1, source_target_pairs={{0,8},{4,12},{8,0},{12,4},{1,9},{5,13},{9,1},{13,5},{2,10},{6,14},... | collective-permute-start | bytes 147464 | tf_op jit(solution)/shard_map/ppermute | solution.py:38
  5.0 0.1 collective-permute-start
  5.1 2.3 %shard_map.82 = (bf16[128,4096]{1,0:T(8,128)(2,1)S(1)}, bf16[128,4096]{1,0:T(8,128)(2,1)S(1)}, bf16[128,4096]{1,0:T(8,128)(2,1)S(1)}, bf16[128,4096]{1,0:T(8,128...) custom-call(bf16[128,4096]{1,0:T(8,128)(2,1)} %bitcast.8, bf16[128,4096]{1,0:T(8,128)(2,1)} %bitcast.9, ...), custom_call_target="tpu_custom_call" | custom-call | flops 1073741824 | bytes 65536 | tf_op jit(solution)/shard_map/pallas_call | solution.py:26
  7.4 0.2 collective-permute-done.6.refs_1_.refs_0_
  7.6 2.1 %collective-permute-start.7 = (bf16[96,512]{1,0:T(8,128)(2,1)S(1)}, bf16[96,512]{1,0:T(8,128)(2,1)S(1)}, u32[]{:S(2)}, u32[]{:S(2)}) collective-permute-start(bf16[96,512]{1,0:T(8,128)(2,1)S(1)} %shard_map.86), channel_id=1, source_target_pairs={{0,4},{4,0},{8,12},{12,8},{1,5},{5,1},{9,13},{13,9},{2,6},{6,2},{1... | collective-permute-start | bytes 294920 | tf_op jit(solution)/shard_map/ppermute | solution.py:38
  9.7 3.4 %collective-permute-start.4 = (bf16[48,1024]{1,0:T(8,128)(2,1)S(1)}, bf16[48,1024]{1,0:T(8,128)(2,1)S(1)}, u32[]{:S(2)}, u32[]{:S(2)}) collective-permute-start(bf16[48,1024]{1,0:T(8,128)(2,1)S(1)} %get-tuple-element.23.refs_0_), channel_id=1, source_target_pairs={{0,8},{4,12},{8,0},{12,4},{1,9},{5,13},{9,1},{13,5},{2,10},{6,14},... | collective-permute-start | bytes 294920 | tf_op jit(solution)/shard_map/ppermute | solution.py:38
  13.1 0.0 collective-permute-done.refs_1_.refs_0_
  13.1 0.1 collective-permute-start.1
  13.3 0.0 collective-permute-done.7.refs_1_
  13.3 1.6 %collective-permute-start.8 = (bf16[144,512]{1,0:T(8,128)(2,1)S(1)}, bf16[144,512]{1,0:T(8,128)(2,1)S(1)}, u32[]{:S(2)}, u32[]{:S(2)}) collective-permute-start(bf16[144,512]{1,0:T(8,128)(2,1)S(1)} %shard_map.87.refs_6_), channel_id=1, source_target_pairs={{0,2},{2,0},{16,18},{18,16},{1,3},{3,1},{17,19},{19,17},{4,6},{6,4... | collective-permute-start | bytes 442376 | tf_op jit(solution)/shard_map/ppermute | solution.py:38
  14.9 1.5 %collective-permute-start.9 = (bf16[144,512]{1,0:T(8,128)(2,1)S(1)}, bf16[144,512]{1,0:T(8,128)(2,1)S(1)}, u32[]{:S(2)}, u32[]{:S(2)}) collective-permute-start(bf16[144,512]{1,0:T(8,128)(2,1)S(1)} %shard_map.87.refs_6_), channel_id=1, source_target_pairs={{0,16},{2,18},{16,0},{18,2},{1,17},{3,19},{17,1},{19,3},{4,20},{6,... | collective-permute-start | bytes 442376 | tf_op jit(solution)/shard_map/ppermute | solution.py:38
  16.4 1.0 %collective-permute-done.4.refs_1_.refs_8_ = bf16[48,1024]{1,0:T(8,128)(2,1)S(1)} collective-permute-done((bf16[48,1024]{1,0:T(8,128)(2,1)S(1)}, bf16[48,1024]{1,0:T(8,128)(2,1)S(1)}, u32[]{:S(2)}, u32[]{:S(2)}) %collective-permute-start.4) | collective-permute-done | bytes 98336 | tf_op jit(solution)/shard_map/ppermute | solution.py:38
  17.4 1.5 %collective-permute-start.5 = (bf16[96,1024]{1,0:T(8,128)(2,1)S(1)}, bf16[96,1024]{1,0:T(8,128)(2,1)S(1)}, u32[]{:S(2)}, u32[]{:S(2)}) collective-permute-start(bf16[96,1024]{1,0:T(8,128)(2,1)S(1)} %shard_map.85), channel_id=1, source_target_pairs={{0,4},{4,0},{8,12},{12,8},{1,5},{5,1},{9,13},{13,9},{2,6},{6,2},{1... | collective-permute-start | bytes 589832 | tf_op jit(solution)/shard_map/ppermute | solution.py:38
  18.9 0.0 collective-permute-done.1.refs_1_
  18.9 1.6 %collective-permute-start.2 = (bf16[144,512]{1,0:T(8,128)(2,1)S(1)}, bf16[144,512]{1,0:T(8,128)(2,1)S(1)}, u32[]{:S(2)}, u32[]{:S(2)}) collective-permute-start(bf16[144,512]{1,0:T(8,128)(2,1)S(1)} %shard_map.84.refs_7_), channel_id=1, source_target_pairs={{0,2},{2,0},{16,18},{18,16},{1,3},{3,1},{17,19},{19,17},{4,6},{6,4... | collective-permute-start | bytes 442376 | tf_op jit(solution)/shard_map/ppermute | solution.py:38
  20.5 1.5 %collective-permute-start.3 = (bf16[144,512]{1,0:T(8,128)(2,1)S(1)}, bf16[144,512]{1,0:T(8,128)(2,1)S(1)}, u32[]{:S(2)}, u32[]{:S(2)}) collective-permute-start(bf16[144,512]{1,0:T(8,128)(2,1)S(1)} %shard_map.84.refs_7_), channel_id=1, source_target_pairs={{0,16},{2,18},{16,0},{18,2},{1,17},{3,19},{17,1},{19,3},{4,20},{6,... | collective-permute-start | bytes 442376 | tf_op jit(solution)/shard_map/ppermute | solution.py:38
  22.0 0.5 shard_map.88.refs_8_
  22.6 0.0 collective-permute-done.8.refs_6_
  22.6 0.0 collective-permute-done.9.refs_7_
  22.6 0.5 shard_map.89.refs_10_
  23.1 1.0 %collective-permute-done.2.refs_6_ = bf16[144,512]{1,0:T(8,128)(2,1)S(1)} collective-permute-done((bf16[144,512]{1,0:T(8,128)(2,1)S(1)}, bf16[144,512]{1,0:T(8,128)(2,1)S(1)}, u32[]{:S(2)}, u32[]{:S(2)}) %collective-permute-start.2) | collective-permute-done | bytes 147488 | tf_op jit(solution)/shard_map/ppermute | solution.py:38
  24.2 1.5 %collective-permute-done.3.refs_7_ = bf16[144,512]{1,0:T(8,128)(2,1)S(1)} collective-permute-done((bf16[144,512]{1,0:T(8,128)(2,1)S(1)}, bf16[144,512]{1,0:T(8,128)(2,1)S(1)}, u32[]{:S(2)}, u32[]{:S(2)}) %collective-permute-start.3) | collective-permute-done | bytes 147488 | tf_op jit(solution)/shard_map/ppermute | solution.py:38
  25.7 0.0 collective-permute-done.5.refs_9_
  25.7 0.8 %shard_map.90.mine = f32[384,128]{1,0:T(8,128)S(1)} custom-call(bf16[128,4096]{1,0:T(8,128)(2,1)S(1)} %get-tuple-element.14.refs_0_, bf16[128,4096]{1,0:T(8,128)(2,1)S(1)} %get-tuple-element.15.refs_1_, bf16[128,4096]{1,0:T(8,128)(2,1)S(1)} %get-tuple-element.16.refs_2_, bf16[128,4096]{1,0:T(8,128)(2,1)S(1)} %get-tuple-element.17.refs_3_, ...), custom_call_target="tpu_custom_call" | custom-call | flops 1073741824 | bytes 65536 | tf_op jit(solution)/shard_map/pallas_call | solution.py:26
  26.5 0.1 collective-permute-start.10
  27.9 0.1 collective-permute-done.10.other
  28.0 0.5 shard_map.91
  28.5 0.7 %collective-permute-start.15 = (f32[1,64,128]{2,1,0:T(8,128)S(1)}, f32[1,64,128]{2,1,0:T(8,128)S(1)}, u32[]{:S(2)}, u32[]{:S(2)}) collective-permute-start(f32[1,64,128]{2,1,0:T(8,128)S(1)} %get-tuple-element.22), channel_id=1, source_target_pairs={{1,9},{5,13},{9,1},{13,5},{3,11},{7,15},{11,3},{15,7},{17,25},{21,... | collective-permute-start | bytes 98312 | tf_op jit(solution)/shard_map/ppermute | solution.py:43
  29.1 2.4 %collective-permute-start.11 = (f32[136,128]{1,0:T(8,128)S(1)}, f32[136,128]{1,0:T(8,128)S(1)}, u32[]{:S(2)}, u32[]{:S(2)}) collective-permute-start(f32[136,128]{1,0:T(8,128)S(1)} %get-tuple-element.20), channel_id=1, source_target_pairs={{0,2},{2,0},{4,6},{6,4},{8,10},{10,8},{12,14},{14,12},{16,18},{18,... | collective-permute-start | bytes 208904 | tf_op jit(solution)/shard_map/ppermute | solution.py:43
  31.6 0.0 collective-permute-done.15
  31.6 0.7 %collective-permute-start.16 = (f32[2,64,128]{2,1,0:T(8,128)S(1)}, f32[2,64,128]{2,1,0:T(8,128)S(1)}, u32[]{:S(2)}, u32[]{:S(2)}) collective-permute-start(f32[2,64,128]{2,1,0:T(8,128)S(1)} %pad_maximum_fusion.1), channel_id=1, source_target_pairs={{1,5},{5,1},{9,13},{13,9},{3,7},{7,3},{11,15},{15,11},{17,21},{21,... | collective-permute-start | bytes 196616 | tf_op jit(solution)/shard_map/ppermute | solution.py:43
  32.3 3.0 %collective-permute-done.11 = f32[136,128]{1,0:T(8,128)S(1)} collective-permute-done((f32[136,128]{1,0:T(8,128)S(1)}, f32[136,128]{1,0:T(8,128)S(1)}, u32[]{:S(2)}, u32[]{:S(2)}) %collective-permute-start.11) | collective-permute-done | bytes 69664 | tf_op jit(solution)/shard_map/ppermute | solution.py:43
  35.3 6.1 %collective-permute-start.12 = (f32[136,128]{1,0:T(8,128)S(1)}, f32[136,128]{1,0:T(8,128)S(1)}, u32[]{:S(2)}, u32[]{:S(2)}) collective-permute-start(f32[136,128]{1,0:T(8,128)S(1)} %add.21), channel_id=1, source_target_pairs={{0,8},{4,12},{8,0},{12,4},{2,10},{6,14},{10,2},{14,6},{16,24},{20,... | collective-permute-start | bytes 208904 | tf_op jit(solution)/shard_map/ppermute | solution.py:43
  41.4 0.0 collective-permute-done.16
  41.5 0.7 %collective-permute-start.17 = (f32[4,64,128]{2,1,0:T(8,128)S(1)}, f32[4,64,128]{2,1,0:T(8,128)S(1)}, u32[]{:S(2)}, u32[]{:S(2)}) collective-permute-start(f32[4,64,128]{2,1,0:T(8,128)S(1)} %pad_maximum_fusion), channel_id=1, source_target_pairs={{1,3},{3,1},{5,7},{7,5},{9,11},{11,9},{13,15},{15,13},{17,19},{19,... | collective-permute-start | bytes 393224 | tf_op jit(solution)/shard_map/ppermute | solution.py:43
  42.2 2.0 %collective-permute-done.12 = f32[136,128]{1,0:T(8,128)S(1)} collective-permute-done((f32[136,128]{1,0:T(8,128)S(1)}, f32[136,128]{1,0:T(8,128)S(1)}, u32[]{:S(2)}, u32[]{:S(2)}) %collective-permute-start.12) | collective-permute-done | bytes 69664 | tf_op jit(solution)/shard_map/ppermute | solution.py:43
  44.2 2.2 %collective-permute-start.13 = (f32[136,128]{1,0:T(8,128)S(1)}, f32[136,128]{1,0:T(8,128)S(1)}, u32[]{:S(2)}, u32[]{:S(2)}) collective-permute-start(f32[136,128]{1,0:T(8,128)S(1)} %add.22), channel_id=1, source_target_pairs={{0,4},{4,0},{8,12},{12,8},{2,6},{6,2},{10,14},{14,10},{16,20},{20,... | collective-permute-start | bytes 208904 | tf_op jit(solution)/shard_map/ppermute | solution.py:43
  46.4 4.0 %collective-permute-done.13 = f32[136,128]{1,0:T(8,128)S(1)} collective-permute-done((f32[136,128]{1,0:T(8,128)S(1)}, f32[136,128]{1,0:T(8,128)S(1)}, u32[]{:S(2)}, u32[]{:S(2)}) %collective-permute-start.13) | collective-permute-done | bytes 69664 | tf_op jit(solution)/shard_map/ppermute | solution.py:43
  50.4 1.3 %collective-permute-start.14 = (f32[136,128]{1,0:T(8,128)S(1)}, f32[136,128]{1,0:T(8,128)S(1)}, u32[]{:S(2)}, u32[]{:S(2)}) collective-permute-start(f32[136,128]{1,0:T(8,128)S(1)} %add.23.fac_ref), channel_id=1, source_target_pairs={{0,1},{2,3},{4,5},{6,7},{8,9},{10,11},{12,13},{14,15},{16,17},{18,... | collective-permute-start | bytes 208904 | tf_op jit(solution)/shard_map/ppermute | solution.py:341
  51.7 0.0 collective-permute-done.17
  51.7 1.3 %collective-permute-start.18 = (f32[8,64,128]{2,1,0:T(8,128)S(1)}, f32[8,64,128]{2,1,0:T(8,128)S(1)}, u32[]{:S(2)}, u32[]{:S(2)}) collective-permute-start(f32[8,64,128]{2,1,0:T(8,128)S(1)} %constant_dynamic-update-slice_fusion.gte_ref), channel_id=1, source_target_pairs={{1,0},{3,2},{5,4},{7,6},{9,8},{11,10},{13,12},{15,14},{17,16},{19,... | collective-permute-start | bytes 786440 | tf_op jit(solution)/shard_map/ppermute | solution.py:342
  53.0 0.0 collective-permute-done.14.other_ref
  53.0 3.8 %shard_map.92.side_ref = f32[64,128]{1,0:T(8,128)S(1)} custom-call(f32[136,128]{1,0:T(8,128)S(1)} %add.23.fac_ref, f32[136,128]{1,0:T(8,128)S(1)} %collective-permute-done.14.other_ref, f32[128,64]{1,0:T(8,128)S(1)} %get-tuple-element.21.gtr_ref), custom_call_target="tpu_custom_call" | custom-call | flops 4294967296 | bytes 65536 | tf_op jit(solution)/shard_map/pallas_call | solution.py:26
  56.8 0.0 collective-permute-done.18.other_ref
  56.8 0.7 %shard_map.93 = f32[1,8]{1,0:T(1,128)} custom-call(f32[64,128]{1,0:T(8,128)S(1)} %shard_map.92.side_ref, f32[8,64,128]{2,1,0:T(8,128)S(1)} %constant_dynamic-update-slice_fusion.gte_ref, f32[8,64,128]{2,1,0:T(8,128)S(1)} %collective-permute-done.18.other_ref), custom_call_target="tpu_custom_call" | custom-call | bytes 65536 | tf_op jit(solution)/shard_map/pallas_call | solution.py:26
  (15 shorter events, 0.1 us)
Async XLA Ops:
  0.9 6.7 %collective-permute-start.6 = (bf16[48,512]{1,0:T(8,128)(2,1)S(1)}, bf16[48,512]{1,0:T(8,128)(2,1)S(1)}, u32[]{:S(2)}, u32[]{:S(2)}) collective-permute-start(bf16[48,512]{1,0:T(8,128)(2,1)S(1)} %get-tuple-element.25.refs_0_), channel_id=1, source_target_pairs={{0,8},{4,12},{8,0},{12,4},{1,9},{5,13},{9,1},{13,5},{2,10},{6,14},... | collective-permute-start | bytes 147464 | tf_op jit(solution)/shard_map/ppermute | solution.py:38
  5.0 8.1 %collective-permute-start = (bf16[48,512]{1,0:T(8,128)(2,1)S(1)}, bf16[48,512]{1,0:T(8,128)(2,1)S(1)}, u32[]{:S(2)}, u32[]{:S(2)}) collective-permute-start(bf16[48,512]{1,0:T(8,128)(2,1)S(1)} %get-tuple-element.26.refs_0_), channel_id=1, source_target_pairs={{0,8},{4,12},{8,0},{12,4},{1,9},{5,13},{9,1},{13,5},{2,10},{6,14},... | collective-permute-start | bytes 147464 | tf_op jit(solution)/shard_map/ppermute | solution.py:38
  7.6 5.7 %collective-permute-start.7 = (bf16[96,512]{1,0:T(8,128)(2,1)S(1)}, bf16[96,512]{1,0:T(8,128)(2,1)S(1)}, u32[]{:S(2)}, u32[]{:S(2)}) collective-permute-start(bf16[96,512]{1,0:T(8,128)(2,1)S(1)} %shard_map.86), channel_id=1, source_target_pairs={{0,4},{4,0},{8,12},{12,8},{1,5},{5,1},{9,13},{13,9},{2,6},{6,2},{1... | collective-permute-start | bytes 294920 | tf_op jit(solution)/shard_map/ppermute | solution.py:38
  9.7 7.7 %collective-permute-start.4 = (bf16[48,1024]{1,0:T(8,128)(2,1)S(1)}, bf16[48,1024]{1,0:T(8,128)(2,1)S(1)}, u32[]{:S(2)}, u32[]{:S(2)}) collective-permute-start(bf16[48,1024]{1,0:T(8,128)(2,1)S(1)} %get-tuple-element.23.refs_0_), channel_id=1, source_target_pairs={{0,8},{4,12},{8,0},{12,4},{1,9},{5,13},{9,1},{13,5},{2,10},{6,14},... | collective-permute-start | bytes 294920 | tf_op jit(solution)/shard_map/ppermute | solution.py:38
  13.1 5.8 %collective-permute-start.1 = (bf16[96,512]{1,0:T(8,128)(2,1)S(1)}, bf16[96,512]{1,0:T(8,128)(2,1)S(1)}, u32[]{:S(2)}, u32[]{:S(2)}) collective-permute-start(bf16[96,512]{1,0:T(8,128)(2,1)S(1)} %shard_map.83), channel_id=1, source_target_pairs={{0,4},{4,0},{8,12},{12,8},{1,5},{5,1},{9,13},{13,9},{2,6},{6,2},{1... | collective-permute-start | bytes 294920 | tf_op jit(solution)/shard_map/ppermute | solution.py:38
  13.3 9.3 %collective-permute-start.8 = (bf16[144,512]{1,0:T(8,128)(2,1)S(1)}, bf16[144,512]{1,0:T(8,128)(2,1)S(1)}, u32[]{:S(2)}, u32[]{:S(2)}) collective-permute-start(bf16[144,512]{1,0:T(8,128)(2,1)S(1)} %shard_map.87.refs_6_), channel_id=1, source_target_pairs={{0,2},{2,0},{16,18},{18,16},{1,3},{3,1},{17,19},{19,17},{4,6},{6,4... | collective-permute-start | bytes 442376 | tf_op jit(solution)/shard_map/ppermute | solution.py:38
  14.9 7.7 %collective-permute-start.9 = (bf16[144,512]{1,0:T(8,128)(2,1)S(1)}, bf16[144,512]{1,0:T(8,128)(2,1)S(1)}, u32[]{:S(2)}, u32[]{:S(2)}) collective-permute-start(bf16[144,512]{1,0:T(8,128)(2,1)S(1)} %shard_map.87.refs_6_), channel_id=1, source_target_pairs={{0,16},{2,18},{16,0},{18,2},{1,17},{3,19},{17,1},{19,3},{4,20},{6,... | collective-permute-start | bytes 442376 | tf_op jit(solution)/shard_map/ppermute | solution.py:38
  17.4 8.3 %collective-permute-start.5 = (bf16[96,1024]{1,0:T(8,128)(2,1)S(1)}, bf16[96,1024]{1,0:T(8,128)(2,1)S(1)}, u32[]{:S(2)}, u32[]{:S(2)}) collective-permute-start(bf16[96,1024]{1,0:T(8,128)(2,1)S(1)} %shard_map.85), channel_id=1, source_target_pairs={{0,4},{4,0},{8,12},{12,8},{1,5},{5,1},{9,13},{13,9},{2,6},{6,2},{1... | collective-permute-start | bytes 589832 | tf_op jit(solution)/shard_map/ppermute | solution.py:38
  18.9 5.2 %collective-permute-start.2 = (bf16[144,512]{1,0:T(8,128)(2,1)S(1)}, bf16[144,512]{1,0:T(8,128)(2,1)S(1)}, u32[]{:S(2)}, u32[]{:S(2)}) collective-permute-start(bf16[144,512]{1,0:T(8,128)(2,1)S(1)} %shard_map.84.refs_7_), channel_id=1, source_target_pairs={{0,2},{2,0},{16,18},{18,16},{1,3},{3,1},{17,19},{19,17},{4,6},{6,4... | collective-permute-start | bytes 442376 | tf_op jit(solution)/shard_map/ppermute | solution.py:38
  20.5 5.1 %collective-permute-start.3 = (bf16[144,512]{1,0:T(8,128)(2,1)S(1)}, bf16[144,512]{1,0:T(8,128)(2,1)S(1)}, u32[]{:S(2)}, u32[]{:S(2)}) collective-permute-start(bf16[144,512]{1,0:T(8,128)(2,1)S(1)} %shard_map.84.refs_7_), channel_id=1, source_target_pairs={{0,16},{2,18},{16,0},{18,2},{1,17},{3,19},{17,1},{19,3},{4,20},{6,... | collective-permute-start | bytes 442376 | tf_op jit(solution)/shard_map/ppermute | solution.py:38
  26.5 1.5 %collective-permute-start.10 = (f32[384,128]{1,0:T(8,128)S(1)}, f32[384,128]{1,0:T(8,128)S(1)}, u32[]{:S(2)}, u32[]{:S(2)}) collective-permute-start(f32[384,128]{1,0:T(8,128)S(1)} %shard_map.90.mine), channel_id=1, source_target_pairs={{0,1},{1,0},{2,3},{3,2},{4,5},{5,4},{6,7},{7,6},{8,9},{9,8},{10,11... | collective-permute-start | bytes 589832 | tf_op jit(solution)/shard_map/ppermute | solution.py:38
  28.5 3.1 %collective-permute-start.15 = (f32[1,64,128]{2,1,0:T(8,128)S(1)}, f32[1,64,128]{2,1,0:T(8,128)S(1)}, u32[]{:S(2)}, u32[]{:S(2)}) collective-permute-start(f32[1,64,128]{2,1,0:T(8,128)S(1)} %get-tuple-element.22), channel_id=1, source_target_pairs={{1,9},{5,13},{9,1},{13,5},{3,11},{7,15},{11,3},{15,7},{17,25},{21,... | collective-permute-start | bytes 98312 | tf_op jit(solution)/shard_map/ppermute | solution.py:43
  29.1 6.2 %collective-permute-start.11 = (f32[136,128]{1,0:T(8,128)S(1)}, f32[136,128]{1,0:T(8,128)S(1)}, u32[]{:S(2)}, u32[]{:S(2)}) collective-permute-start(f32[136,128]{1,0:T(8,128)S(1)} %get-tuple-element.20), channel_id=1, source_target_pairs={{0,2},{2,0},{4,6},{6,4},{8,10},{10,8},{12,14},{14,12},{16,18},{18,... | collective-permute-start | bytes 208904 | tf_op jit(solution)/shard_map/ppermute | solution.py:43
  31.6 9.8 %collective-permute-start.16 = (f32[2,64,128]{2,1,0:T(8,128)S(1)}, f32[2,64,128]{2,1,0:T(8,128)S(1)}, u32[]{:S(2)}, u32[]{:S(2)}) collective-permute-start(f32[2,64,128]{2,1,0:T(8,128)S(1)} %pad_maximum_fusion.1), channel_id=1, source_target_pairs={{1,5},{5,1},{9,13},{13,9},{3,7},{7,3},{11,15},{15,11},{17,21},{21,... | collective-permute-start | bytes 196616 | tf_op jit(solution)/shard_map/ppermute | solution.py:43
  35.3 8.8 %collective-permute-start.12 = (f32[136,128]{1,0:T(8,128)S(1)}, f32[136,128]{1,0:T(8,128)S(1)}, u32[]{:S(2)}, u32[]{:S(2)}) collective-permute-start(f32[136,128]{1,0:T(8,128)S(1)} %add.21), channel_id=1, source_target_pairs={{0,8},{4,12},{8,0},{12,4},{2,10},{6,14},{10,2},{14,6},{16,24},{20,... | collective-permute-start | bytes 208904 | tf_op jit(solution)/shard_map/ppermute | solution.py:43
  41.5 10.2 %collective-permute-start.17 = (f32[4,64,128]{2,1,0:T(8,128)S(1)}, f32[4,64,128]{2,1,0:T(8,128)S(1)}, u32[]{:S(2)}, u32[]{:S(2)}) collective-permute-start(f32[4,64,128]{2,1,0:T(8,128)S(1)} %pad_maximum_fusion), channel_id=1, source_target_pairs={{1,3},{3,1},{5,7},{7,5},{9,11},{11,9},{13,15},{15,13},{17,19},{19,... | collective-permute-start | bytes 393224 | tf_op jit(solution)/shard_map/ppermute | solution.py:43
  44.2 6.2 %collective-permute-start.13 = (f32[136,128]{1,0:T(8,128)S(1)}, f32[136,128]{1,0:T(8,128)S(1)}, u32[]{:S(2)}, u32[]{:S(2)}) collective-permute-start(f32[136,128]{1,0:T(8,128)S(1)} %add.22), channel_id=1, source_target_pairs={{0,4},{4,0},{8,12},{12,8},{2,6},{6,2},{10,14},{14,10},{16,20},{20,... | collective-permute-start | bytes 208904 | tf_op jit(solution)/shard_map/ppermute | solution.py:43
  50.4 2.6 %collective-permute-start.14 = (f32[136,128]{1,0:T(8,128)S(1)}, f32[136,128]{1,0:T(8,128)S(1)}, u32[]{:S(2)}, u32[]{:S(2)}) collective-permute-start(f32[136,128]{1,0:T(8,128)S(1)} %add.23.fac_ref), channel_id=1, source_target_pairs={{0,1},{2,3},{4,5},{6,7},{8,9},{10,11},{12,13},{14,15},{16,17},{18,... | collective-permute-start | bytes 208904 | tf_op jit(solution)/shard_map/ppermute | solution.py:341
  51.7 5.1 %collective-permute-start.18 = (f32[8,64,128]{2,1,0:T(8,128)S(1)}, f32[8,64,128]{2,1,0:T(8,128)S(1)}, u32[]{:S(2)}, u32[]{:S(2)}) collective-permute-start(f32[8,64,128]{2,1,0:T(8,128)S(1)} %constant_dynamic-update-slice_fusion.gte_ref), channel_id=1, source_target_pairs={{1,0},{3,2},{5,4},{7,6},{9,8},{11,10},{13,12},{15,14},{17,16},{19,... | collective-permute-start | bytes 786440 | tf_op jit(solution)/shard_map/ppermute | solution.py:342

commit v8 on v5

--- a/solution.py
+++ b/solution.py
@@ -151,12 +151,12 @@
     fac_ref[:half, :] = c_in[:half, :]
     fac_ref[half:ki, :half] = c_in[half:, half:]
     fac_ref[half:ki, half:] = c_out
-    fac_ref[ki:, :] = jnp.full((8, ki), n_tr.astype(jnp.float32))
     grad_tr = dot(x_tr, g_tr) / n_tr.astype(jnp.float32)
     grad_te = dot(x_te, g_te) / n_te.astype(jnp.float32)
     gtr_ref[...] = grad_tr
-    gte_ref[0, :, :ko] = grad_te[:half]
-    gte_ref[0, :, ko:] = grad_te[half:]
+    gte_ref[0, :half, :ko] = grad_te[:half]
+    gte_ref[0, :half, ko:] = grad_te[half:]
+    gte_ref[0, half:, :] = jnp.full((8, ki), n_tr.astype(jnp.float32))
 
 
 def damped(c):
@@ -207,23 +207,25 @@
     c_in = jnp.concatenate(
         [top, jnp.concatenate([top[:, half:].T, low[:, :half]], axis=1)], axis=0
     )
-    count = fac_ref[ki : ki + 1, :1]
     inv_in, inv_out = inverses([c_in, low[:, half:]])
-    side = mm(mm(inv_in, gtr_ref[...]), inv_out) * (count * count)
+    side = mm(mm(inv_in, gtr_ref[...]), inv_out)
     out_ref[:, :half] = side[:half]
     out_ref[:, half:] = side[half:]
 
 
-def scores_kernel(order, n_blk, side_ref, gte_ref, out_ref):
-    z = lax.axis_index("dp")
-    b = lax.axis_index("blk")
+def scores_kernel(side_ref, gte_ref, out_ref):
     lane = lax.broadcasted_iota(jnp.int32, out_ref.shape, 1)
     row = jnp.zeros(out_ref.shape, jnp.float32)
     side = side_ref[...]
-    for p, (dz, db) in enumerate(order):
-        value = jnp.sum(side * gte_ref[p], axis=(0, 1), keepdims=True)
-        row = jnp.where(lane == (z ^ dz) * n_blk + (b ^ db), value, row)
-    out_ref[...] = row
+    half, peers = side.shape[0], gte_ref.shape[0]
+    sums = [jnp.sum(side * gte_ref[p, :half], axis=0, keepdims=True) for p in range(peers)]
+    values = jnp.sum(jnp.concatenate(sums, axis=0), axis=1, keepdims=True)
+    count = gte_ref[0, half : half + 1, :1]
+    for p in range(1, peers):
+        count += gte_ref[p, half : half + 1, :1]
+    for p in range(peers):
+        row = jnp.where(lane == p, values[p : p + 1, :], row)
+    out_ref[...] = row * (count * count)
 
 
 def project(xs, w_in, w_out, n_groups, n_dp, n_blk):
@@ -312,19 +314,19 @@
     fac, gte, gtr = call(
         moments_kernel,
         (
-            jax.ShapeDtypeStruct((ki + 8, ki), jnp.float32),
-            jax.ShapeDtypeStruct((1, ki // 2, ki), jnp.float32),
+            jax.ShapeDtypeStruct((ki, ki), jnp.float32),
+            jax.ShapeDtypeStruct((1, ki // 2 + 8, ki), jnp.float32),
             jax.ShapeDtypeStruct((ki, ko), jnp.float32),
         ),
         [smem(), smem(), vmem(), vmem()],
         (train_lengths, test_lengths, part, other),
     )
-    order = [(0, 0)]
-    for axis, count in (("blk", n_blk), ("dp", n_dp)):
-        for k in bits(count):
-            fac = fac + swap(fac, axis, count, k)
-            gte = jnp.concatenate([gte, swap(gte, axis, count, k)], axis=0)
-            order += [(dz ^ k, db) if axis == "dp" else (dz, db ^ k) for dz, db in order]
+    count = n_dp * n_blk
+    peers = ("dp", "blk")
+    slices = lax.all_to_all(fac.reshape(count, ki // count, ki), peers, 0, 0, tiled=True)
+    mine = jnp.broadcast_to(jnp.sum(slices, axis=0, keepdims=True), slices.shape)
+    fac = lax.all_to_all(mine, peers, 0, 0, tiled=True).reshape(ki, ki)
+    gte = lax.all_to_all(jnp.broadcast_to(gte, (count, *gte.shape[1:])), peers, 0, 0, tiled=True)
     side = call(
         side_kernel,
         jax.ShapeDtypeStruct((ki // 2, ki), jnp.float32),
@@ -333,7 +335,7 @@
         flops=4 << 30,
     )
     return call(
-        functools.partial(scores_kernel, order, n_blk),
+        scores_kernel,
         jax.ShapeDtypeStruct((1, n_dp * n_blk), jnp.float32),
         [vmem()] * 2,
         (side, gte),

time: 50.9 us -> 64.4 us (1.27)
  blocking collectives: 0 us -> 22.4 us
  waiting for transfers between devices: 14.1 us -> 8.5 us
  starting transfers between devices: 25.1 us -> 21 us
  local copies, waits for them, and re-layouts: 0.01 us -> 0.74 us
    all_to_all x0 -> x2, blocking collectives: none -> 22.4 us  [the longest x1 13.1 us: per_device(): lax.all_to_all(fac.reshape(count, ki // count, ki), peers, 0, 0, tiled=True)]
    ppermute x17 -> x11, waiting for transfers between devices: 14.1 us -> 3.86 us  [swap(): return lax.ppermute(x, axis, [(i, i ^ k) for i in range(count)])]
    ppermute x17 -> x11, starting transfers between devices: 25.1 us -> 17.6 us  [swap(): return lax.ppermute(x, axis, [(i, i ^ k) for i in range(count)])]
    all_to_all x0 -> x1, waiting for transfers between devices: none -> 4.63 us  [per_device(): lax.all_to_all(jnp.broadcast_to(gte, (count, *gte.shape[1:])), peers, 0,...]
    all_to_all x0 -> x1, starting transfers between devices: none -> 3.42 us  [per_device(): lax.all_to_all(jnp.broadcast_to(gte, (count, *gte.shape[1:])), peers, 0,...]
    broadcast_in_dim x0 -> x2, local copies, waits for them, and re-layouts: none -> 0.73 us  [the longest x1 0.72 us: per_device(): jnp.broadcast_to(gte, (count, *gte.shape[1:]))]
  transfers between devices with their start and end apart: 17 -> 12, of which waited for: 9 -> 6; matrix products, arithmetic and copies ran while one was open for 0% -> 0% of each run, Pallas kernels for 14% -> 11%
where the time goes in v8:
time: 64.4 us; the launch traced here: 64 us
  blocking collectives  22.4 us (35%)
  starting transfers between devices  21 us (33%)
  Pallas kernels  9.12 us (14%)
  waiting for transfers between devices  8.5 us (13%)
  between operations  1.39 us (2%)
  other arithmetic  0.9 us (1%)
  local copies, waits for them, and re-layouts  0.74 us (1%)
    ppermute x11, starting transfers between devices, swap(): return lax.ppermute(x, axis, [(i, i ^ k) for i in range(count)])  17.6 us
    all_to_all x1, blocking collectives, per_device(): lax.all_to_all(fac.reshape(count, ki // count, ki), peers, 0, 0, tiled=True)  13.1 us
    all_to_all x1, blocking collectives, per_device(): fac = lax.all_to_all(mine, peers, 0, 0, tiled=True).reshape(ki, ki)  9.29 us
    pallas_call x12, Pallas kernels, call(): pl.pallas_call(kernel, out_shape=out_shape, in_specs=in_specs, out_specs=...  9.12 us
    all_to_all x1, waiting for transfers between devices, per_device(): lax.all_to_all(jnp.broadcast_to(gte, (count, *gte.shape[1:])), peers, 0,...  4.63 us
    ppermute x11, waiting for transfers between devices, swap(): return lax.ppermute(x, axis, [(i, i ^ k) for i in range(count)])  3.86 us
    all_to_all x1, starting transfers between devices, per_device(): lax.all_to_all(jnp.broadcast_to(gte, (count, *gte.shape[1:])), peers, 0,...  3.42 us
  transfers between devices with their start and end apart: 12, of which 6 were waited for; matrix products, arithmetic and copies ran while one was open for 0% of the time, Pallas kernels for 11%

profile of v8, /device:TPU:0, one launch (start us, length us, event | category | flops | bytes accessed | tf_op | source)
XLA Modules:
  0.0 64.0 jit_solution(7195962413444100557)
XLA Ops:
  0.0 0.9 %fusion = (bf16[48,1024]{1,0:T(8,128)(2,1)S(1)}, bf16[48,1024]{1,0:T(8,128)(2,1)S(1)}) fusion(s32[]{:T(128)S(6)} %select_n.7, bf16[32,4096]{1,0:T(8,128)(2,1)} %bitcast.12, bf16[16,4096]{1,0:T(8,128)(2,1)} %bitcast.18, s32[]{:T(128)S(6)} %select_n.6), kind=kLoop, calls=%fused_computation.4 | loop fusion | flops 393216 | bytes 589832 | tf_op jit(solution)/shard_map/concatenate | solution.py:244
  0.9 4.1 %collective-permute-start.6 = (bf16[48,512]{1,0:T(8,128)(2,1)S(1)}, bf16[48,512]{1,0:T(8,128)(2,1)S(1)}, u32[]{:S(2)}, u32[]{:S(2)}) collective-permute-start(bf16[48,512]{1,0:T(8,128)(2,1)S(1)} %get-tuple-element.25.refs_0_), channel_id=1, source_target_pairs={{0,8},{4,12},{8,0},{12,4},{1,9},{5,13},{9,1},{13,5},{2,10},{6,14},... | collective-permute-start | bytes 147464 | tf_op jit(solution)/shard_map/ppermute | solution.py:38
  5.0 0.1 collective-permute-start
  5.1 2.3 %shard_map.82 = (bf16[128,4096]{1,0:T(8,128)(2,1)S(1)}, bf16[128,4096]{1,0:T(8,128)(2,1)S(1)}, bf16[128,4096]{1,0:T(8,128)(2,1)S(1)}, bf16[128,4096]{1,0:T(8,128...) custom-call(bf16[128,4096]{1,0:T(8,128)(2,1)} %bitcast.14, bf16[128,4096]{1,0:T(8,128)(2,1)} %bitcast.15, ...), custom_call_target="tpu_custom_call" | custom-call | flops 1073741824 | bytes 65536 | tf_op jit(solution)/shard_map/pallas_call | solution.py:26
  7.4 0.2 collective-permute-done.6.refs_1_.refs_0_
  7.6 2.1 %collective-permute-start.7 = (bf16[96,512]{1,0:T(8,128)(2,1)S(1)}, bf16[96,512]{1,0:T(8,128)(2,1)S(1)}, u32[]{:S(2)}, u32[]{:S(2)}) collective-permute-start(bf16[96,512]{1,0:T(8,128)(2,1)S(1)} %shard_map.86), channel_id=1, source_target_pairs={{0,4},{4,0},{8,12},{12,8},{1,5},{5,1},{9,13},{13,9},{2,6},{6,2},{1... | collective-permute-start | bytes 294920 | tf_op jit(solution)/shard_map/ppermute | solution.py:38
  9.7 3.4 %collective-permute-start.4 = (bf16[48,1024]{1,0:T(8,128)(2,1)S(1)}, bf16[48,1024]{1,0:T(8,128)(2,1)S(1)}, u32[]{:S(2)}, u32[]{:S(2)}) collective-permute-start(bf16[48,1024]{1,0:T(8,128)(2,1)S(1)} %get-tuple-element.23.refs_0_), channel_id=1, source_target_pairs={{0,8},{4,12},{8,0},{12,4},{1,9},{5,13},{9,1},{13,5},{2,10},{6,14},... | collective-permute-start | bytes 294920 | tf_op jit(solution)/shard_map/ppermute | solution.py:38
  13.1 0.0 collective-permute-done.refs_1_.refs_0_
  13.1 0.1 collective-permute-start.1
  13.3 0.0 collective-permute-done.7.refs_1_
  13.3 1.6 %collective-permute-start.8 = (bf16[144,512]{1,0:T(8,128)(2,1)S(1)}, bf16[144,512]{1,0:T(8,128)(2,1)S(1)}, u32[]{:S(2)}, u32[]{:S(2)}) collective-permute-start(bf16[144,512]{1,0:T(8,128)(2,1)S(1)} %shard_map.87.refs_6_), channel_id=1, source_target_pairs={{0,2},{2,0},{16,18},{18,16},{1,3},{3,1},{17,19},{19,17},{4,6},{6,4... | collective-permute-start | bytes 442376 | tf_op jit(solution)/shard_map/ppermute | solution.py:38
  14.9 1.5 %collective-permute-start.9 = (bf16[144,512]{1,0:T(8,128)(2,1)S(1)}, bf16[144,512]{1,0:T(8,128)(2,1)S(1)}, u32[]{:S(2)}, u32[]{:S(2)}) collective-permute-start(bf16[144,512]{1,0:T(8,128)(2,1)S(1)} %shard_map.87.refs_6_), channel_id=1, source_target_pairs={{0,16},{2,18},{16,0},{18,2},{1,17},{3,19},{17,1},{19,3},{4,20},{6,... | collective-permute-start | bytes 442376 | tf_op jit(solution)/shard_map/ppermute | solution.py:38
  16.4 1.0 %collective-permute-done.4.refs_1_.refs_8_ = bf16[48,1024]{1,0:T(8,128)(2,1)S(1)} collective-permute-done((bf16[48,1024]{1,0:T(8,128)(2,1)S(1)}, bf16[48,1024]{1,0:T(8,128)(2,1)S(1)}, u32[]{:S(2)}, u32[]{:S(2)}) %collective-permute-start.4) | collective-permute-done | bytes 98336 | tf_op jit(solution)/shard_map/ppermute | solution.py:38
  17.4 1.5 %collective-permute-start.5 = (bf16[96,1024]{1,0:T(8,128)(2,1)S(1)}, bf16[96,1024]{1,0:T(8,128)(2,1)S(1)}, u32[]{:S(2)}, u32[]{:S(2)}) collective-permute-start(bf16[96,1024]{1,0:T(8,128)(2,1)S(1)} %shard_map.85), channel_id=1, source_target_pairs={{0,4},{4,0},{8,12},{12,8},{1,5},{5,1},{9,13},{13,9},{2,6},{6,2},{1... | collective-permute-start | bytes 589832 | tf_op jit(solution)/shard_map/ppermute | solution.py:38
  18.9 0.0 collective-permute-done.1.refs_1_
  18.9 1.6 %collective-permute-start.2 = (bf16[144,512]{1,0:T(8,128)(2,1)S(1)}, bf16[144,512]{1,0:T(8,128)(2,1)S(1)}, u32[]{:S(2)}, u32[]{:S(2)}) collective-permute-start(bf16[144,512]{1,0:T(8,128)(2,1)S(1)} %shard_map.84.refs_7_), channel_id=1, source_target_pairs={{0,2},{2,0},{16,18},{18,16},{1,3},{3,1},{17,19},{19,17},{4,6},{6,4... | collective-permute-start | bytes 442376 | tf_op jit(solution)/shard_map/ppermute | solution.py:38
  20.5 1.5 %collective-permute-start.3 = (bf16[144,512]{1,0:T(8,128)(2,1)S(1)}, bf16[144,512]{1,0:T(8,128)(2,1)S(1)}, u32[]{:S(2)}, u32[]{:S(2)}) collective-permute-start(bf16[144,512]{1,0:T(8,128)(2,1)S(1)} %shard_map.84.refs_7_), channel_id=1, source_target_pairs={{0,16},{2,18},{16,0},{18,2},{1,17},{3,19},{17,1},{19,3},{4,20},{6,... | collective-permute-start | bytes 442376 | tf_op jit(solution)/shard_map/ppermute | solution.py:38
  22.0 0.5 shard_map.88.refs_8_
  22.6 0.0 collective-permute-done.8.refs_6_
  22.6 0.0 collective-permute-done.9.refs_7_
  22.6 0.5 shard_map.89.refs_10_
  23.1 1.0 %collective-permute-done.2.refs_6_ = bf16[144,512]{1,0:T(8,128)(2,1)S(1)} collective-permute-done((bf16[144,512]{1,0:T(8,128)(2,1)S(1)}, bf16[144,512]{1,0:T(8,128)(2,1)S(1)}, u32[]{:S(2)}, u32[]{:S(2)}) %collective-permute-start.2) | collective-permute-done | bytes 147488 | tf_op jit(solution)/shard_map/ppermute | solution.py:38
  24.2 1.5 %collective-permute-done.3.refs_7_ = bf16[144,512]{1,0:T(8,128)(2,1)S(1)} collective-permute-done((bf16[144,512]{1,0:T(8,128)(2,1)S(1)}, bf16[144,512]{1,0:T(8,128)(2,1)S(1)}, u32[]{:S(2)}, u32[]{:S(2)}) %collective-permute-start.3) | collective-permute-done | bytes 147488 | tf_op jit(solution)/shard_map/ppermute | solution.py:38
  25.7 0.0 collective-permute-done.5.refs_9_
  25.7 0.8 %shard_map.90.mine = f32[384,128]{1,0:T(8,128)S(1)} custom-call(bf16[128,4096]{1,0:T(8,128)(2,1)S(1)} %get-tuple-element.14.refs_0_, bf16[128,4096]{1,0:T(8,128)(2,1)S(1)} %get-tuple-element.15.refs_1_, bf16[128,4096]{1,0:T(8,128)(2,1)S(1)} %get-tuple-element.16.refs_2_, bf16[128,4096]{1,0:T(8,128)(2,1)S(1)} %get-tuple-element.17.refs_3_, ...), custom_call_target="tpu_custom_call" | custom-call | flops 1073741824 | bytes 65536 | tf_op jit(solution)/shard_map/pallas_call | solution.py:26
  26.5 0.1 collective-permute-start.10
  27.9 0.1 collective-permute-done.10.other
  28.0 0.5 shard_map.91
  28.5 13.1 %all_to_all.15 = f32[8,16,128]{2,1,0:T(8,128)S(1)} all-to-all(f32[8,16,128]{2,1,0:T(8,128)S(1)} %bitcast.10), channel_id=1, replica_groups=mesh['groups'=2,'dp'=4,'blk'=2,'mp'=2] {'dp','blk'}, dimensions={0} | all-to-all | bytes 131072 | tf_op jit(solution)/shard_map/all_to_all | solution.py:326
  41.6 9.3 %all_to_all.16 = f32[8,16,128]{2,1,0:T(8,128)S(1)} all-to-all(f32[8,16,128]{2,1,0:T(8,128)S(1)} %broadcast_in_dim.6), channel_id=1, replica_groups=mesh['groups'=2,'dp'=4,'blk'=2,'mp'=2] {'dp','blk'}, dimensions={0} | all-to-all | bytes 131072 | tf_op jit(solution)/shard_map/all_to_all | solution.py:328
  50.9 0.7 %broadcast_in_dim.15 = f32[8,72,128]{2,1,0:T(8,128)} broadcast(f32[72,128]{1,0:T(8,128)S(1)} %bitcast.11), dimensions={1,2} | broadcast | bytes 331776 | tf_op jit(solution)/shard_map/broadcast_in_dim | solution.py:329
  51.6 3.4 %all-to-all-start.2 = ((f32[8,72,128]{2,1,0:T(8,128)}), f32[8,72,128]{2,1,0:T(8,128)S(1)}, u32[]{:S(2)}, u32[]{:S(2)}) async-start(f32[8,72,128]{2,1,0:T(8,128)} %broadcast_in_dim.15), calls=%async_computation.2 | async-start | bytes 589824 | tf_op jit(solution)/shard_map/all_to_all | solution.py:329
  55.0 3.7 %shard_map.92.side_ref = f32[64,128]{1,0:T(8,128)S(1)} custom-call(f32[128,128]{1,0:T(8,128)S(1)} %bitcast.9, f32[128,64]{1,0:T(8,128)S(1)} %get-tuple-element.21.gtr_ref), custom_call_target="tpu_custom_call" | custom-call | flops 4294967296 | bytes 65536 | tf_op jit(solution)/shard_map/pallas_call | solution.py:26
  58.8 4.6 %all-to-all-done.2.gte_ref = f32[8,72,128]{2,1,0:T(8,128)S(1)} async-done(((f32[8,72,128]{2,1,0:T(8,128)}), f32[8,72,128]{2,1,0:T(8,128)S(1)}, u32[]{:S(2)}, u32[]{:S(2)}) %all-to-all-start.2) | async-done | bytes 294944 | tf_op jit(solution)/shard_map/all_to_all | solution.py:329
  63.4 0.6 shard_map.93
  (8 shorter events, 0.1 us)
Async XLA Ops:
  0.9 6.7 %collective-permute-start.6 = (bf16[48,512]{1,0:T(8,128)(2,1)S(1)}, bf16[48,512]{1,0:T(8,128)(2,1)S(1)}, u32[]{:S(2)}, u32[]{:S(2)}) collective-permute-start(bf16[48,512]{1,0:T(8,128)(2,1)S(1)} %get-tuple-element.25.refs_0_), channel_id=1, source_target_pairs={{0,8},{4,12},{8,0},{12,4},{1,9},{5,13},{9,1},{13,5},{2,10},{6,14},... | collective-permute-start | bytes 147464 | tf_op jit(solution)/shard_map/ppermute | solution.py:38
  5.0 8.1 %collective-permute-start = (bf16[48,512]{1,0:T(8,128)(2,1)S(1)}, bf16[48,512]{1,0:T(8,128)(2,1)S(1)}, u32[]{:S(2)}, u32[]{:S(2)}) collective-permute-start(bf16[48,512]{1,0:T(8,128)(2,1)S(1)} %get-tuple-element.26.refs_0_), channel_id=1, source_target_pairs={{0,8},{4,12},{8,0},{12,4},{1,9},{5,13},{9,1},{13,5},{2,10},{6,14},... | collective-permute-start | bytes 147464 | tf_op jit(solution)/shard_map/ppermute | solution.py:38
  7.6 5.7 %collective-permute-start.7 = (bf16[96,512]{1,0:T(8,128)(2,1)S(1)}, bf16[96,512]{1,0:T(8,128)(2,1)S(1)}, u32[]{:S(2)}, u32[]{:S(2)}) collective-permute-start(bf16[96,512]{1,0:T(8,128)(2,1)S(1)} %shard_map.86), channel_id=1, source_target_pairs={{0,4},{4,0},{8,12},{12,8},{1,5},{5,1},{9,13},{13,9},{2,6},{6,2},{1... | collective-permute-start | bytes 294920 | tf_op jit(solution)/shard_map/ppermute | solution.py:38
  9.7 7.7 %collective-permute-start.4 = (bf16[48,1024]{1,0:T(8,128)(2,1)S(1)}, bf16[48,1024]{1,0:T(8,128)(2,1)S(1)}, u32[]{:S(2)}, u32[]{:S(2)}) collective-permute-start(bf16[48,1024]{1,0:T(8,128)(2,1)S(1)} %get-tuple-element.23.refs_0_), channel_id=1, source_target_pairs={{0,8},{4,12},{8,0},{12,4},{1,9},{5,13},{9,1},{13,5},{2,10},{6,14},... | collective-permute-start | bytes 294920 | tf_op jit(solution)/shard_map/ppermute | solution.py:38
  13.1 5.8 %collective-permute-start.1 = (bf16[96,512]{1,0:T(8,128)(2,1)S(1)}, bf16[96,512]{1,0:T(8,128)(2,1)S(1)}, u32[]{:S(2)}, u32[]{:S(2)}) collective-permute-start(bf16[96,512]{1,0:T(8,128)(2,1)S(1)} %shard_map.83), channel_id=1, source_target_pairs={{0,4},{4,0},{8,12},{12,8},{1,5},{5,1},{9,13},{13,9},{2,6},{6,2},{1... | collective-permute-start | bytes 294920 | tf_op jit(solution)/shard_map/ppermute | solution.py:38
  13.3 9.3 %collective-permute-start.8 = (bf16[144,512]{1,0:T(8,128)(2,1)S(1)}, bf16[144,512]{1,0:T(8,128)(2,1)S(1)}, u32[]{:S(2)}, u32[]{:S(2)}) collective-permute-start(bf16[144,512]{1,0:T(8,128)(2,1)S(1)} %shard_map.87.refs_6_), channel_id=1, source_target_pairs={{0,2},{2,0},{16,18},{18,16},{1,3},{3,1},{17,19},{19,17},{4,6},{6,4... | collective-permute-start | bytes 442376 | tf_op jit(solution)/shard_map/ppermute | solution.py:38
  14.9 7.7 %collective-permute-start.9 = (bf16[144,512]{1,0:T(8,128)(2,1)S(1)}, bf16[144,512]{1,0:T(8,128)(2,1)S(1)}, u32[]{:S(2)}, u32[]{:S(2)}) collective-permute-start(bf16[144,512]{1,0:T(8,128)(2,1)S(1)} %shard_map.87.refs_6_), channel_id=1, source_target_pairs={{0,16},{2,18},{16,0},{18,2},{1,17},{3,19},{17,1},{19,3},{4,20},{6,... | collective-permute-start | bytes 442376 | tf_op jit(solution)/shard_map/ppermute | solution.py:38
  17.4 8.3 %collective-permute-start.5 = (bf16[96,1024]{1,0:T(8,128)(2,1)S(1)}, bf16[96,1024]{1,0:T(8,128)(2,1)S(1)}, u32[]{:S(2)}, u32[]{:S(2)}) collective-permute-start(bf16[96,1024]{1,0:T(8,128)(2,1)S(1)} %shard_map.85), channel_id=1, source_target_pairs={{0,4},{4,0},{8,12},{12,8},{1,5},{5,1},{9,13},{13,9},{2,6},{6,2},{1... | collective-permute-start | bytes 589832 | tf_op jit(solution)/shard_map/ppermute | solution.py:38
  18.9 5.2 %collective-permute-start.2 = (bf16[144,512]{1,0:T(8,128)(2,1)S(1)}, bf16[144,512]{1,0:T(8,128)(2,1)S(1)}, u32[]{:S(2)}, u32[]{:S(2)}) collective-permute-start(bf16[144,512]{1,0:T(8,128)(2,1)S(1)} %shard_map.84.refs_7_), channel_id=1, source_target_pairs={{0,2},{2,0},{16,18},{18,16},{1,3},{3,1},{17,19},{19,17},{4,6},{6,4... | collective-permute-start | bytes 442376 | tf_op jit(solution)/shard_map/ppermute | solution.py:38
  20.5 5.1 %collective-permute-start.3 = (bf16[144,512]{1,0:T(8,128)(2,1)S(1)}, bf16[144,512]{1,0:T(8,128)(2,1)S(1)}, u32[]{:S(2)}, u32[]{:S(2)}) collective-permute-start(bf16[144,512]{1,0:T(8,128)(2,1)S(1)} %shard_map.84.refs_7_), channel_id=1, source_target_pairs={{0,16},{2,18},{16,0},{18,2},{1,17},{3,19},{17,1},{19,3},{4,20},{6,... | collective-permute-start | bytes 442376 | tf_op jit(solution)/shard_map/ppermute | solution.py:38
  26.5 1.5 %collective-permute-start.10 = (f32[384,128]{1,0:T(8,128)S(1)}, f32[384,128]{1,0:T(8,128)S(1)}, u32[]{:S(2)}, u32[]{:S(2)}) collective-permute-start(f32[384,128]{1,0:T(8,128)S(1)} %shard_map.90.mine), channel_id=1, source_target_pairs={{0,1},{1,0},{2,3},{3,2},{4,5},{5,4},{6,7},{7,6},{8,9},{9,8},{10,11... | collective-permute-start | bytes 589832 | tf_op jit(solution)/shard_map/ppermute | solution.py:38
  51.6 11.8 %all-to-all-start.2 = ((f32[8,72,128]{2,1,0:T(8,128)}), f32[8,72,128]{2,1,0:T(8,128)S(1)}, u32[]{:S(2)}, u32[]{:S(2)}) async-start(f32[8,72,128]{2,1,0:T(8,128)} %broadcast_in_dim.15), calls=%async_computation.2 | async-start | bytes 589824 | tf_op jit(solution)/shard_map/all_to_all | solution.py:329

commit v9 on v5

--- a/solution.py
+++ b/solution.py
@@ -129,7 +129,7 @@
     store_products(xs, gs, acc_ref, out_ref)
 
 
-def moments_kernel(len_tr, len_te, mine, other, fac_ref, gte_ref, gtr_ref):
+def moments_kernel(len_tr, len_te, mine, other, msg_ref, gtr_ref):
     tokens = mine.shape[0] // 3
     ki = mine.shape[1]
     ko = ki // 2
@@ -145,18 +145,37 @@
         lax.dot_general, dimension_numbers=TN, precision=HI,
         preferred_element_type=jnp.float32,
     )
-    c_in = dot(x_tr, x_tr)
-    c_out = dot(g_tr, g_tr)
     half = ki // 2
-    fac_ref[:half, :] = c_in[:half, :]
-    fac_ref[half:ki, :half] = c_in[half:, half:]
-    fac_ref[half:ki, half:] = c_out
-    fac_ref[ki:, :] = jnp.full((8, ki), n_tr.astype(jnp.float32))
-    grad_tr = dot(x_tr, g_tr) / n_tr.astype(jnp.float32)
-    grad_te = dot(x_te, g_te) / n_te.astype(jnp.float32)
-    gtr_ref[...] = grad_tr
-    gte_ref[0, :, :ko] = grad_te[:half]
-    gte_ref[0, :, ko:] = grad_te[half:]
+    core = lax.axis_index("mp")
+    gtr_ref[...] = dot(x_tr, g_tr) / n_tr.astype(jnp.float32)
+
+    @pl.when(core == 0)
+    def _():
+        c_in = dot(x_tr, x_tr)
+        msg_ref[:half, :] = c_in[:half, :]
+        msg_ref[half:ki, :half] = c_in[half:, half:]
+        msg_ref[half:ki, half:] = dot(g_tr, g_tr)
+        msg_ref[ki:, :] = jnp.full((8, ki), n_tr.astype(jnp.float32))
+
+    @pl.when(core == 1)
+    def _():
+        grad_te = dot(x_te, g_te) / n_te.astype(jnp.float32)
+        msg_ref[:half, :ko] = grad_te[:half]
+        msg_ref[:half, ko:] = grad_te[half:]
+        msg_ref[half:, :] = jnp.zeros((half + 8, ki), jnp.float32)
+
+
+def round_kernel(fac_rows, grad_rows, mine, other, out_ref):
+    core = lax.axis_index("mp")
+
+    @pl.when(core == 0)
+    def _():
+        out_ref[:fac_rows, :] = mine[:fac_rows, :] + other[:fac_rows, :]
+
+    @pl.when(core == 1)
+    def _():
+        out_ref[:grad_rows, :] = mine[:grad_rows, :]
+        out_ref[grad_rows : 2 * grad_rows, :] = other[:grad_rows, :]
 
 
 def damped(c):
@@ -199,30 +218,32 @@
     return [2.0 * x - mm(x, mm(a, x)) for a, m, x, r in state]
 
 
-def side_kernel(fac_ref, gtr_ref, out_ref):
-    ki = fac_ref.shape[1]
+def scores_kernel(order, n_blk, mine, other, gtr_ref, out_ref):
+    ki, ko = gtr_ref.shape
     half = ki // 2
-    top = fac_ref[:half, :]
-    low = fac_ref[half:ki, :]
+    first = lax.axis_index("mp") == 0
+    total = jnp.where(first, mine[: ki + 8, :], other[: ki + 8, :])
+    top = total[:half]
+    low = total[half:ki]
     c_in = jnp.concatenate(
         [top, jnp.concatenate([top[:, half:].T, low[:, :half]], axis=1)], axis=0
     )
-    count = fac_ref[ki : ki + 1, :1]
+    count = total[ki : ki + 1, :1]
     inv_in, inv_out = inverses([c_in, low[:, half:]])
     side = mm(mm(inv_in, gtr_ref[...]), inv_out) * (count * count)
-    out_ref[:, :half] = side[:half]
-    out_ref[:, half:] = side[half:]
-
-
-def scores_kernel(order, n_blk, side_ref, gte_ref, out_ref):
+    side = jnp.concatenate([side[:half], side[half:]], axis=1)
+    sums = []
+    for p in range(len(order)):
+        rows = slice(p * half, (p + 1) * half)
+        grad = jnp.where(first, other[rows, :], mine[rows, :])
+        sums.append(jnp.sum(side * grad, axis=0, keepdims=True))
+    values = jnp.sum(jnp.concatenate(sums, axis=0), axis=1, keepdims=True)
     z = lax.axis_index("dp")
     b = lax.axis_index("blk")
     lane = lax.broadcasted_iota(jnp.int32, out_ref.shape, 1)
     row = jnp.zeros(out_ref.shape, jnp.float32)
-    side = side_ref[...]
     for p, (dz, db) in enumerate(order):
-        value = jnp.sum(side * gte_ref[p], axis=(0, 1), keepdims=True)
-        row = jnp.where(lane == (z ^ dz) * n_blk + (b ^ db), value, row)
+        row = jnp.where(lane == (z ^ dz) * n_blk + (b ^ db), values[p : p + 1, :], row)
     out_ref[...] = row
 
 
@@ -309,34 +330,42 @@
     ki = part.shape[1]
     ko = ki // 2
     other = swap(part, "mp", 2, 1)
-    fac, gte, gtr = call(
+    fac_rows, grad_rows = ki + 8, ki // 2
+    msg, gtr = call(
         moments_kernel,
         (
-            jax.ShapeDtypeStruct((ki + 8, ki), jnp.float32),
-            jax.ShapeDtypeStruct((1, ki // 2, ki), jnp.float32),
+            jax.ShapeDtypeStruct((fac_rows, ki), jnp.float32),
             jax.ShapeDtypeStruct((ki, ko), jnp.float32),
         ),
         [smem(), smem(), vmem(), vmem()],
         (train_lengths, test_lengths, part, other),
     )
+    steps_z = [(k, 0) for k in bits(n_dp)]
+    steps_x = [(0, k) for k in bits(n_blk)]
     order = [(0, 0)]
-    for axis, count in (("blk", n_blk), ("dp", n_dp)):
-        for k in bits(count):
-            fac = fac + swap(fac, axis, count, k)
-            gte = jnp.concatenate([gte, swap(gte, axis, count, k)], axis=0)
-            order += [(dz ^ k, db) if axis == "dp" else (dz, db ^ k) for dz, db in order]
-    side = call(
-        side_kernel,
-        jax.ShapeDtypeStruct((ki // 2, ki), jnp.float32),
-        [vmem()] * 2,
-        (fac, gtr),
-        flops=4 << 30,
-    )
+    for step0, step1 in zip(steps_x + steps_z, steps_z + steps_x):
+        pairs = []
+        for z in range(n_dp):
+            for b in range(n_blk):
+                for core, (dz, db) in enumerate((step0, step1)):
+                    pairs.append((
+                        (z * n_blk + b) * 2 + core, ((z ^ dz) * n_blk + (b ^ db)) * 2 + core))
+        recv = lax.ppermute(msg, ("dp", "blk", "mp"), pairs)
+        rows = len(order) * grad_rows
+        msg = call(
+            functools.partial(round_kernel, fac_rows, rows),
+            jax.ShapeDtypeStruct((max(fac_rows, 2 * rows), ki), jnp.float32),
+            [vmem()] * 2,
+            (msg, recv),
+        )
+        order += [(dz ^ step1[0], db ^ step1[1]) for dz, db in order]
+    recv = swap(msg, "mp", 2, 1)
     return call(
         functools.partial(scores_kernel, order, n_blk),
         jax.ShapeDtypeStruct((1, n_dp * n_blk), jnp.float32),
-        [vmem()] * 2,
-        (side, gte),
+        [vmem()] * 3,
+        (msg, recv, gtr),
+        flops=4 << 30,
     )
 
 

time: 50.9 us -> 51 us (level)
  waiting for transfers between devices: 14.1 us -> 16.6 us
  starting transfers between devices: 25.1 us -> 22.6 us
    ppermute x0 -> x3, waiting for transfers between devices: none -> 11.2 us  [per_device(): recv = lax.ppermute(msg, ('dp', 'blk', 'mp'), pairs)]
    ppermute x17 -> x12, waiting for transfers between devices: 14.1 us -> 5.38 us  [swap(): return lax.ppermute(x, axis, [(i, i ^ k) for i in range(count)])]
    ppermute x17 -> x12, starting transfers between devices: 25.1 us -> 17.7 us  [swap(): return lax.ppermute(x, axis, [(i, i ^ k) for i in range(count)])]
    ppermute x0 -> x3, starting transfers between devices: none -> 4.92 us  [per_device(): recv = lax.ppermute(msg, ('dp', 'blk', 'mp'), pairs)]
    pallas_call x12 -> x14, Pallas kernels: 9.15 us -> 9.3 us  [call(): pl.pallas_call(kernel, out_shape=out_shape, in_specs=in_specs, out_specs=...]
  transfers between devices with their start and end apart: 17 -> 15, of which waited for: 9 -> 9; matrix products, arithmetic and copies ran while one was open for 0% -> 0% of each run, Pallas kernels for 14% -> 7%
where the time goes in v9:
time: 51 us; the launch traced here: 50.8 us
  starting transfers between devices  22.6 us (44%)
  waiting for transfers between devices  16.6 us (33%)
  Pallas kernels  9.3 us (18%)
  between operations  1.41 us (3%)
  other arithmetic  0.89 us (2%)
    ppermute x12, starting transfers between devices, swap(): return lax.ppermute(x, axis, [(i, i ^ k) for i in range(count)])  17.7 us
    ppermute x3, waiting for transfers between devices, per_device(): recv = lax.ppermute(msg, ('dp', 'blk', 'mp'), pairs)  11.2 us
    pallas_call x14, Pallas kernels, call(): pl.pallas_call(kernel, out_shape=out_shape, in_specs=in_specs, out_specs=...  9.3 us
    ppermute x12, waiting for transfers between devices, swap(): return lax.ppermute(x, axis, [(i, i ^ k) for i in range(count)])  5.38 us
    ppermute x3, starting transfers between devices, per_device(): recv = lax.ppermute(msg, ('dp', 'blk', 'mp'), pairs)  4.92 us
  transfers between devices with their start and end apart: 15, of which 9 were waited for; matrix products, arithmetic and copies ran while one was open for 0% of the time, Pallas kernels for 7%

profile of v9, /device:TPU:0, one launch (start us, length us, event | category | flops | bytes accessed | tf_op | source)
XLA Modules:
  0.0 50.8 jit_solution(2396007580662593972)
XLA Ops:
  0.0 0.9 %fusion = (bf16[48,1024]{1,0:T(8,128)(2,1)S(1)}, bf16[48,1024]{1,0:T(8,128)(2,1)S(1)}) fusion(s32[]{:T(128)S(6)} %select_n.7, bf16[32,4096]{1,0:T(8,128)(2,1)} %bitcast.6, bf16[16,4096]{1,0:T(8,128)(2,1)} %bitcast.12, s32[]{:T(128)S(6)} %select_n.6), kind=kLoop, calls=%fused_computation.4 | loop fusion | flops 393216 | bytes 589832 | tf_op jit(solution)/shard_map/concatenate | solution.py:263
  0.9 4.1 %collective-permute-start.6 = (bf16[48,512]{1,0:T(8,128)(2,1)S(1)}, bf16[48,512]{1,0:T(8,128)(2,1)S(1)}, u32[]{:S(2)}, u32[]{:S(2)}) collective-permute-start(bf16[48,512]{1,0:T(8,128)(2,1)S(1)} %get-tuple-element.23.refs_0_), channel_id=1, source_target_pairs={{0,8},{4,12},{8,0},{12,4},{1,9},{5,13},{9,1},{13,5},{2,10},{6,14},... | collective-permute-start | bytes 147464 | tf_op jit(solution)/shard_map/ppermute | solution.py:38
  5.0 0.1 collective-permute-start
  5.1 2.3 %shard_map.82 = (bf16[128,4096]{1,0:T(8,128)(2,1)S(1)}, bf16[128,4096]{1,0:T(8,128)(2,1)S(1)}, bf16[128,4096]{1,0:T(8,128)(2,1)S(1)}, bf16[128,4096]{1,0:T(8,128...) custom-call(bf16[128,4096]{1,0:T(8,128)(2,1)} %bitcast.8, bf16[128,4096]{1,0:T(8,128)(2,1)} %bitcast.9, ...), custom_call_target="tpu_custom_call" | custom-call | flops 1073741824 | bytes 65536 | tf_op jit(solution)/shard_map/pallas_call | solution.py:26
  7.4 0.2 collective-permute-done.6.refs_1_.refs_0_
  7.6 2.1 %collective-permute-start.7 = (bf16[96,512]{1,0:T(8,128)(2,1)S(1)}, bf16[96,512]{1,0:T(8,128)(2,1)S(1)}, u32[]{:S(2)}, u32[]{:S(2)}) collective-permute-start(bf16[96,512]{1,0:T(8,128)(2,1)S(1)} %shard_map.86), channel_id=1, source_target_pairs={{0,4},{4,0},{8,12},{12,8},{1,5},{5,1},{9,13},{13,9},{2,6},{6,2},{1... | collective-permute-start | bytes 294920 | tf_op jit(solution)/shard_map/ppermute | solution.py:38
  9.7 3.4 %collective-permute-start.4 = (bf16[48,1024]{1,0:T(8,128)(2,1)S(1)}, bf16[48,1024]{1,0:T(8,128)(2,1)S(1)}, u32[]{:S(2)}, u32[]{:S(2)}) collective-permute-start(bf16[48,1024]{1,0:T(8,128)(2,1)S(1)} %get-tuple-element.21.refs_0_), channel_id=1, source_target_pairs={{0,8},{4,12},{8,0},{12,4},{1,9},{5,13},{9,1},{13,5},{2,10},{6,14},... | collective-permute-start | bytes 294920 | tf_op jit(solution)/shard_map/ppermute | solution.py:38
  13.1 0.0 collective-permute-done.refs_1_.refs_0_
  13.1 0.1 collective-permute-start.1
  13.3 0.0 collective-permute-done.7.refs_1_
  13.3 1.6 %collective-permute-start.8 = (bf16[144,512]{1,0:T(8,128)(2,1)S(1)}, bf16[144,512]{1,0:T(8,128)(2,1)S(1)}, u32[]{:S(2)}, u32[]{:S(2)}) collective-permute-start(bf16[144,512]{1,0:T(8,128)(2,1)S(1)} %shard_map.87.refs_6_), channel_id=1, source_target_pairs={{0,2},{2,0},{16,18},{18,16},{1,3},{3,1},{17,19},{19,17},{4,6},{6,4... | collective-permute-start | bytes 442376 | tf_op jit(solution)/shard_map/ppermute | solution.py:38
  14.9 1.5 %collective-permute-start.9 = (bf16[144,512]{1,0:T(8,128)(2,1)S(1)}, bf16[144,512]{1,0:T(8,128)(2,1)S(1)}, u32[]{:S(2)}, u32[]{:S(2)}) collective-permute-start(bf16[144,512]{1,0:T(8,128)(2,1)S(1)} %shard_map.87.refs_6_), channel_id=1, source_target_pairs={{0,16},{2,18},{16,0},{18,2},{1,17},{3,19},{17,1},{19,3},{4,20},{6,... | collective-permute-start | bytes 442376 | tf_op jit(solution)/shard_map/ppermute | solution.py:38
  16.4 1.0 %collective-permute-done.4.refs_1_.refs_8_ = bf16[48,1024]{1,0:T(8,128)(2,1)S(1)} collective-permute-done((bf16[48,1024]{1,0:T(8,128)(2,1)S(1)}, bf16[48,1024]{1,0:T(8,128)(2,1)S(1)}, u32[]{:S(2)}, u32[]{:S(2)}) %collective-permute-start.4) | collective-permute-done | bytes 98336 | tf_op jit(solution)/shard_map/ppermute | solution.py:38
  17.4 1.5 %collective-permute-start.5 = (bf16[96,1024]{1,0:T(8,128)(2,1)S(1)}, bf16[96,1024]{1,0:T(8,128)(2,1)S(1)}, u32[]{:S(2)}, u32[]{:S(2)}) collective-permute-start(bf16[96,1024]{1,0:T(8,128)(2,1)S(1)} %shard_map.85), channel_id=1, source_target_pairs={{0,4},{4,0},{8,12},{12,8},{1,5},{5,1},{9,13},{13,9},{2,6},{6,2},{1... | collective-permute-start | bytes 589832 | tf_op jit(solution)/shard_map/ppermute | solution.py:38
  18.9 0.0 collective-permute-done.1.refs_1_
  18.9 1.6 %collective-permute-start.2 = (bf16[144,512]{1,0:T(8,128)(2,1)S(1)}, bf16[144,512]{1,0:T(8,128)(2,1)S(1)}, u32[]{:S(2)}, u32[]{:S(2)}) collective-permute-start(bf16[144,512]{1,0:T(8,128)(2,1)S(1)} %shard_map.84.refs_7_), channel_id=1, source_target_pairs={{0,2},{2,0},{16,18},{18,16},{1,3},{3,1},{17,19},{19,17},{4,6},{6,4... | collective-permute-start | bytes 442376 | tf_op jit(solution)/shard_map/ppermute | solution.py:38
  20.5 1.5 %collective-permute-start.3 = (bf16[144,512]{1,0:T(8,128)(2,1)S(1)}, bf16[144,512]{1,0:T(8,128)(2,1)S(1)}, u32[]{:S(2)}, u32[]{:S(2)}) collective-permute-start(bf16[144,512]{1,0:T(8,128)(2,1)S(1)} %shard_map.84.refs_7_), channel_id=1, source_target_pairs={{0,16},{2,18},{16,0},{18,2},{1,17},{3,19},{17,1},{19,3},{4,20},{6,... | collective-permute-start | bytes 442376 | tf_op jit(solution)/shard_map/ppermute | solution.py:38
  22.0 0.5 %shard_map.88.refs_8_ = f32[384,128]{1,0:T(8,128)S(1)} custom-call(bf16[128,4096]{1,0:T(8,128)(2,1)S(1)} %get-tuple-element.13.refs_0_, bf16[128,4096]{1,0:T(8,128)(2,1)S(1)} %get-tuple-element.14.refs_1_, bf16[128,4096]{1,0:T(8,128)(2,1)S(1)} %get-tuple-element.15.refs_2_, bf16[128,4096]{1,0:T(8,128)(2,1)S(1)} %get-tuple-element.16.refs_3_, ...), custom_call_target="tpu_custom_call" | custom-call | flops 1073741824 | bytes 65536 | tf_op jit(solution)/shard_map/pallas_call | solution.py:26
  22.6 0.0 collective-permute-done.8.refs_6_
  22.6 0.0 collective-permute-done.9.refs_7_
  22.6 0.5 %shard_map.89.refs_10_ = f32[384,128]{1,0:T(8,128)S(1)} custom-call(bf16[128,4096]{1,0:T(8,128)(2,1)S(1)} %get-tuple-element.13.refs_0_, bf16[128,4096]{1,0:T(8,128)(2,1)S(1)} %get-tuple-element.14.refs_1_, bf16[128,4096]{1,0:T(8,128)(2,1)S(1)} %get-tuple-element.15.refs_2_, bf16[128,4096]{1,0:T(8,128)(2,1)S(1)} %get-tuple-element.16.refs_3_, ...), custom_call_target="tpu_custom_call" | custom-call | flops 1073741824 | bytes 65536 | tf_op jit(solution)/shard_map/pallas_call | solution.py:26
  23.1 1.0 %collective-permute-done.2.refs_6_ = bf16[144,512]{1,0:T(8,128)(2,1)S(1)} collective-permute-done((bf16[144,512]{1,0:T(8,128)(2,1)S(1)}, bf16[144,512]{1,0:T(8,128)(2,1)S(1)}, u32[]{:S(2)}, u32[]{:S(2)}) %collective-permute-start.2) | collective-permute-done | bytes 147488 | tf_op jit(solution)/shard_map/ppermute | solution.py:38
  24.2 1.5 %collective-permute-done.3.refs_7_ = bf16[144,512]{1,0:T(8,128)(2,1)S(1)} collective-permute-done((bf16[144,512]{1,0:T(8,128)(2,1)S(1)}, bf16[144,512]{1,0:T(8,128)(2,1)S(1)}, u32[]{:S(2)}, u32[]{:S(2)}) %collective-permute-start.3) | collective-permute-done | bytes 147488 | tf_op jit(solution)/shard_map/ppermute | solution.py:38
  25.7 0.0 collective-permute-done.5.refs_9_
  25.7 0.8 %shard_map.90.mine = f32[384,128]{1,0:T(8,128)S(1)} custom-call(bf16[128,4096]{1,0:T(8,128)(2,1)S(1)} %get-tuple-element.13.refs_0_, bf16[128,4096]{1,0:T(8,128)(2,1)S(1)} %get-tuple-element.14.refs_1_, bf16[128,4096]{1,0:T(8,128)(2,1)S(1)} %get-tuple-element.15.refs_2_, bf16[128,4096]{1,0:T(8,128)(2,1)S(1)} %get-tuple-element.16.refs_3_, ...), custom_call_target="tpu_custom_call" | custom-call | flops 1073741824 | bytes 65536 | tf_op jit(solution)/shard_map/pallas_call | solution.py:26
  26.5 0.1 collective-permute-start.10
  27.9 0.1 collective-permute-done.10.other
  28.0 0.6 %shard_map.91 = (f32[136,128]{1,0:T(8,128)S(1)}, f32[128,64]{1,0:T(8,128)S(1)}) custom-call(s32[1]{0:T(128)S(6)} %copy.9.len_tr, s32[1]{0:T(128)S(6)} %copy.10.len_te, f32[384,128]{1,0:T(8,128)S(1)} %shard_map.90.mine, f32[384,128]{1,0:T(8,128)S(1)} %collective-permute-done.10.other), custom_call_target="tpu_custom_call" | custom-call | bytes 65536 | tf_op jit(solution)/shard_map/pallas_call | solution.py:26
  28.6 0.6 %collective-permute-start.11 = (f32[136,128]{1,0:T(8,128)S(1)}, f32[136,128]{1,0:T(8,128)S(1)}, u32[]{:S(2)}, u32[]{:S(2)}) collective-permute-start(f32[136,128]{1,0:T(8,128)S(1)} %get-tuple-element.19.mine), channel_id=1, source_target_pairs={{0,2},{1,9},{2,0},{3,11},{4,6},{5,13},{6,4},{7,15},{8,10},{9,1},{1... | collective-permute-start | bytes 208904 | tf_op jit(solution)/shard_map/ppermute | solution.py:353
  29.2 3.8 %collective-permute-done.11.other = f32[136,128]{1,0:T(8,128)S(1)} collective-permute-done((f32[136,128]{1,0:T(8,128)S(1)}, f32[136,128]{1,0:T(8,128)S(1)}, u32[]{:S(2)}, u32[]{:S(2)}) %collective-permute-start.11) | collective-permute-done | bytes 69664 | tf_op jit(solution)/shard_map/ppermute | solution.py:353
  33.0 4.3 %collective-permute-start.12 = (f32[136,128]{1,0:T(8,128)S(1)}, f32[136,128]{1,0:T(8,128)S(1)}, u32[]{:S(2)}, u32[]{:S(2)}) collective-permute-start(f32[136,128]{1,0:T(8,128)S(1)} %shard_map.92.mine), channel_id=1, source_target_pairs={{0,8},{1,5},{2,10},{3,7},{4,12},{5,1},{6,14},{7,3},{8,0},{9,13},{1... | collective-permute-start | bytes 208904 | tf_op jit(solution)/shard_map/ppermute | solution.py:353
  37.2 2.5 %collective-permute-done.12.other = f32[136,128]{1,0:T(8,128)S(1)} collective-permute-done((f32[136,128]{1,0:T(8,128)S(1)}, f32[136,128]{1,0:T(8,128)S(1)}, u32[]{:S(2)}, u32[]{:S(2)}) %collective-permute-start.12) | collective-permute-done | bytes 69664 | tf_op jit(solution)/shard_map/ppermute | solution.py:353
  39.8 0.1 collective-permute-start.13
  39.8 5.0 %collective-permute-done.13.other = f32[256,128]{1,0:T(8,128)S(1)} collective-permute-done((f32[256,128]{1,0:T(8,128)S(1)}, f32[256,128]{1,0:T(8,128)S(1)}, u32[]{:S(2)}, u32[]{:S(2)}) %collective-permute-start.13) | collective-permute-done | bytes 131104 | tf_op jit(solution)/shard_map/ppermute | solution.py:353
  44.8 0.1 collective-permute-start.14
  44.9 1.5 %collective-permute-done.14.other = f32[512,128]{1,0:T(8,128)S(1)} collective-permute-done((f32[512,128]{1,0:T(8,128)S(1)}, f32[512,128]{1,0:T(8,128)S(1)}, u32[]{:S(2)}, u32[]{:S(2)}) %collective-permute-start.14) | collective-permute-done | bytes 262176 | tf_op jit(solution)/shard_map/ppermute | solution.py:38
  46.4 4.4 %shard_map.95 = f32[1,8]{1,0:T(1,128)} custom-call(f32[512,128]{1,0:T(8,128)S(1)} %shard_map.94.mine, f32[512,128]{1,0:T(8,128)S(1)} %collective-permute-done.14.other, f32[128,64]{1,0:T(8,128)S(1)} %get-tuple-element.20.gtr_ref), custom_call_target="tpu_custom_call" | custom-call | flops 4294967296 | bytes 65536 | tf_op jit(solution)/shard_map/pallas_call | solution.py:26
  (9 shorter events, 0.1 us)
Async XLA Ops:
  0.9 6.7 %collective-permute-start.6 = (bf16[48,512]{1,0:T(8,128)(2,1)S(1)}, bf16[48,512]{1,0:T(8,128)(2,1)S(1)}, u32[]{:S(2)}, u32[]{:S(2)}) collective-permute-start(bf16[48,512]{1,0:T(8,128)(2,1)S(1)} %get-tuple-element.23.refs_0_), channel_id=1, source_target_pairs={{0,8},{4,12},{8,0},{12,4},{1,9},{5,13},{9,1},{13,5},{2,10},{6,14},... | collective-permute-start | bytes 147464 | tf_op jit(solution)/shard_map/ppermute | solution.py:38
  5.0 8.1 %collective-permute-start = (bf16[48,512]{1,0:T(8,128)(2,1)S(1)}, bf16[48,512]{1,0:T(8,128)(2,1)S(1)}, u32[]{:S(2)}, u32[]{:S(2)}) collective-permute-start(bf16[48,512]{1,0:T(8,128)(2,1)S(1)} %get-tuple-element.24.refs_0_), channel_id=1, source_target_pairs={{0,8},{4,12},{8,0},{12,4},{1,9},{5,13},{9,1},{13,5},{2,10},{6,14},... | collective-permute-start | bytes 147464 | tf_op jit(solution)/shard_map/ppermute | solution.py:38
  7.6 5.7 %collective-permute-start.7 = (bf16[96,512]{1,0:T(8,128)(2,1)S(1)}, bf16[96,512]{1,0:T(8,128)(2,1)S(1)}, u32[]{:S(2)}, u32[]{:S(2)}) collective-permute-start(bf16[96,512]{1,0:T(8,128)(2,1)S(1)} %shard_map.86), channel_id=1, source_target_pairs={{0,4},{4,0},{8,12},{12,8},{1,5},{5,1},{9,13},{13,9},{2,6},{6,2},{1... | collective-permute-start | bytes 294920 | tf_op jit(solution)/shard_map/ppermute | solution.py:38
  9.7 7.7 %collective-permute-start.4 = (bf16[48,1024]{1,0:T(8,128)(2,1)S(1)}, bf16[48,1024]{1,0:T(8,128)(2,1)S(1)}, u32[]{:S(2)}, u32[]{:S(2)}) collective-permute-start(bf16[48,1024]{1,0:T(8,128)(2,1)S(1)} %get-tuple-element.21.refs_0_), channel_id=1, source_target_pairs={{0,8},{4,12},{8,0},{12,4},{1,9},{5,13},{9,1},{13,5},{2,10},{6,14},... | collective-permute-start | bytes 294920 | tf_op jit(solution)/shard_map/ppermute | solution.py:38
  13.1 5.8 %collective-permute-start.1 = (bf16[96,512]{1,0:T(8,128)(2,1)S(1)}, bf16[96,512]{1,0:T(8,128)(2,1)S(1)}, u32[]{:S(2)}, u32[]{:S(2)}) collective-permute-start(bf16[96,512]{1,0:T(8,128)(2,1)S(1)} %shard_map.83), channel_id=1, source_target_pairs={{0,4},{4,0},{8,12},{12,8},{1,5},{5,1},{9,13},{13,9},{2,6},{6,2},{1... | collective-permute-start | bytes 294920 | tf_op jit(solution)/shard_map/ppermute | solution.py:38
  13.3 9.3 %collective-permute-start.8 = (bf16[144,512]{1,0:T(8,128)(2,1)S(1)}, bf16[144,512]{1,0:T(8,128)(2,1)S(1)}, u32[]{:S(2)}, u32[]{:S(2)}) collective-permute-start(bf16[144,512]{1,0:T(8,128)(2,1)S(1)} %shard_map.87.refs_6_), channel_id=1, source_target_pairs={{0,2},{2,0},{16,18},{18,16},{1,3},{3,1},{17,19},{19,17},{4,6},{6,4... | collective-permute-start | bytes 442376 | tf_op jit(solution)/shard_map/ppermute | solution.py:38
  14.9 7.7 %collective-permute-start.9 = (bf16[144,512]{1,0:T(8,128)(2,1)S(1)}, bf16[144,512]{1,0:T(8,128)(2,1)S(1)}, u32[]{:S(2)}, u32[]{:S(2)}) collective-permute-start(bf16[144,512]{1,0:T(8,128)(2,1)S(1)} %shard_map.87.refs_6_), channel_id=1, source_target_pairs={{0,16},{2,18},{16,0},{18,2},{1,17},{3,19},{17,1},{19,3},{4,20},{6,... | collective-permute-start | bytes 442376 | tf_op jit(solution)/shard_map/ppermute | solution.py:38
  17.4 8.3 %collective-permute-start.5 = (bf16[96,1024]{1,0:T(8,128)(2,1)S(1)}, bf16[96,1024]{1,0:T(8,128)(2,1)S(1)}, u32[]{:S(2)}, u32[]{:S(2)}) collective-permute-start(bf16[96,1024]{1,0:T(8,128)(2,1)S(1)} %shard_map.85), channel_id=1, source_target_pairs={{0,4},{4,0},{8,12},{12,8},{1,5},{5,1},{9,13},{13,9},{2,6},{6,2},{1... | collective-permute-start | bytes 589832 | tf_op jit(solution)/shard_map/ppermute | solution.py:38
  18.9 5.2 %collective-permute-start.2 = (bf16[144,512]{1,0:T(8,128)(2,1)S(1)}, bf16[144,512]{1,0:T(8,128)(2,1)S(1)}, u32[]{:S(2)}, u32[]{:S(2)}) collective-permute-start(bf16[144,512]{1,0:T(8,128)(2,1)S(1)} %shard_map.84.refs_7_), channel_id=1, source_target_pairs={{0,2},{2,0},{16,18},{18,16},{1,3},{3,1},{17,19},{19,17},{4,6},{6,4... | collective-permute-start | bytes 442376 | tf_op jit(solution)/shard_map/ppermute | solution.py:38
  20.5 5.1 %collective-permute-start.3 = (bf16[144,512]{1,0:T(8,128)(2,1)S(1)}, bf16[144,512]{1,0:T(8,128)(2,1)S(1)}, u32[]{:S(2)}, u32[]{:S(2)}) collective-permute-start(bf16[144,512]{1,0:T(8,128)(2,1)S(1)} %shard_map.84.refs_7_), channel_id=1, source_target_pairs={{0,16},{2,18},{16,0},{18,2},{1,17},{3,19},{17,1},{19,3},{4,20},{6,... | collective-permute-start | bytes 442376 | tf_op jit(solution)/shard_map/ppermute | solution.py:38
  26.5 1.5 %collective-permute-start.10 = (f32[384,128]{1,0:T(8,128)S(1)}, f32[384,128]{1,0:T(8,128)S(1)}, u32[]{:S(2)}, u32[]{:S(2)}) collective-permute-start(f32[384,128]{1,0:T(8,128)S(1)} %shard_map.90.mine), channel_id=1, source_target_pairs={{0,1},{1,0},{2,3},{3,2},{4,5},{5,4},{6,7},{7,6},{8,9},{9,8},{10,11... | collective-permute-start | bytes 589832 | tf_op jit(solution)/shard_map/ppermute | solution.py:38
  28.6 4.4 %collective-permute-start.11 = (f32[136,128]{1,0:T(8,128)S(1)}, f32[136,128]{1,0:T(8,128)S(1)}, u32[]{:S(2)}, u32[]{:S(2)}) collective-permute-start(f32[136,128]{1,0:T(8,128)S(1)} %get-tuple-element.19.mine), channel_id=1, source_target_pairs={{0,2},{1,9},{2,0},{3,11},{4,6},{5,13},{6,4},{7,15},{8,10},{9,1},{1... | collective-permute-start | bytes 208904 | tf_op jit(solution)/shard_map/ppermute | solution.py:353
  33.0 6.8 %collective-permute-start.12 = (f32[136,128]{1,0:T(8,128)S(1)}, f32[136,128]{1,0:T(8,128)S(1)}, u32[]{:S(2)}, u32[]{:S(2)}) collective-permute-start(f32[136,128]{1,0:T(8,128)S(1)} %shard_map.92.mine), channel_id=1, source_target_pairs={{0,8},{1,5},{2,10},{3,7},{4,12},{5,1},{6,14},{7,3},{8,0},{9,13},{1... | collective-permute-start | bytes 208904 | tf_op jit(solution)/shard_map/ppermute | solution.py:353
  39.8 5.0 %collective-permute-start.13 = (f32[256,128]{1,0:T(8,128)S(1)}, f32[256,128]{1,0:T(8,128)S(1)}, u32[]{:S(2)}, u32[]{:S(2)}) collective-permute-start(f32[256,128]{1,0:T(8,128)S(1)} %shard_map.93.mine), channel_id=1, source_target_pairs={{0,4},{1,3},{2,6},{3,1},{4,0},{5,7},{6,2},{7,5},{8,12},{9,11},{10,... | collective-permute-start | bytes 393224 | tf_op jit(solution)/shard_map/ppermute | solution.py:353
  44.8 1.6 %collective-permute-start.14 = (f32[512,128]{1,0:T(8,128)S(1)}, f32[512,128]{1,0:T(8,128)S(1)}, u32[]{:S(2)}, u32[]{:S(2)}) collective-permute-start(f32[512,128]{1,0:T(8,128)S(1)} %shard_map.94.mine), channel_id=1, source_target_pairs={{0,1},{1,0},{2,3},{3,2},{4,5},{5,4},{6,7},{7,6},{8,9},{9,8},{10,11... | collective-permute-start | bytes 786440 | tf_op jit(solution)/shard_map/ppermute | solution.py:38

commit v10 on v6

--- a/solution.py
+++ b/solution.py
@@ -36,6 +36,18 @@
 
 def swap(x, axis, count, k):
     return lax.ppermute(x, axis, [(i, i ^ k) for i in range(count)])
+
+
+def mixed(x, axes, counts, step0, step1):
+    pairs = []
+    for i in range(counts[0]):
+        for j in range(counts[1]):
+            for core, (di, dj) in enumerate((step0, step1)):
+                pairs.append((
+                    (i * counts[1] + j) * 2 + core,
+                    ((i ^ di) * counts[1] + (j ^ dj)) * 2 + core,
+                ))
+    return lax.ppermute(x, (*axes, "mp"), pairs)
 
 
 def bits(count):
@@ -107,12 +119,14 @@
     out_ref, w_in, w_out = refs[6 + n_pieces + with_acc :]
     z = lax.axis_index("dp")
     q = lax.axis_index(PLANE)
+    core = lax.axis_index("mp")
     rin, rout = own_in.shape[0], own_out.shape[0]
     quarter = own_in.shape[1] // 4
     xs, gs = [0.0, 0.0], [0.0, 0.0]
     at = 0
     for dq, col, width, rows in plan:
-        start = pl.multiple_of((q ^ dq) * quarter + col, 128)
+        other = q ^ (core * (3 ^ dq) + (1 - core) * dq) if dq in (1, 2) else q ^ dq
+        start = pl.multiple_of(other * quarter + col, 128)
         cols = pl.ds(start, width)
         here = slice(at, at + width)
         at += width
@@ -260,11 +274,14 @@
     both_b = stack((halves[1], far[1]))
     near_b = swap(both_b, "dp", n_dp, 1)
     za = stack((far[0], near_a))
-    xa, ya = swap(za, PLANE, 4, 1), swap(za, PLANE, 4, 2)
+    along_x, along_y = (0, 1), (1, 0)
+    xa = mixed(za, PLANE, (n_groups, n_blk), along_x, along_y)
+    ya = mixed(za, PLANE, (n_groups, n_blk), along_y, along_x)
     both_op = stack((opposite, far_op))
     near_op = swap(both_op, "dp", n_dp, 1)
     zb = stack((far[1], near_b))
-    xb, yb = swap(zb, PLANE, 4, 1), swap(zb, PLANE, 4, 2)
+    xb = mixed(zb, PLANE, (n_groups, n_blk), along_x, along_y)
+    yb = mixed(zb, PLANE, (n_groups, n_blk), along_y, along_x)
 
     def accumulate(plan, pieces, acc):
         args = (*xs, w_in, w_out, *pieces) + (() if acc is None else (acc,))
@@ -325,9 +342,10 @@
         for k in bits(count):
             gte = jnp.concatenate([gte, swap(gte, axis, count, k)], axis=0)
             order += [(dz ^ k, db) if axis == "dp" else (dz, db ^ k) for dz, db in order]
-    for axis, count in (("blk", n_blk), ("dp", n_dp)):
-        for k in bits(count):
-            fac = fac + swap(fac, axis, count, k)
+    steps_z = [(k, 0) for k in bits(n_dp)]
+    steps_x = [(0, k) for k in bits(n_blk)]
+    for step0, step1 in zip(steps_x + steps_z, steps_z + steps_x):
+        fac = fac + mixed(fac, ("dp", "blk"), (n_dp, n_blk), step0, step1)
     side = call(
         side_kernel,
         jax.ShapeDtypeStruct((ki // 2, ki), jnp.float32),

time: 49.2 us -> 48.7 us (0.990)
    ppermute x17 -> x10, starting transfers between devices: 28.1 us -> 18.2 us  [swap(): return lax.ppermute(x, axis, [(i, i ^ k) for i in range(count)])]
    ppermute x0 -> x7, starting transfers between devices: none -> 9.68 us  [mixed(): return lax.ppermute(x, (*axes, 'mp'), pairs)]
    ppermute x17 -> x10, waiting for transfers between devices: 9.45 us -> 2.96 us  [swap(): return lax.ppermute(x, axis, [(i, i ^ k) for i in range(count)])]
    ppermute x0 -> x7, waiting for transfers between devices: none -> 6.17 us  [mixed(): return lax.ppermute(x, (*axes, 'mp'), pairs)]
where the time goes in v10:
time: 48.7 us; the launch traced here: 48.5 us
  starting transfers between devices  27.9 us (57%)
  Pallas kernels  9.13 us (19%)
  waiting for transfers between devices  9.13 us (19%)
  between operations  1.4 us (3%)
  other arithmetic  0.95 us (2%)
    ppermute x10, starting transfers between devices, swap(): return lax.ppermute(x, axis, [(i, i ^ k) for i in range(count)])  18.2 us
    ppermute x7, starting transfers between devices, mixed(): return lax.ppermute(x, (*axes, 'mp'), pairs)  9.68 us
    pallas_call x12, Pallas kernels, call(): pl.pallas_call(kernel, out_shape=out_shape, in_specs=in_specs, out_specs=...  9.13 us
    ppermute x7, waiting for transfers between devices, mixed(): return lax.ppermute(x, (*axes, 'mp'), pairs)  6.17 us
    ppermute x10, waiting for transfers between devices, swap(): return lax.ppermute(x, axis, [(i, i ^ k) for i in range(count)])  2.96 us
  transfers between devices with their start and end apart: 17, of which 8 were waited for; matrix products, arithmetic and copies ran while one was open for 0% of the time, Pallas kernels for 15%

profile of v10, /device:TPU:0, one launch (start us, length us, event | category | flops | bytes accessed | tf_op | source)
XLA Modules:
  0.0 48.5 jit_solution(7287056177678631167)
XLA Ops:
  0.0 0.9 %fusion = (bf16[48,1024]{1,0:T(8,128)(2,1)S(1)}, bf16[48,1024]{1,0:T(8,128)(2,1)S(1)}) fusion(s32[]{:T(128)S(6)} %select_n.7, bf16[32,4096]{1,0:T(8,128)(2,1)} %bitcast.6, bf16[16,4096]{1,0:T(8,128)(2,1)} %bitcast.12, s32[]{:T(128)S(6)} %select_n.6), kind=kLoop, calls=%fused_computation.6 | loop fusion | flops 393216 | bytes 589832 | tf_op jit(solution)/shard_map/concatenate | solution.py:257
  0.9 4.1 %collective-permute-start.6 = (bf16[48,512]{1,0:T(8,128)(2,1)S(1)}, bf16[48,512]{1,0:T(8,128)(2,1)S(1)}, u32[]{:S(2)}, u32[]{:S(2)}) collective-permute-start(bf16[48,512]{1,0:T(8,128)(2,1)S(1)} %get-tuple-element.25.refs_0_), channel_id=1, source_target_pairs={{0,8},{4,12},{8,0},{12,4},{1,9},{5,13},{9,1},{13,5},{2,10},{6,14},... | collective-permute-start | bytes 147464 | tf_op jit(solution)/shard_map/ppermute | solution.py:38
  5.0 0.1 collective-permute-start
  5.1 2.3 %shard_map.82 = (bf16[128,4096]{1,0:T(8,128)(2,1)S(1)}, bf16[128,4096]{1,0:T(8,128)(2,1)S(1)}, bf16[128,4096]{1,0:T(8,128)(2,1)S(1)}, bf16[128,4096]{1,0:T(8,128...) custom-call(bf16[128,4096]{1,0:T(8,128)(2,1)} %bitcast.8, bf16[128,4096]{1,0:T(8,128)(2,1)} %bitcast.9, ...), custom_call_target="tpu_custom_call" | custom-call | flops 1073741824 | bytes 65536 | tf_op jit(solution)/shard_map/pallas_call | solution.py:26
  7.4 0.2 collective-permute-done.6.refs_1_.refs_0_
  7.6 2.1 %collective-permute-start.7 = (bf16[96,512]{1,0:T(8,128)(2,1)S(1)}, bf16[96,512]{1,0:T(8,128)(2,1)S(1)}, u32[]{:S(2)}, u32[]{:S(2)}) collective-permute-start(bf16[96,512]{1,0:T(8,128)(2,1)S(1)} %shard_map.86), channel_id=1, source_target_pairs={{0,4},{4,0},{8,12},{12,8},{1,5},{5,1},{9,13},{13,9},{2,6},{6,2},{1... | collective-permute-start | bytes 294920 | tf_op jit(solution)/shard_map/ppermute | solution.py:38
  9.7 3.4 %collective-permute-start.4 = (bf16[48,1024]{1,0:T(8,128)(2,1)S(1)}, bf16[48,1024]{1,0:T(8,128)(2,1)S(1)}, u32[]{:S(2)}, u32[]{:S(2)}) collective-permute-start(bf16[48,1024]{1,0:T(8,128)(2,1)S(1)} %get-tuple-element.23.refs_0_), channel_id=1, source_target_pairs={{0,8},{4,12},{8,0},{12,4},{1,9},{5,13},{9,1},{13,5},{2,10},{6,14},... | collective-permute-start | bytes 294920 | tf_op jit(solution)/shard_map/ppermute | solution.py:38
  13.1 0.0 collective-permute-done.refs_1_.refs_0_
  13.1 0.1 collective-permute-start.1
  13.3 0.0 collective-permute-done.7.refs_1_
  13.3 1.6 %collective-permute-start.8 = (bf16[144,512]{1,0:T(8,128)(2,1)S(1)}, bf16[144,512]{1,0:T(8,128)(2,1)S(1)}, u32[]{:S(2)}, u32[]{:S(2)}) collective-permute-start(bf16[144,512]{1,0:T(8,128)(2,1)S(1)} %shard_map.87.refs_6_), channel_id=1, source_target_pairs={{0,2},{1,17},{2,0},{3,19},{16,18},{17,1},{18,16},{19,3},{4,6},{5,2... | collective-permute-start | bytes 442376 | tf_op jit(solution)/shard_map/ppermute | solution.py:50
  14.9 1.5 %collective-permute-start.9 = (bf16[144,512]{1,0:T(8,128)(2,1)S(1)}, bf16[144,512]{1,0:T(8,128)(2,1)S(1)}, u32[]{:S(2)}, u32[]{:S(2)}) collective-permute-start(bf16[144,512]{1,0:T(8,128)(2,1)S(1)} %shard_map.87.refs_6_), channel_id=1, source_target_pairs={{0,16},{1,3},{2,18},{3,1},{16,0},{17,19},{18,2},{19,17},{4,20},{5,... | collective-permute-start | bytes 442376 | tf_op jit(solution)/shard_map/ppermute | solution.py:50
  16.4 1.0 %collective-permute-done.4.refs_1_.refs_8_ = bf16[48,1024]{1,0:T(8,128)(2,1)S(1)} collective-permute-done((bf16[48,1024]{1,0:T(8,128)(2,1)S(1)}, bf16[48,1024]{1,0:T(8,128)(2,1)S(1)}, u32[]{:S(2)}, u32[]{:S(2)}) %collective-permute-start.4) | collective-permute-done | bytes 98336 | tf_op jit(solution)/shard_map/ppermute | solution.py:38
  17.4 1.5 %collective-permute-start.5 = (bf16[96,1024]{1,0:T(8,128)(2,1)S(1)}, bf16[96,1024]{1,0:T(8,128)(2,1)S(1)}, u32[]{:S(2)}, u32[]{:S(2)}) collective-permute-start(bf16[96,1024]{1,0:T(8,128)(2,1)S(1)} %shard_map.85), channel_id=1, source_target_pairs={{0,4},{4,0},{8,12},{12,8},{1,5},{5,1},{9,13},{13,9},{2,6},{6,2},{1... | collective-permute-start | bytes 589832 | tf_op jit(solution)/shard_map/ppermute | solution.py:38
  18.9 0.0 collective-permute-done.1.refs_1_
  18.9 1.6 %collective-permute-start.2 = (bf16[144,512]{1,0:T(8,128)(2,1)S(1)}, bf16[144,512]{1,0:T(8,128)(2,1)S(1)}, u32[]{:S(2)}, u32[]{:S(2)}) collective-permute-start(bf16[144,512]{1,0:T(8,128)(2,1)S(1)} %shard_map.84.refs_7_), channel_id=1, source_target_pairs={{0,2},{1,17},{2,0},{3,19},{16,18},{17,1},{18,16},{19,3},{4,6},{5,2... | collective-permute-start | bytes 442376 | tf_op jit(solution)/shard_map/ppermute | solution.py:50
  20.5 1.5 %collective-permute-start.3 = (bf16[144,512]{1,0:T(8,128)(2,1)S(1)}, bf16[144,512]{1,0:T(8,128)(2,1)S(1)}, u32[]{:S(2)}, u32[]{:S(2)}) collective-permute-start(bf16[144,512]{1,0:T(8,128)(2,1)S(1)} %shard_map.84.refs_7_), channel_id=1, source_target_pairs={{0,16},{1,3},{2,18},{3,1},{16,0},{17,19},{18,2},{19,17},{4,20},{5,... | collective-permute-start | bytes 442376 | tf_op jit(solution)/shard_map/ppermute | solution.py:50
  22.0 0.5 %shard_map.88.refs_8_ = f32[384,128]{1,0:T(8,128)S(1)} custom-call(bf16[128,4096]{1,0:T(8,128)(2,1)S(1)} %get-tuple-element.14.refs_0_, bf16[128,4096]{1,0:T(8,128)(2,1)S(1)} %get-tuple-element.15.refs_1_, bf16[128,4096]{1,0:T(8,128)(2,1)S(1)} %get-tuple-element.16.refs_2_, bf16[128,4096]{1,0:T(8,128)(2,1)S(1)} %get-tuple-element.17.refs_3_, ...), custom_call_target="tpu_custom_call" | custom-call | flops 1073741824 | bytes 65536 | tf_op jit(solution)/shard_map/pallas_call | solution.py:26
  22.6 0.0 collective-permute-done.8.refs_6_
  22.6 0.0 collective-permute-done.9.refs_7_
  22.6 0.6 %shard_map.89.refs_10_ = f32[384,128]{1,0:T(8,128)S(1)} custom-call(bf16[128,4096]{1,0:T(8,128)(2,1)S(1)} %get-tuple-element.14.refs_0_, bf16[128,4096]{1,0:T(8,128)(2,1)S(1)} %get-tuple-element.15.refs_1_, bf16[128,4096]{1,0:T(8,128)(2,1)S(1)} %get-tuple-element.16.refs_2_, bf16[128,4096]{1,0:T(8,128)(2,1)S(1)} %get-tuple-element.17.refs_3_, ...), custom_call_target="tpu_custom_call" | custom-call | flops 1073741824 | bytes 65536 | tf_op jit(solution)/shard_map/pallas_call | solution.py:26
  23.1 1.2 %collective-permute-done.2.refs_6_ = bf16[144,512]{1,0:T(8,128)(2,1)S(1)} collective-permute-done((bf16[144,512]{1,0:T(8,128)(2,1)S(1)}, bf16[144,512]{1,0:T(8,128)(2,1)S(1)}, u32[]{:S(2)}, u32[]{:S(2)}) %collective-permute-start.2) | collective-permute-done | bytes 147488 | tf_op jit(solution)/shard_map/ppermute | solution.py:50
  24.4 1.3 %collective-permute-done.3.refs_7_ = bf16[144,512]{1,0:T(8,128)(2,1)S(1)} collective-permute-done((bf16[144,512]{1,0:T(8,128)(2,1)S(1)}, bf16[144,512]{1,0:T(8,128)(2,1)S(1)}, u32[]{:S(2)}, u32[]{:S(2)}) %collective-permute-start.3) | collective-permute-done | bytes 147488 | tf_op jit(solution)/shard_map/ppermute | solution.py:50
  25.7 0.0 collective-permute-done.5.refs_9_
  25.7 0.8 %shard_map.90.mine = f32[384,128]{1,0:T(8,128)S(1)} custom-call(bf16[128,4096]{1,0:T(8,128)(2,1)S(1)} %get-tuple-element.14.refs_0_, bf16[128,4096]{1,0:T(8,128)(2,1)S(1)} %get-tuple-element.15.refs_1_, bf16[128,4096]{1,0:T(8,128)(2,1)S(1)} %get-tuple-element.16.refs_2_, bf16[128,4096]{1,0:T(8,128)(2,1)S(1)} %get-tuple-element.17.refs_3_, ...), custom_call_target="tpu_custom_call" | custom-call | flops 1073741824 | bytes 65536 | tf_op jit(solution)/shard_map/pallas_call | solution.py:26
  26.5 0.1 collective-permute-start.10
  27.9 0.1 collective-permute-done.10.other
  28.0 0.5 shard_map.91
  28.5 0.6 %collective-permute-start.11 = (f32[136,128]{1,0:T(8,128)S(1)}, f32[136,128]{1,0:T(8,128)S(1)}, u32[]{:S(2)}, u32[]{:S(2)}) collective-permute-start(f32[136,128]{1,0:T(8,128)S(1)} %get-tuple-element.20), channel_id=1, source_target_pairs={{0,2},{1,9},{2,0},{3,11},{4,6},{5,13},{6,4},{7,15},{8,10},{9,1},{1... | collective-permute-start | bytes 208904 | tf_op jit(solution)/shard_map/ppermute | solution.py:50
  29.0 5.2 %collective-permute-start.14 = (f32[1,64,128]{2,1,0:T(8,128)S(1)}, f32[1,64,128]{2,1,0:T(8,128)S(1)}, u32[]{:S(2)}, u32[]{:S(2)}) collective-permute-start(f32[1,64,128]{2,1,0:T(8,128)S(1)} %get-tuple-element.22), channel_id=1, source_target_pairs={{0,8},{4,12},{8,0},{12,4},{1,9},{5,13},{9,1},{13,5},{2,10},{6,14},... | collective-permute-start | bytes 98312 | tf_op jit(solution)/shard_map/ppermute | solution.py:38
  34.2 0.0 collective-permute-done.11
  34.2 2.9 %collective-permute-start.12 = (f32[136,128]{1,0:T(8,128)S(1)}, f32[136,128]{1,0:T(8,128)S(1)}, u32[]{:S(2)}, u32[]{:S(2)}) collective-permute-start(f32[136,128]{1,0:T(8,128)S(1)} %add.21), channel_id=1, source_target_pairs={{0,8},{1,5},{2,10},{3,7},{4,12},{5,1},{6,14},{7,3},{8,0},{9,13},{1... | collective-permute-start | bytes 208904 | tf_op jit(solution)/shard_map/ppermute | solution.py:50
  37.1 0.0 collective-permute-done.14
  37.1 0.1 collective-permute-start.15
  37.2 2.5 %collective-permute-done.12 = f32[136,128]{1,0:T(8,128)S(1)} collective-permute-done((f32[136,128]{1,0:T(8,128)S(1)}, f32[136,128]{1,0:T(8,128)S(1)}, u32[]{:S(2)}, u32[]{:S(2)}) %collective-permute-start.12) | collective-permute-done | bytes 69664 | tf_op jit(solution)/shard_map/ppermute | solution.py:50
  39.7 0.1 collective-permute-start.13
  39.8 1.6 %collective-permute-done.15 = f32[2,64,128]{2,1,0:T(8,128)S(1)} collective-permute-done((f32[2,64,128]{2,1,0:T(8,128)S(1)}, f32[2,64,128]{2,1,0:T(8,128)S(1)}, u32[]{:S(2)}, u32[]{:S(2)}) %collective-permute-start.15) | collective-permute-done | bytes 65568 | tf_op jit(solution)/shard_map/ppermute | solution.py:38
  41.4 1.6 %collective-permute-start.16 = (f32[4,64,128]{2,1,0:T(8,128)S(1)}, f32[4,64,128]{2,1,0:T(8,128)S(1)}, u32[]{:S(2)}, u32[]{:S(2)}) collective-permute-start(f32[4,64,128]{2,1,0:T(8,128)S(1)} %pad_maximum_fusion.1), channel_id=1, source_target_pairs={{0,2},{2,0},{1,3},{3,1},{4,6},{6,4},{5,7},{7,5},{8,10},{10,8},{9,1... | collective-permute-start | bytes 393224 | tf_op jit(solution)/shard_map/ppermute | solution.py:38
  43.0 1.1 %collective-permute-done.13 = f32[136,128]{1,0:T(8,128)S(1)} collective-permute-done((f32[136,128]{1,0:T(8,128)S(1)}, f32[136,128]{1,0:T(8,128)S(1)}, u32[]{:S(2)}, u32[]{:S(2)}) %collective-permute-start.13) | collective-permute-done | bytes 69664 | tf_op jit(solution)/shard_map/ppermute | solution.py:50
  44.1 3.8 %shard_map.92.side_ref = f32[64,128]{1,0:T(8,128)S(1)} custom-call(f32[136,128]{1,0:T(8,128)S(1)} %add.23.fac_ref, f32[128,64]{1,0:T(8,128)S(1)} %get-tuple-element.21.gtr_ref), custom_call_target="tpu_custom_call" | custom-call | flops 4294967296 | bytes 65536 | tf_op jit(solution)/shard_map/pallas_call | solution.py:26
  47.9 0.0 collective-permute-done.16
  47.9 0.6 %shard_map.93 = f32[1,8]{1,0:T(1,128)} custom-call(f32[64,128]{1,0:T(8,128)S(1)} %shard_map.92.side_ref, f32[8,64,128]{2,1,0:T(8,128)S(1)} %pad_maximum_fusion.gte_ref), custom_call_target="tpu_custom_call" | custom-call | bytes 65536 | tf_op jit(solution)/shard_map/pallas_call | solution.py:26
  (12 shorter events, 0.1 us)
Async XLA Ops:
  0.9 6.7 %collective-permute-start.6 = (bf16[48,512]{1,0:T(8,128)(2,1)S(1)}, bf16[48,512]{1,0:T(8,128)(2,1)S(1)}, u32[]{:S(2)}, u32[]{:S(2)}) collective-permute-start(bf16[48,512]{1,0:T(8,128)(2,1)S(1)} %get-tuple-element.25.refs_0_), channel_id=1, source_target_pairs={{0,8},{4,12},{8,0},{12,4},{1,9},{5,13},{9,1},{13,5},{2,10},{6,14},... | collective-permute-start | bytes 147464 | tf_op jit(solution)/shard_map/ppermute | solution.py:38
  5.0 8.1 %collective-permute-start = (bf16[48,512]{1,0:T(8,128)(2,1)S(1)}, bf16[48,512]{1,0:T(8,128)(2,1)S(1)}, u32[]{:S(2)}, u32[]{:S(2)}) collective-permute-start(bf16[48,512]{1,0:T(8,128)(2,1)S(1)} %get-tuple-element.26.refs_0_), channel_id=1, source_target_pairs={{0,8},{4,12},{8,0},{12,4},{1,9},{5,13},{9,1},{13,5},{2,10},{6,14},... | collective-permute-start | bytes 147464 | tf_op jit(solution)/shard_map/ppermute | solution.py:38
  7.6 5.7 %collective-permute-start.7 = (bf16[96,512]{1,0:T(8,128)(2,1)S(1)}, bf16[96,512]{1,0:T(8,128)(2,1)S(1)}, u32[]{:S(2)}, u32[]{:S(2)}) collective-permute-start(bf16[96,512]{1,0:T(8,128)(2,1)S(1)} %shard_map.86), channel_id=1, source_target_pairs={{0,4},{4,0},{8,12},{12,8},{1,5},{5,1},{9,13},{13,9},{2,6},{6,2},{1... | collective-permute-start | bytes 294920 | tf_op jit(solution)/shard_map/ppermute | solution.py:38
  9.7 7.7 %collective-permute-start.4 = (bf16[48,1024]{1,0:T(8,128)(2,1)S(1)}, bf16[48,1024]{1,0:T(8,128)(2,1)S(1)}, u32[]{:S(2)}, u32[]{:S(2)}) collective-permute-start(bf16[48,1024]{1,0:T(8,128)(2,1)S(1)} %get-tuple-element.23.refs_0_), channel_id=1, source_target_pairs={{0,8},{4,12},{8,0},{12,4},{1,9},{5,13},{9,1},{13,5},{2,10},{6,14},... | collective-permute-start | bytes 294920 | tf_op jit(solution)/shard_map/ppermute | solution.py:38
  13.1 5.8 %collective-permute-start.1 = (bf16[96,512]{1,0:T(8,128)(2,1)S(1)}, bf16[96,512]{1,0:T(8,128)(2,1)S(1)}, u32[]{:S(2)}, u32[]{:S(2)}) collective-permute-start(bf16[96,512]{1,0:T(8,128)(2,1)S(1)} %shard_map.83), channel_id=1, source_target_pairs={{0,4},{4,0},{8,12},{12,8},{1,5},{5,1},{9,13},{13,9},{2,6},{6,2},{1... | collective-permute-start | bytes 294920 | tf_op jit(solution)/shard_map/ppermute | solution.py:38
  13.3 9.3 %collective-permute-start.8 = (bf16[144,512]{1,0:T(8,128)(2,1)S(1)}, bf16[144,512]{1,0:T(8,128)(2,1)S(1)}, u32[]{:S(2)}, u32[]{:S(2)}) collective-permute-start(bf16[144,512]{1,0:T(8,128)(2,1)S(1)} %shard_map.87.refs_6_), channel_id=1, source_target_pairs={{0,2},{1,17},{2,0},{3,19},{16,18},{17,1},{18,16},{19,3},{4,6},{5,2... | collective-permute-start | bytes 442376 | tf_op jit(solution)/shard_map/ppermute | solution.py:50
  14.9 7.7 %collective-permute-start.9 = (bf16[144,512]{1,0:T(8,128)(2,1)S(1)}, bf16[144,512]{1,0:T(8,128)(2,1)S(1)}, u32[]{:S(2)}, u32[]{:S(2)}) collective-permute-start(bf16[144,512]{1,0:T(8,128)(2,1)S(1)} %shard_map.87.refs_6_), channel_id=1, source_target_pairs={{0,16},{1,3},{2,18},{3,1},{16,0},{17,19},{18,2},{19,17},{4,20},{5,... | collective-permute-start | bytes 442376 | tf_op jit(solution)/shard_map/ppermute | solution.py:50
  17.4 8.3 %collective-permute-start.5 = (bf16[96,1024]{1,0:T(8,128)(2,1)S(1)}, bf16[96,1024]{1,0:T(8,128)(2,1)S(1)}, u32[]{:S(2)}, u32[]{:S(2)}) collective-permute-start(bf16[96,1024]{1,0:T(8,128)(2,1)S(1)} %shard_map.85), channel_id=1, source_target_pairs={{0,4},{4,0},{8,12},{12,8},{1,5},{5,1},{9,13},{13,9},{2,6},{6,2},{1... | collective-permute-start | bytes 589832 | tf_op jit(solution)/shard_map/ppermute | solution.py:38
  18.9 5.4 %collective-permute-start.2 = (bf16[144,512]{1,0:T(8,128)(2,1)S(1)}, bf16[144,512]{1,0:T(8,128)(2,1)S(1)}, u32[]{:S(2)}, u32[]{:S(2)}) collective-permute-start(bf16[144,512]{1,0:T(8,128)(2,1)S(1)} %shard_map.84.refs_7_), channel_id=1, source_target_pairs={{0,2},{1,17},{2,0},{3,19},{16,18},{17,1},{18,16},{19,3},{4,6},{5,2... | collective-permute-start | bytes 442376 | tf_op jit(solution)/shard_map/ppermute | solution.py:50
  20.5 5.1 %collective-permute-start.3 = (bf16[144,512]{1,0:T(8,128)(2,1)S(1)}, bf16[144,512]{1,0:T(8,128)(2,1)S(1)}, u32[]{:S(2)}, u32[]{:S(2)}) collective-permute-start(bf16[144,512]{1,0:T(8,128)(2,1)S(1)} %shard_map.84.refs_7_), channel_id=1, source_target_pairs={{0,16},{1,3},{2,18},{3,1},{16,0},{17,19},{18,2},{19,17},{4,20},{5,... | collective-permute-start | bytes 442376 | tf_op jit(solution)/shard_map/ppermute | solution.py:50
  26.5 1.5 %collective-permute-start.10 = (f32[384,128]{1,0:T(8,128)S(1)}, f32[384,128]{1,0:T(8,128)S(1)}, u32[]{:S(2)}, u32[]{:S(2)}) collective-permute-start(f32[384,128]{1,0:T(8,128)S(1)} %shard_map.90.mine), channel_id=1, source_target_pairs={{0,1},{1,0},{2,3},{3,2},{4,5},{5,4},{6,7},{7,6},{8,9},{9,8},{10,11... | collective-permute-start | bytes 589832 | tf_op jit(solution)/shard_map/ppermute | solution.py:38
  28.5 5.7 %collective-permute-start.11 = (f32[136,128]{1,0:T(8,128)S(1)}, f32[136,128]{1,0:T(8,128)S(1)}, u32[]{:S(2)}, u32[]{:S(2)}) collective-permute-start(f32[136,128]{1,0:T(8,128)S(1)} %get-tuple-element.20), channel_id=1, source_target_pairs={{0,2},{1,9},{2,0},{3,11},{4,6},{5,13},{6,4},{7,15},{8,10},{9,1},{1... | collective-permute-start | bytes 208904 | tf_op jit(solution)/shard_map/ppermute | solution.py:50
  29.0 8.1 %collective-permute-start.14 = (f32[1,64,128]{2,1,0:T(8,128)S(1)}, f32[1,64,128]{2,1,0:T(8,128)S(1)}, u32[]{:S(2)}, u32[]{:S(2)}) collective-permute-start(f32[1,64,128]{2,1,0:T(8,128)S(1)} %get-tuple-element.22), channel_id=1, source_target_pairs={{0,8},{4,12},{8,0},{12,4},{1,9},{5,13},{9,1},{13,5},{2,10},{6,14},... | collective-permute-start | bytes 98312 | tf_op jit(solution)/shard_map/ppermute | solution.py:38
  34.2 5.5 %collective-permute-start.12 = (f32[136,128]{1,0:T(8,128)S(1)}, f32[136,128]{1,0:T(8,128)S(1)}, u32[]{:S(2)}, u32[]{:S(2)}) collective-permute-start(f32[136,128]{1,0:T(8,128)S(1)} %add.21), channel_id=1, source_target_pairs={{0,8},{1,5},{2,10},{3,7},{4,12},{5,1},{6,14},{7,3},{8,0},{9,13},{1... | collective-permute-start | bytes 208904 | tf_op jit(solution)/shard_map/ppermute | solution.py:50
  37.1 4.3 %collective-permute-start.15 = (f32[2,64,128]{2,1,0:T(8,128)S(1)}, f32[2,64,128]{2,1,0:T(8,128)S(1)}, u32[]{:S(2)}, u32[]{:S(2)}) collective-permute-start(f32[2,64,128]{2,1,0:T(8,128)S(1)} %pad_maximum_fusion.2), channel_id=1, source_target_pairs={{0,4},{4,0},{8,12},{12,8},{1,5},{5,1},{9,13},{13,9},{2,6},{6,2},{1... | collective-permute-start | bytes 196616 | tf_op jit(solution)/shard_map/ppermute | solution.py:38
  39.7 4.4 %collective-permute-start.13 = (f32[136,128]{1,0:T(8,128)S(1)}, f32[136,128]{1,0:T(8,128)S(1)}, u32[]{:S(2)}, u32[]{:S(2)}) collective-permute-start(f32[136,128]{1,0:T(8,128)S(1)} %add.22), channel_id=1, source_target_pairs={{0,4},{1,3},{2,6},{3,1},{4,0},{5,7},{6,2},{7,5},{8,12},{9,11},{10,... | collective-permute-start | bytes 208904 | tf_op jit(solution)/shard_map/ppermute | solution.py:50
  41.4 6.4 %collective-permute-start.16 = (f32[4,64,128]{2,1,0:T(8,128)S(1)}, f32[4,64,128]{2,1,0:T(8,128)S(1)}, u32[]{:S(2)}, u32[]{:S(2)}) collective-permute-start(f32[4,64,128]{2,1,0:T(8,128)S(1)} %pad_maximum_fusion.1), channel_id=1, source_target_pairs={{0,2},{2,0},{1,3},{3,1},{4,6},{6,4},{5,7},{7,5},{8,10},{10,8},{9,1... | collective-permute-start | bytes 393224 | tf_op jit(solution)/shard_map/ppermute | solution.py:38

commit v11 on v10

--- a/solution.py
+++ b/solution.py
@@ -12,6 +12,7 @@
 TN = (((0,), (0,)), ((), ()))
 NEWTON_STEPS = 7
 PLANE = ("groups", "blk")
+LANES = 128
 
 
 def vmem():
@@ -173,20 +174,43 @@
     gte_ref[0, :, ko:] = grad_te[half:]
 
 
+def wide(x, rows, cols=LANES):
+    if x.shape[1] < cols:
+        x = jnp.concatenate([x, jnp.zeros((x.shape[0], cols - x.shape[1]), x.dtype)], axis=1)
+    if x.shape[0] < rows:
+        x = jnp.concatenate([x, jnp.zeros((rows - x.shape[0], cols), x.dtype)], axis=0)
+    return x
+
+
+def parts(x):
+    high = x.astype(jnp.bfloat16)
+    return high, (x - high.astype(jnp.float32)).astype(jnp.bfloat16)
+
+
+def right(x):
+    high, low = parts(wide(x, LANES))
+    upper = jnp.concatenate([high, low], axis=1)
+    lower = jnp.concatenate([jnp.zeros_like(high), high], axis=1)
+    return jnp.concatenate([upper, lower], axis=0)
+
+
+def mm3(x, packed):
+    both = jnp.dot(
+        jnp.concatenate(parts(x), axis=1), packed, preferred_element_type=jnp.float32
+    )
+    return both[:, :LANES] + both[:, LANES:]
+
+
 def damped(c):
     n = c.shape[0]
-    i = lax.broadcasted_iota(jnp.int32, (n, n), 0)
-    j = lax.broadcasted_iota(jnp.int32, (n, n), 1)
+    i = lax.broadcasted_iota(jnp.int32, c.shape, 0)
+    j = lax.broadcasted_iota(jnp.int32, c.shape, 1)
     eye = (i == j).astype(jnp.float32)
-    trace = jnp.sum(c * eye, axis=(0, 1), keepdims=True)
+    trace = jnp.sum(jnp.sum(c * eye, axis=0, keepdims=True), axis=1, keepdims=True)
     low = 0.1 * trace / n
     a = c + low * eye
     high = jnp.max(jnp.sum(jnp.abs(a), axis=0, keepdims=True), axis=1, keepdims=True)
     return a, eye, low, jnp.minimum(high, trace + low)
-
-
-def mm(a, b):
-    return jnp.dot(a, b, precision=HI, preferred_element_type=jnp.float32)
 
 
 def inverses(matrices):
@@ -195,22 +219,29 @@
         a, eye, low, high = damped(c)
         scale = 2.0 / (low + high)
         r = (high - low) / (high + low)
-        state.append((a, scale * a, scale * eye, r))
+        state.append((a, eye, scale * a, scale * eye, scale, r))
     for step in range(NEWTON_STEPS):
         nxt = []
-        for a, m, x, r in state:
+        for a, eye, m, x, scale, r in state:
             s = 2.0 / (2.0 - r * r)
             n = m.shape[0]
             if step == 0:
-                mx = s * (2.0 * m - mm(m, m))
-                xx = s * (2.0 * x - x[:1, :1] * m)
+                mx = s * (2.0 * m - mm3(m, right(m)))
+                xx = s * (2.0 * x - scale * m)
             else:
-                both = mm(jnp.concatenate([m, x], axis=0), m)
+                both = mm3(jnp.concatenate([m, x], axis=0), right(m))
                 mx = s * (2.0 * m - both[:n])
                 xx = s * (2.0 * x - both[n:])
-            nxt.append((a, mx, xx, r * r / (2.0 - r * r)))
+            nxt.append((a, eye, mx, xx, scale, r * r / (2.0 - r * r)))
         state = nxt
-    return [2.0 * x - mm(x, mm(a, x)) for a, m, x, r in state]
+    result = []
+    for a, eye, m, x, scale, r in state:
+        n = a.shape[0]
+        residual = eye - jnp.dot(
+            a[:, :n], x, precision=HI, preferred_element_type=jnp.float32
+        )
+        result.append(x + mm3(x, right(residual)))
+    return result
 
 
 def side_kernel(fac_ref, gtr_ref, out_ref):
@@ -222,10 +253,10 @@
         [top, jnp.concatenate([top[:, half:].T, low[:, :half]], axis=1)], axis=0
     )
     count = fac_ref[ki : ki + 1, :1]
-    inv_in, inv_out = inverses([c_in, low[:, half:]])
-    side = mm(mm(inv_in, gtr_ref[...]), inv_out) * (count * count)
-    out_ref[:, :half] = side[:half]
-    out_ref[:, half:] = side[half:]
+    inv_in, inv_out = inverses([c_in, wide(low[:, half:], half)])
+    side = mm3(mm3(inv_in, right(gtr_ref[...])), right(inv_out)) * (count * count)
+    out_ref[:, :half] = side[:half, :half]
+    out_ref[:, half:] = side[half:, :half]
 
 
 def scores_kernel(order, n_blk, side_ref, gte_ref, out_ref):

time: 48.7 us -> 47.4 us (0.973)
  Pallas kernels: 9.13 us -> 7.84 us
    pallas_call x12, Pallas kernels: 9.13 us -> 7.84 us  [call(): pl.pallas_call(kernel, out_shape=out_shape, in_specs=in_specs, out_specs=...]
  transfers between devices with their start and end apart: 17 -> 17, of which waited for: 8 -> 8; matrix products, arithmetic and copies ran while one was open for 0% -> 0% of each run, Pallas kernels for 15% -> 13%
where the time goes in v11:
time: 47.4 us; the launch traced here: 47.3 us
  starting transfers between devices  27.9 us (59%)
  waiting for transfers between devices  9.14 us (19%)
  Pallas kernels  7.84 us (17%)
  between operations  1.41 us (3%)
  other arithmetic  0.95 us (2%)
    ppermute x10, starting transfers between devices, swap(): return lax.ppermute(x, axis, [(i, i ^ k) for i in range(count)])  18.2 us
    ppermute x7, starting transfers between devices, mixed(): return lax.ppermute(x, (*axes, 'mp'), pairs)  9.68 us
    pallas_call x12, Pallas kernels, call(): pl.pallas_call(kernel, out_shape=out_shape, in_specs=in_specs, out_specs=...  7.84 us
    ppermute x7, waiting for transfers between devices, mixed(): return lax.ppermute(x, (*axes, 'mp'), pairs)  6.17 us
    ppermute x10, waiting for transfers between devices, swap(): return lax.ppermute(x, axis, [(i, i ^ k) for i in range(count)])  2.97 us
  transfers between devices with their start and end apart: 17, of which 8 were waited for; matrix products, arithmetic and copies ran while one was open for 0% of the time, Pallas kernels for 13%

profile of v11, /device:TPU:0, one launch (start us, length us, event | category | flops | bytes accessed | tf_op | source)
XLA Modules:
  0.0 47.3 jit_solution(2936053976926057431)
XLA Ops:
  0.0 0.9 %fusion = (bf16[48,1024]{1,0:T(8,128)(2,1)S(1)}, bf16[48,1024]{1,0:T(8,128)(2,1)S(1)}) fusion(s32[]{:T(128)S(6)} %select_n.7, bf16[32,4096]{1,0:T(8,128)(2,1)} %bitcast.6, bf16[16,4096]{1,0:T(8,128)(2,1)} %bitcast.12, s32[]{:T(128)S(6)} %select_n.6), kind=kLoop, calls=%fused_computation.6 | loop fusion | flops 393216 | bytes 589832 | tf_op jit(solution)/shard_map/concatenate | solution.py:288
  0.9 4.1 %collective-permute-start.6 = (bf16[48,512]{1,0:T(8,128)(2,1)S(1)}, bf16[48,512]{1,0:T(8,128)(2,1)S(1)}, u32[]{:S(2)}, u32[]{:S(2)}) collective-permute-start(bf16[48,512]{1,0:T(8,128)(2,1)S(1)} %get-tuple-element.25.refs_0_), channel_id=1, source_target_pairs={{0,8},{4,12},{8,0},{12,4},{1,9},{5,13},{9,1},{13,5},{2,10},{6,14},... | collective-permute-start | bytes 147464 | tf_op jit(solution)/shard_map/ppermute | solution.py:39
  5.0 0.1 collective-permute-start
  5.1 2.3 %shard_map.82 = (bf16[128,4096]{1,0:T(8,128)(2,1)S(1)}, bf16[128,4096]{1,0:T(8,128)(2,1)S(1)}, bf16[128,4096]{1,0:T(8,128)(2,1)S(1)}, bf16[128,4096]{1,0:T(8,128...) custom-call(bf16[128,4096]{1,0:T(8,128)(2,1)} %bitcast.8, bf16[128,4096]{1,0:T(8,128)(2,1)} %bitcast.9, ...), custom_call_target="tpu_custom_call" | custom-call | flops 1073741824 | bytes 65536 | tf_op jit(solution)/shard_map/pallas_call | solution.py:27
  7.4 0.2 collective-permute-done.6.refs_1_.refs_0_
  7.6 2.1 %collective-permute-start.7 = (bf16[96,512]{1,0:T(8,128)(2,1)S(1)}, bf16[96,512]{1,0:T(8,128)(2,1)S(1)}, u32[]{:S(2)}, u32[]{:S(2)}) collective-permute-start(bf16[96,512]{1,0:T(8,128)(2,1)S(1)} %shard_map.86), channel_id=1, source_target_pairs={{0,4},{4,0},{8,12},{12,8},{1,5},{5,1},{9,13},{13,9},{2,6},{6,2},{1... | collective-permute-start | bytes 294920 | tf_op jit(solution)/shard_map/ppermute | solution.py:39
  9.7 3.4 %collective-permute-start.4 = (bf16[48,1024]{1,0:T(8,128)(2,1)S(1)}, bf16[48,1024]{1,0:T(8,128)(2,1)S(1)}, u32[]{:S(2)}, u32[]{:S(2)}) collective-permute-start(bf16[48,1024]{1,0:T(8,128)(2,1)S(1)} %get-tuple-element.23.refs_0_), channel_id=1, source_target_pairs={{0,8},{4,12},{8,0},{12,4},{1,9},{5,13},{9,1},{13,5},{2,10},{6,14},... | collective-permute-start | bytes 294920 | tf_op jit(solution)/shard_map/ppermute | solution.py:39
  13.1 0.0 collective-permute-done.refs_1_.refs_0_
  13.1 0.1 collective-permute-start.1
  13.3 0.0 collective-permute-done.7.refs_1_
  13.3 1.6 %collective-permute-start.8 = (bf16[144,512]{1,0:T(8,128)(2,1)S(1)}, bf16[144,512]{1,0:T(8,128)(2,1)S(1)}, u32[]{:S(2)}, u32[]{:S(2)}) collective-permute-start(bf16[144,512]{1,0:T(8,128)(2,1)S(1)} %shard_map.87.refs_6_), channel_id=1, source_target_pairs={{0,2},{1,17},{2,0},{3,19},{16,18},{17,1},{18,16},{19,3},{4,6},{5,2... | collective-permute-start | bytes 442376 | tf_op jit(solution)/shard_map/ppermute | solution.py:51
  14.9 1.5 %collective-permute-start.9 = (bf16[144,512]{1,0:T(8,128)(2,1)S(1)}, bf16[144,512]{1,0:T(8,128)(2,1)S(1)}, u32[]{:S(2)}, u32[]{:S(2)}) collective-permute-start(bf16[144,512]{1,0:T(8,128)(2,1)S(1)} %shard_map.87.refs_6_), channel_id=1, source_target_pairs={{0,16},{1,3},{2,18},{3,1},{16,0},{17,19},{18,2},{19,17},{4,20},{5,... | collective-permute-start | bytes 442376 | tf_op jit(solution)/shard_map/ppermute | solution.py:51
  16.4 1.0 %collective-permute-done.4.refs_1_.refs_8_ = bf16[48,1024]{1,0:T(8,128)(2,1)S(1)} collective-permute-done((bf16[48,1024]{1,0:T(8,128)(2,1)S(1)}, bf16[48,1024]{1,0:T(8,128)(2,1)S(1)}, u32[]{:S(2)}, u32[]{:S(2)}) %collective-permute-start.4) | collective-permute-done | bytes 98336 | tf_op jit(solution)/shard_map/ppermute | solution.py:39
  17.4 1.5 %collective-permute-start.5 = (bf16[96,1024]{1,0:T(8,128)(2,1)S(1)}, bf16[96,1024]{1,0:T(8,128)(2,1)S(1)}, u32[]{:S(2)}, u32[]{:S(2)}) collective-permute-start(bf16[96,1024]{1,0:T(8,128)(2,1)S(1)} %shard_map.85), channel_id=1, source_target_pairs={{0,4},{4,0},{8,12},{12,8},{1,5},{5,1},{9,13},{13,9},{2,6},{6,2},{1... | collective-permute-start | bytes 589832 | tf_op jit(solution)/shard_map/ppermute | solution.py:39
  18.9 0.0 collective-permute-done.1.refs_1_
  18.9 1.6 %collective-permute-start.2 = (bf16[144,512]{1,0:T(8,128)(2,1)S(1)}, bf16[144,512]{1,0:T(8,128)(2,1)S(1)}, u32[]{:S(2)}, u32[]{:S(2)}) collective-permute-start(bf16[144,512]{1,0:T(8,128)(2,1)S(1)} %shard_map.84.refs_7_), channel_id=1, source_target_pairs={{0,2},{1,17},{2,0},{3,19},{16,18},{17,1},{18,16},{19,3},{4,6},{5,2... | collective-permute-start | bytes 442376 | tf_op jit(solution)/shard_map/ppermute | solution.py:51
  20.5 1.5 %collective-permute-start.3 = (bf16[144,512]{1,0:T(8,128)(2,1)S(1)}, bf16[144,512]{1,0:T(8,128)(2,1)S(1)}, u32[]{:S(2)}, u32[]{:S(2)}) collective-permute-start(bf16[144,512]{1,0:T(8,128)(2,1)S(1)} %shard_map.84.refs_7_), channel_id=1, source_target_pairs={{0,16},{1,3},{2,18},{3,1},{16,0},{17,19},{18,2},{19,17},{4,20},{5,... | collective-permute-start | bytes 442376 | tf_op jit(solution)/shard_map/ppermute | solution.py:51
  22.0 0.5 %shard_map.88.refs_8_ = f32[384,128]{1,0:T(8,128)S(1)} custom-call(bf16[128,4096]{1,0:T(8,128)(2,1)S(1)} %get-tuple-element.14.refs_0_, bf16[128,4096]{1,0:T(8,128)(2,1)S(1)} %get-tuple-element.15.refs_1_, bf16[128,4096]{1,0:T(8,128)(2,1)S(1)} %get-tuple-element.16.refs_2_, bf16[128,4096]{1,0:T(8,128)(2,1)S(1)} %get-tuple-element.17.refs_3_, ...), custom_call_target="tpu_custom_call" | custom-call | flops 1073741824 | bytes 65536 | tf_op jit(solution)/shard_map/pallas_call | solution.py:27
  22.6 0.0 collective-permute-done.8.refs_6_
  22.6 0.0 collective-permute-done.9.refs_7_
  22.6 0.6 %shard_map.89.refs_10_ = f32[384,128]{1,0:T(8,128)S(1)} custom-call(bf16[128,4096]{1,0:T(8,128)(2,1)S(1)} %get-tuple-element.14.refs_0_, bf16[128,4096]{1,0:T(8,128)(2,1)S(1)} %get-tuple-element.15.refs_1_, bf16[128,4096]{1,0:T(8,128)(2,1)S(1)} %get-tuple-element.16.refs_2_, bf16[128,4096]{1,0:T(8,128)(2,1)S(1)} %get-tuple-element.17.refs_3_, ...), custom_call_target="tpu_custom_call" | custom-call | flops 1073741824 | bytes 65536 | tf_op jit(solution)/shard_map/pallas_call | solution.py:27
  23.1 1.2 %collective-permute-done.2.refs_6_ = bf16[144,512]{1,0:T(8,128)(2,1)S(1)} collective-permute-done((bf16[144,512]{1,0:T(8,128)(2,1)S(1)}, bf16[144,512]{1,0:T(8,128)(2,1)S(1)}, u32[]{:S(2)}, u32[]{:S(2)}) %collective-permute-start.2) | collective-permute-done | bytes 147488 | tf_op jit(solution)/shard_map/ppermute | solution.py:51
  24.4 1.3 %collective-permute-done.3.refs_7_ = bf16[144,512]{1,0:T(8,128)(2,1)S(1)} collective-permute-done((bf16[144,512]{1,0:T(8,128)(2,1)S(1)}, bf16[144,512]{1,0:T(8,128)(2,1)S(1)}, u32[]{:S(2)}, u32[]{:S(2)}) %collective-permute-start.3) | collective-permute-done | bytes 147488 | tf_op jit(solution)/shard_map/ppermute | solution.py:51
  25.7 0.0 collective-permute-done.5.refs_9_
  25.7 0.8 %shard_map.90.mine = f32[384,128]{1,0:T(8,128)S(1)} custom-call(bf16[128,4096]{1,0:T(8,128)(2,1)S(1)} %get-tuple-element.14.refs_0_, bf16[128,4096]{1,0:T(8,128)(2,1)S(1)} %get-tuple-element.15.refs_1_, bf16[128,4096]{1,0:T(8,128)(2,1)S(1)} %get-tuple-element.16.refs_2_, bf16[128,4096]{1,0:T(8,128)(2,1)S(1)} %get-tuple-element.17.refs_3_, ...), custom_call_target="tpu_custom_call" | custom-call | flops 1073741824 | bytes 65536 | tf_op jit(solution)/shard_map/pallas_call | solution.py:27
  26.5 0.1 collective-permute-start.10
  27.9 0.1 collective-permute-done.10.other
  28.0 0.5 shard_map.91
  28.5 0.6 %collective-permute-start.11 = (f32[136,128]{1,0:T(8,128)S(1)}, f32[136,128]{1,0:T(8,128)S(1)}, u32[]{:S(2)}, u32[]{:S(2)}) collective-permute-start(f32[136,128]{1,0:T(8,128)S(1)} %get-tuple-element.20), channel_id=1, source_target_pairs={{0,2},{1,9},{2,0},{3,11},{4,6},{5,13},{6,4},{7,15},{8,10},{9,1},{1... | collective-permute-start | bytes 208904 | tf_op jit(solution)/shard_map/ppermute | solution.py:51
  29.0 5.2 %collective-permute-start.14 = (f32[1,64,128]{2,1,0:T(8,128)S(1)}, f32[1,64,128]{2,1,0:T(8,128)S(1)}, u32[]{:S(2)}, u32[]{:S(2)}) collective-permute-start(f32[1,64,128]{2,1,0:T(8,128)S(1)} %get-tuple-element.22), channel_id=1, source_target_pairs={{0,8},{4,12},{8,0},{12,4},{1,9},{5,13},{9,1},{13,5},{2,10},{6,14},... | collective-permute-start | bytes 98312 | tf_op jit(solution)/shard_map/ppermute | solution.py:39
  34.2 0.0 collective-permute-done.11
  34.2 2.9 %collective-permute-start.12 = (f32[136,128]{1,0:T(8,128)S(1)}, f32[136,128]{1,0:T(8,128)S(1)}, u32[]{:S(2)}, u32[]{:S(2)}) collective-permute-start(f32[136,128]{1,0:T(8,128)S(1)} %add.21), channel_id=1, source_target_pairs={{0,8},{1,5},{2,10},{3,7},{4,12},{5,1},{6,14},{7,3},{8,0},{9,13},{1... | collective-permute-start | bytes 208904 | tf_op jit(solution)/shard_map/ppermute | solution.py:51
  37.1 0.0 collective-permute-done.14
  37.1 0.1 collective-permute-start.15
  37.2 2.5 %collective-permute-done.12 = f32[136,128]{1,0:T(8,128)S(1)} collective-permute-done((f32[136,128]{1,0:T(8,128)S(1)}, f32[136,128]{1,0:T(8,128)S(1)}, u32[]{:S(2)}, u32[]{:S(2)}) %collective-permute-start.12) | collective-permute-done | bytes 69664 | tf_op jit(solution)/shard_map/ppermute | solution.py:51
  39.7 0.1 collective-permute-start.13
  39.8 1.6 %collective-permute-done.15 = f32[2,64,128]{2,1,0:T(8,128)S(1)} collective-permute-done((f32[2,64,128]{2,1,0:T(8,128)S(1)}, f32[2,64,128]{2,1,0:T(8,128)S(1)}, u32[]{:S(2)}, u32[]{:S(2)}) %collective-permute-start.15) | collective-permute-done | bytes 65568 | tf_op jit(solution)/shard_map/ppermute | solution.py:39
  41.4 1.6 %collective-permute-start.16 = (f32[4,64,128]{2,1,0:T(8,128)S(1)}, f32[4,64,128]{2,1,0:T(8,128)S(1)}, u32[]{:S(2)}, u32[]{:S(2)}) collective-permute-start(f32[4,64,128]{2,1,0:T(8,128)S(1)} %pad_maximum_fusion.1), channel_id=1, source_target_pairs={{0,2},{2,0},{1,3},{3,1},{4,6},{6,4},{5,7},{7,5},{8,10},{10,8},{9,1... | collective-permute-start | bytes 393224 | tf_op jit(solution)/shard_map/ppermute | solution.py:39
  43.0 1.1 %collective-permute-done.13 = f32[136,128]{1,0:T(8,128)S(1)} collective-permute-done((f32[136,128]{1,0:T(8,128)S(1)}, f32[136,128]{1,0:T(8,128)S(1)}, u32[]{:S(2)}, u32[]{:S(2)}) %collective-permute-start.13) | collective-permute-done | bytes 69664 | tf_op jit(solution)/shard_map/ppermute | solution.py:51
  44.1 2.5 %shard_map.92.side_ref = f32[64,128]{1,0:T(8,128)S(1)} custom-call(f32[136,128]{1,0:T(8,128)S(1)} %add.23.fac_ref, f32[128,64]{1,0:T(8,128)S(1)} %get-tuple-element.21.gtr_ref), custom_call_target="tpu_custom_call" | custom-call | flops 4294967296 | bytes 65536 | tf_op jit(solution)/shard_map/pallas_call | solution.py:27
  46.6 0.0 collective-permute-done.16
  46.6 0.6 %shard_map.93 = f32[1,8]{1,0:T(1,128)} custom-call(f32[64,128]{1,0:T(8,128)S(1)} %shard_map.92.side_ref, f32[8,64,128]{2,1,0:T(8,128)S(1)} %pad_maximum_fusion.gte_ref), custom_call_target="tpu_custom_call" | custom-call | bytes 65536 | tf_op jit(solution)/shard_map/pallas_call | solution.py:27
  (12 shorter events, 0.1 us)
Async XLA Ops:
  0.9 6.7 %collective-permute-start.6 = (bf16[48,512]{1,0:T(8,128)(2,1)S(1)}, bf16[48,512]{1,0:T(8,128)(2,1)S(1)}, u32[]{:S(2)}, u32[]{:S(2)}) collective-permute-start(bf16[48,512]{1,0:T(8,128)(2,1)S(1)} %get-tuple-element.25.refs_0_), channel_id=1, source_target_pairs={{0,8},{4,12},{8,0},{12,4},{1,9},{5,13},{9,1},{13,5},{2,10},{6,14},... | collective-permute-start | bytes 147464 | tf_op jit(solution)/shard_map/ppermute | solution.py:39
  5.0 8.1 %collective-permute-start = (bf16[48,512]{1,0:T(8,128)(2,1)S(1)}, bf16[48,512]{1,0:T(8,128)(2,1)S(1)}, u32[]{:S(2)}, u32[]{:S(2)}) collective-permute-start(bf16[48,512]{1,0:T(8,128)(2,1)S(1)} %get-tuple-element.26.refs_0_), channel_id=1, source_target_pairs={{0,8},{4,12},{8,0},{12,4},{1,9},{5,13},{9,1},{13,5},{2,10},{6,14},... | collective-permute-start | bytes 147464 | tf_op jit(solution)/shard_map/ppermute | solution.py:39
  7.6 5.7 %collective-permute-start.7 = (bf16[96,512]{1,0:T(8,128)(2,1)S(1)}, bf16[96,512]{1,0:T(8,128)(2,1)S(1)}, u32[]{:S(2)}, u32[]{:S(2)}) collective-permute-start(bf16[96,512]{1,0:T(8,128)(2,1)S(1)} %shard_map.86), channel_id=1, source_target_pairs={{0,4},{4,0},{8,12},{12,8},{1,5},{5,1},{9,13},{13,9},{2,6},{6,2},{1... | collective-permute-start | bytes 294920 | tf_op jit(solution)/shard_map/ppermute | solution.py:39
  9.7 7.7 %collective-permute-start.4 = (bf16[48,1024]{1,0:T(8,128)(2,1)S(1)}, bf16[48,1024]{1,0:T(8,128)(2,1)S(1)}, u32[]{:S(2)}, u32[]{:S(2)}) collective-permute-start(bf16[48,1024]{1,0:T(8,128)(2,1)S(1)} %get-tuple-element.23.refs_0_), channel_id=1, source_target_pairs={{0,8},{4,12},{8,0},{12,4},{1,9},{5,13},{9,1},{13,5},{2,10},{6,14},... | collective-permute-start | bytes 294920 | tf_op jit(solution)/shard_map/ppermute | solution.py:39
  13.1 5.8 %collective-permute-start.1 = (bf16[96,512]{1,0:T(8,128)(2,1)S(1)}, bf16[96,512]{1,0:T(8,128)(2,1)S(1)}, u32[]{:S(2)}, u32[]{:S(2)}) collective-permute-start(bf16[96,512]{1,0:T(8,128)(2,1)S(1)} %shard_map.83), channel_id=1, source_target_pairs={{0,4},{4,0},{8,12},{12,8},{1,5},{5,1},{9,13},{13,9},{2,6},{6,2},{1... | collective-permute-start | bytes 294920 | tf_op jit(solution)/shard_map/ppermute | solution.py:39
  13.3 9.3 %collective-permute-start.8 = (bf16[144,512]{1,0:T(8,128)(2,1)S(1)}, bf16[144,512]{1,0:T(8,128)(2,1)S(1)}, u32[]{:S(2)}, u32[]{:S(2)}) collective-permute-start(bf16[144,512]{1,0:T(8,128)(2,1)S(1)} %shard_map.87.refs_6_), channel_id=1, source_target_pairs={{0,2},{1,17},{2,0},{3,19},{16,18},{17,1},{18,16},{19,3},{4,6},{5,2... | collective-permute-start | bytes 442376 | tf_op jit(solution)/shard_map/ppermute | solution.py:51
  14.9 7.7 %collective-permute-start.9 = (bf16[144,512]{1,0:T(8,128)(2,1)S(1)}, bf16[144,512]{1,0:T(8,128)(2,1)S(1)}, u32[]{:S(2)}, u32[]{:S(2)}) collective-permute-start(bf16[144,512]{1,0:T(8,128)(2,1)S(1)} %shard_map.87.refs_6_), channel_id=1, source_target_pairs={{0,16},{1,3},{2,18},{3,1},{16,0},{17,19},{18,2},{19,17},{4,20},{5,... | collective-permute-start | bytes 442376 | tf_op jit(solution)/shard_map/ppermute | solution.py:51
  17.4 8.3 %collective-permute-start.5 = (bf16[96,1024]{1,0:T(8,128)(2,1)S(1)}, bf16[96,1024]{1,0:T(8,128)(2,1)S(1)}, u32[]{:S(2)}, u32[]{:S(2)}) collective-permute-start(bf16[96,1024]{1,0:T(8,128)(2,1)S(1)} %shard_map.85), channel_id=1, source_target_pairs={{0,4},{4,0},{8,12},{12,8},{1,5},{5,1},{9,13},{13,9},{2,6},{6,2},{1... | collective-permute-start | bytes 589832 | tf_op jit(solution)/shard_map/ppermute | solution.py:39
  18.9 5.4 %collective-permute-start.2 = (bf16[144,512]{1,0:T(8,128)(2,1)S(1)}, bf16[144,512]{1,0:T(8,128)(2,1)S(1)}, u32[]{:S(2)}, u32[]{:S(2)}) collective-permute-start(bf16[144,512]{1,0:T(8,128)(2,1)S(1)} %shard_map.84.refs_7_), channel_id=1, source_target_pairs={{0,2},{1,17},{2,0},{3,19},{16,18},{17,1},{18,16},{19,3},{4,6},{5,2... | collective-permute-start | bytes 442376 | tf_op jit(solution)/shard_map/ppermute | solution.py:51
  20.5 5.1 %collective-permute-start.3 = (bf16[144,512]{1,0:T(8,128)(2,1)S(1)}, bf16[144,512]{1,0:T(8,128)(2,1)S(1)}, u32[]{:S(2)}, u32[]{:S(2)}) collective-permute-start(bf16[144,512]{1,0:T(8,128)(2,1)S(1)} %shard_map.84.refs_7_), channel_id=1, source_target_pairs={{0,16},{1,3},{2,18},{3,1},{16,0},{17,19},{18,2},{19,17},{4,20},{5,... | collective-permute-start | bytes 442376 | tf_op jit(solution)/shard_map/ppermute | solution.py:51
  26.5 1.5 %collective-permute-start.10 = (f32[384,128]{1,0:T(8,128)S(1)}, f32[384,128]{1,0:T(8,128)S(1)}, u32[]{:S(2)}, u32[]{:S(2)}) collective-permute-start(f32[384,128]{1,0:T(8,128)S(1)} %shard_map.90.mine), channel_id=1, source_target_pairs={{0,1},{1,0},{2,3},{3,2},{4,5},{5,4},{6,7},{7,6},{8,9},{9,8},{10,11... | collective-permute-start | bytes 589832 | tf_op jit(solution)/shard_map/ppermute | solution.py:39
  28.5 5.7 %collective-permute-start.11 = (f32[136,128]{1,0:T(8,128)S(1)}, f32[136,128]{1,0:T(8,128)S(1)}, u32[]{:S(2)}, u32[]{:S(2)}) collective-permute-start(f32[136,128]{1,0:T(8,128)S(1)} %get-tuple-element.20), channel_id=1, source_target_pairs={{0,2},{1,9},{2,0},{3,11},{4,6},{5,13},{6,4},{7,15},{8,10},{9,1},{1... | collective-permute-start | bytes 208904 | tf_op jit(solution)/shard_map/ppermute | solution.py:51
  29.0 8.1 %collective-permute-start.14 = (f32[1,64,128]{2,1,0:T(8,128)S(1)}, f32[1,64,128]{2,1,0:T(8,128)S(1)}, u32[]{:S(2)}, u32[]{:S(2)}) collective-permute-start(f32[1,64,128]{2,1,0:T(8,128)S(1)} %get-tuple-element.22), channel_id=1, source_target_pairs={{0,8},{4,12},{8,0},{12,4},{1,9},{5,13},{9,1},{13,5},{2,10},{6,14},... | collective-permute-start | bytes 98312 | tf_op jit(solution)/shard_map/ppermute | solution.py:39
  34.2 5.5 %collective-permute-start.12 = (f32[136,128]{1,0:T(8,128)S(1)}, f32[136,128]{1,0:T(8,128)S(1)}, u32[]{:S(2)}, u32[]{:S(2)}) collective-permute-start(f32[136,128]{1,0:T(8,128)S(1)} %add.21), channel_id=1, source_target_pairs={{0,8},{1,5},{2,10},{3,7},{4,12},{5,1},{6,14},{7,3},{8,0},{9,13},{1... | collective-permute-start | bytes 208904 | tf_op jit(solution)/shard_map/ppermute | solution.py:51
  37.1 4.3 %collective-permute-start.15 = (f32[2,64,128]{2,1,0:T(8,128)S(1)}, f32[2,64,128]{2,1,0:T(8,128)S(1)}, u32[]{:S(2)}, u32[]{:S(2)}) collective-permute-start(f32[2,64,128]{2,1,0:T(8,128)S(1)} %pad_maximum_fusion.2), channel_id=1, source_target_pairs={{0,4},{4,0},{8,12},{12,8},{1,5},{5,1},{9,13},{13,9},{2,6},{6,2},{1... | collective-permute-start | bytes 196616 | tf_op jit(solution)/shard_map/ppermute | solution.py:39
  39.7 4.4 %collective-permute-start.13 = (f32[136,128]{1,0:T(8,128)S(1)}, f32[136,128]{1,0:T(8,128)S(1)}, u32[]{:S(2)}, u32[]{:S(2)}) collective-permute-start(f32[136,128]{1,0:T(8,128)S(1)} %add.22), channel_id=1, source_target_pairs={{0,4},{1,3},{2,6},{3,1},{4,0},{5,7},{6,2},{7,5},{8,12},{9,11},{10,... | collective-permute-start | bytes 208904 | tf_op jit(solution)/shard_map/ppermute | solution.py:51
  41.4 5.2 %collective-permute-start.16 = (f32[4,64,128]{2,1,0:T(8,128)S(1)}, f32[4,64,128]{2,1,0:T(8,128)S(1)}, u32[]{:S(2)}, u32[]{:S(2)}) collective-permute-start(f32[4,64,128]{2,1,0:T(8,128)S(1)} %pad_maximum_fusion.1), channel_id=1, source_target_pairs={{0,2},{2,0},{1,3},{3,1},{4,6},{6,4},{5,7},{7,5},{8,10},{10,8},{9,1... | collective-permute-start | bytes 393224 | tf_op jit(solution)/shard_map/ppermute | solution.py:39

commit v12 on v11

--- a/solution.py
+++ b/solution.py
@@ -69,6 +69,23 @@
         c.wait()
 
 
+def slice_kernel(w_in, w_out, first, second, opposite, sem):
+    q = lax.axis_index(PLANE)
+    rin = w_in.shape[0]
+    half = first.shape[1]
+    copies = []
+    for dst, start in ((first, 2 * q * half), (second, (2 * q + 1) * half),
+                       (opposite, 2 * (q ^ 3) * half)):
+        cols = pl.ds(pl.multiple_of(start, half), dst.shape[1])
+        for src, rows in ((w_in, pl.ds(0, rin)), (w_out, pl.ds(rin, w_out.shape[0]))):
+            copies.append(pltpu.make_async_copy(
+                src.at[:, cols], dst.at[rows, :], sem.at[len(copies)]))
+    for c in copies:
+        c.start()
+    for c in copies:
+        c.wait()
+
+
 def stack_kernel(n, *refs):
     at = 0
     for src in refs[:n]:
@@ -88,18 +105,17 @@
     )
 
 
-def store_products(x_parts, g_parts, acc_ref, out_ref):
+def store_products(xs, gs, acc_ref, out_ref):
     tokens = out_ref.shape[0] // 3
-    ko = g_parts[0].shape[1]
-    for n in range(2):
-        rows = slice(n * tokens, (n + 1) * tokens)
-        prior = 0.0 if acc_ref is None else acc_ref[rows, :]
-        out_ref[rows, :] = prior + x_parts[n]
-    rows = slice(2 * tokens, 3 * tokens)
-    for n in range(2):
-        cols = slice(n * ko, (n + 1) * ko)
-        prior = 0.0 if acc_ref is None else acc_ref[rows, cols]
-        out_ref[rows, cols] = prior + g_parts[n]
+    sides = jnp.concatenate([gs[:tokens], gs[tokens:]], axis=1)
+    prior = 0.0 if acc_ref is None else acc_ref[: 2 * tokens, :]
+    out_ref[: 2 * tokens, :] = prior + xs
+    prior = 0.0 if acc_ref is None else acc_ref[2 * tokens :, :]
+    out_ref[2 * tokens :, :] = prior + sides
+
+
+def both(train, test, cols):
+    return jnp.concatenate([train[:, cols], test[:, cols]], axis=0)
 
 
 def nt(a, b):
@@ -108,8 +124,9 @@
 
 def project_kernel(*refs):
     x_refs, (w_in, w_out, out_ref) = refs[:4], refs[4:]
-    xs = [nt(x_refs[n][...], w_in[...]) for n in (0, 2)]
-    gs = [nt(x_refs[n][...], w_out[...]) for n in (1, 3)]
+    every = slice(None)
+    xs = nt(both(x_refs[0], x_refs[2], every), w_in[...])
+    gs = nt(both(x_refs[1], x_refs[3], every), w_out[...])
     store_products(xs, gs, None, out_ref)
 
 
@@ -123,7 +140,7 @@
     core = lax.axis_index("mp")
     rin, rout = own_in.shape[0], own_out.shape[0]
     quarter = own_in.shape[1] // 4
-    xs, gs = [0.0, 0.0], [0.0, 0.0]
+    xs, gs = 0.0, 0.0
     at = 0
     for dq, col, width, rows in plan:
         other = q ^ (core * (3 ^ dq) + (1 - core) * dq) if dq in (1, 2) else q ^ dq
@@ -138,9 +155,8 @@
             dst_out = pl.multiple_of((z ^ k) * rout, rout)
             w_in[pl.ds(dst_in, rin), here] = pieces[p][row : row + rin, :]
             w_out[pl.ds(dst_out, rout), here] = pieces[p][row + rin : row + rin + rout, :]
-        for m in range(2):
-            xs[m] += nt(x_refs[2 * m][:, cols], w_in[:, here])
-            gs[m] += nt(x_refs[2 * m + 1][:, cols], w_out[:, here])
+        xs += nt(both(x_refs[0], x_refs[2], cols), w_in[:, here])
+        gs += nt(both(x_refs[1], x_refs[3], cols), w_out[:, here])
     store_products(xs, gs, acc_ref, out_ref)
 
 
@@ -284,10 +300,16 @@
 
     part = width // 8
     shard = rin + rout
-    q = lax.axis_index(PLANE)
-    whole = jnp.concatenate([w_in, w_out], axis=0)
-    mine = lax.dynamic_slice(whole, (0, q * 2 * part), (shard, 2 * part))
-    opposite = lax.dynamic_slice(whole, (0, (q ^ 3) * 2 * part), (shard, 2 * part))
+    in_hbm = [pltpu.with_memory_space_constraint(w, pltpu.HBM) for w in (w_in, w_out)]
+    *halves, opposite = call(
+        slice_kernel,
+        tuple(
+            pltpu.VMEM((shard, n), jnp.bfloat16) for n in (part, part, 2 * part)),
+        [pl.BlockSpec(memory_space=pltpu.HBM)] * 2,
+        in_hbm,
+        limit=1,
+        scratch_shapes=[pltpu.SemaphoreType.DMA((6,))],
+    )
     operands = (*xs, w_in, w_out)
     *xs, w_in, w_out = call(
         functools.partial(load_kernel, 6),
@@ -297,7 +319,6 @@
         flops=1 << 30,
         scratch_shapes=[pltpu.SemaphoreType.DMA((12,))],
     )
-    halves = [mine[:, :part], mine[:, part:]]
     far = [swap(h, "dp", n_dp, 2) for h in halves]
     far_op = swap(opposite, "dp", n_dp, 2)
     both_a = stack((halves[0], far[0]), w_out)

time: 47.4 us -> 47.5 us (level)
  Pallas kernels: 7.84 us -> 8.78 us
  other arithmetic: 0.95 us -> 0.07 us
    pallas_call x12 -> x13, Pallas kernels: 7.84 us -> 8.78 us  [call(): pl.pallas_call(kernel, out_shape=out_shape, in_specs=in_specs, out_specs=...]
    concatenate x1 -> x0, other arithmetic: 0.89 us -> none  [project(): whole = jnp.concatenate([w_in, w_out], axis=0)]
  transfers between devices with their start and end apart: 17 -> 17, of which waited for: 8 -> 8; matrix products, arithmetic and copies ran while one was open for 0% -> 0% of each run, Pallas kernels for 13% -> 12%
where the time goes in v12:
time: 47.5 us; the launch traced here: 47.3 us
  starting transfers between devices  27.9 us (59%)
  waiting for transfers between devices  9.14 us (19%)
  Pallas kernels  8.78 us (18%)
  between operations  1.42 us (3%)
    ppermute x10, starting transfers between devices, swap(): return lax.ppermute(x, axis, [(i, i ^ k) for i in range(count)])  18.2 us
    ppermute x7, starting transfers between devices, mixed(): return lax.ppermute(x, (*axes, 'mp'), pairs)  9.68 us
    pallas_call x13, Pallas kernels, call(): pl.pallas_call(kernel, out_shape=out_shape, in_specs=in_specs, out_specs=...  8.78 us
    ppermute x7, waiting for transfers between devices, mixed(): return lax.ppermute(x, (*axes, 'mp'), pairs)  6.18 us
    ppermute x10, waiting for transfers between devices, swap(): return lax.ppermute(x, axis, [(i, i ^ k) for i in range(count)])  2.96 us
  transfers between devices with their start and end apart: 17, of which 8 were waited for; matrix products, arithmetic and copies ran while one was open for 0% of the time, Pallas kernels for 12%

profile of v12, /device:TPU:0, one launch (start us, length us, event | category | flops | bytes accessed | tf_op | source)
XLA Modules:
  0.0 47.3 jit_solution(89159851013663687)
XLA Ops:
  0.0 1.0 %shard_map.83 = (bf16[48,512]{1,0:T(8,128)(2,1)S(1)}, bf16[48,512]{1,0:T(8,128)(2,1)S(1)}, bf16[48,1024]{1,0:T(8,128)(2,1)S(1)}) custom-call(bf16[32,4096]{1,0:T(8,128)(2,1)} %bitcast.6, bf16[16,4096]{1,0:T(8,128)(2,1)} %bitcast.12), custom_call_target="tpu_custom_call" | custom-call | bytes 65536 | tf_op jit(solution)/shard_map/pallas_call | solution.py:27
  1.0 4.1 %collective-permute-start.6 = (bf16[48,512]{1,0:T(8,128)(2,1)S(1)}, bf16[48,512]{1,0:T(8,128)(2,1)S(1)}, u32[]{:S(2)}, u32[]{:S(2)}) collective-permute-start(bf16[48,512]{1,0:T(8,128)(2,1)S(1)} %get-tuple-element.25.refs_0_), channel_id=1, source_target_pairs={{0,8},{4,12},{8,0},{12,4},{1,9},{5,13},{9,1},{13,5},{2,10},{6,14},... | collective-permute-start | bytes 147464 | tf_op jit(solution)/shard_map/ppermute | solution.py:39
  5.1 0.1 collective-permute-start
  5.2 2.3 %shard_map.82 = (bf16[128,4096]{1,0:T(8,128)(2,1)S(1)}, bf16[128,4096]{1,0:T(8,128)(2,1)S(1)}, bf16[128,4096]{1,0:T(8,128)(2,1)S(1)}, bf16[128,4096]{1,0:T(8,128...) custom-call(bf16[128,4096]{1,0:T(8,128)(2,1)} %bitcast.8, bf16[128,4096]{1,0:T(8,128)(2,1)} %bitcast.9, ...), custom_call_target="tpu_custom_call" | custom-call | flops 1073741824 | bytes 65536 | tf_op jit(solution)/shard_map/pallas_call | solution.py:27
  7.5 0.2 collective-permute-done.6.refs_1_.refs_0_
  7.7 2.1 %collective-permute-start.7 = (bf16[96,512]{1,0:T(8,128)(2,1)S(1)}, bf16[96,512]{1,0:T(8,128)(2,1)S(1)}, u32[]{:S(2)}, u32[]{:S(2)}) collective-permute-start(bf16[96,512]{1,0:T(8,128)(2,1)S(1)} %shard_map.87), channel_id=1, source_target_pairs={{0,4},{4,0},{8,12},{12,8},{1,5},{5,1},{9,13},{13,9},{2,6},{6,2},{1... | collective-permute-start | bytes 294920 | tf_op jit(solution)/shard_map/ppermute | solution.py:39
  9.7 3.4 %collective-permute-start.4 = (bf16[48,1024]{1,0:T(8,128)(2,1)S(1)}, bf16[48,1024]{1,0:T(8,128)(2,1)S(1)}, u32[]{:S(2)}, u32[]{:S(2)}) collective-permute-start(bf16[48,1024]{1,0:T(8,128)(2,1)S(1)} %get-tuple-element.24.refs_0_), channel_id=1, source_target_pairs={{0,8},{4,12},{8,0},{12,4},{1,9},{5,13},{9,1},{13,5},{2,10},{6,14},... | collective-permute-start | bytes 294920 | tf_op jit(solution)/shard_map/ppermute | solution.py:39
  13.2 0.0 collective-permute-done.refs_1_.refs_0_
  13.2 0.1 collective-permute-start.1
  13.4 0.0 collective-permute-done.7.refs_1_
  13.4 1.6 %collective-permute-start.8 = (bf16[144,512]{1,0:T(8,128)(2,1)S(1)}, bf16[144,512]{1,0:T(8,128)(2,1)S(1)}, u32[]{:S(2)}, u32[]{:S(2)}) collective-permute-start(bf16[144,512]{1,0:T(8,128)(2,1)S(1)} %shard_map.88.refs_6_), channel_id=1, source_target_pairs={{0,2},{1,17},{2,0},{3,19},{16,18},{17,1},{18,16},{19,3},{4,6},{5,2... | collective-permute-start | bytes 442376 | tf_op jit(solution)/shard_map/ppermute | solution.py:51
  14.9 1.5 %collective-permute-start.9 = (bf16[144,512]{1,0:T(8,128)(2,1)S(1)}, bf16[144,512]{1,0:T(8,128)(2,1)S(1)}, u32[]{:S(2)}, u32[]{:S(2)}) collective-permute-start(bf16[144,512]{1,0:T(8,128)(2,1)S(1)} %shard_map.88.refs_6_), channel_id=1, source_target_pairs={{0,16},{1,3},{2,18},{3,1},{16,0},{17,19},{18,2},{19,17},{4,20},{5,... | collective-permute-start | bytes 442376 | tf_op jit(solution)/shard_map/ppermute | solution.py:51
  16.4 1.0 %collective-permute-done.4.refs_1_.refs_8_ = bf16[48,1024]{1,0:T(8,128)(2,1)S(1)} collective-permute-done((bf16[48,1024]{1,0:T(8,128)(2,1)S(1)}, bf16[48,1024]{1,0:T(8,128)(2,1)S(1)}, u32[]{:S(2)}, u32[]{:S(2)}) %collective-permute-start.4) | collective-permute-done | bytes 98336 | tf_op jit(solution)/shard_map/ppermute | solution.py:39
  17.5 1.5 %collective-permute-start.5 = (bf16[96,1024]{1,0:T(8,128)(2,1)S(1)}, bf16[96,1024]{1,0:T(8,128)(2,1)S(1)}, u32[]{:S(2)}, u32[]{:S(2)}) collective-permute-start(bf16[96,1024]{1,0:T(8,128)(2,1)S(1)} %shard_map.86), channel_id=1, source_target_pairs={{0,4},{4,0},{8,12},{12,8},{1,5},{5,1},{9,13},{13,9},{2,6},{6,2},{1... | collective-permute-start | bytes 589832 | tf_op jit(solution)/shard_map/ppermute | solution.py:39
  19.0 0.0 collective-permute-done.1.refs_1_
  19.0 1.6 %collective-permute-start.2 = (bf16[144,512]{1,0:T(8,128)(2,1)S(1)}, bf16[144,512]{1,0:T(8,128)(2,1)S(1)}, u32[]{:S(2)}, u32[]{:S(2)}) collective-permute-start(bf16[144,512]{1,0:T(8,128)(2,1)S(1)} %shard_map.85.refs_7_), channel_id=1, source_target_pairs={{0,2},{1,17},{2,0},{3,19},{16,18},{17,1},{18,16},{19,3},{4,6},{5,2... | collective-permute-start | bytes 442376 | tf_op jit(solution)/shard_map/ppermute | solution.py:51
  20.6 1.5 %collective-permute-start.3 = (bf16[144,512]{1,0:T(8,128)(2,1)S(1)}, bf16[144,512]{1,0:T(8,128)(2,1)S(1)}, u32[]{:S(2)}, u32[]{:S(2)}) collective-permute-start(bf16[144,512]{1,0:T(8,128)(2,1)S(1)} %shard_map.85.refs_7_), channel_id=1, source_target_pairs={{0,16},{1,3},{2,18},{3,1},{16,0},{17,19},{18,2},{19,17},{4,20},{5,... | collective-permute-start | bytes 442376 | tf_op jit(solution)/shard_map/ppermute | solution.py:51
  22.1 0.5 %shard_map.89.refs_8_ = f32[384,128]{1,0:T(8,128)S(1)} custom-call(bf16[128,4096]{1,0:T(8,128)(2,1)S(1)} %get-tuple-element.17.refs_0_, bf16[128,4096]{1,0:T(8,128)(2,1)S(1)} %get-tuple-element.18.refs_1_, bf16[128,4096]{1,0:T(8,128)(2,1)S(1)} %get-tuple-element.19.refs_2_, bf16[128,4096]{1,0:T(8,128)(2,1)S(1)} %get-tuple-element.20.refs_3_, ...), custom_call_target="tpu_custom_call" | custom-call | flops 1073741824 | bytes 65536 | tf_op jit(solution)/shard_map/pallas_call | solution.py:27
  22.6 0.0 collective-permute-done.8.refs_6_
  22.6 0.0 collective-permute-done.9.refs_7_
  22.6 0.5 %shard_map.90.refs_10_ = f32[384,128]{1,0:T(8,128)S(1)} custom-call(bf16[128,4096]{1,0:T(8,128)(2,1)S(1)} %get-tuple-element.17.refs_0_, bf16[128,4096]{1,0:T(8,128)(2,1)S(1)} %get-tuple-element.18.refs_1_, bf16[128,4096]{1,0:T(8,128)(2,1)S(1)} %get-tuple-element.19.refs_2_, bf16[128,4096]{1,0:T(8,128)(2,1)S(1)} %get-tuple-element.20.refs_3_, ...), custom_call_target="tpu_custom_call" | custom-call | flops 1073741824 | bytes 65536 | tf_op jit(solution)/shard_map/pallas_call | solution.py:27
  23.2 1.2 %collective-permute-done.2.refs_6_ = bf16[144,512]{1,0:T(8,128)(2,1)S(1)} collective-permute-done((bf16[144,512]{1,0:T(8,128)(2,1)S(1)}, bf16[144,512]{1,0:T(8,128)(2,1)S(1)}, u32[]{:S(2)}, u32[]{:S(2)}) %collective-permute-start.2) | collective-permute-done | bytes 147488 | tf_op jit(solution)/shard_map/ppermute | solution.py:51
  24.4 1.3 %collective-permute-done.3.refs_7_ = bf16[144,512]{1,0:T(8,128)(2,1)S(1)} collective-permute-done((bf16[144,512]{1,0:T(8,128)(2,1)S(1)}, bf16[144,512]{1,0:T(8,128)(2,1)S(1)}, u32[]{:S(2)}, u32[]{:S(2)}) %collective-permute-start.3) | collective-permute-done | bytes 147488 | tf_op jit(solution)/shard_map/ppermute | solution.py:51
  25.7 0.0 collective-permute-done.5.refs_9_
  25.7 0.8 %shard_map.91.mine = f32[384,128]{1,0:T(8,128)S(1)} custom-call(bf16[128,4096]{1,0:T(8,128)(2,1)S(1)} %get-tuple-element.17.refs_0_, bf16[128,4096]{1,0:T(8,128)(2,1)S(1)} %get-tuple-element.18.refs_1_, bf16[128,4096]{1,0:T(8,128)(2,1)S(1)} %get-tuple-element.19.refs_2_, bf16[128,4096]{1,0:T(8,128)(2,1)S(1)} %get-tuple-element.20.refs_3_, ...), custom_call_target="tpu_custom_call" | custom-call | flops 1073741824 | bytes 65536 | tf_op jit(solution)/shard_map/pallas_call | solution.py:27
  26.5 0.1 collective-permute-start.10
  27.9 0.1 collective-permute-done.10.other
  28.0 0.5 shard_map.92
  28.5 0.6 %collective-permute-start.11 = (f32[136,128]{1,0:T(8,128)S(1)}, f32[136,128]{1,0:T(8,128)S(1)}, u32[]{:S(2)}, u32[]{:S(2)}) collective-permute-start(f32[136,128]{1,0:T(8,128)S(1)} %get-tuple-element.26), channel_id=1, source_target_pairs={{0,2},{1,9},{2,0},{3,11},{4,6},{5,13},{6,4},{7,15},{8,10},{9,1},{1... | collective-permute-start | bytes 208904 | tf_op jit(solution)/shard_map/ppermute | solution.py:51
  29.1 5.2 %collective-permute-start.14 = (f32[1,64,128]{2,1,0:T(8,128)S(1)}, f32[1,64,128]{2,1,0:T(8,128)S(1)}, u32[]{:S(2)}, u32[]{:S(2)}) collective-permute-start(f32[1,64,128]{2,1,0:T(8,128)S(1)} %get-tuple-element.28), channel_id=1, source_target_pairs={{0,8},{4,12},{8,0},{12,4},{1,9},{5,13},{9,1},{13,5},{2,10},{6,14},... | collective-permute-start | bytes 98312 | tf_op jit(solution)/shard_map/ppermute | solution.py:39
  34.2 0.0 collective-permute-done.11
  34.3 2.9 %collective-permute-start.12 = (f32[136,128]{1,0:T(8,128)S(1)}, f32[136,128]{1,0:T(8,128)S(1)}, u32[]{:S(2)}, u32[]{:S(2)}) collective-permute-start(f32[136,128]{1,0:T(8,128)S(1)} %add.9), channel_id=1, source_target_pairs={{0,8},{1,5},{2,10},{3,7},{4,12},{5,1},{6,14},{7,3},{8,0},{9,13},{1... | collective-permute-start | bytes 208904 | tf_op jit(solution)/shard_map/ppermute | solution.py:51
  37.1 0.0 collective-permute-done.14
  37.2 0.1 collective-permute-start.15
  37.2 2.5 %collective-permute-done.12 = f32[136,128]{1,0:T(8,128)S(1)} collective-permute-done((f32[136,128]{1,0:T(8,128)S(1)}, f32[136,128]{1,0:T(8,128)S(1)}, u32[]{:S(2)}, u32[]{:S(2)}) %collective-permute-start.12) | collective-permute-done | bytes 69664 | tf_op jit(solution)/shard_map/ppermute | solution.py:51
  39.8 0.1 collective-permute-start.13
  39.9 1.6 %collective-permute-done.15 = f32[2,64,128]{2,1,0:T(8,128)S(1)} collective-permute-done((f32[2,64,128]{2,1,0:T(8,128)S(1)}, f32[2,64,128]{2,1,0:T(8,128)S(1)}, u32[]{:S(2)}, u32[]{:S(2)}) %collective-permute-start.15) | collective-permute-done | bytes 65568 | tf_op jit(solution)/shard_map/ppermute | solution.py:39
  41.5 1.6 %collective-permute-start.16 = (f32[4,64,128]{2,1,0:T(8,128)S(1)}, f32[4,64,128]{2,1,0:T(8,128)S(1)}, u32[]{:S(2)}, u32[]{:S(2)}) collective-permute-start(f32[4,64,128]{2,1,0:T(8,128)S(1)} %pad_maximum_fusion.1), channel_id=1, source_target_pairs={{0,2},{2,0},{1,3},{3,1},{4,6},{6,4},{5,7},{7,5},{8,10},{10,8},{9,1... | collective-permute-start | bytes 393224 | tf_op jit(solution)/shard_map/ppermute | solution.py:39
  43.1 1.1 %collective-permute-done.13 = f32[136,128]{1,0:T(8,128)S(1)} collective-permute-done((f32[136,128]{1,0:T(8,128)S(1)}, f32[136,128]{1,0:T(8,128)S(1)}, u32[]{:S(2)}, u32[]{:S(2)}) %collective-permute-start.13) | collective-permute-done | bytes 69664 | tf_op jit(solution)/shard_map/ppermute | solution.py:51
  44.2 2.5 %shard_map.93.side_ref = f32[64,128]{1,0:T(8,128)S(1)} custom-call(f32[136,128]{1,0:T(8,128)S(1)} %add.11.fac_ref, f32[128,64]{1,0:T(8,128)S(1)} %get-tuple-element.27.gtr_ref), custom_call_target="tpu_custom_call" | custom-call | flops 4294967296 | bytes 65536 | tf_op jit(solution)/shard_map/pallas_call | solution.py:27
  46.6 0.0 collective-permute-done.16
  46.7 0.6 %shard_map.94 = f32[1,8]{1,0:T(1,128)} custom-call(f32[64,128]{1,0:T(8,128)S(1)} %shard_map.93.side_ref, f32[8,64,128]{2,1,0:T(8,128)S(1)} %pad_maximum_fusion.gte_ref), custom_call_target="tpu_custom_call" | custom-call | bytes 65536 | tf_op jit(solution)/shard_map/pallas_call | solution.py:27
  (11 shorter events, 0.1 us)
Async XLA Ops:
  1.0 6.7 %collective-permute-start.6 = (bf16[48,512]{1,0:T(8,128)(2,1)S(1)}, bf16[48,512]{1,0:T(8,128)(2,1)S(1)}, u32[]{:S(2)}, u32[]{:S(2)}) collective-permute-start(bf16[48,512]{1,0:T(8,128)(2,1)S(1)} %get-tuple-element.25.refs_0_), channel_id=1, source_target_pairs={{0,8},{4,12},{8,0},{12,4},{1,9},{5,13},{9,1},{13,5},{2,10},{6,14},... | collective-permute-start | bytes 147464 | tf_op jit(solution)/shard_map/ppermute | solution.py:39
  5.1 8.1 %collective-permute-start = (bf16[48,512]{1,0:T(8,128)(2,1)S(1)}, bf16[48,512]{1,0:T(8,128)(2,1)S(1)}, u32[]{:S(2)}, u32[]{:S(2)}) collective-permute-start(bf16[48,512]{1,0:T(8,128)(2,1)S(1)} %get-tuple-element.23.refs_0_), channel_id=1, source_target_pairs={{0,8},{4,12},{8,0},{12,4},{1,9},{5,13},{9,1},{13,5},{2,10},{6,14},... | collective-permute-start | bytes 147464 | tf_op jit(solution)/shard_map/ppermute | solution.py:39
  7.7 5.7 %collective-permute-start.7 = (bf16[96,512]{1,0:T(8,128)(2,1)S(1)}, bf16[96,512]{1,0:T(8,128)(2,1)S(1)}, u32[]{:S(2)}, u32[]{:S(2)}) collective-permute-start(bf16[96,512]{1,0:T(8,128)(2,1)S(1)} %shard_map.87), channel_id=1, source_target_pairs={{0,4},{4,0},{8,12},{12,8},{1,5},{5,1},{9,13},{13,9},{2,6},{6,2},{1... | collective-permute-start | bytes 294920 | tf_op jit(solution)/shard_map/ppermute | solution.py:39
  9.7 7.7 %collective-permute-start.4 = (bf16[48,1024]{1,0:T(8,128)(2,1)S(1)}, bf16[48,1024]{1,0:T(8,128)(2,1)S(1)}, u32[]{:S(2)}, u32[]{:S(2)}) collective-permute-start(bf16[48,1024]{1,0:T(8,128)(2,1)S(1)} %get-tuple-element.24.refs_0_), channel_id=1, source_target_pairs={{0,8},{4,12},{8,0},{12,4},{1,9},{5,13},{9,1},{13,5},{2,10},{6,14},... | collective-permute-start | bytes 294920 | tf_op jit(solution)/shard_map/ppermute | solution.py:39
  13.2 5.8 %collective-permute-start.1 = (bf16[96,512]{1,0:T(8,128)(2,1)S(1)}, bf16[96,512]{1,0:T(8,128)(2,1)S(1)}, u32[]{:S(2)}, u32[]{:S(2)}) collective-permute-start(bf16[96,512]{1,0:T(8,128)(2,1)S(1)} %shard_map.84), channel_id=1, source_target_pairs={{0,4},{4,0},{8,12},{12,8},{1,5},{5,1},{9,13},{13,9},{2,6},{6,2},{1... | collective-permute-start | bytes 294920 | tf_op jit(solution)/shard_map/ppermute | solution.py:39
  13.4 9.3 %collective-permute-start.8 = (bf16[144,512]{1,0:T(8,128)(2,1)S(1)}, bf16[144,512]{1,0:T(8,128)(2,1)S(1)}, u32[]{:S(2)}, u32[]{:S(2)}) collective-permute-start(bf16[144,512]{1,0:T(8,128)(2,1)S(1)} %shard_map.88.refs_6_), channel_id=1, source_target_pairs={{0,2},{1,17},{2,0},{3,19},{16,18},{17,1},{18,16},{19,3},{4,6},{5,2... | collective-permute-start | bytes 442376 | tf_op jit(solution)/shard_map/ppermute | solution.py:51
  14.9 7.7 %collective-permute-start.9 = (bf16[144,512]{1,0:T(8,128)(2,1)S(1)}, bf16[144,512]{1,0:T(8,128)(2,1)S(1)}, u32[]{:S(2)}, u32[]{:S(2)}) collective-permute-start(bf16[144,512]{1,0:T(8,128)(2,1)S(1)} %shard_map.88.refs_6_), channel_id=1, source_target_pairs={{0,16},{1,3},{2,18},{3,1},{16,0},{17,19},{18,2},{19,17},{4,20},{5,... | collective-permute-start | bytes 442376 | tf_op jit(solution)/shard_map/ppermute | solution.py:51
  17.5 8.3 %collective-permute-start.5 = (bf16[96,1024]{1,0:T(8,128)(2,1)S(1)}, bf16[96,1024]{1,0:T(8,128)(2,1)S(1)}, u32[]{:S(2)}, u32[]{:S(2)}) collective-permute-start(bf16[96,1024]{1,0:T(8,128)(2,1)S(1)} %shard_map.86), channel_id=1, source_target_pairs={{0,4},{4,0},{8,12},{12,8},{1,5},{5,1},{9,13},{13,9},{2,6},{6,2},{1... | collective-permute-start | bytes 589832 | tf_op jit(solution)/shard_map/ppermute | solution.py:39
  19.0 5.4 %collective-permute-start.2 = (bf16[144,512]{1,0:T(8,128)(2,1)S(1)}, bf16[144,512]{1,0:T(8,128)(2,1)S(1)}, u32[]{:S(2)}, u32[]{:S(2)}) collective-permute-start(bf16[144,512]{1,0:T(8,128)(2,1)S(1)} %shard_map.85.refs_7_), channel_id=1, source_target_pairs={{0,2},{1,17},{2,0},{3,19},{16,18},{17,1},{18,16},{19,3},{4,6},{5,2... | collective-permute-start | bytes 442376 | tf_op jit(solution)/shard_map/ppermute | solution.py:51
  20.6 5.1 %collective-permute-start.3 = (bf16[144,512]{1,0:T(8,128)(2,1)S(1)}, bf16[144,512]{1,0:T(8,128)(2,1)S(1)}, u32[]{:S(2)}, u32[]{:S(2)}) collective-permute-start(bf16[144,512]{1,0:T(8,128)(2,1)S(1)} %shard_map.85.refs_7_), channel_id=1, source_target_pairs={{0,16},{1,3},{2,18},{3,1},{16,0},{17,19},{18,2},{19,17},{4,20},{5,... | collective-permute-start | bytes 442376 | tf_op jit(solution)/shard_map/ppermute | solution.py:51
  26.5 1.5 %collective-permute-start.10 = (f32[384,128]{1,0:T(8,128)S(1)}, f32[384,128]{1,0:T(8,128)S(1)}, u32[]{:S(2)}, u32[]{:S(2)}) collective-permute-start(f32[384,128]{1,0:T(8,128)S(1)} %shard_map.91.mine), channel_id=1, source_target_pairs={{0,1},{1,0},{2,3},{3,2},{4,5},{5,4},{6,7},{7,6},{8,9},{9,8},{10,11... | collective-permute-start | bytes 589832 | tf_op jit(solution)/shard_map/ppermute | solution.py:39
  28.5 5.7 %collective-permute-start.11 = (f32[136,128]{1,0:T(8,128)S(1)}, f32[136,128]{1,0:T(8,128)S(1)}, u32[]{:S(2)}, u32[]{:S(2)}) collective-permute-start(f32[136,128]{1,0:T(8,128)S(1)} %get-tuple-element.26), channel_id=1, source_target_pairs={{0,2},{1,9},{2,0},{3,11},{4,6},{5,13},{6,4},{7,15},{8,10},{9,1},{1... | collective-permute-start | bytes 208904 | tf_op jit(solution)/shard_map/ppermute | solution.py:51
  29.1 8.1 %collective-permute-start.14 = (f32[1,64,128]{2,1,0:T(8,128)S(1)}, f32[1,64,128]{2,1,0:T(8,128)S(1)}, u32[]{:S(2)}, u32[]{:S(2)}) collective-permute-start(f32[1,64,128]{2,1,0:T(8,128)S(1)} %get-tuple-element.28), channel_id=1, source_target_pairs={{0,8},{4,12},{8,0},{12,4},{1,9},{5,13},{9,1},{13,5},{2,10},{6,14},... | collective-permute-start | bytes 98312 | tf_op jit(solution)/shard_map/ppermute | solution.py:39
  34.3 5.5 %collective-permute-start.12 = (f32[136,128]{1,0:T(8,128)S(1)}, f32[136,128]{1,0:T(8,128)S(1)}, u32[]{:S(2)}, u32[]{:S(2)}) collective-permute-start(f32[136,128]{1,0:T(8,128)S(1)} %add.9), channel_id=1, source_target_pairs={{0,8},{1,5},{2,10},{3,7},{4,12},{5,1},{6,14},{7,3},{8,0},{9,13},{1... | collective-permute-start | bytes 208904 | tf_op jit(solution)/shard_map/ppermute | solution.py:51
  37.2 4.3 %collective-permute-start.15 = (f32[2,64,128]{2,1,0:T(8,128)S(1)}, f32[2,64,128]{2,1,0:T(8,128)S(1)}, u32[]{:S(2)}, u32[]{:S(2)}) collective-permute-start(f32[2,64,128]{2,1,0:T(8,128)S(1)} %pad_maximum_fusion.2), channel_id=1, source_target_pairs={{0,4},{4,0},{8,12},{12,8},{1,5},{5,1},{9,13},{13,9},{2,6},{6,2},{1... | collective-permute-start | bytes 196616 | tf_op jit(solution)/shard_map/ppermute | solution.py:39
  39.8 4.4 %collective-permute-start.13 = (f32[136,128]{1,0:T(8,128)S(1)}, f32[136,128]{1,0:T(8,128)S(1)}, u32[]{:S(2)}, u32[]{:S(2)}) collective-permute-start(f32[136,128]{1,0:T(8,128)S(1)} %add.10), channel_id=1, source_target_pairs={{0,4},{1,3},{2,6},{3,1},{4,0},{5,7},{6,2},{7,5},{8,12},{9,11},{10,... | collective-permute-start | bytes 208904 | tf_op jit(solution)/shard_map/ppermute | solution.py:51
  41.5 5.2 %collective-permute-start.16 = (f32[4,64,128]{2,1,0:T(8,128)S(1)}, f32[4,64,128]{2,1,0:T(8,128)S(1)}, u32[]{:S(2)}, u32[]{:S(2)}) collective-permute-start(f32[4,64,128]{2,1,0:T(8,128)S(1)} %pad_maximum_fusion.1), channel_id=1, source_target_pairs={{0,2},{2,0},{1,3},{3,1},{4,6},{6,4},{5,7},{7,5},{8,10},{10,8},{9,1... | collective-permute-start | bytes 393224 | tf_op jit(solution)/shard_map/ppermute | solution.py:39

commit v13 on v11

--- a/solution.py
+++ b/solution.py
@@ -262,14 +262,16 @@
 def scores_kernel(order, n_blk, side_ref, gte_ref, out_ref):
     z = lax.axis_index("dp")
     b = lax.axis_index("blk")
-    lane = lax.broadcasted_iota(jnp.int32, out_ref.shape, 1)
-    row = jnp.zeros(out_ref.shape, jnp.float32)
     side = side_ref[...]
-    sums = [jnp.sum(side * gte_ref[p], axis=0, keepdims=True) for p in range(len(order))]
-    values = jnp.sum(jnp.concatenate(sums, axis=0), axis=1, keepdims=True)
+    peers = gte_ref.shape[0]
+    sums = jnp.sum(side[None] * gte_ref[...], axis=1)
+    values = jnp.sum(sums, axis=1, keepdims=True)
+    where = lax.broadcasted_iota(jnp.int32, (peers, out_ref.shape[1]), 0)
+    lane = lax.broadcasted_iota(jnp.int32, (peers, out_ref.shape[1]), 1)
+    place = jnp.zeros_like(lane)
     for p, (dz, db) in enumerate(order):
-        row = jnp.where(lane == (z ^ dz) * n_blk + (b ^ db), values[p : p + 1, :], row)
-    out_ref[...] = row
+        place = jnp.where(where == p, (z ^ dz) * n_blk + (b ^ db), place)
+    out_ref[...] = jnp.sum(jnp.where(lane == place, values, 0.0), axis=0, keepdims=True)
 
 
 def project(xs, w_in, w_out, n_groups, n_dp, n_blk):
@@ -336,15 +338,10 @@
         ((0, 0, part, stacked(0)), (0, part, part, stacked(1))), (za, zb), None)
     acc = accumulate(
         ((1, 0, part, stacked(0)), (2, 0, part, stacked(1))), (xa, ya), acc)
+    acc = accumulate(
+        ((3, 0, 2 * part, ((0, 0, 2), (1, 0, 1), (1, shard, 3))),), (far_op, near_op), acc)
     return accumulate(
-        (
-            (1, part, part, stacked(0)),
-            (2, part, part, stacked(1)),
-            (3, 0, 2 * part, ((2, 0, 2), (3, 0, 1), (3, shard, 3))),
-        ),
-        (xb, yb, far_op, near_op),
-        acc,
-    )
+        ((1, part, part, stacked(0)), (2, part, part, stacked(1))), (xb, yb), acc)
 
 
 def per_device(

time: 47.4 us -> 47.6 us (level)
  waiting for transfers between devices: 9.14 us -> 8.55 us
  starting transfers between devices: 27.9 us -> 28.4 us
    pallas_call x12 -> x13, Pallas kernels: 7.84 us -> 8.08 us  [call(): pl.pallas_call(kernel, out_shape=out_shape, in_specs=in_specs, out_specs=...]
  transfers between devices with their start and end apart: 17 -> 17, of which waited for: 8 -> 8; matrix products, arithmetic and copies ran while one was open for 0% -> 0% of each run, Pallas kernels for 13% -> 14%
where the time goes in v13:
time: 47.6 us; the launch traced here: 47.4 us
  starting transfers between devices  28.4 us (60%)
  waiting for transfers between devices  8.55 us (18%)
  Pallas kernels  8.08 us (17%)
  between operations  1.42 us (3%)
  other arithmetic  0.95 us (2%)
    ppermute x10, starting transfers between devices, swap(): return lax.ppermute(x, axis, [(i, i ^ k) for i in range(count)])  18.7 us
    ppermute x7, starting transfers between devices, mixed(): return lax.ppermute(x, (*axes, 'mp'), pairs)  9.68 us
    pallas_call x13, Pallas kernels, call(): pl.pallas_call(kernel, out_shape=out_shape, in_specs=in_specs, out_specs=...  8.08 us
    ppermute x7, waiting for transfers between devices, mixed(): return lax.ppermute(x, (*axes, 'mp'), pairs)  6.01 us
    ppermute x10, waiting for transfers between devices, swap(): return lax.ppermute(x, axis, [(i, i ^ k) for i in range(count)])  2.55 us
  transfers between devices with their start and end apart: 17, of which 8 were waited for; matrix products, arithmetic and copies ran while one was open for 0% of the time, Pallas kernels for 14%

profile of v13, /device:TPU:0, one launch (start us, length us, event | category | flops | bytes accessed | tf_op | source)
XLA Modules:
  0.0 47.4 jit_solution(16018576439533086036)
XLA Ops:
  0.0 0.9 %fusion = (bf16[48,1024]{1,0:T(8,128)(2,1)S(1)}, bf16[48,1024]{1,0:T(8,128)(2,1)S(1)}) fusion(s32[]{:T(128)S(6)} %select_n.7, bf16[32,4096]{1,0:T(8,128)(2,1)} %bitcast.6, bf16[16,4096]{1,0:T(8,128)(2,1)} %bitcast.12, s32[]{:T(128)S(6)} %select_n.6), kind=kLoop, calls=%fused_computation.6 | loop fusion | flops 393216 | bytes 589832 | tf_op jit(solution)/shard_map/concatenate | solution.py:290
  0.9 4.1 %collective-permute-start.6 = (bf16[48,512]{1,0:T(8,128)(2,1)S(1)}, bf16[48,512]{1,0:T(8,128)(2,1)S(1)}, u32[]{:S(2)}, u32[]{:S(2)}) collective-permute-start(bf16[48,512]{1,0:T(8,128)(2,1)S(1)} %get-tuple-element.25.refs_0_), channel_id=1, source_target_pairs={{0,8},{4,12},{8,0},{12,4},{1,9},{5,13},{9,1},{13,5},{2,10},{6,14},... | collective-permute-start | bytes 147464 | tf_op jit(solution)/shard_map/ppermute | solution.py:39
  5.0 0.1 collective-permute-start
  5.1 2.3 %shard_map.82 = (bf16[128,4096]{1,0:T(8,128)(2,1)S(1)}, bf16[128,4096]{1,0:T(8,128)(2,1)S(1)}, bf16[128,4096]{1,0:T(8,128)(2,1)S(1)}, bf16[128,4096]{1,0:T(8,128...) custom-call(bf16[128,4096]{1,0:T(8,128)(2,1)} %bitcast.8, bf16[128,4096]{1,0:T(8,128)(2,1)} %bitcast.9, ...), custom_call_target="tpu_custom_call" | custom-call | flops 1073741824 | bytes 65536 | tf_op jit(solution)/shard_map/pallas_call | solution.py:27
  7.4 0.2 collective-permute-done.6.refs_1_.refs_0_
  7.6 2.1 %collective-permute-start.7 = (bf16[96,512]{1,0:T(8,128)(2,1)S(1)}, bf16[96,512]{1,0:T(8,128)(2,1)S(1)}, u32[]{:S(2)}, u32[]{:S(2)}) collective-permute-start(bf16[96,512]{1,0:T(8,128)(2,1)S(1)} %shard_map.86), channel_id=1, source_target_pairs={{0,4},{4,0},{8,12},{12,8},{1,5},{5,1},{9,13},{13,9},{2,6},{6,2},{1... | collective-permute-start | bytes 294920 | tf_op jit(solution)/shard_map/ppermute | solution.py:39
  9.7 3.4 %collective-permute-start.4 = (bf16[48,1024]{1,0:T(8,128)(2,1)S(1)}, bf16[48,1024]{1,0:T(8,128)(2,1)S(1)}, u32[]{:S(2)}, u32[]{:S(2)}) collective-permute-start(bf16[48,1024]{1,0:T(8,128)(2,1)S(1)} %get-tuple-element.23.refs_0_), channel_id=1, source_target_pairs={{0,8},{4,12},{8,0},{12,4},{1,9},{5,13},{9,1},{13,5},{2,10},{6,14},... | collective-permute-start | bytes 294920 | tf_op jit(solution)/shard_map/ppermute | solution.py:39
  13.1 0.0 collective-permute-done.refs_1_.refs_0_
  13.1 0.1 collective-permute-start.1
  13.3 0.0 collective-permute-done.7.refs_1_
  13.3 1.6 %collective-permute-start.8 = (bf16[144,512]{1,0:T(8,128)(2,1)S(1)}, bf16[144,512]{1,0:T(8,128)(2,1)S(1)}, u32[]{:S(2)}, u32[]{:S(2)}) collective-permute-start(bf16[144,512]{1,0:T(8,128)(2,1)S(1)} %shard_map.87.refs_6_), channel_id=1, source_target_pairs={{0,2},{1,17},{2,0},{3,19},{16,18},{17,1},{18,16},{19,3},{4,6},{5,2... | collective-permute-start | bytes 442376 | tf_op jit(solution)/shard_map/ppermute | solution.py:51
  14.9 1.5 %collective-permute-start.9 = (bf16[144,512]{1,0:T(8,128)(2,1)S(1)}, bf16[144,512]{1,0:T(8,128)(2,1)S(1)}, u32[]{:S(2)}, u32[]{:S(2)}) collective-permute-start(bf16[144,512]{1,0:T(8,128)(2,1)S(1)} %shard_map.87.refs_6_), channel_id=1, source_target_pairs={{0,16},{1,3},{2,18},{3,1},{16,0},{17,19},{18,2},{19,17},{4,20},{5,... | collective-permute-start | bytes 442376 | tf_op jit(solution)/shard_map/ppermute | solution.py:51
  16.4 1.0 %collective-permute-done.4.refs_1_.refs_6_ = bf16[48,1024]{1,0:T(8,128)(2,1)S(1)} collective-permute-done((bf16[48,1024]{1,0:T(8,128)(2,1)S(1)}, bf16[48,1024]{1,0:T(8,128)(2,1)S(1)}, u32[]{:S(2)}, u32[]{:S(2)}) %collective-permute-start.4) | collective-permute-done | bytes 98336 | tf_op jit(solution)/shard_map/ppermute | solution.py:39
  17.4 1.5 %collective-permute-start.5 = (bf16[96,1024]{1,0:T(8,128)(2,1)S(1)}, bf16[96,1024]{1,0:T(8,128)(2,1)S(1)}, u32[]{:S(2)}, u32[]{:S(2)}) collective-permute-start(bf16[96,1024]{1,0:T(8,128)(2,1)S(1)} %shard_map.85), channel_id=1, source_target_pairs={{0,4},{4,0},{8,12},{12,8},{1,5},{5,1},{9,13},{13,9},{2,6},{6,2},{1... | collective-permute-start | bytes 589832 | tf_op jit(solution)/shard_map/ppermute | solution.py:39
  18.9 0.0 collective-permute-done.1.refs_1_
  18.9 1.6 %collective-permute-start.2 = (bf16[144,512]{1,0:T(8,128)(2,1)S(1)}, bf16[144,512]{1,0:T(8,128)(2,1)S(1)}, u32[]{:S(2)}, u32[]{:S(2)}) collective-permute-start(bf16[144,512]{1,0:T(8,128)(2,1)S(1)} %shard_map.84.refs_7_), channel_id=1, source_target_pairs={{0,2},{1,17},{2,0},{3,19},{16,18},{17,1},{18,16},{19,3},{4,6},{5,2... | collective-permute-start | bytes 442376 | tf_op jit(solution)/shard_map/ppermute | solution.py:51
  20.5 1.5 %collective-permute-start.3 = (bf16[144,512]{1,0:T(8,128)(2,1)S(1)}, bf16[144,512]{1,0:T(8,128)(2,1)S(1)}, u32[]{:S(2)}, u32[]{:S(2)}) collective-permute-start(bf16[144,512]{1,0:T(8,128)(2,1)S(1)} %shard_map.84.refs_7_), channel_id=1, source_target_pairs={{0,16},{1,3},{2,18},{3,1},{16,0},{17,19},{18,2},{19,17},{4,20},{5,... | collective-permute-start | bytes 442376 | tf_op jit(solution)/shard_map/ppermute | solution.py:51
  22.0 0.5 %shard_map.88.refs_8_ = f32[384,128]{1,0:T(8,128)S(1)} custom-call(bf16[128,4096]{1,0:T(8,128)(2,1)S(1)} %get-tuple-element.14.refs_0_, bf16[128,4096]{1,0:T(8,128)(2,1)S(1)} %get-tuple-element.15.refs_1_, bf16[128,4096]{1,0:T(8,128)(2,1)S(1)} %get-tuple-element.16.refs_2_, bf16[128,4096]{1,0:T(8,128)(2,1)S(1)} %get-tuple-element.17.refs_3_, ...), custom_call_target="tpu_custom_call" | custom-call | flops 1073741824 | bytes 65536 | tf_op jit(solution)/shard_map/pallas_call | solution.py:27
  22.6 0.0 collective-permute-done.8.refs_6_
  22.6 0.0 collective-permute-done.9.refs_7_
  22.6 0.6 %shard_map.89.refs_8_ = f32[384,128]{1,0:T(8,128)S(1)} custom-call(bf16[128,4096]{1,0:T(8,128)(2,1)S(1)} %get-tuple-element.14.refs_0_, bf16[128,4096]{1,0:T(8,128)(2,1)S(1)} %get-tuple-element.15.refs_1_, bf16[128,4096]{1,0:T(8,128)(2,1)S(1)} %get-tuple-element.16.refs_2_, bf16[128,4096]{1,0:T(8,128)(2,1)S(1)} %get-tuple-element.17.refs_3_, ...), custom_call_target="tpu_custom_call" | custom-call | flops 1073741824 | bytes 65536 | tf_op jit(solution)/shard_map/pallas_call | solution.py:27
  23.1 0.0 collective-permute-done.5.refs_7_
  23.1 0.5 %shard_map.90.refs_8_ = f32[384,128]{1,0:T(8,128)S(1)} custom-call(bf16[128,4096]{1,0:T(8,128)(2,1)S(1)} %get-tuple-element.14.refs_0_, bf16[128,4096]{1,0:T(8,128)(2,1)S(1)} %get-tuple-element.15.refs_1_, bf16[128,4096]{1,0:T(8,128)(2,1)S(1)} %get-tuple-element.16.refs_2_, bf16[128,4096]{1,0:T(8,128)(2,1)S(1)} %get-tuple-element.17.refs_3_, ...), custom_call_target="tpu_custom_call" | custom-call | flops 1073741824 | bytes 65536 | tf_op jit(solution)/shard_map/pallas_call | solution.py:27
  23.7 0.7 %collective-permute-done.2.refs_6_ = bf16[144,512]{1,0:T(8,128)(2,1)S(1)} collective-permute-done((bf16[144,512]{1,0:T(8,128)(2,1)S(1)}, bf16[144,512]{1,0:T(8,128)(2,1)S(1)}, u32[]{:S(2)}, u32[]{:S(2)}) %collective-permute-start.2) | collective-permute-done | bytes 147488 | tf_op jit(solution)/shard_map/ppermute | solution.py:51
  24.4 1.3 %collective-permute-done.3.refs_7_ = bf16[144,512]{1,0:T(8,128)(2,1)S(1)} collective-permute-done((bf16[144,512]{1,0:T(8,128)(2,1)S(1)}, bf16[144,512]{1,0:T(8,128)(2,1)S(1)}, u32[]{:S(2)}, u32[]{:S(2)}) %collective-permute-start.3) | collective-permute-done | bytes 147488 | tf_op jit(solution)/shard_map/ppermute | solution.py:51
  25.7 0.5 %shard_map.91.mine = f32[384,128]{1,0:T(8,128)S(1)} custom-call(bf16[128,4096]{1,0:T(8,128)(2,1)S(1)} %get-tuple-element.14.refs_0_, bf16[128,4096]{1,0:T(8,128)(2,1)S(1)} %get-tuple-element.15.refs_1_, bf16[128,4096]{1,0:T(8,128)(2,1)S(1)} %get-tuple-element.16.refs_2_, bf16[128,4096]{1,0:T(8,128)(2,1)S(1)} %get-tuple-element.17.refs_3_, ...), custom_call_target="tpu_custom_call" | custom-call | flops 1073741824 | bytes 65536 | tf_op jit(solution)/shard_map/pallas_call | solution.py:27
  26.2 0.1 collective-permute-start.10
  27.6 0.1 collective-permute-done.10.other
  27.7 0.5 shard_map.92
  28.2 0.6 %collective-permute-start.11 = (f32[136,128]{1,0:T(8,128)S(1)}, f32[136,128]{1,0:T(8,128)S(1)}, u32[]{:S(2)}, u32[]{:S(2)}) collective-permute-start(f32[136,128]{1,0:T(8,128)S(1)} %get-tuple-element.20), channel_id=1, source_target_pairs={{0,2},{1,9},{2,0},{3,11},{4,6},{5,13},{6,4},{7,15},{8,10},{9,1},{1... | collective-permute-start | bytes 208904 | tf_op jit(solution)/shard_map/ppermute | solution.py:51
  28.7 5.2 %collective-permute-start.14 = (f32[1,64,128]{2,1,0:T(8,128)S(1)}, f32[1,64,128]{2,1,0:T(8,128)S(1)}, u32[]{:S(2)}, u32[]{:S(2)}) collective-permute-start(f32[1,64,128]{2,1,0:T(8,128)S(1)} %get-tuple-element.22), channel_id=1, source_target_pairs={{0,8},{4,12},{8,0},{12,4},{1,9},{5,13},{9,1},{13,5},{2,10},{6,14},... | collective-permute-start | bytes 98312 | tf_op jit(solution)/shard_map/ppermute | solution.py:39
  33.9 0.0 collective-permute-done.11
  33.9 2.9 %collective-permute-start.12 = (f32[136,128]{1,0:T(8,128)S(1)}, f32[136,128]{1,0:T(8,128)S(1)}, u32[]{:S(2)}, u32[]{:S(2)}) collective-permute-start(f32[136,128]{1,0:T(8,128)S(1)} %add.21), channel_id=1, source_target_pairs={{0,8},{1,5},{2,10},{3,7},{4,12},{5,1},{6,14},{7,3},{8,0},{9,13},{1... | collective-permute-start | bytes 208904 | tf_op jit(solution)/shard_map/ppermute | solution.py:51
  36.8 0.0 collective-permute-done.14
  36.8 0.5 %collective-permute-start.15 = (f32[2,64,128]{2,1,0:T(8,128)S(1)}, f32[2,64,128]{2,1,0:T(8,128)S(1)}, u32[]{:S(2)}, u32[]{:S(2)}) collective-permute-start(f32[2,64,128]{2,1,0:T(8,128)S(1)} %pad_maximum_fusion.2), channel_id=1, source_target_pairs={{0,4},{4,0},{8,12},{12,8},{1,5},{5,1},{9,13},{13,9},{2,6},{6,2},{1... | collective-permute-start | bytes 196616 | tf_op jit(solution)/shard_map/ppermute | solution.py:39
  37.3 2.5 %collective-permute-done.12 = f32[136,128]{1,0:T(8,128)S(1)} collective-permute-done((f32[136,128]{1,0:T(8,128)S(1)}, f32[136,128]{1,0:T(8,128)S(1)}, u32[]{:S(2)}, u32[]{:S(2)}) %collective-permute-start.12) | collective-permute-done | bytes 69664 | tf_op jit(solution)/shard_map/ppermute | solution.py:51
  39.9 0.1 collective-permute-start.13
  39.9 1.2 %collective-permute-done.15 = f32[2,64,128]{2,1,0:T(8,128)S(1)} collective-permute-done((f32[2,64,128]{2,1,0:T(8,128)S(1)}, f32[2,64,128]{2,1,0:T(8,128)S(1)}, u32[]{:S(2)}, u32[]{:S(2)}) %collective-permute-start.15) | collective-permute-done | bytes 65568 | tf_op jit(solution)/shard_map/ppermute | solution.py:39
  41.1 1.6 %collective-permute-start.16 = (f32[4,64,128]{2,1,0:T(8,128)S(1)}, f32[4,64,128]{2,1,0:T(8,128)S(1)}, u32[]{:S(2)}, u32[]{:S(2)}) collective-permute-start(f32[4,64,128]{2,1,0:T(8,128)S(1)} %pad_maximum_fusion.1), channel_id=1, source_target_pairs={{0,2},{2,0},{1,3},{3,1},{4,6},{6,4},{5,7},{7,5},{8,10},{10,8},{9,1... | collective-permute-start | bytes 393224 | tf_op jit(solution)/shard_map/ppermute | solution.py:39
  42.7 1.5 %collective-permute-done.13 = f32[136,128]{1,0:T(8,128)S(1)} collective-permute-done((f32[136,128]{1,0:T(8,128)S(1)}, f32[136,128]{1,0:T(8,128)S(1)}, u32[]{:S(2)}, u32[]{:S(2)}) %collective-permute-start.13) | collective-permute-done | bytes 69664 | tf_op jit(solution)/shard_map/ppermute | solution.py:51
  44.2 2.5 %shard_map.93.side_ref = f32[64,128]{1,0:T(8,128)S(1)} custom-call(f32[136,128]{1,0:T(8,128)S(1)} %add.23.fac_ref, f32[128,64]{1,0:T(8,128)S(1)} %get-tuple-element.21.gtr_ref), custom_call_target="tpu_custom_call" | custom-call | flops 4294967296 | bytes 65536 | tf_op jit(solution)/shard_map/pallas_call | solution.py:27
  46.7 0.0 collective-permute-done.16
  46.8 0.6 %shard_map.94 = f32[1,8]{1,0:T(1,128)} custom-call(f32[64,128]{1,0:T(8,128)S(1)} %shard_map.93.side_ref, f32[8,64,128]{2,1,0:T(8,128)S(1)} %pad_maximum_fusion.gte_ref), custom_call_target="tpu_custom_call" | custom-call | bytes 65536 | tf_op jit(solution)/shard_map/pallas_call | solution.py:27
  (12 shorter events, 0.1 us)
Async XLA Ops:
  0.9 6.7 %collective-permute-start.6 = (bf16[48,512]{1,0:T(8,128)(2,1)S(1)}, bf16[48,512]{1,0:T(8,128)(2,1)S(1)}, u32[]{:S(2)}, u32[]{:S(2)}) collective-permute-start(bf16[48,512]{1,0:T(8,128)(2,1)S(1)} %get-tuple-element.25.refs_0_), channel_id=1, source_target_pairs={{0,8},{4,12},{8,0},{12,4},{1,9},{5,13},{9,1},{13,5},{2,10},{6,14},... | collective-permute-start | bytes 147464 | tf_op jit(solution)/shard_map/ppermute | solution.py:39
  5.0 8.1 %collective-permute-start = (bf16[48,512]{1,0:T(8,128)(2,1)S(1)}, bf16[48,512]{1,0:T(8,128)(2,1)S(1)}, u32[]{:S(2)}, u32[]{:S(2)}) collective-permute-start(bf16[48,512]{1,0:T(8,128)(2,1)S(1)} %get-tuple-element.26.refs_0_), channel_id=1, source_target_pairs={{0,8},{4,12},{8,0},{12,4},{1,9},{5,13},{9,1},{13,5},{2,10},{6,14},... | collective-permute-start | bytes 147464 | tf_op jit(solution)/shard_map/ppermute | solution.py:39
  7.6 5.7 %collective-permute-start.7 = (bf16[96,512]{1,0:T(8,128)(2,1)S(1)}, bf16[96,512]{1,0:T(8,128)(2,1)S(1)}, u32[]{:S(2)}, u32[]{:S(2)}) collective-permute-start(bf16[96,512]{1,0:T(8,128)(2,1)S(1)} %shard_map.86), channel_id=1, source_target_pairs={{0,4},{4,0},{8,12},{12,8},{1,5},{5,1},{9,13},{13,9},{2,6},{6,2},{1... | collective-permute-start | bytes 294920 | tf_op jit(solution)/shard_map/ppermute | solution.py:39
  9.7 7.7 %collective-permute-start.4 = (bf16[48,1024]{1,0:T(8,128)(2,1)S(1)}, bf16[48,1024]{1,0:T(8,128)(2,1)S(1)}, u32[]{:S(2)}, u32[]{:S(2)}) collective-permute-start(bf16[48,1024]{1,0:T(8,128)(2,1)S(1)} %get-tuple-element.23.refs_0_), channel_id=1, source_target_pairs={{0,8},{4,12},{8,0},{12,4},{1,9},{5,13},{9,1},{13,5},{2,10},{6,14},... | collective-permute-start | bytes 294920 | tf_op jit(solution)/shard_map/ppermute | solution.py:39
  13.1 5.8 %collective-permute-start.1 = (bf16[96,512]{1,0:T(8,128)(2,1)S(1)}, bf16[96,512]{1,0:T(8,128)(2,1)S(1)}, u32[]{:S(2)}, u32[]{:S(2)}) collective-permute-start(bf16[96,512]{1,0:T(8,128)(2,1)S(1)} %shard_map.83), channel_id=1, source_target_pairs={{0,4},{4,0},{8,12},{12,8},{1,5},{5,1},{9,13},{13,9},{2,6},{6,2},{1... | collective-permute-start | bytes 294920 | tf_op jit(solution)/shard_map/ppermute | solution.py:39
  13.3 9.3 %collective-permute-start.8 = (bf16[144,512]{1,0:T(8,128)(2,1)S(1)}, bf16[144,512]{1,0:T(8,128)(2,1)S(1)}, u32[]{:S(2)}, u32[]{:S(2)}) collective-permute-start(bf16[144,512]{1,0:T(8,128)(2,1)S(1)} %shard_map.87.refs_6_), channel_id=1, source_target_pairs={{0,2},{1,17},{2,0},{3,19},{16,18},{17,1},{18,16},{19,3},{4,6},{5,2... | collective-permute-start | bytes 442376 | tf_op jit(solution)/shard_map/ppermute | solution.py:51
  14.9 7.7 %collective-permute-start.9 = (bf16[144,512]{1,0:T(8,128)(2,1)S(1)}, bf16[144,512]{1,0:T(8,128)(2,1)S(1)}, u32[]{:S(2)}, u32[]{:S(2)}) collective-permute-start(bf16[144,512]{1,0:T(8,128)(2,1)S(1)} %shard_map.87.refs_6_), channel_id=1, source_target_pairs={{0,16},{1,3},{2,18},{3,1},{16,0},{17,19},{18,2},{19,17},{4,20},{5,... | collective-permute-start | bytes 442376 | tf_op jit(solution)/shard_map/ppermute | solution.py:51
  17.4 5.7 %collective-permute-start.5 = (bf16[96,1024]{1,0:T(8,128)(2,1)S(1)}, bf16[96,1024]{1,0:T(8,128)(2,1)S(1)}, u32[]{:S(2)}, u32[]{:S(2)}) collective-permute-start(bf16[96,1024]{1,0:T(8,128)(2,1)S(1)} %shard_map.85), channel_id=1, source_target_pairs={{0,4},{4,0},{8,12},{12,8},{1,5},{5,1},{9,13},{13,9},{2,6},{6,2},{1... | collective-permute-start | bytes 589832 | tf_op jit(solution)/shard_map/ppermute | solution.py:39
  18.9 5.4 %collective-permute-start.2 = (bf16[144,512]{1,0:T(8,128)(2,1)S(1)}, bf16[144,512]{1,0:T(8,128)(2,1)S(1)}, u32[]{:S(2)}, u32[]{:S(2)}) collective-permute-start(bf16[144,512]{1,0:T(8,128)(2,1)S(1)} %shard_map.84.refs_7_), channel_id=1, source_target_pairs={{0,2},{1,17},{2,0},{3,19},{16,18},{17,1},{18,16},{19,3},{4,6},{5,2... | collective-permute-start | bytes 442376 | tf_op jit(solution)/shard_map/ppermute | solution.py:51
  20.5 5.1 %collective-permute-start.3 = (bf16[144,512]{1,0:T(8,128)(2,1)S(1)}, bf16[144,512]{1,0:T(8,128)(2,1)S(1)}, u32[]{:S(2)}, u32[]{:S(2)}) collective-permute-start(bf16[144,512]{1,0:T(8,128)(2,1)S(1)} %shard_map.84.refs_7_), channel_id=1, source_target_pairs={{0,16},{1,3},{2,18},{3,1},{16,0},{17,19},{18,2},{19,17},{4,20},{5,... | collective-permute-start | bytes 442376 | tf_op jit(solution)/shard_map/ppermute | solution.py:51
  26.2 1.5 %collective-permute-start.10 = (f32[384,128]{1,0:T(8,128)S(1)}, f32[384,128]{1,0:T(8,128)S(1)}, u32[]{:S(2)}, u32[]{:S(2)}) collective-permute-start(f32[384,128]{1,0:T(8,128)S(1)} %shard_map.91.mine), channel_id=1, source_target_pairs={{0,1},{1,0},{2,3},{3,2},{4,5},{5,4},{6,7},{7,6},{8,9},{9,8},{10,11... | collective-permute-start | bytes 589832 | tf_op jit(solution)/shard_map/ppermute | solution.py:39
  28.2 5.7 %collective-permute-start.11 = (f32[136,128]{1,0:T(8,128)S(1)}, f32[136,128]{1,0:T(8,128)S(1)}, u32[]{:S(2)}, u32[]{:S(2)}) collective-permute-start(f32[136,128]{1,0:T(8,128)S(1)} %get-tuple-element.20), channel_id=1, source_target_pairs={{0,2},{1,9},{2,0},{3,11},{4,6},{5,13},{6,4},{7,15},{8,10},{9,1},{1... | collective-permute-start | bytes 208904 | tf_op jit(solution)/shard_map/ppermute | solution.py:51
  28.7 8.1 %collective-permute-start.14 = (f32[1,64,128]{2,1,0:T(8,128)S(1)}, f32[1,64,128]{2,1,0:T(8,128)S(1)}, u32[]{:S(2)}, u32[]{:S(2)}) collective-permute-start(f32[1,64,128]{2,1,0:T(8,128)S(1)} %get-tuple-element.22), channel_id=1, source_target_pairs={{0,8},{4,12},{8,0},{12,4},{1,9},{5,13},{9,1},{13,5},{2,10},{6,14},... | collective-permute-start | bytes 98312 | tf_op jit(solution)/shard_map/ppermute | solution.py:39
  33.9 5.9 %collective-permute-start.12 = (f32[136,128]{1,0:T(8,128)S(1)}, f32[136,128]{1,0:T(8,128)S(1)}, u32[]{:S(2)}, u32[]{:S(2)}) collective-permute-start(f32[136,128]{1,0:T(8,128)S(1)} %add.21), channel_id=1, source_target_pairs={{0,8},{1,5},{2,10},{3,7},{4,12},{5,1},{6,14},{7,3},{8,0},{9,13},{1... | collective-permute-start | bytes 208904 | tf_op jit(solution)/shard_map/ppermute | solution.py:51
  36.8 4.3 %collective-permute-start.15 = (f32[2,64,128]{2,1,0:T(8,128)S(1)}, f32[2,64,128]{2,1,0:T(8,128)S(1)}, u32[]{:S(2)}, u32[]{:S(2)}) collective-permute-start(f32[2,64,128]{2,1,0:T(8,128)S(1)} %pad_maximum_fusion.2), channel_id=1, source_target_pairs={{0,4},{4,0},{8,12},{12,8},{1,5},{5,1},{9,13},{13,9},{2,6},{6,2},{1... | collective-permute-start | bytes 196616 | tf_op jit(solution)/shard_map/ppermute | solution.py:39
  39.9 4.4 %collective-permute-start.13 = (f32[136,128]{1,0:T(8,128)S(1)}, f32[136,128]{1,0:T(8,128)S(1)}, u32[]{:S(2)}, u32[]{:S(2)}) collective-permute-start(f32[136,128]{1,0:T(8,128)S(1)} %add.22), channel_id=1, source_target_pairs={{0,4},{1,3},{2,6},{3,1},{4,0},{5,7},{6,2},{7,5},{8,12},{9,11},{10,... | collective-permute-start | bytes 208904 | tf_op jit(solution)/shard_map/ppermute | solution.py:51
  41.1 5.6 %collective-permute-start.16 = (f32[4,64,128]{2,1,0:T(8,128)S(1)}, f32[4,64,128]{2,1,0:T(8,128)S(1)}, u32[]{:S(2)}, u32[]{:S(2)}) collective-permute-start(f32[4,64,128]{2,1,0:T(8,128)S(1)} %pad_maximum_fusion.1), channel_id=1, source_target_pairs={{0,2},{2,0},{1,3},{3,1},{4,6},{6,4},{5,7},{7,5},{8,10},{10,8},{9,1... | collective-permute-start | bytes 393224 | tf_op jit(solution)/shard_map/ppermute | solution.py:39

commit v14 on v11

--- a/solution.py
+++ b/solution.py
@@ -322,7 +322,7 @@
             out_shape,
             [vmem()] * len(args),
             args,
-            flops=1 << 30,
+            flops=1 << 28,
             scratch_shapes=[
                 pltpu.VMEM((ki, total), jnp.bfloat16),
                 pltpu.VMEM((ko, total), jnp.bfloat16),

time: 47.4 us -> 46.9 us (0.989)
  starting transfers between devices: 27.9 us -> 25.5 us
  waiting for transfers between devices: 9.14 us -> 11 us
    ppermute x10, starting transfers between devices: 18.2 us -> 15.2 us  [swap(): return lax.ppermute(x, axis, [(i, i ^ k) for i in range(count)])]
    ppermute x10, waiting for transfers between devices: 2.97 us -> 4.27 us  [swap(): return lax.ppermute(x, axis, [(i, i ^ k) for i in range(count)])]
    ppermute x7, starting transfers between devices: 9.68 us -> 10.2 us  [mixed(): return lax.ppermute(x, (*axes, 'mp'), pairs)]
    ppermute x7, waiting for transfers between devices: 6.17 us -> 6.72 us  [mixed(): return lax.ppermute(x, (*axes, 'mp'), pairs)]
  transfers between devices with their start and end apart: 17 -> 17, of which waited for: 8 -> 10; matrix products, arithmetic and copies ran while one was open for 0% -> 0% of each run, Pallas kernels for 13% -> 13%
where the time goes in v14:
time: 46.9 us; the launch traced here: 46.7 us
  starting transfers between devices  25.5 us (54%)
  waiting for transfers between devices  11 us (23%)
  Pallas kernels  7.82 us (17%)
  between operations  1.41 us (3%)
  other arithmetic  0.95 us (2%)
    ppermute x10, starting transfers between devices, swap(): return lax.ppermute(x, axis, [(i, i ^ k) for i in range(count)])  15.2 us
    ppermute x7, starting transfers between devices, mixed(): return lax.ppermute(x, (*axes, 'mp'), pairs)  10.2 us
    pallas_call x12, Pallas kernels, call(): pl.pallas_call(kernel, out_shape=out_shape, in_specs=in_specs, out_specs=...  7.82 us
    ppermute x7, waiting for transfers between devices, mixed(): return lax.ppermute(x, (*axes, 'mp'), pairs)  6.72 us
    ppermute x10, waiting for transfers between devices, swap(): return lax.ppermute(x, axis, [(i, i ^ k) for i in range(count)])  4.27 us
  transfers between devices with their start and end apart: 17, of which 10 were waited for; matrix products, arithmetic and copies ran while one was open for 0% of the time, Pallas kernels for 13%

profile of v14, /device:TPU:0, one launch (start us, length us, event | category | flops | bytes accessed | tf_op | source)
XLA Modules:
  0.0 46.7 jit_solution(8290582924547552632)
XLA Ops:
  0.0 0.9 %fusion = (bf16[48,1024]{1,0:T(8,128)(2,1)S(1)}, bf16[48,1024]{1,0:T(8,128)(2,1)S(1)}) fusion(s32[]{:T(128)S(6)} %select_n.7, bf16[32,4096]{1,0:T(8,128)(2,1)} %bitcast.6, bf16[16,4096]{1,0:T(8,128)(2,1)} %bitcast.12, s32[]{:T(128)S(6)} %select_n.6), kind=kLoop, calls=%fused_computation.6 | loop fusion | flops 393216 | bytes 589832 | tf_op jit(solution)/shard_map/concatenate | solution.py:288
  0.9 4.1 %collective-permute-start.6 = (bf16[48,512]{1,0:T(8,128)(2,1)S(1)}, bf16[48,512]{1,0:T(8,128)(2,1)S(1)}, u32[]{:S(2)}, u32[]{:S(2)}) collective-permute-start(bf16[48,512]{1,0:T(8,128)(2,1)S(1)} %get-tuple-element.25.refs_0_), channel_id=1, source_target_pairs={{0,8},{4,12},{8,0},{12,4},{1,9},{5,13},{9,1},{13,5},{2,10},{6,14},... | collective-permute-start | bytes 147464 | tf_op jit(solution)/shard_map/ppermute | solution.py:39
  5.0 0.1 collective-permute-start
  5.1 2.8 %collective-permute-start.4 = (bf16[48,1024]{1,0:T(8,128)(2,1)S(1)}, bf16[48,1024]{1,0:T(8,128)(2,1)S(1)}, u32[]{:S(2)}, u32[]{:S(2)}) collective-permute-start(bf16[48,1024]{1,0:T(8,128)(2,1)S(1)} %get-tuple-element.23.refs_0_), channel_id=1, source_target_pairs={{0,8},{4,12},{8,0},{12,4},{1,9},{5,13},{9,1},{13,5},{2,10},{6,14},... | collective-permute-start | bytes 294920 | tf_op jit(solution)/shard_map/ppermute | solution.py:39
  7.9 2.3 %shard_map.82 = (bf16[128,4096]{1,0:T(8,128)(2,1)S(1)}, bf16[128,4096]{1,0:T(8,128)(2,1)S(1)}, bf16[128,4096]{1,0:T(8,128)(2,1)S(1)}, bf16[128,4096]{1,0:T(8,128...) custom-call(bf16[128,4096]{1,0:T(8,128)(2,1)} %bitcast.8, bf16[128,4096]{1,0:T(8,128)(2,1)} %bitcast.9, ...), custom_call_target="tpu_custom_call" | custom-call | flops 1073741824 | bytes 65536 | tf_op jit(solution)/shard_map/pallas_call | solution.py:27
  10.3 0.0 collective-permute-done.6.refs_1_.refs_0_
  10.3 1.6 %collective-permute-start.7 = (bf16[96,512]{1,0:T(8,128)(2,1)S(1)}, bf16[96,512]{1,0:T(8,128)(2,1)S(1)}, u32[]{:S(2)}, u32[]{:S(2)}) collective-permute-start(bf16[96,512]{1,0:T(8,128)(2,1)S(1)} %shard_map.86), channel_id=1, source_target_pairs={{0,4},{4,0},{8,12},{12,8},{1,5},{5,1},{9,13},{13,9},{2,6},{6,2},{1... | collective-permute-start | bytes 294920 | tf_op jit(solution)/shard_map/ppermute | solution.py:39
  11.9 1.6 %collective-permute-done.refs_1_.refs_0_ = bf16[48,512]{1,0:T(8,128)(2,1)S(1)} collective-permute-done((bf16[48,512]{1,0:T(8,128)(2,1)S(1)}, bf16[48,512]{1,0:T(8,128)(2,1)S(1)}, u32[]{:S(2)}, u32[]{:S(2)}) %collective-permute-start) | collective-permute-done | bytes 49184 | tf_op jit(solution)/shard_map/ppermute | solution.py:39
  13.5 0.1 collective-permute-start.1
  13.6 1.2 %collective-permute-done.4.refs_1_.refs_8_ = bf16[48,1024]{1,0:T(8,128)(2,1)S(1)} collective-permute-done((bf16[48,1024]{1,0:T(8,128)(2,1)S(1)}, bf16[48,1024]{1,0:T(8,128)(2,1)S(1)}, u32[]{:S(2)}, u32[]{:S(2)}) %collective-permute-start.4) | collective-permute-done | bytes 98336 | tf_op jit(solution)/shard_map/ppermute | solution.py:39
  14.9 0.9 %collective-permute-start.5 = (bf16[96,1024]{1,0:T(8,128)(2,1)S(1)}, bf16[96,1024]{1,0:T(8,128)(2,1)S(1)}, u32[]{:S(2)}, u32[]{:S(2)}) collective-permute-start(bf16[96,1024]{1,0:T(8,128)(2,1)S(1)} %shard_map.85), channel_id=1, source_target_pairs={{0,4},{4,0},{8,12},{12,8},{1,5},{5,1},{9,13},{13,9},{2,6},{6,2},{1... | collective-permute-start | bytes 589832 | tf_op jit(solution)/shard_map/ppermute | solution.py:39
  15.7 1.3 %collective-permute-done.7.refs_1_ = bf16[96,512]{1,0:T(8,128)(2,1)S(1)} collective-permute-done((bf16[96,512]{1,0:T(8,128)(2,1)S(1)}, bf16[96,512]{1,0:T(8,128)(2,1)S(1)}, u32[]{:S(2)}, u32[]{:S(2)}) %collective-permute-start.7) | collective-permute-done | bytes 98336 | tf_op jit(solution)/shard_map/ppermute | solution.py:39
  17.0 1.6 %collective-permute-start.8 = (bf16[144,512]{1,0:T(8,128)(2,1)S(1)}, bf16[144,512]{1,0:T(8,128)(2,1)S(1)}, u32[]{:S(2)}, u32[]{:S(2)}) collective-permute-start(bf16[144,512]{1,0:T(8,128)(2,1)S(1)} %shard_map.87.refs_6_), channel_id=1, source_target_pairs={{0,2},{1,17},{2,0},{3,19},{16,18},{17,1},{18,16},{19,3},{4,6},{5,2... | collective-permute-start | bytes 442376 | tf_op jit(solution)/shard_map/ppermute | solution.py:51
  18.6 1.5 %collective-permute-start.9 = (bf16[144,512]{1,0:T(8,128)(2,1)S(1)}, bf16[144,512]{1,0:T(8,128)(2,1)S(1)}, u32[]{:S(2)}, u32[]{:S(2)}) collective-permute-start(bf16[144,512]{1,0:T(8,128)(2,1)S(1)} %shard_map.87.refs_6_), channel_id=1, source_target_pairs={{0,16},{1,3},{2,18},{3,1},{16,0},{17,19},{18,2},{19,17},{4,20},{5,... | collective-permute-start | bytes 442376 | tf_op jit(solution)/shard_map/ppermute | solution.py:51
  20.1 0.0 collective-permute-done.1.refs_1_
  20.1 0.8 %collective-permute-start.2 = (bf16[144,512]{1,0:T(8,128)(2,1)S(1)}, bf16[144,512]{1,0:T(8,128)(2,1)S(1)}, u32[]{:S(2)}, u32[]{:S(2)}) collective-permute-start(bf16[144,512]{1,0:T(8,128)(2,1)S(1)} %shard_map.84.refs_7_), channel_id=1, source_target_pairs={{0,2},{1,17},{2,0},{3,19},{16,18},{17,1},{18,16},{19,3},{4,6},{5,2... | collective-permute-start | bytes 442376 | tf_op jit(solution)/shard_map/ppermute | solution.py:51
  20.9 1.5 %collective-permute-start.3 = (bf16[144,512]{1,0:T(8,128)(2,1)S(1)}, bf16[144,512]{1,0:T(8,128)(2,1)S(1)}, u32[]{:S(2)}, u32[]{:S(2)}) collective-permute-start(bf16[144,512]{1,0:T(8,128)(2,1)S(1)} %shard_map.84.refs_7_), channel_id=1, source_target_pairs={{0,16},{1,3},{2,18},{3,1},{16,0},{17,19},{18,2},{19,17},{4,20},{5,... | collective-permute-start | bytes 442376 | tf_op jit(solution)/shard_map/ppermute | solution.py:51
  22.4 0.5 %shard_map.88.refs_8_ = f32[384,128]{1,0:T(8,128)S(1)} custom-call(bf16[128,4096]{1,0:T(8,128)(2,1)S(1)} %get-tuple-element.14.refs_0_, bf16[128,4096]{1,0:T(8,128)(2,1)S(1)} %get-tuple-element.15.refs_1_, bf16[128,4096]{1,0:T(8,128)(2,1)S(1)} %get-tuple-element.16.refs_2_, bf16[128,4096]{1,0:T(8,128)(2,1)S(1)} %get-tuple-element.17.refs_3_, ...), custom_call_target="tpu_custom_call" | custom-call | flops 268435456 | bytes 65536 | tf_op jit(solution)/shard_map/pallas_call | solution.py:27
  23.0 0.8 %collective-permute-done.8.refs_6_ = bf16[144,512]{1,0:T(8,128)(2,1)S(1)} collective-permute-done((bf16[144,512]{1,0:T(8,128)(2,1)S(1)}, bf16[144,512]{1,0:T(8,128)(2,1)S(1)}, u32[]{:S(2)}, u32[]{:S(2)}) %collective-permute-start.8) | collective-permute-done | bytes 147488 | tf_op jit(solution)/shard_map/ppermute | solution.py:51
  23.8 0.6 %collective-permute-done.9.refs_7_ = bf16[144,512]{1,0:T(8,128)(2,1)S(1)} collective-permute-done((bf16[144,512]{1,0:T(8,128)(2,1)S(1)}, bf16[144,512]{1,0:T(8,128)(2,1)S(1)}, u32[]{:S(2)}, u32[]{:S(2)}) %collective-permute-start.9) | collective-permute-done | bytes 147488 | tf_op jit(solution)/shard_map/ppermute | solution.py:51
  24.4 0.5 %shard_map.89.refs_10_ = f32[384,128]{1,0:T(8,128)S(1)} custom-call(bf16[128,4096]{1,0:T(8,128)(2,1)S(1)} %get-tuple-element.14.refs_0_, bf16[128,4096]{1,0:T(8,128)(2,1)S(1)} %get-tuple-element.15.refs_1_, bf16[128,4096]{1,0:T(8,128)(2,1)S(1)} %get-tuple-element.16.refs_2_, bf16[128,4096]{1,0:T(8,128)(2,1)S(1)} %get-tuple-element.17.refs_3_, ...), custom_call_target="tpu_custom_call" | custom-call | flops 268435456 | bytes 65536 | tf_op jit(solution)/shard_map/pallas_call | solution.py:27
  24.9 1.3 %collective-permute-done.2.refs_6_ = bf16[144,512]{1,0:T(8,128)(2,1)S(1)} collective-permute-done((bf16[144,512]{1,0:T(8,128)(2,1)S(1)}, bf16[144,512]{1,0:T(8,128)(2,1)S(1)}, u32[]{:S(2)}, u32[]{:S(2)}) %collective-permute-start.2) | collective-permute-done | bytes 147488 | tf_op jit(solution)/shard_map/ppermute | solution.py:51
  26.2 0.0 collective-permute-done.3.refs_7_
  26.2 0.0 collective-permute-done.5.refs_9_
  26.2 0.8 %shard_map.90.mine = f32[384,128]{1,0:T(8,128)S(1)} custom-call(bf16[128,4096]{1,0:T(8,128)(2,1)S(1)} %get-tuple-element.14.refs_0_, bf16[128,4096]{1,0:T(8,128)(2,1)S(1)} %get-tuple-element.15.refs_1_, bf16[128,4096]{1,0:T(8,128)(2,1)S(1)} %get-tuple-element.16.refs_2_, bf16[128,4096]{1,0:T(8,128)(2,1)S(1)} %get-tuple-element.17.refs_3_, ...), custom_call_target="tpu_custom_call" | custom-call | flops 268435456 | bytes 65536 | tf_op jit(solution)/shard_map/pallas_call | solution.py:27
  27.1 0.1 collective-permute-start.10
  28.4 0.1 collective-permute-done.10.other
  28.6 0.5 %shard_map.91 = (f32[136,128]{1,0:T(8,128)S(1)}, f32[1,64,128]{2,1,0:T(8,128)S(1)}, f32[128,64]{1,0:T(8,128)S(1)}) custom-call(s32[1]{0:T(128)S(6)} %copy.9.len_tr, s32[1]{0:T(128)S(6)} %copy.10.len_te, f32[384,128]{1,0:T(8,128)S(1)} %shard_map.90.mine, f32[384,128]{1,0:T(8,128)S(1)} %collective-permute-done.10.other), custom_call_target="tpu_custom_call" | custom-call | bytes 65536 | tf_op jit(solution)/shard_map/pallas_call | solution.py:27
  29.0 1.5 %collective-permute-start.11 = (f32[136,128]{1,0:T(8,128)S(1)}, f32[136,128]{1,0:T(8,128)S(1)}, u32[]{:S(2)}, u32[]{:S(2)}) collective-permute-start(f32[136,128]{1,0:T(8,128)S(1)} %get-tuple-element.20), channel_id=1, source_target_pairs={{0,2},{1,9},{2,0},{3,11},{4,6},{5,13},{6,4},{7,15},{8,10},{9,1},{1... | collective-permute-start | bytes 208904 | tf_op jit(solution)/shard_map/ppermute | solution.py:51
  30.6 2.0 %collective-permute-start.14 = (f32[1,64,128]{2,1,0:T(8,128)S(1)}, f32[1,64,128]{2,1,0:T(8,128)S(1)}, u32[]{:S(2)}, u32[]{:S(2)}) collective-permute-start(f32[1,64,128]{2,1,0:T(8,128)S(1)} %get-tuple-element.22), channel_id=1, source_target_pairs={{0,8},{4,12},{8,0},{12,4},{1,9},{5,13},{9,1},{13,5},{2,10},{6,14},... | collective-permute-start | bytes 98312 | tf_op jit(solution)/shard_map/ppermute | solution.py:39
  32.6 0.8 %collective-permute-done.11 = f32[136,128]{1,0:T(8,128)S(1)} collective-permute-done((f32[136,128]{1,0:T(8,128)S(1)}, f32[136,128]{1,0:T(8,128)S(1)}, u32[]{:S(2)}, u32[]{:S(2)}) %collective-permute-start.11) | collective-permute-done | bytes 69664 | tf_op jit(solution)/shard_map/ppermute | solution.py:51
  33.4 2.1 %collective-permute-start.12 = (f32[136,128]{1,0:T(8,128)S(1)}, f32[136,128]{1,0:T(8,128)S(1)}, u32[]{:S(2)}, u32[]{:S(2)}) collective-permute-start(f32[136,128]{1,0:T(8,128)S(1)} %add.21), channel_id=1, source_target_pairs={{0,8},{1,5},{2,10},{3,7},{4,12},{5,1},{6,14},{7,3},{8,0},{9,13},{1... | collective-permute-start | bytes 208904 | tf_op jit(solution)/shard_map/ppermute | solution.py:51
  35.5 0.0 collective-permute-done.14
  35.5 1.8 %collective-permute-start.15 = (f32[2,64,128]{2,1,0:T(8,128)S(1)}, f32[2,64,128]{2,1,0:T(8,128)S(1)}, u32[]{:S(2)}, u32[]{:S(2)}) collective-permute-start(f32[2,64,128]{2,1,0:T(8,128)S(1)} %pad_maximum_fusion.2), channel_id=1, source_target_pairs={{0,4},{4,0},{8,12},{12,8},{1,5},{5,1},{9,13},{13,9},{2,6},{6,2},{1... | collective-permute-start | bytes 196616 | tf_op jit(solution)/shard_map/ppermute | solution.py:39
  37.4 1.8 %collective-permute-done.12 = f32[136,128]{1,0:T(8,128)S(1)} collective-permute-done((f32[136,128]{1,0:T(8,128)S(1)}, f32[136,128]{1,0:T(8,128)S(1)}, u32[]{:S(2)}, u32[]{:S(2)}) %collective-permute-start.12) | collective-permute-done | bytes 69664 | tf_op jit(solution)/shard_map/ppermute | solution.py:51
  39.2 1.2 %collective-permute-start.13 = (f32[136,128]{1,0:T(8,128)S(1)}, f32[136,128]{1,0:T(8,128)S(1)}, u32[]{:S(2)}, u32[]{:S(2)}) collective-permute-start(f32[136,128]{1,0:T(8,128)S(1)} %add.22), channel_id=1, source_target_pairs={{0,4},{1,3},{2,6},{3,1},{4,0},{5,7},{6,2},{7,5},{8,12},{9,11},{10,... | collective-permute-start | bytes 208904 | tf_op jit(solution)/shard_map/ppermute | solution.py:51
  40.4 0.0 collective-permute-done.15
  40.4 1.7 %collective-permute-start.16 = (f32[4,64,128]{2,1,0:T(8,128)S(1)}, f32[4,64,128]{2,1,0:T(8,128)S(1)}, u32[]{:S(2)}, u32[]{:S(2)}) collective-permute-start(f32[4,64,128]{2,1,0:T(8,128)S(1)} %pad_maximum_fusion.1), channel_id=1, source_target_pairs={{0,2},{2,0},{1,3},{3,1},{4,6},{6,4},{5,7},{7,5},{8,10},{10,8},{9,1... | collective-permute-start | bytes 393224 | tf_op jit(solution)/shard_map/ppermute | solution.py:39
  42.1 1.4 %collective-permute-done.13 = f32[136,128]{1,0:T(8,128)S(1)} collective-permute-done((f32[136,128]{1,0:T(8,128)S(1)}, f32[136,128]{1,0:T(8,128)S(1)}, u32[]{:S(2)}, u32[]{:S(2)}) %collective-permute-start.13) | collective-permute-done | bytes 69664 | tf_op jit(solution)/shard_map/ppermute | solution.py:51
  43.5 2.5 %shard_map.92.side_ref = f32[64,128]{1,0:T(8,128)S(1)} custom-call(f32[136,128]{1,0:T(8,128)S(1)} %add.23.fac_ref, f32[128,64]{1,0:T(8,128)S(1)} %get-tuple-element.21.gtr_ref), custom_call_target="tpu_custom_call" | custom-call | flops 4294967296 | bytes 65536 | tf_op jit(solution)/shard_map/pallas_call | solution.py:27
  46.0 0.0 collective-permute-done.16
  46.0 0.6 %shard_map.93 = f32[1,8]{1,0:T(1,128)} custom-call(f32[64,128]{1,0:T(8,128)S(1)} %shard_map.92.side_ref, f32[8,64,128]{2,1,0:T(8,128)S(1)} %pad_maximum_fusion.gte_ref), custom_call_target="tpu_custom_call" | custom-call | bytes 65536 | tf_op jit(solution)/shard_map/pallas_call | solution.py:27
  (12 shorter events, 0.1 us)
Async XLA Ops:
  0.9 9.3 %collective-permute-start.6 = (bf16[48,512]{1,0:T(8,128)(2,1)S(1)}, bf16[48,512]{1,0:T(8,128)(2,1)S(1)}, u32[]{:S(2)}, u32[]{:S(2)}) collective-permute-start(bf16[48,512]{1,0:T(8,128)(2,1)S(1)} %get-tuple-element.25.refs_0_), channel_id=1, source_target_pairs={{0,8},{4,12},{8,0},{12,4},{1,9},{5,13},{9,1},{13,5},{2,10},{6,14},... | collective-permute-start | bytes 147464 | tf_op jit(solution)/shard_map/ppermute | solution.py:39
  5.0 8.5 %collective-permute-start = (bf16[48,512]{1,0:T(8,128)(2,1)S(1)}, bf16[48,512]{1,0:T(8,128)(2,1)S(1)}, u32[]{:S(2)}, u32[]{:S(2)}) collective-permute-start(bf16[48,512]{1,0:T(8,128)(2,1)S(1)} %get-tuple-element.26.refs_0_), channel_id=1, source_target_pairs={{0,8},{4,12},{8,0},{12,4},{1,9},{5,13},{9,1},{13,5},{2,10},{6,14},... | collective-permute-start | bytes 147464 | tf_op jit(solution)/shard_map/ppermute | solution.py:39
  5.1 9.8 %collective-permute-start.4 = (bf16[48,1024]{1,0:T(8,128)(2,1)S(1)}, bf16[48,1024]{1,0:T(8,128)(2,1)S(1)}, u32[]{:S(2)}, u32[]{:S(2)}) collective-permute-start(bf16[48,1024]{1,0:T(8,128)(2,1)S(1)} %get-tuple-element.23.refs_0_), channel_id=1, source_target_pairs={{0,8},{4,12},{8,0},{12,4},{1,9},{5,13},{9,1},{13,5},{2,10},{6,14},... | collective-permute-start | bytes 294920 | tf_op jit(solution)/shard_map/ppermute | solution.py:39
  10.3 6.7 %collective-permute-start.7 = (bf16[96,512]{1,0:T(8,128)(2,1)S(1)}, bf16[96,512]{1,0:T(8,128)(2,1)S(1)}, u32[]{:S(2)}, u32[]{:S(2)}) collective-permute-start(bf16[96,512]{1,0:T(8,128)(2,1)S(1)} %shard_map.86), channel_id=1, source_target_pairs={{0,4},{4,0},{8,12},{12,8},{1,5},{5,1},{9,13},{13,9},{2,6},{6,2},{1... | collective-permute-start | bytes 294920 | tf_op jit(solution)/shard_map/ppermute | solution.py:39
  13.5 6.6 %collective-permute-start.1 = (bf16[96,512]{1,0:T(8,128)(2,1)S(1)}, bf16[96,512]{1,0:T(8,128)(2,1)S(1)}, u32[]{:S(2)}, u32[]{:S(2)}) collective-permute-start(bf16[96,512]{1,0:T(8,128)(2,1)S(1)} %shard_map.83), channel_id=1, source_target_pairs={{0,4},{4,0},{8,12},{12,8},{1,5},{5,1},{9,13},{13,9},{2,6},{6,2},{1... | collective-permute-start | bytes 294920 | tf_op jit(solution)/shard_map/ppermute | solution.py:39
  14.9 11.4 %collective-permute-start.5 = (bf16[96,1024]{1,0:T(8,128)(2,1)S(1)}, bf16[96,1024]{1,0:T(8,128)(2,1)S(1)}, u32[]{:S(2)}, u32[]{:S(2)}) collective-permute-start(bf16[96,1024]{1,0:T(8,128)(2,1)S(1)} %shard_map.85), channel_id=1, source_target_pairs={{0,4},{4,0},{8,12},{12,8},{1,5},{5,1},{9,13},{13,9},{2,6},{6,2},{1... | collective-permute-start | bytes 589832 | tf_op jit(solution)/shard_map/ppermute | solution.py:39
  17.0 6.7 %collective-permute-start.8 = (bf16[144,512]{1,0:T(8,128)(2,1)S(1)}, bf16[144,512]{1,0:T(8,128)(2,1)S(1)}, u32[]{:S(2)}, u32[]{:S(2)}) collective-permute-start(bf16[144,512]{1,0:T(8,128)(2,1)S(1)} %shard_map.87.refs_6_), channel_id=1, source_target_pairs={{0,2},{1,17},{2,0},{3,19},{16,18},{17,1},{18,16},{19,3},{4,6},{5,2... | collective-permute-start | bytes 442376 | tf_op jit(solution)/shard_map/ppermute | solution.py:51
  18.6 5.8 %collective-permute-start.9 = (bf16[144,512]{1,0:T(8,128)(2,1)S(1)}, bf16[144,512]{1,0:T(8,128)(2,1)S(1)}, u32[]{:S(2)}, u32[]{:S(2)}) collective-permute-start(bf16[144,512]{1,0:T(8,128)(2,1)S(1)} %shard_map.87.refs_6_), channel_id=1, source_target_pairs={{0,16},{1,3},{2,18},{3,1},{16,0},{17,19},{18,2},{19,17},{4,20},{5,... | collective-permute-start | bytes 442376 | tf_op jit(solution)/shard_map/ppermute | solution.py:51
  20.1 6.1 %collective-permute-start.2 = (bf16[144,512]{1,0:T(8,128)(2,1)S(1)}, bf16[144,512]{1,0:T(8,128)(2,1)S(1)}, u32[]{:S(2)}, u32[]{:S(2)}) collective-permute-start(bf16[144,512]{1,0:T(8,128)(2,1)S(1)} %shard_map.84.refs_7_), channel_id=1, source_target_pairs={{0,2},{1,17},{2,0},{3,19},{16,18},{17,1},{18,16},{19,3},{4,6},{5,2... | collective-permute-start | bytes 442376 | tf_op jit(solution)/shard_map/ppermute | solution.py:51
  20.9 5.3 %collective-permute-start.3 = (bf16[144,512]{1,0:T(8,128)(2,1)S(1)}, bf16[144,512]{1,0:T(8,128)(2,1)S(1)}, u32[]{:S(2)}, u32[]{:S(2)}) collective-permute-start(bf16[144,512]{1,0:T(8,128)(2,1)S(1)} %shard_map.84.refs_7_), channel_id=1, source_target_pairs={{0,16},{1,3},{2,18},{3,1},{16,0},{17,19},{18,2},{19,17},{4,20},{5,... | collective-permute-start | bytes 442376 | tf_op jit(solution)/shard_map/ppermute | solution.py:51
  27.1 1.5 %collective-permute-start.10 = (f32[384,128]{1,0:T(8,128)S(1)}, f32[384,128]{1,0:T(8,128)S(1)}, u32[]{:S(2)}, u32[]{:S(2)}) collective-permute-start(f32[384,128]{1,0:T(8,128)S(1)} %shard_map.90.mine), channel_id=1, source_target_pairs={{0,1},{1,0},{2,3},{3,2},{4,5},{5,4},{6,7},{7,6},{8,9},{9,8},{10,11... | collective-permute-start | bytes 589832 | tf_op jit(solution)/shard_map/ppermute | solution.py:39
  29.0 4.3 %collective-permute-start.11 = (f32[136,128]{1,0:T(8,128)S(1)}, f32[136,128]{1,0:T(8,128)S(1)}, u32[]{:S(2)}, u32[]{:S(2)}) collective-permute-start(f32[136,128]{1,0:T(8,128)S(1)} %get-tuple-element.20), channel_id=1, source_target_pairs={{0,2},{1,9},{2,0},{3,11},{4,6},{5,13},{6,4},{7,15},{8,10},{9,1},{1... | collective-permute-start | bytes 208904 | tf_op jit(solution)/shard_map/ppermute | solution.py:51
  30.6 5.0 %collective-permute-start.14 = (f32[1,64,128]{2,1,0:T(8,128)S(1)}, f32[1,64,128]{2,1,0:T(8,128)S(1)}, u32[]{:S(2)}, u32[]{:S(2)}) collective-permute-start(f32[1,64,128]{2,1,0:T(8,128)S(1)} %get-tuple-element.22), channel_id=1, source_target_pairs={{0,8},{4,12},{8,0},{12,4},{1,9},{5,13},{9,1},{13,5},{2,10},{6,14},... | collective-permute-start | bytes 98312 | tf_op jit(solution)/shard_map/ppermute | solution.py:39
  33.4 5.7 %collective-permute-start.12 = (f32[136,128]{1,0:T(8,128)S(1)}, f32[136,128]{1,0:T(8,128)S(1)}, u32[]{:S(2)}, u32[]{:S(2)}) collective-permute-start(f32[136,128]{1,0:T(8,128)S(1)} %add.21), channel_id=1, source_target_pairs={{0,8},{1,5},{2,10},{3,7},{4,12},{5,1},{6,14},{7,3},{8,0},{9,13},{1... | collective-permute-start | bytes 208904 | tf_op jit(solution)/shard_map/ppermute | solution.py:51
  35.5 4.8 %collective-permute-start.15 = (f32[2,64,128]{2,1,0:T(8,128)S(1)}, f32[2,64,128]{2,1,0:T(8,128)S(1)}, u32[]{:S(2)}, u32[]{:S(2)}) collective-permute-start(f32[2,64,128]{2,1,0:T(8,128)S(1)} %pad_maximum_fusion.2), channel_id=1, source_target_pairs={{0,4},{4,0},{8,12},{12,8},{1,5},{5,1},{9,13},{13,9},{2,6},{6,2},{1... | collective-permute-start | bytes 196616 | tf_op jit(solution)/shard_map/ppermute | solution.py:39
  39.2 4.4 %collective-permute-start.13 = (f32[136,128]{1,0:T(8,128)S(1)}, f32[136,128]{1,0:T(8,128)S(1)}, u32[]{:S(2)}, u32[]{:S(2)}) collective-permute-start(f32[136,128]{1,0:T(8,128)S(1)} %add.22), channel_id=1, source_target_pairs={{0,4},{1,3},{2,6},{3,1},{4,0},{5,7},{6,2},{7,5},{8,12},{9,11},{10,... | collective-permute-start | bytes 208904 | tf_op jit(solution)/shard_map/ppermute | solution.py:51
  40.4 5.6 %collective-permute-start.16 = (f32[4,64,128]{2,1,0:T(8,128)S(1)}, f32[4,64,128]{2,1,0:T(8,128)S(1)}, u32[]{:S(2)}, u32[]{:S(2)}) collective-permute-start(f32[4,64,128]{2,1,0:T(8,128)S(1)} %pad_maximum_fusion.1), channel_id=1, source_target_pairs={{0,2},{2,0},{1,3},{3,1},{4,6},{6,4},{5,7},{7,5},{8,10},{10,8},{9,1... | collective-permute-start | bytes 393224 | tf_op jit(solution)/shard_map/ppermute | solution.py:39

commit v15 on v11

--- a/solution.py
+++ b/solution.py
@@ -299,15 +299,14 @@
     )
     halves = [mine[:, :part], mine[:, part:]]
     far = [swap(h, "dp", n_dp, 2) for h in halves]
-    far_op = swap(opposite, "dp", n_dp, 2)
-    both_a = stack((halves[0], far[0]), w_out)
-    near_a = swap(both_a, "dp", n_dp, 1)
-    both_b = stack((halves[1], far[1]))
-    near_b = swap(both_b, "dp", n_dp, 1)
-    za = stack((far[0], near_a))
+    near_a, cross_a = [swap(halves[0], "dp", n_dp, k) for k in (1, 3)]
+    za = stack((far[0], near_a, cross_a))
     along_x, along_y = (0, 1), (1, 0)
     xa = mixed(za, PLANE, (n_groups, n_blk), along_x, along_y)
     ya = mixed(za, PLANE, (n_groups, n_blk), along_y, along_x)
+    both_b = stack((halves[1], far[1]), za)
+    near_b = swap(both_b, "dp", n_dp, 1)
+    far_op = swap(opposite, "dp", n_dp, 2)
     both_op = stack((opposite, far_op))
     near_op = swap(both_op, "dp", n_dp, 1)
     zb = stack((far[1], near_b))

time: 47.4 us -> 49.4 us (1.042)
  waiting for transfers between devices: 9.14 us -> 14.4 us
  starting transfers between devices: 27.9 us -> 24.6 us
    ppermute x7, waiting for transfers between devices: 6.17 us -> 8.85 us  [mixed(): return lax.ppermute(x, (*axes, 'mp'), pairs)]
    ppermute x10 -> x11, starting transfers between devices: 18.2 us -> 15.6 us  [swap(): return lax.ppermute(x, axis, [(i, i ^ k) for i in range(count)])]
    ppermute x10 -> x11, waiting for transfers between devices: 2.97 us -> 5.58 us  [swap(): return lax.ppermute(x, axis, [(i, i ^ k) for i in range(count)])]
    ppermute x7, starting transfers between devices: 9.68 us -> 9 us  [mixed(): return lax.ppermute(x, (*axes, 'mp'), pairs)]
    pallas_call x12 -> x11, Pallas kernels: 7.84 us -> 7.82 us  [call(): pl.pallas_call(kernel, out_shape=out_shape, in_specs=in_specs, out_specs=...]
  transfers between devices with their start and end apart: 17 -> 18, of which waited for: 8 -> 11; matrix products, arithmetic and copies ran while one was open for 0% -> 0% of each run, Pallas kernels for 13% -> 12%
where the time goes in v15:
time: 49.4 us; the launch traced here: 49.2 us
  starting transfers between devices  24.6 us (50%)
  waiting for transfers between devices  14.4 us (29%)
  Pallas kernels  7.82 us (16%)
  between operations  1.41 us (3%)
  other arithmetic  0.95 us (2%)
    ppermute x11, starting transfers between devices, swap(): return lax.ppermute(x, axis, [(i, i ^ k) for i in range(count)])  15.6 us
    ppermute x7, starting transfers between devices, mixed(): return lax.ppermute(x, (*axes, 'mp'), pairs)  9 us
    ppermute x7, waiting for transfers between devices, mixed(): return lax.ppermute(x, (*axes, 'mp'), pairs)  8.85 us
    pallas_call x11, Pallas kernels, call(): pl.pallas_call(kernel, out_shape=out_shape, in_specs=in_specs, out_specs=...  7.82 us
    ppermute x11, waiting for transfers between devices, swap(): return lax.ppermute(x, axis, [(i, i ^ k) for i in range(count)])  5.58 us
  transfers between devices with their start and end apart: 18, of which 11 were waited for; matrix products, arithmetic and copies ran while one was open for 0% of the time, Pallas kernels for 12%

profile of v15, /device:TPU:0, one launch (start us, length us, event | category | flops | bytes accessed | tf_op | source)
XLA Modules:
  0.0 49.2 jit_solution(8609916264949503743)
XLA Ops:
  0.0 0.9 %fusion = (bf16[48,1024]{1,0:T(8,128)(2,1)S(1)}, bf16[48,1024]{1,0:T(8,128)(2,1)S(1)}) fusion(s32[]{:T(128)S(6)} %select_n.7, bf16[32,4096]{1,0:T(8,128)(2,1)} %bitcast.6, bf16[16,4096]{1,0:T(8,128)(2,1)} %bitcast.12, s32[]{:T(128)S(6)} %select_n.6), kind=kLoop, calls=%fused_computation.6 | loop fusion | flops 393216 | bytes 589832 | tf_op jit(solution)/shard_map/concatenate | solution.py:288
  0.9 4.1 %collective-permute-start.1 = (bf16[48,512]{1,0:T(8,128)(2,1)S(1)}, bf16[48,512]{1,0:T(8,128)(2,1)S(1)}, u32[]{:S(2)}, u32[]{:S(2)}) collective-permute-start(bf16[48,512]{1,0:T(8,128)(2,1)S(1)} %get-tuple-element.25), channel_id=1, source_target_pairs={{0,8},{4,12},{8,0},{12,4},{1,9},{5,13},{9,1},{13,5},{2,10},{6,14},... | collective-permute-start | bytes 147464 | tf_op jit(solution)/shard_map/ppermute | solution.py:39
  5.0 1.6 %collective-permute-start.2 = (bf16[48,512]{1,0:T(8,128)(2,1)S(1)}, bf16[48,512]{1,0:T(8,128)(2,1)S(1)}, u32[]{:S(2)}, u32[]{:S(2)}) collective-permute-start(bf16[48,512]{1,0:T(8,128)(2,1)S(1)} %get-tuple-element.25), channel_id=1, source_target_pairs={{0,4},{4,0},{8,12},{12,8},{1,5},{5,1},{9,13},{13,9},{2,6},{6,2},{1... | collective-permute-start | bytes 147464 | tf_op jit(solution)/shard_map/ppermute | solution.py:39
  6.6 0.0 collective-permute-start.3
  6.6 1.9 %collective-permute-start = (bf16[48,512]{1,0:T(8,128)(2,1)S(1)}, bf16[48,512]{1,0:T(8,128)(2,1)S(1)}, u32[]{:S(2)}, u32[]{:S(2)}) collective-permute-start(bf16[48,512]{1,0:T(8,128)(2,1)S(1)} %get-tuple-element.26.refs_0_), channel_id=1, source_target_pairs={{0,8},{4,12},{8,0},{12,4},{1,9},{5,13},{9,1},{13,5},{2,10},{6,14},... | collective-permute-start | bytes 147464 | tf_op jit(solution)/shard_map/ppermute | solution.py:39
  8.5 1.0 %collective-permute-start.7 = (bf16[48,1024]{1,0:T(8,128)(2,1)S(1)}, bf16[48,1024]{1,0:T(8,128)(2,1)S(1)}, u32[]{:S(2)}, u32[]{:S(2)}) collective-permute-start(bf16[48,1024]{1,0:T(8,128)(2,1)S(1)} %get-tuple-element.23.refs_0_), channel_id=1, source_target_pairs={{0,8},{4,12},{8,0},{12,4},{1,9},{5,13},{9,1},{13,5},{2,10},{6,14},... | collective-permute-start | bytes 294920 | tf_op jit(solution)/shard_map/ppermute | solution.py:39
  9.5 0.0 collective-permute-done.1.refs_0_
  9.5 0.0 collective-permute-done.2.refs_1_
  9.5 3.1 %collective-permute-done.3.refs_2_ = bf16[48,512]{1,0:T(8,128)(2,1)S(1)} collective-permute-done((bf16[48,512]{1,0:T(8,128)(2,1)S(1)}, bf16[48,512]{1,0:T(8,128)(2,1)S(1)}, u32[]{:S(2)}, u32[]{:S(2)}) %collective-permute-start.3) | collective-permute-done | bytes 49184 | tf_op jit(solution)/shard_map/ppermute | solution.py:39
  12.6 1.6 %collective-permute-start.10 = (bf16[144,512]{1,0:T(8,128)(2,1)S(1)}, bf16[144,512]{1,0:T(8,128)(2,1)S(1)}, u32[]{:S(2)}, u32[]{:S(2)}) collective-permute-start(bf16[144,512]{1,0:T(8,128)(2,1)S(1)} %shard_map.83.refs_2_.refs_6_), channel_id=1, source_target_pairs={{0,16},{1,3},{2,18},{3,1},{16,0},{17,19},{18,2},{19,17},{4,20},{5,... | collective-permute-start | bytes 442376 | tf_op jit(solution)/shard_map/ppermute | solution.py:51
  14.2 1.5 %collective-permute-start.9 = (bf16[144,512]{1,0:T(8,128)(2,1)S(1)}, bf16[144,512]{1,0:T(8,128)(2,1)S(1)}, u32[]{:S(2)}, u32[]{:S(2)}) collective-permute-start(bf16[144,512]{1,0:T(8,128)(2,1)S(1)} %shard_map.83.refs_2_.refs_6_), channel_id=1, source_target_pairs={{0,2},{1,17},{2,0},{3,19},{16,18},{17,1},{18,16},{19,3},{4,6},{5,2... | collective-permute-start | bytes 442376 | tf_op jit(solution)/shard_map/ppermute | solution.py:51
  15.7 0.4 collective-permute-done.refs_1_.refs_0_
  16.1 1.4 %collective-permute-start.4 = (bf16[96,512]{1,0:T(8,128)(2,1)S(1)}, bf16[96,512]{1,0:T(8,128)(2,1)S(1)}, u32[]{:S(2)}, u32[]{:S(2)}) collective-permute-start(bf16[96,512]{1,0:T(8,128)(2,1)S(1)} %shard_map.84), channel_id=1, source_target_pairs={{0,4},{4,0},{8,12},{12,8},{1,5},{5,1},{9,13},{13,9},{2,6},{6,2},{1... | collective-permute-start | bytes 294920 | tf_op jit(solution)/shard_map/ppermute | solution.py:39
  17.4 2.3 %shard_map.82 = (bf16[128,4096]{1,0:T(8,128)(2,1)S(1)}, bf16[128,4096]{1,0:T(8,128)(2,1)S(1)}, bf16[128,4096]{1,0:T(8,128)(2,1)S(1)}, bf16[128,4096]{1,0:T(8,128...) custom-call(bf16[128,4096]{1,0:T(8,128)(2,1)} %bitcast.8, bf16[128,4096]{1,0:T(8,128)(2,1)} %bitcast.9, ...), custom_call_target="tpu_custom_call" | custom-call | flops 1073741824 | bytes 65536 | tf_op jit(solution)/shard_map/pallas_call | solution.py:27
  19.7 0.0 collective-permute-done.7.refs_1_.refs_8_
  19.8 0.8 %collective-permute-start.8 = (bf16[96,1024]{1,0:T(8,128)(2,1)S(1)}, bf16[96,1024]{1,0:T(8,128)(2,1)S(1)}, u32[]{:S(2)}, u32[]{:S(2)}) collective-permute-start(bf16[96,1024]{1,0:T(8,128)(2,1)S(1)} %shard_map.86), channel_id=1, source_target_pairs={{0,4},{4,0},{8,12},{12,8},{1,5},{5,1},{9,13},{13,9},{2,6},{6,2},{1... | collective-permute-start | bytes 589832 | tf_op jit(solution)/shard_map/ppermute | solution.py:39
  20.6 1.2 %collective-permute-done.4.refs_1_ = bf16[96,512]{1,0:T(8,128)(2,1)S(1)} collective-permute-done((bf16[96,512]{1,0:T(8,128)(2,1)S(1)}, bf16[96,512]{1,0:T(8,128)(2,1)S(1)}, u32[]{:S(2)}, u32[]{:S(2)}) %collective-permute-start.4) | collective-permute-done | bytes 98336 | tf_op jit(solution)/shard_map/ppermute | solution.py:39
  21.8 1.6 %collective-permute-start.5 = (bf16[144,512]{1,0:T(8,128)(2,1)S(1)}, bf16[144,512]{1,0:T(8,128)(2,1)S(1)}, u32[]{:S(2)}, u32[]{:S(2)}) collective-permute-start(bf16[144,512]{1,0:T(8,128)(2,1)S(1)} %shard_map.85.refs_7_), channel_id=1, source_target_pairs={{0,2},{1,17},{2,0},{3,19},{16,18},{17,1},{18,16},{19,3},{4,6},{5,2... | collective-permute-start | bytes 442376 | tf_op jit(solution)/shard_map/ppermute | solution.py:51
  23.4 1.5 %collective-permute-start.6 = (bf16[144,512]{1,0:T(8,128)(2,1)S(1)}, bf16[144,512]{1,0:T(8,128)(2,1)S(1)}, u32[]{:S(2)}, u32[]{:S(2)}) collective-permute-start(bf16[144,512]{1,0:T(8,128)(2,1)S(1)} %shard_map.85.refs_7_), channel_id=1, source_target_pairs={{0,16},{1,3},{2,18},{3,1},{16,0},{17,19},{18,2},{19,17},{4,20},{5,... | collective-permute-start | bytes 442376 | tf_op jit(solution)/shard_map/ppermute | solution.py:51
  24.9 0.5 %shard_map.87.refs_8_ = f32[384,128]{1,0:T(8,128)S(1)} custom-call(bf16[128,4096]{1,0:T(8,128)(2,1)S(1)} %get-tuple-element.14.refs_0_, bf16[128,4096]{1,0:T(8,128)(2,1)S(1)} %get-tuple-element.15.refs_1_, bf16[128,4096]{1,0:T(8,128)(2,1)S(1)} %get-tuple-element.16.refs_2_, bf16[128,4096]{1,0:T(8,128)(2,1)S(1)} %get-tuple-element.17.refs_3_, ...), custom_call_target="tpu_custom_call" | custom-call | flops 1073741824 | bytes 65536 | tf_op jit(solution)/shard_map/pallas_call | solution.py:27
  25.4 0.0 collective-permute-done.10.refs_7_
  25.4 0.0 collective-permute-done.9.refs_6_
  25.4 0.5 %shard_map.88.refs_10_ = f32[384,128]{1,0:T(8,128)S(1)} custom-call(bf16[128,4096]{1,0:T(8,128)(2,1)S(1)} %get-tuple-element.14.refs_0_, bf16[128,4096]{1,0:T(8,128)(2,1)S(1)} %get-tuple-element.15.refs_1_, bf16[128,4096]{1,0:T(8,128)(2,1)S(1)} %get-tuple-element.16.refs_2_, bf16[128,4096]{1,0:T(8,128)(2,1)S(1)} %get-tuple-element.17.refs_3_, ...), custom_call_target="tpu_custom_call" | custom-call | flops 1073741824 | bytes 65536 | tf_op jit(solution)/shard_map/pallas_call | solution.py:27
  26.0 1.0 %collective-permute-done.5.refs_6_ = bf16[144,512]{1,0:T(8,128)(2,1)S(1)} collective-permute-done((bf16[144,512]{1,0:T(8,128)(2,1)S(1)}, bf16[144,512]{1,0:T(8,128)(2,1)S(1)}, u32[]{:S(2)}, u32[]{:S(2)}) %collective-permute-start.5) | collective-permute-done | bytes 147488 | tf_op jit(solution)/shard_map/ppermute | solution.py:51
  27.0 1.5 %collective-permute-done.6.refs_7_ = bf16[144,512]{1,0:T(8,128)(2,1)S(1)} collective-permute-done((bf16[144,512]{1,0:T(8,128)(2,1)S(1)}, bf16[144,512]{1,0:T(8,128)(2,1)S(1)}, u32[]{:S(2)}, u32[]{:S(2)}) %collective-permute-start.6) | collective-permute-done | bytes 147488 | tf_op jit(solution)/shard_map/ppermute | solution.py:51
  28.5 0.0 collective-permute-done.8.refs_9_
  28.5 0.8 %shard_map.89.mine = f32[384,128]{1,0:T(8,128)S(1)} custom-call(bf16[128,4096]{1,0:T(8,128)(2,1)S(1)} %get-tuple-element.14.refs_0_, bf16[128,4096]{1,0:T(8,128)(2,1)S(1)} %get-tuple-element.15.refs_1_, bf16[128,4096]{1,0:T(8,128)(2,1)S(1)} %get-tuple-element.16.refs_2_, bf16[128,4096]{1,0:T(8,128)(2,1)S(1)} %get-tuple-element.17.refs_3_, ...), custom_call_target="tpu_custom_call" | custom-call | flops 1073741824 | bytes 65536 | tf_op jit(solution)/shard_map/pallas_call | solution.py:27
  29.3 0.1 collective-permute-start.11
  30.7 0.1 collective-permute-done.11.other
  30.8 0.5 shard_map.90
  31.3 0.6 %collective-permute-start.12 = (f32[136,128]{1,0:T(8,128)S(1)}, f32[136,128]{1,0:T(8,128)S(1)}, u32[]{:S(2)}, u32[]{:S(2)}) collective-permute-start(f32[136,128]{1,0:T(8,128)S(1)} %get-tuple-element.20), channel_id=1, source_target_pairs={{0,2},{1,9},{2,0},{3,11},{4,6},{5,13},{6,4},{7,15},{8,10},{9,1},{1... | collective-permute-start | bytes 208904 | tf_op jit(solution)/shard_map/ppermute | solution.py:51
  31.9 3.2 %collective-permute-start.15 = (f32[1,64,128]{2,1,0:T(8,128)S(1)}, f32[1,64,128]{2,1,0:T(8,128)S(1)}, u32[]{:S(2)}, u32[]{:S(2)}) collective-permute-start(f32[1,64,128]{2,1,0:T(8,128)S(1)} %get-tuple-element.22), channel_id=1, source_target_pairs={{0,8},{4,12},{8,0},{12,4},{1,9},{5,13},{9,1},{13,5},{2,10},{6,14},... | collective-permute-start | bytes 98312 | tf_op jit(solution)/shard_map/ppermute | solution.py:39
  35.1 0.6 %collective-permute-done.12 = f32[136,128]{1,0:T(8,128)S(1)} collective-permute-done((f32[136,128]{1,0:T(8,128)S(1)}, f32[136,128]{1,0:T(8,128)S(1)}, u32[]{:S(2)}, u32[]{:S(2)}) %collective-permute-start.12) | collective-permute-done | bytes 69664 | tf_op jit(solution)/shard_map/ppermute | solution.py:51
  35.7 1.9 %collective-permute-start.13 = (f32[136,128]{1,0:T(8,128)S(1)}, f32[136,128]{1,0:T(8,128)S(1)}, u32[]{:S(2)}, u32[]{:S(2)}) collective-permute-start(f32[136,128]{1,0:T(8,128)S(1)} %add.21), channel_id=1, source_target_pairs={{0,8},{1,5},{2,10},{3,7},{4,12},{5,1},{6,14},{7,3},{8,0},{9,13},{1... | collective-permute-start | bytes 208904 | tf_op jit(solution)/shard_map/ppermute | solution.py:51
  37.5 0.3 collective-permute-done.15
  37.9 0.1 collective-permute-start.16
  38.0 3.7 %collective-permute-done.13 = f32[136,128]{1,0:T(8,128)S(1)} collective-permute-done((f32[136,128]{1,0:T(8,128)S(1)}, f32[136,128]{1,0:T(8,128)S(1)}, u32[]{:S(2)}, u32[]{:S(2)}) %collective-permute-start.13) | collective-permute-done | bytes 69664 | tf_op jit(solution)/shard_map/ppermute | solution.py:51
  41.7 0.4 collective-permute-start.14
  42.1 0.4 collective-permute-done.16
  42.6 1.4 %collective-permute-start.17 = (f32[4,64,128]{2,1,0:T(8,128)S(1)}, f32[4,64,128]{2,1,0:T(8,128)S(1)}, u32[]{:S(2)}, u32[]{:S(2)}) collective-permute-start(f32[4,64,128]{2,1,0:T(8,128)S(1)} %pad_maximum_fusion.1), channel_id=1, source_target_pairs={{0,2},{2,0},{1,3},{3,1},{4,6},{6,4},{5,7},{7,5},{8,10},{10,8},{9,1... | collective-permute-start | bytes 393224 | tf_op jit(solution)/shard_map/ppermute | solution.py:39
  44.0 2.1 %collective-permute-done.14 = f32[136,128]{1,0:T(8,128)S(1)} collective-permute-done((f32[136,128]{1,0:T(8,128)S(1)}, f32[136,128]{1,0:T(8,128)S(1)}, u32[]{:S(2)}, u32[]{:S(2)}) %collective-permute-start.14) | collective-permute-done | bytes 69664 | tf_op jit(solution)/shard_map/ppermute | solution.py:51
  46.1 2.5 %shard_map.91.side_ref = f32[64,128]{1,0:T(8,128)S(1)} custom-call(f32[136,128]{1,0:T(8,128)S(1)} %add.23.fac_ref, f32[128,64]{1,0:T(8,128)S(1)} %get-tuple-element.21.gtr_ref), custom_call_target="tpu_custom_call" | custom-call | flops 4294967296 | bytes 65536 | tf_op jit(solution)/shard_map/pallas_call | solution.py:27
  48.5 0.0 collective-permute-done.17
  48.6 0.6 %shard_map.92 = f32[1,8]{1,0:T(1,128)} custom-call(f32[64,128]{1,0:T(8,128)S(1)} %shard_map.91.side_ref, f32[8,64,128]{2,1,0:T(8,128)S(1)} %pad_maximum_fusion.gte_ref), custom_call_target="tpu_custom_call" | custom-call | bytes 65536 | tf_op jit(solution)/shard_map/pallas_call | solution.py:27
  (11 shorter events, 0.1 us)
Async XLA Ops:
  0.9 8.6 %collective-permute-start.1 = (bf16[48,512]{1,0:T(8,128)(2,1)S(1)}, bf16[48,512]{1,0:T(8,128)(2,1)S(1)}, u32[]{:S(2)}, u32[]{:S(2)}) collective-permute-start(bf16[48,512]{1,0:T(8,128)(2,1)S(1)} %get-tuple-element.25), channel_id=1, source_target_pairs={{0,8},{4,12},{8,0},{12,4},{1,9},{5,13},{9,1},{13,5},{2,10},{6,14},... | collective-permute-start | bytes 147464 | tf_op jit(solution)/shard_map/ppermute | solution.py:39
  5.0 4.5 %collective-permute-start.2 = (bf16[48,512]{1,0:T(8,128)(2,1)S(1)}, bf16[48,512]{1,0:T(8,128)(2,1)S(1)}, u32[]{:S(2)}, u32[]{:S(2)}) collective-permute-start(bf16[48,512]{1,0:T(8,128)(2,1)S(1)} %get-tuple-element.25), channel_id=1, source_target_pairs={{0,4},{4,0},{8,12},{12,8},{1,5},{5,1},{9,13},{13,9},{2,6},{6,2},{1... | collective-permute-start | bytes 147464 | tf_op jit(solution)/shard_map/ppermute | solution.py:39
  6.6 6.0 %collective-permute-start.3 = (bf16[48,512]{1,0:T(8,128)(2,1)S(1)}, bf16[48,512]{1,0:T(8,128)(2,1)S(1)}, u32[]{:S(2)}, u32[]{:S(2)}) collective-permute-start(bf16[48,512]{1,0:T(8,128)(2,1)S(1)} %get-tuple-element.25), channel_id=1, source_target_pairs={{0,12},{4,8},{8,4},{12,0},{1,13},{5,9},{9,5},{13,1},{2,14},{6,10},... | collective-permute-start | bytes 147464 | tf_op jit(solution)/shard_map/ppermute | solution.py:39
  6.6 9.5 %collective-permute-start = (bf16[48,512]{1,0:T(8,128)(2,1)S(1)}, bf16[48,512]{1,0:T(8,128)(2,1)S(1)}, u32[]{:S(2)}, u32[]{:S(2)}) collective-permute-start(bf16[48,512]{1,0:T(8,128)(2,1)S(1)} %get-tuple-element.26.refs_0_), channel_id=1, source_target_pairs={{0,8},{4,12},{8,0},{12,4},{1,9},{5,13},{9,1},{13,5},{2,10},{6,14},... | collective-permute-start | bytes 147464 | tf_op jit(solution)/shard_map/ppermute | solution.py:39
  8.5 11.2 %collective-permute-start.7 = (bf16[48,1024]{1,0:T(8,128)(2,1)S(1)}, bf16[48,1024]{1,0:T(8,128)(2,1)S(1)}, u32[]{:S(2)}, u32[]{:S(2)}) collective-permute-start(bf16[48,1024]{1,0:T(8,128)(2,1)S(1)} %get-tuple-element.23.refs_0_), channel_id=1, source_target_pairs={{0,8},{4,12},{8,0},{12,4},{1,9},{5,13},{9,1},{13,5},{2,10},{6,14},... | collective-permute-start | bytes 294920 | tf_op jit(solution)/shard_map/ppermute | solution.py:39
  12.6 12.8 %collective-permute-start.10 = (bf16[144,512]{1,0:T(8,128)(2,1)S(1)}, bf16[144,512]{1,0:T(8,128)(2,1)S(1)}, u32[]{:S(2)}, u32[]{:S(2)}) collective-permute-start(bf16[144,512]{1,0:T(8,128)(2,1)S(1)} %shard_map.83.refs_2_.refs_6_), channel_id=1, source_target_pairs={{0,16},{1,3},{2,18},{3,1},{16,0},{17,19},{18,2},{19,17},{4,20},{5,... | collective-permute-start | bytes 442376 | tf_op jit(solution)/shard_map/ppermute | solution.py:51
  14.2 11.2 %collective-permute-start.9 = (bf16[144,512]{1,0:T(8,128)(2,1)S(1)}, bf16[144,512]{1,0:T(8,128)(2,1)S(1)}, u32[]{:S(2)}, u32[]{:S(2)}) collective-permute-start(bf16[144,512]{1,0:T(8,128)(2,1)S(1)} %shard_map.83.refs_2_.refs_6_), channel_id=1, source_target_pairs={{0,2},{1,17},{2,0},{3,19},{16,18},{17,1},{18,16},{19,3},{4,6},{5,2... | collective-permute-start | bytes 442376 | tf_op jit(solution)/shard_map/ppermute | solution.py:51
  16.1 5.7 %collective-permute-start.4 = (bf16[96,512]{1,0:T(8,128)(2,1)S(1)}, bf16[96,512]{1,0:T(8,128)(2,1)S(1)}, u32[]{:S(2)}, u32[]{:S(2)}) collective-permute-start(bf16[96,512]{1,0:T(8,128)(2,1)S(1)} %shard_map.84), channel_id=1, source_target_pairs={{0,4},{4,0},{8,12},{12,8},{1,5},{5,1},{9,13},{13,9},{2,6},{6,2},{1... | collective-permute-start | bytes 294920 | tf_op jit(solution)/shard_map/ppermute | solution.py:39
  19.8 8.7 %collective-permute-start.8 = (bf16[96,1024]{1,0:T(8,128)(2,1)S(1)}, bf16[96,1024]{1,0:T(8,128)(2,1)S(1)}, u32[]{:S(2)}, u32[]{:S(2)}) collective-permute-start(bf16[96,1024]{1,0:T(8,128)(2,1)S(1)} %shard_map.86), channel_id=1, source_target_pairs={{0,4},{4,0},{8,12},{12,8},{1,5},{5,1},{9,13},{13,9},{2,6},{6,2},{1... | collective-permute-start | bytes 589832 | tf_op jit(solution)/shard_map/ppermute | solution.py:39
  21.8 5.2 %collective-permute-start.5 = (bf16[144,512]{1,0:T(8,128)(2,1)S(1)}, bf16[144,512]{1,0:T(8,128)(2,1)S(1)}, u32[]{:S(2)}, u32[]{:S(2)}) collective-permute-start(bf16[144,512]{1,0:T(8,128)(2,1)S(1)} %shard_map.85.refs_7_), channel_id=1, source_target_pairs={{0,2},{1,17},{2,0},{3,19},{16,18},{17,1},{18,16},{19,3},{4,6},{5,2... | collective-permute-start | bytes 442376 | tf_op jit(solution)/shard_map/ppermute | solution.py:51
  23.4 5.1 %collective-permute-start.6 = (bf16[144,512]{1,0:T(8,128)(2,1)S(1)}, bf16[144,512]{1,0:T(8,128)(2,1)S(1)}, u32[]{:S(2)}, u32[]{:S(2)}) collective-permute-start(bf16[144,512]{1,0:T(8,128)(2,1)S(1)} %shard_map.85.refs_7_), channel_id=1, source_target_pairs={{0,16},{1,3},{2,18},{3,1},{16,0},{17,19},{18,2},{19,17},{4,20},{5,... | collective-permute-start | bytes 442376 | tf_op jit(solution)/shard_map/ppermute | solution.py:51
  29.3 1.5 %collective-permute-start.11 = (f32[384,128]{1,0:T(8,128)S(1)}, f32[384,128]{1,0:T(8,128)S(1)}, u32[]{:S(2)}, u32[]{:S(2)}) collective-permute-start(f32[384,128]{1,0:T(8,128)S(1)} %shard_map.89.mine), channel_id=1, source_target_pairs={{0,1},{1,0},{2,3},{3,2},{4,5},{5,4},{6,7},{7,6},{8,9},{9,8},{10,11... | collective-permute-start | bytes 589832 | tf_op jit(solution)/shard_map/ppermute | solution.py:39
  31.3 4.3 %collective-permute-start.12 = (f32[136,128]{1,0:T(8,128)S(1)}, f32[136,128]{1,0:T(8,128)S(1)}, u32[]{:S(2)}, u32[]{:S(2)}) collective-permute-start(f32[136,128]{1,0:T(8,128)S(1)} %get-tuple-element.20), channel_id=1, source_target_pairs={{0,2},{1,9},{2,0},{3,11},{4,6},{5,13},{6,4},{7,15},{8,10},{9,1},{1... | collective-permute-start | bytes 208904 | tf_op jit(solution)/shard_map/ppermute | solution.py:51
  31.9 6.0 %collective-permute-start.15 = (f32[1,64,128]{2,1,0:T(8,128)S(1)}, f32[1,64,128]{2,1,0:T(8,128)S(1)}, u32[]{:S(2)}, u32[]{:S(2)}) collective-permute-start(f32[1,64,128]{2,1,0:T(8,128)S(1)} %get-tuple-element.22), channel_id=1, source_target_pairs={{0,8},{4,12},{8,0},{12,4},{1,9},{5,13},{9,1},{13,5},{2,10},{6,14},... | collective-permute-start | bytes 98312 | tf_op jit(solution)/shard_map/ppermute | solution.py:39
  35.7 6.0 %collective-permute-start.13 = (f32[136,128]{1,0:T(8,128)S(1)}, f32[136,128]{1,0:T(8,128)S(1)}, u32[]{:S(2)}, u32[]{:S(2)}) collective-permute-start(f32[136,128]{1,0:T(8,128)S(1)} %add.21), channel_id=1, source_target_pairs={{0,8},{1,5},{2,10},{3,7},{4,12},{5,1},{6,14},{7,3},{8,0},{9,13},{1... | collective-permute-start | bytes 208904 | tf_op jit(solution)/shard_map/ppermute | solution.py:51
  37.9 4.7 %collective-permute-start.16 = (f32[2,64,128]{2,1,0:T(8,128)S(1)}, f32[2,64,128]{2,1,0:T(8,128)S(1)}, u32[]{:S(2)}, u32[]{:S(2)}) collective-permute-start(f32[2,64,128]{2,1,0:T(8,128)S(1)} %pad_maximum_fusion.2), channel_id=1, source_target_pairs={{0,4},{4,0},{8,12},{12,8},{1,5},{5,1},{9,13},{13,9},{2,6},{6,2},{1... | collective-permute-start | bytes 196616 | tf_op jit(solution)/shard_map/ppermute | solution.py:39
  41.7 4.4 %collective-permute-start.14 = (f32[136,128]{1,0:T(8,128)S(1)}, f32[136,128]{1,0:T(8,128)S(1)}, u32[]{:S(2)}, u32[]{:S(2)}) collective-permute-start(f32[136,128]{1,0:T(8,128)S(1)} %add.22), channel_id=1, source_target_pairs={{0,4},{1,3},{2,6},{3,1},{4,0},{5,7},{6,2},{7,5},{8,12},{9,11},{10,... | collective-permute-start | bytes 208904 | tf_op jit(solution)/shard_map/ppermute | solution.py:51
  42.6 6.0 %collective-permute-start.17 = (f32[4,64,128]{2,1,0:T(8,128)S(1)}, f32[4,64,128]{2,1,0:T(8,128)S(1)}, u32[]{:S(2)}, u32[]{:S(2)}) collective-permute-start(f32[4,64,128]{2,1,0:T(8,128)S(1)} %pad_maximum_fusion.1), channel_id=1, source_target_pairs={{0,2},{2,0},{1,3},{3,1},{4,6},{6,4},{5,7},{7,5},{8,10},{10,8},{9,1... | collective-permute-start | bytes 393224 | tf_op jit(solution)/shard_map/ppermute | solution.py:39

commit v16 on v14

--- a/solution.py
+++ b/solution.py
@@ -282,12 +282,13 @@
         w_out = lax.all_gather(w_out, "dp", axis=0, tiled=True)
         return call(project_kernel, out_shape, [vmem()] * 6, (*xs, w_in, w_out))
 
-    part = width // 8
+    quarter = width // 4
+    part = quarter * 3 // 8
     shard = rin + rout
     q = lax.axis_index(PLANE)
     whole = jnp.concatenate([w_in, w_out], axis=0)
-    mine = lax.dynamic_slice(whole, (0, q * 2 * part), (shard, 2 * part))
-    opposite = lax.dynamic_slice(whole, (0, (q ^ 3) * 2 * part), (shard, 2 * part))
+    mine = lax.dynamic_slice(whole, (0, q * quarter), (shard, quarter))
+    opposite = lax.dynamic_slice(whole, (0, (q ^ 3) * quarter), (shard, quarter))
     operands = (*xs, w_in, w_out)
     *xs, w_in, w_out = call(
         functools.partial(load_kernel, 6),
@@ -332,15 +333,16 @@
     def stacked(p):
         return tuple((p, i * shard, k) for i, k in enumerate((2, 1, 3)))
 
+    rest = quarter - part
     acc = accumulate(
-        ((0, 0, part, stacked(0)), (0, part, part, stacked(1))), (za, zb), None)
+        ((0, 0, part, stacked(0)), (0, part, rest, stacked(1))), (za, zb), None)
     acc = accumulate(
         ((1, 0, part, stacked(0)), (2, 0, part, stacked(1))), (xa, ya), acc)
     return accumulate(
         (
-            (1, part, part, stacked(0)),
-            (2, part, part, stacked(1)),
-            (3, 0, 2 * part, ((2, 0, 2), (3, 0, 1), (3, shard, 3))),
+            (1, part, rest, stacked(0)),
+            (2, part, rest, stacked(1)),
+            (3, 0, quarter, ((2, 0, 2), (3, 0, 1), (3, shard, 3))),
         ),
         (xb, yb, far_op, near_op),
         acc,

time: 46.9 us -> 48.4 us (1.032)
  starting transfers between devices: 25.5 us -> 29.1 us
  waiting for transfers between devices: 11 us -> 8.76 us
    ppermute x10, starting transfers between devices: 15.2 us -> 18.6 us  [swap(): return lax.ppermute(x, axis, [(i, i ^ k) for i in range(count)])]
    ppermute x10, waiting for transfers between devices: 4.27 us -> 1.24 us  [swap(): return lax.ppermute(x, axis, [(i, i ^ k) for i in range(count)])]
    ppermute x7, waiting for transfers between devices: 6.72 us -> 7.51 us  [mixed(): return lax.ppermute(x, (*axes, 'mp'), pairs)]
  transfers between devices with their start and end apart: 17 -> 17, of which waited for: 10 -> 7; matrix products, arithmetic and copies ran while one was open for 0% -> 0% of each run, Pallas kernels for 13% -> 12%
where the time goes in v16:
time: 48.4 us; the launch traced here: 48.2 us
  starting transfers between devices  29.1 us (60%)
  waiting for transfers between devices  8.76 us (18%)
  Pallas kernels  8 us (17%)
  between operations  1.44 us (3%)
  other arithmetic  0.95 us (2%)
    ppermute x10, starting transfers between devices, swap(): return lax.ppermute(x, axis, [(i, i ^ k) for i in range(count)])  18.6 us
    ppermute x7, starting transfers between devices, mixed(): return lax.ppermute(x, (*axes, 'mp'), pairs)  10.4 us
    pallas_call x12, Pallas kernels, call(): pl.pallas_call(kernel, out_shape=out_shape, in_specs=in_specs, out_specs=...  8 us
    ppermute x7, waiting for transfers between devices, mixed(): return lax.ppermute(x, (*axes, 'mp'), pairs)  7.51 us
    ppermute x10, waiting for transfers between devices, swap(): return lax.ppermute(x, axis, [(i, i ^ k) for i in range(count)])  1.24 us
  transfers between devices with their start and end apart: 17, of which 7 were waited for; matrix products, arithmetic and copies ran while one was open for 0% of the time, Pallas kernels for 12%

profile of v16, /device:TPU:0, one launch (start us, length us, event | category | flops | bytes accessed | tf_op | source)
XLA Modules:
  0.0 48.2 jit_solution(18154783028527049079)
XLA Ops:
  0.0 0.9 %fusion = (bf16[48,1024]{1,0:T(8,128)(2,1)S(1)}, bf16[48,1024]{1,0:T(8,128)(2,1)S(1)}) fusion(s32[]{:T(128)S(6)} %select_n.7, bf16[32,4096]{1,0:T(8,128)(2,1)} %bitcast.6, bf16[16,4096]{1,0:T(8,128)(2,1)} %bitcast.12, s32[]{:T(128)S(6)} %select_n.6), kind=kLoop, calls=%fused_computation.6 | loop fusion | flops 393216 | bytes 589832 | tf_op jit(solution)/shard_map/concatenate | solution.py:289
  0.9 4.1 %collective-permute-start = (bf16[48,640]{1,0:T(8,128)(2,1)S(1)}, bf16[48,640]{1,0:T(8,128)(2,1)S(1)}, u32[]{:S(2)}, u32[]{:S(2)}) collective-permute-start(bf16[48,640]{1,0:T(8,128)(2,1)S(1)} %slice.8.refs_0_), channel_id=1, source_target_pairs={{0,8},{4,12},{8,0},{12,4},{1,9},{5,13},{9,1},{13,5},{2,10},{6,14},... | collective-permute-start | bytes 184328 | tf_op jit(solution)/shard_map/ppermute | solution.py:39
  5.0 0.1 collective-permute-start.6
  5.1 2.8 %collective-permute-start.4 = (bf16[48,1024]{1,0:T(8,128)(2,1)S(1)}, bf16[48,1024]{1,0:T(8,128)(2,1)S(1)}, u32[]{:S(2)}, u32[]{:S(2)}) collective-permute-start(bf16[48,1024]{1,0:T(8,128)(2,1)S(1)} %get-tuple-element.23.refs_0_), channel_id=1, source_target_pairs={{0,8},{4,12},{8,0},{12,4},{1,9},{5,13},{9,1},{13,5},{2,10},{6,14},... | collective-permute-start | bytes 294920 | tf_op jit(solution)/shard_map/ppermute | solution.py:39
  7.9 0.0 collective-permute-done.refs_1_.refs_0_
  8.0 4.1 %collective-permute-start.1 = (bf16[96,640]{1,0:T(8,128)(2,1)S(1)}, bf16[96,640]{1,0:T(8,128)(2,1)S(1)}, u32[]{:S(2)}, u32[]{:S(2)}) collective-permute-start(bf16[96,640]{1,0:T(8,128)(2,1)S(1)} %shard_map.83), channel_id=1, source_target_pairs={{0,4},{4,0},{8,12},{12,8},{1,5},{5,1},{9,13},{13,9},{2,6},{6,2},{1... | collective-permute-start | bytes 368648 | tf_op jit(solution)/shard_map/ppermute | solution.py:39
  12.1 2.3 %shard_map.82 = (bf16[128,4096]{1,0:T(8,128)(2,1)S(1)}, bf16[128,4096]{1,0:T(8,128)(2,1)S(1)}, bf16[128,4096]{1,0:T(8,128)(2,1)S(1)}, bf16[128,4096]{1,0:T(8,128...) custom-call(bf16[128,4096]{1,0:T(8,128)(2,1)} %bitcast.8, bf16[128,4096]{1,0:T(8,128)(2,1)} %bitcast.9, ...), custom_call_target="tpu_custom_call" | custom-call | flops 1073741824 | bytes 65536 | tf_op jit(solution)/shard_map/pallas_call | solution.py:27
  14.4 0.0 collective-permute-done.6.refs_1_.refs_0_
  14.4 0.1 collective-permute-start.7
  14.5 0.0 collective-permute-done.4.refs_1_.refs_8_
  14.5 2.1 %collective-permute-start.5 = (bf16[96,1024]{1,0:T(8,128)(2,1)S(1)}, bf16[96,1024]{1,0:T(8,128)(2,1)S(1)}, u32[]{:S(2)}, u32[]{:S(2)}) collective-permute-start(bf16[96,1024]{1,0:T(8,128)(2,1)S(1)} %shard_map.85), channel_id=1, source_target_pairs={{0,4},{4,0},{8,12},{12,8},{1,5},{5,1},{9,13},{13,9},{2,6},{6,2},{1... | collective-permute-start | bytes 589832 | tf_op jit(solution)/shard_map/ppermute | solution.py:39
  16.6 0.6 %collective-permute-done.1.refs_1_ = bf16[96,640]{1,0:T(8,128)(2,1)S(1)} collective-permute-done((bf16[96,640]{1,0:T(8,128)(2,1)S(1)}, bf16[96,640]{1,0:T(8,128)(2,1)S(1)}, u32[]{:S(2)}, u32[]{:S(2)}) %collective-permute-start.1) | collective-permute-done | bytes 122912 | tf_op jit(solution)/shard_map/ppermute | solution.py:39
  17.2 1.8 %collective-permute-start.2 = (bf16[144,640]{1,0:T(8,128)(2,1)S(1)}, bf16[144,640]{1,0:T(8,128)(2,1)S(1)}, u32[]{:S(2)}, u32[]{:S(2)}) collective-permute-start(bf16[144,640]{1,0:T(8,128)(2,1)S(1)} %shard_map.84.refs_7_), channel_id=1, source_target_pairs={{0,2},{1,17},{2,0},{3,19},{16,18},{17,1},{18,16},{19,3},{4,6},{5,2... | collective-permute-start | bytes 552968 | tf_op jit(solution)/shard_map/ppermute | solution.py:51
  18.9 1.5 %collective-permute-start.3 = (bf16[144,640]{1,0:T(8,128)(2,1)S(1)}, bf16[144,640]{1,0:T(8,128)(2,1)S(1)}, u32[]{:S(2)}, u32[]{:S(2)}) collective-permute-start(bf16[144,640]{1,0:T(8,128)(2,1)S(1)} %shard_map.84.refs_7_), channel_id=1, source_target_pairs={{0,16},{1,3},{2,18},{3,1},{16,0},{17,19},{18,2},{19,17},{4,20},{5,... | collective-permute-start | bytes 552968 | tf_op jit(solution)/shard_map/ppermute | solution.py:51
  20.4 0.0 collective-permute-done.7.refs_1_
  20.4 0.8 %collective-permute-start.8 = (bf16[144,384]{1,0:T(8,128)(2,1)S(1)}, bf16[144,384]{1,0:T(8,128)(2,1)S(1)}, u32[]{:S(2)}, u32[]{:S(2)}) collective-permute-start(bf16[144,384]{1,0:T(8,128)(2,1)S(1)} %shard_map.87.refs_6_), channel_id=1, source_target_pairs={{0,2},{1,17},{2,0},{3,19},{16,18},{17,1},{18,16},{19,3},{4,6},{5,2... | collective-permute-start | bytes 331784 | tf_op jit(solution)/shard_map/ppermute | solution.py:51
  21.3 1.5 %collective-permute-start.9 = (bf16[144,384]{1,0:T(8,128)(2,1)S(1)}, bf16[144,384]{1,0:T(8,128)(2,1)S(1)}, u32[]{:S(2)}, u32[]{:S(2)}) collective-permute-start(bf16[144,384]{1,0:T(8,128)(2,1)S(1)} %shard_map.87.refs_6_), channel_id=1, source_target_pairs={{0,16},{1,3},{2,18},{3,1},{16,0},{17,19},{18,2},{19,17},{4,20},{5,... | collective-permute-start | bytes 331784 | tf_op jit(solution)/shard_map/ppermute | solution.py:51
  22.8 0.6 %shard_map.88.refs_8_ = f32[384,128]{1,0:T(8,128)S(1)} custom-call(bf16[128,4096]{1,0:T(8,128)(2,1)S(1)} %get-tuple-element.14.refs_0_, bf16[128,4096]{1,0:T(8,128)(2,1)S(1)} %get-tuple-element.15.refs_1_, bf16[128,4096]{1,0:T(8,128)(2,1)S(1)} %get-tuple-element.16.refs_2_, bf16[128,4096]{1,0:T(8,128)(2,1)S(1)} %get-tuple-element.17.refs_3_, ...), custom_call_target="tpu_custom_call" | custom-call | flops 268435456 | bytes 65536 | tf_op jit(solution)/shard_map/pallas_call | solution.py:27
  23.4 3.3 %collective-permute-done.8.refs_6_ = bf16[144,384]{1,0:T(8,128)(2,1)S(1)} collective-permute-done((bf16[144,384]{1,0:T(8,128)(2,1)S(1)}, bf16[144,384]{1,0:T(8,128)(2,1)S(1)}, u32[]{:S(2)}, u32[]{:S(2)}) %collective-permute-start.8) | collective-permute-done | bytes 110624 | tf_op jit(solution)/shard_map/ppermute | solution.py:51
  26.7 0.0 collective-permute-done.9.refs_7_
  26.7 0.5 %shard_map.89.refs_10_ = f32[384,128]{1,0:T(8,128)S(1)} custom-call(bf16[128,4096]{1,0:T(8,128)(2,1)S(1)} %get-tuple-element.14.refs_0_, bf16[128,4096]{1,0:T(8,128)(2,1)S(1)} %get-tuple-element.15.refs_1_, bf16[128,4096]{1,0:T(8,128)(2,1)S(1)} %get-tuple-element.16.refs_2_, bf16[128,4096]{1,0:T(8,128)(2,1)S(1)} %get-tuple-element.17.refs_3_, ...), custom_call_target="tpu_custom_call" | custom-call | flops 268435456 | bytes 65536 | tf_op jit(solution)/shard_map/pallas_call | solution.py:27
  27.2 0.0 collective-permute-done.5.refs_9_
  27.2 0.0 collective-permute-done.2.refs_6_
  27.3 0.0 collective-permute-done.3.refs_7_
  27.3 1.0 %shard_map.90.mine = f32[384,128]{1,0:T(8,128)S(1)} custom-call(bf16[128,4096]{1,0:T(8,128)(2,1)S(1)} %get-tuple-element.14.refs_0_, bf16[128,4096]{1,0:T(8,128)(2,1)S(1)} %get-tuple-element.15.refs_1_, bf16[128,4096]{1,0:T(8,128)(2,1)S(1)} %get-tuple-element.16.refs_2_, bf16[128,4096]{1,0:T(8,128)(2,1)S(1)} %get-tuple-element.17.refs_3_, ...), custom_call_target="tpu_custom_call" | custom-call | flops 268435456 | bytes 65536 | tf_op jit(solution)/shard_map/pallas_call | solution.py:27
  28.2 0.1 collective-permute-start.10
  29.6 0.1 collective-permute-done.10.other
  29.7 0.5 shard_map.91
  30.2 1.5 %collective-permute-start.11 = (f32[136,128]{1,0:T(8,128)S(1)}, f32[136,128]{1,0:T(8,128)S(1)}, u32[]{:S(2)}, u32[]{:S(2)}) collective-permute-start(f32[136,128]{1,0:T(8,128)S(1)} %get-tuple-element.20), channel_id=1, source_target_pairs={{0,2},{1,9},{2,0},{3,11},{4,6},{5,13},{6,4},{7,15},{8,10},{9,1},{1... | collective-permute-start | bytes 208904 | tf_op jit(solution)/shard_map/ppermute | solution.py:51
  31.8 2.6 %collective-permute-start.14 = (f32[1,64,128]{2,1,0:T(8,128)S(1)}, f32[1,64,128]{2,1,0:T(8,128)S(1)}, u32[]{:S(2)}, u32[]{:S(2)}) collective-permute-start(f32[1,64,128]{2,1,0:T(8,128)S(1)} %get-tuple-element.22), channel_id=1, source_target_pairs={{0,8},{4,12},{8,0},{12,4},{1,9},{5,13},{9,1},{13,5},{2,10},{6,14},... | collective-permute-start | bytes 98312 | tf_op jit(solution)/shard_map/ppermute | solution.py:39
  34.4 0.2 collective-permute-done.11
  34.6 2.8 %collective-permute-start.12 = (f32[136,128]{1,0:T(8,128)S(1)}, f32[136,128]{1,0:T(8,128)S(1)}, u32[]{:S(2)}, u32[]{:S(2)}) collective-permute-start(f32[136,128]{1,0:T(8,128)S(1)} %add.21), channel_id=1, source_target_pairs={{0,8},{1,5},{2,10},{3,7},{4,12},{5,1},{6,14},{7,3},{8,0},{9,13},{1... | collective-permute-start | bytes 208904 | tf_op jit(solution)/shard_map/ppermute | solution.py:51
  37.4 0.0 collective-permute-done.14
  37.4 1.0 %collective-permute-start.15 = (f32[2,64,128]{2,1,0:T(8,128)S(1)}, f32[2,64,128]{2,1,0:T(8,128)S(1)}, u32[]{:S(2)}, u32[]{:S(2)}) collective-permute-start(f32[2,64,128]{2,1,0:T(8,128)S(1)} %pad_maximum_fusion.2), channel_id=1, source_target_pairs={{0,4},{4,0},{8,12},{12,8},{1,5},{5,1},{9,13},{13,9},{2,6},{6,2},{1... | collective-permute-start | bytes 196616 | tf_op jit(solution)/shard_map/ppermute | solution.py:39
  38.4 2.3 %collective-permute-done.12 = f32[136,128]{1,0:T(8,128)S(1)} collective-permute-done((f32[136,128]{1,0:T(8,128)S(1)}, f32[136,128]{1,0:T(8,128)S(1)}, u32[]{:S(2)}, u32[]{:S(2)}) %collective-permute-start.12) | collective-permute-done | bytes 69664 | tf_op jit(solution)/shard_map/ppermute | solution.py:51
  40.7 0.5 %collective-permute-start.13 = (f32[136,128]{1,0:T(8,128)S(1)}, f32[136,128]{1,0:T(8,128)S(1)}, u32[]{:S(2)}, u32[]{:S(2)}) collective-permute-start(f32[136,128]{1,0:T(8,128)S(1)} %add.22), channel_id=1, source_target_pairs={{0,4},{1,3},{2,6},{3,1},{4,0},{5,7},{6,2},{7,5},{8,12},{9,11},{10,... | collective-permute-start | bytes 208904 | tf_op jit(solution)/shard_map/ppermute | solution.py:51
  41.2 0.5 %collective-permute-done.15 = f32[2,64,128]{2,1,0:T(8,128)S(1)} collective-permute-done((f32[2,64,128]{2,1,0:T(8,128)S(1)}, f32[2,64,128]{2,1,0:T(8,128)S(1)}, u32[]{:S(2)}, u32[]{:S(2)}) %collective-permute-start.15) | collective-permute-done | bytes 65568 | tf_op jit(solution)/shard_map/ppermute | solution.py:39
  41.8 1.7 %collective-permute-start.16 = (f32[4,64,128]{2,1,0:T(8,128)S(1)}, f32[4,64,128]{2,1,0:T(8,128)S(1)}, u32[]{:S(2)}, u32[]{:S(2)}) collective-permute-start(f32[4,64,128]{2,1,0:T(8,128)S(1)} %pad_maximum_fusion.1), channel_id=1, source_target_pairs={{0,2},{2,0},{1,3},{3,1},{4,6},{6,4},{5,7},{7,5},{8,10},{10,8},{9,1... | collective-permute-start | bytes 393224 | tf_op jit(solution)/shard_map/ppermute | solution.py:39
  43.4 1.7 %collective-permute-done.13 = f32[136,128]{1,0:T(8,128)S(1)} collective-permute-done((f32[136,128]{1,0:T(8,128)S(1)}, f32[136,128]{1,0:T(8,128)S(1)}, u32[]{:S(2)}, u32[]{:S(2)}) %collective-permute-start.13) | collective-permute-done | bytes 69664 | tf_op jit(solution)/shard_map/ppermute | solution.py:51
  45.1 2.5 %shard_map.92.side_ref = f32[64,128]{1,0:T(8,128)S(1)} custom-call(f32[136,128]{1,0:T(8,128)S(1)} %add.23.fac_ref, f32[128,64]{1,0:T(8,128)S(1)} %get-tuple-element.21.gtr_ref), custom_call_target="tpu_custom_call" | custom-call | flops 4294967296 | bytes 65536 | tf_op jit(solution)/shard_map/pallas_call | solution.py:27
  47.6 0.0 collective-permute-done.16
  47.6 0.6 %shard_map.93 = f32[1,8]{1,0:T(1,128)} custom-call(f32[64,128]{1,0:T(8,128)S(1)} %shard_map.92.side_ref, f32[8,64,128]{2,1,0:T(8,128)S(1)} %pad_maximum_fusion.gte_ref), custom_call_target="tpu_custom_call" | custom-call | bytes 65536 | tf_op jit(solution)/shard_map/pallas_call | solution.py:27
  (13 shorter events, 0.1 us)
Async XLA Ops:
  0.9 7.0 %collective-permute-start = (bf16[48,640]{1,0:T(8,128)(2,1)S(1)}, bf16[48,640]{1,0:T(8,128)(2,1)S(1)}, u32[]{:S(2)}, u32[]{:S(2)}) collective-permute-start(bf16[48,640]{1,0:T(8,128)(2,1)S(1)} %slice.8.refs_0_), channel_id=1, source_target_pairs={{0,8},{4,12},{8,0},{12,4},{1,9},{5,13},{9,1},{13,5},{2,10},{6,14},... | collective-permute-start | bytes 184328 | tf_op jit(solution)/shard_map/ppermute | solution.py:39
  5.0 9.4 %collective-permute-start.6 = (bf16[48,384]{1,0:T(8,128)(2,1)S(1)}, bf16[48,384]{1,0:T(8,128)(2,1)S(1)}, u32[]{:S(2)}, u32[]{:S(2)}) collective-permute-start(bf16[48,384]{1,0:T(8,128)(2,1)S(1)} %slice.9.refs_0_), channel_id=1, source_target_pairs={{0,8},{4,12},{8,0},{12,4},{1,9},{5,13},{9,1},{13,5},{2,10},{6,14},... | collective-permute-start | bytes 110600 | tf_op jit(solution)/shard_map/ppermute | solution.py:39
  5.1 9.4 %collective-permute-start.4 = (bf16[48,1024]{1,0:T(8,128)(2,1)S(1)}, bf16[48,1024]{1,0:T(8,128)(2,1)S(1)}, u32[]{:S(2)}, u32[]{:S(2)}) collective-permute-start(bf16[48,1024]{1,0:T(8,128)(2,1)S(1)} %get-tuple-element.23.refs_0_), channel_id=1, source_target_pairs={{0,8},{4,12},{8,0},{12,4},{1,9},{5,13},{9,1},{13,5},{2,10},{6,14},... | collective-permute-start | bytes 294920 | tf_op jit(solution)/shard_map/ppermute | solution.py:39
  8.0 9.2 %collective-permute-start.1 = (bf16[96,640]{1,0:T(8,128)(2,1)S(1)}, bf16[96,640]{1,0:T(8,128)(2,1)S(1)}, u32[]{:S(2)}, u32[]{:S(2)}) collective-permute-start(bf16[96,640]{1,0:T(8,128)(2,1)S(1)} %shard_map.83), channel_id=1, source_target_pairs={{0,4},{4,0},{8,12},{12,8},{1,5},{5,1},{9,13},{13,9},{2,6},{6,2},{1... | collective-permute-start | bytes 368648 | tf_op jit(solution)/shard_map/ppermute | solution.py:39
  14.4 6.0 %collective-permute-start.7 = (bf16[96,384]{1,0:T(8,128)(2,1)S(1)}, bf16[96,384]{1,0:T(8,128)(2,1)S(1)}, u32[]{:S(2)}, u32[]{:S(2)}) collective-permute-start(bf16[96,384]{1,0:T(8,128)(2,1)S(1)} %shard_map.86), channel_id=1, source_target_pairs={{0,4},{4,0},{8,12},{12,8},{1,5},{5,1},{9,13},{13,9},{2,6},{6,2},{1... | collective-permute-start | bytes 221192 | tf_op jit(solution)/shard_map/ppermute | solution.py:39
  14.5 12.7 %collective-permute-start.5 = (bf16[96,1024]{1,0:T(8,128)(2,1)S(1)}, bf16[96,1024]{1,0:T(8,128)(2,1)S(1)}, u32[]{:S(2)}, u32[]{:S(2)}) collective-permute-start(bf16[96,1024]{1,0:T(8,128)(2,1)S(1)} %shard_map.85), channel_id=1, source_target_pairs={{0,4},{4,0},{8,12},{12,8},{1,5},{5,1},{9,13},{13,9},{2,6},{6,2},{1... | collective-permute-start | bytes 589832 | tf_op jit(solution)/shard_map/ppermute | solution.py:39
  17.2 10.1 %collective-permute-start.2 = (bf16[144,640]{1,0:T(8,128)(2,1)S(1)}, bf16[144,640]{1,0:T(8,128)(2,1)S(1)}, u32[]{:S(2)}, u32[]{:S(2)}) collective-permute-start(bf16[144,640]{1,0:T(8,128)(2,1)S(1)} %shard_map.84.refs_7_), channel_id=1, source_target_pairs={{0,2},{1,17},{2,0},{3,19},{16,18},{17,1},{18,16},{19,3},{4,6},{5,2... | collective-permute-start | bytes 552968 | tf_op jit(solution)/shard_map/ppermute | solution.py:51
  18.9 8.3 %collective-permute-start.3 = (bf16[144,640]{1,0:T(8,128)(2,1)S(1)}, bf16[144,640]{1,0:T(8,128)(2,1)S(1)}, u32[]{:S(2)}, u32[]{:S(2)}) collective-permute-start(bf16[144,640]{1,0:T(8,128)(2,1)S(1)} %shard_map.84.refs_7_), channel_id=1, source_target_pairs={{0,16},{1,3},{2,18},{3,1},{16,0},{17,19},{18,2},{19,17},{4,20},{5,... | collective-permute-start | bytes 552968 | tf_op jit(solution)/shard_map/ppermute | solution.py:51
  20.4 6.3 %collective-permute-start.8 = (bf16[144,384]{1,0:T(8,128)(2,1)S(1)}, bf16[144,384]{1,0:T(8,128)(2,1)S(1)}, u32[]{:S(2)}, u32[]{:S(2)}) collective-permute-start(bf16[144,384]{1,0:T(8,128)(2,1)S(1)} %shard_map.87.refs_6_), channel_id=1, source_target_pairs={{0,2},{1,17},{2,0},{3,19},{16,18},{17,1},{18,16},{19,3},{4,6},{5,2... | collective-permute-start | bytes 331784 | tf_op jit(solution)/shard_map/ppermute | solution.py:51
  21.3 5.5 %collective-permute-start.9 = (bf16[144,384]{1,0:T(8,128)(2,1)S(1)}, bf16[144,384]{1,0:T(8,128)(2,1)S(1)}, u32[]{:S(2)}, u32[]{:S(2)}) collective-permute-start(bf16[144,384]{1,0:T(8,128)(2,1)S(1)} %shard_map.87.refs_6_), channel_id=1, source_target_pairs={{0,16},{1,3},{2,18},{3,1},{16,0},{17,19},{18,2},{19,17},{4,20},{5,... | collective-permute-start | bytes 331784 | tf_op jit(solution)/shard_map/ppermute | solution.py:51
  28.2 1.5 %collective-permute-start.10 = (f32[384,128]{1,0:T(8,128)S(1)}, f32[384,128]{1,0:T(8,128)S(1)}, u32[]{:S(2)}, u32[]{:S(2)}) collective-permute-start(f32[384,128]{1,0:T(8,128)S(1)} %shard_map.90.mine), channel_id=1, source_target_pairs={{0,1},{1,0},{2,3},{3,2},{4,5},{5,4},{6,7},{7,6},{8,9},{9,8},{10,11... | collective-permute-start | bytes 589832 | tf_op jit(solution)/shard_map/ppermute | solution.py:39
  30.2 4.3 %collective-permute-start.11 = (f32[136,128]{1,0:T(8,128)S(1)}, f32[136,128]{1,0:T(8,128)S(1)}, u32[]{:S(2)}, u32[]{:S(2)}) collective-permute-start(f32[136,128]{1,0:T(8,128)S(1)} %get-tuple-element.20), channel_id=1, source_target_pairs={{0,2},{1,9},{2,0},{3,11},{4,6},{5,13},{6,4},{7,15},{8,10},{9,1},{1... | collective-permute-start | bytes 208904 | tf_op jit(solution)/shard_map/ppermute | solution.py:51
  31.8 5.6 %collective-permute-start.14 = (f32[1,64,128]{2,1,0:T(8,128)S(1)}, f32[1,64,128]{2,1,0:T(8,128)S(1)}, u32[]{:S(2)}, u32[]{:S(2)}) collective-permute-start(f32[1,64,128]{2,1,0:T(8,128)S(1)} %get-tuple-element.22), channel_id=1, source_target_pairs={{0,8},{4,12},{8,0},{12,4},{1,9},{5,13},{9,1},{13,5},{2,10},{6,14},... | collective-permute-start | bytes 98312 | tf_op jit(solution)/shard_map/ppermute | solution.py:39
  34.6 6.1 %collective-permute-start.12 = (f32[136,128]{1,0:T(8,128)S(1)}, f32[136,128]{1,0:T(8,128)S(1)}, u32[]{:S(2)}, u32[]{:S(2)}) collective-permute-start(f32[136,128]{1,0:T(8,128)S(1)} %add.21), channel_id=1, source_target_pairs={{0,8},{1,5},{2,10},{3,7},{4,12},{5,1},{6,14},{7,3},{8,0},{9,13},{1... | collective-permute-start | bytes 208904 | tf_op jit(solution)/shard_map/ppermute | solution.py:51
  37.4 4.4 %collective-permute-start.15 = (f32[2,64,128]{2,1,0:T(8,128)S(1)}, f32[2,64,128]{2,1,0:T(8,128)S(1)}, u32[]{:S(2)}, u32[]{:S(2)}) collective-permute-start(f32[2,64,128]{2,1,0:T(8,128)S(1)} %pad_maximum_fusion.2), channel_id=1, source_target_pairs={{0,4},{4,0},{8,12},{12,8},{1,5},{5,1},{9,13},{13,9},{2,6},{6,2},{1... | collective-permute-start | bytes 196616 | tf_op jit(solution)/shard_map/ppermute | solution.py:39
  40.7 4.4 %collective-permute-start.13 = (f32[136,128]{1,0:T(8,128)S(1)}, f32[136,128]{1,0:T(8,128)S(1)}, u32[]{:S(2)}, u32[]{:S(2)}) collective-permute-start(f32[136,128]{1,0:T(8,128)S(1)} %add.22), channel_id=1, source_target_pairs={{0,4},{1,3},{2,6},{3,1},{4,0},{5,7},{6,2},{7,5},{8,12},{9,11},{10,... | collective-permute-start | bytes 208904 | tf_op jit(solution)/shard_map/ppermute | solution.py:51
  41.8 5.8 %collective-permute-start.16 = (f32[4,64,128]{2,1,0:T(8,128)S(1)}, f32[4,64,128]{2,1,0:T(8,128)S(1)}, u32[]{:S(2)}, u32[]{:S(2)}) collective-permute-start(f32[4,64,128]{2,1,0:T(8,128)S(1)} %pad_maximum_fusion.1), channel_id=1, source_target_pairs={{0,2},{2,0},{1,3},{3,1},{4,6},{6,4},{5,7},{7,5},{8,10},{10,8},{9,1... | collective-permute-start | bytes 393224 | tf_op jit(solution)/shard_map/ppermute | solution.py:39

commit v17 on v14

--- a/solution.py
+++ b/solution.py
@@ -160,14 +160,18 @@
         lax.dot_general, dimension_numbers=TN, precision=HI,
         preferred_element_type=jnp.float32,
     )
-    c_in = dot(x_tr, x_tr)
+    products = jnp.dot(
+        x_tr.T, jnp.concatenate([x_tr, g_tr], axis=1), precision=HI,
+        preferred_element_type=jnp.float32,
+    )
+    c_in = products[:, :ki]
     c_out = dot(g_tr, g_tr)
     half = ki // 2
     fac_ref[:half, :] = c_in[:half, :]
     fac_ref[half:ki, :half] = c_in[half:, half:]
     fac_ref[half:ki, half:] = c_out
     fac_ref[ki:, :] = jnp.full((8, ki), n_tr.astype(jnp.float32))
-    grad_tr = dot(x_tr, g_tr) / n_tr.astype(jnp.float32)
+    grad_tr = products[:, ki:] / n_tr.astype(jnp.float32)
     grad_te = dot(x_te, g_te) / n_te.astype(jnp.float32)
     gtr_ref[...] = grad_tr
     gte_ref[0, :, :ko] = grad_te[:half]
@@ -375,7 +379,9 @@
             order += [(dz ^ k, db) if axis == "dp" else (dz, db ^ k) for dz, db in order]
     steps_z = [(k, 0) for k in bits(n_dp)]
     steps_x = [(0, k) for k in bits(n_blk)]
-    for step0, step1 in zip(steps_x + steps_z, steps_z + steps_x):
+    first = steps_x + steps_z[::-1]
+    second = steps_z[:1] + steps_x + steps_z[1:]
+    for step0, step1 in zip(first, second):
         fac = fac + mixed(fac, ("dp", "blk"), (n_dp, n_blk), step0, step1)
     side = call(
         side_kernel,

time: 46.9 us -> 47.2 us (level)
  waiting for transfers between devices: 11 us -> 12.9 us
  starting transfers between devices: 25.5 us -> 23.9 us
    ppermute x10, starting transfers between devices: 15.2 us -> 13.8 us  [swap(): return lax.ppermute(x, axis, [(i, i ^ k) for i in range(count)])]
    ppermute x10, waiting for transfers between devices: 4.27 us -> 5.64 us  [swap(): return lax.ppermute(x, axis, [(i, i ^ k) for i in range(count)])]
    ppermute x7, waiting for transfers between devices: 6.72 us -> 7.26 us  [mixed(): return lax.ppermute(x, (*axes, 'mp'), pairs)]
  transfers between devices with their start and end apart: 17 -> 17, of which waited for: 10 -> 12; matrix products, arithmetic and copies ran while one was open for 0% -> 0% of each run, Pallas kernels for 13% -> 13%
where the time goes in v17:
time: 47.2 us; the launch traced here: 47 us
  starting transfers between devices  23.9 us (51%)
  waiting for transfers between devices  12.9 us (27%)
  Pallas kernels  7.83 us (17%)
  between operations  1.41 us (3%)
  other arithmetic  0.95 us (2%)
    ppermute x10, starting transfers between devices, swap(): return lax.ppermute(x, axis, [(i, i ^ k) for i in range(count)])  13.8 us
    ppermute x7, starting transfers between devices, mixed(): return lax.ppermute(x, (*axes, 'mp'), pairs)  10.1 us
    pallas_call x12, Pallas kernels, call(): pl.pallas_call(kernel, out_shape=out_shape, in_specs=in_specs, out_specs=...  7.83 us
    ppermute x7, waiting for transfers between devices, mixed(): return lax.ppermute(x, (*axes, 'mp'), pairs)  7.26 us
    ppermute x10, waiting for transfers between devices, swap(): return lax.ppermute(x, axis, [(i, i ^ k) for i in range(count)])  5.64 us
  transfers between devices with their start and end apart: 17, of which 12 were waited for; matrix products, arithmetic and copies ran while one was open for 0% of the time, Pallas kernels for 13%

profile of v17, /device:TPU:0, one launch (start us, length us, event | category | flops | bytes accessed | tf_op | source)
XLA Modules:
  0.0 47.0 jit_solution(710708386582147639)
XLA Ops:
  0.0 0.9 %fusion = (bf16[48,1024]{1,0:T(8,128)(2,1)S(1)}, bf16[48,1024]{1,0:T(8,128)(2,1)S(1)}) fusion(s32[]{:T(128)S(6)} %select_n.7, bf16[32,4096]{1,0:T(8,128)(2,1)} %bitcast.6, bf16[16,4096]{1,0:T(8,128)(2,1)} %bitcast.12, s32[]{:T(128)S(6)} %select_n.6), kind=kLoop, calls=%fused_computation.6 | loop fusion | flops 393216 | bytes 589832 | tf_op jit(solution)/shard_map/concatenate | solution.py:292
  0.9 4.1 %collective-permute-start.6 = (bf16[48,512]{1,0:T(8,128)(2,1)S(1)}, bf16[48,512]{1,0:T(8,128)(2,1)S(1)}, u32[]{:S(2)}, u32[]{:S(2)}) collective-permute-start(bf16[48,512]{1,0:T(8,128)(2,1)S(1)} %get-tuple-element.25.refs_0_), channel_id=1, source_target_pairs={{0,8},{4,12},{8,0},{12,4},{1,9},{5,13},{9,1},{13,5},{2,10},{6,14},... | collective-permute-start | bytes 147464 | tf_op jit(solution)/shard_map/ppermute | solution.py:39
  5.0 0.1 collective-permute-start
  5.1 2.8 %collective-permute-start.4 = (bf16[48,1024]{1,0:T(8,128)(2,1)S(1)}, bf16[48,1024]{1,0:T(8,128)(2,1)S(1)}, u32[]{:S(2)}, u32[]{:S(2)}) collective-permute-start(bf16[48,1024]{1,0:T(8,128)(2,1)S(1)} %get-tuple-element.23.refs_0_), channel_id=1, source_target_pairs={{0,8},{4,12},{8,0},{12,4},{1,9},{5,13},{9,1},{13,5},{2,10},{6,14},... | collective-permute-start | bytes 294920 | tf_op jit(solution)/shard_map/ppermute | solution.py:39
  7.9 2.3 %shard_map.82 = (bf16[128,4096]{1,0:T(8,128)(2,1)S(1)}, bf16[128,4096]{1,0:T(8,128)(2,1)S(1)}, bf16[128,4096]{1,0:T(8,128)(2,1)S(1)}, bf16[128,4096]{1,0:T(8,128...) custom-call(bf16[128,4096]{1,0:T(8,128)(2,1)} %bitcast.8, bf16[128,4096]{1,0:T(8,128)(2,1)} %bitcast.9, ...), custom_call_target="tpu_custom_call" | custom-call | flops 1073741824 | bytes 65536 | tf_op jit(solution)/shard_map/pallas_call | solution.py:27
  10.3 0.0 collective-permute-done.6.refs_1_.refs_0_
  10.3 1.6 %collective-permute-start.7 = (bf16[96,512]{1,0:T(8,128)(2,1)S(1)}, bf16[96,512]{1,0:T(8,128)(2,1)S(1)}, u32[]{:S(2)}, u32[]{:S(2)}) collective-permute-start(bf16[96,512]{1,0:T(8,128)(2,1)S(1)} %shard_map.86), channel_id=1, source_target_pairs={{0,4},{4,0},{8,12},{12,8},{1,5},{5,1},{9,13},{13,9},{2,6},{6,2},{1... | collective-permute-start | bytes 294920 | tf_op jit(solution)/shard_map/ppermute | solution.py:39
  11.9 1.6 %collective-permute-done.refs_1_.refs_0_ = bf16[48,512]{1,0:T(8,128)(2,1)S(1)} collective-permute-done((bf16[48,512]{1,0:T(8,128)(2,1)S(1)}, bf16[48,512]{1,0:T(8,128)(2,1)S(1)}, u32[]{:S(2)}, u32[]{:S(2)}) %collective-permute-start) | collective-permute-done | bytes 49184 | tf_op jit(solution)/shard_map/ppermute | solution.py:39
  13.5 0.1 collective-permute-start.1
  13.6 1.2 %collective-permute-done.4.refs_1_.refs_8_ = bf16[48,1024]{1,0:T(8,128)(2,1)S(1)} collective-permute-done((bf16[48,1024]{1,0:T(8,128)(2,1)S(1)}, bf16[48,1024]{1,0:T(8,128)(2,1)S(1)}, u32[]{:S(2)}, u32[]{:S(2)}) %collective-permute-start.4) | collective-permute-done | bytes 98336 | tf_op jit(solution)/shard_map/ppermute | solution.py:39
  14.9 0.9 %collective-permute-start.5 = (bf16[96,1024]{1,0:T(8,128)(2,1)S(1)}, bf16[96,1024]{1,0:T(8,128)(2,1)S(1)}, u32[]{:S(2)}, u32[]{:S(2)}) collective-permute-start(bf16[96,1024]{1,0:T(8,128)(2,1)S(1)} %shard_map.85), channel_id=1, source_target_pairs={{0,4},{4,0},{8,12},{12,8},{1,5},{5,1},{9,13},{13,9},{2,6},{6,2},{1... | collective-permute-start | bytes 589832 | tf_op jit(solution)/shard_map/ppermute | solution.py:39
  15.7 1.3 %collective-permute-done.7.refs_1_ = bf16[96,512]{1,0:T(8,128)(2,1)S(1)} collective-permute-done((bf16[96,512]{1,0:T(8,128)(2,1)S(1)}, bf16[96,512]{1,0:T(8,128)(2,1)S(1)}, u32[]{:S(2)}, u32[]{:S(2)}) %collective-permute-start.7) | collective-permute-done | bytes 98336 | tf_op jit(solution)/shard_map/ppermute | solution.py:39
  17.0 1.6 %collective-permute-start.8 = (bf16[144,512]{1,0:T(8,128)(2,1)S(1)}, bf16[144,512]{1,0:T(8,128)(2,1)S(1)}, u32[]{:S(2)}, u32[]{:S(2)}) collective-permute-start(bf16[144,512]{1,0:T(8,128)(2,1)S(1)} %shard_map.87.refs_6_), channel_id=1, source_target_pairs={{0,2},{1,17},{2,0},{3,19},{16,18},{17,1},{18,16},{19,3},{4,6},{5,2... | collective-permute-start | bytes 442376 | tf_op jit(solution)/shard_map/ppermute | solution.py:51
  18.6 1.5 %collective-permute-start.9 = (bf16[144,512]{1,0:T(8,128)(2,1)S(1)}, bf16[144,512]{1,0:T(8,128)(2,1)S(1)}, u32[]{:S(2)}, u32[]{:S(2)}) collective-permute-start(bf16[144,512]{1,0:T(8,128)(2,1)S(1)} %shard_map.87.refs_6_), channel_id=1, source_target_pairs={{0,16},{1,3},{2,18},{3,1},{16,0},{17,19},{18,2},{19,17},{4,20},{5,... | collective-permute-start | bytes 442376 | tf_op jit(solution)/shard_map/ppermute | solution.py:51
  20.1 0.0 collective-permute-done.1.refs_1_
  20.1 0.8 %collective-permute-start.2 = (bf16[144,512]{1,0:T(8,128)(2,1)S(1)}, bf16[144,512]{1,0:T(8,128)(2,1)S(1)}, u32[]{:S(2)}, u32[]{:S(2)}) collective-permute-start(bf16[144,512]{1,0:T(8,128)(2,1)S(1)} %shard_map.84.refs_7_), channel_id=1, source_target_pairs={{0,2},{1,17},{2,0},{3,19},{16,18},{17,1},{18,16},{19,3},{4,6},{5,2... | collective-permute-start | bytes 442376 | tf_op jit(solution)/shard_map/ppermute | solution.py:51
  20.9 1.5 %collective-permute-start.3 = (bf16[144,512]{1,0:T(8,128)(2,1)S(1)}, bf16[144,512]{1,0:T(8,128)(2,1)S(1)}, u32[]{:S(2)}, u32[]{:S(2)}) collective-permute-start(bf16[144,512]{1,0:T(8,128)(2,1)S(1)} %shard_map.84.refs_7_), channel_id=1, source_target_pairs={{0,16},{1,3},{2,18},{3,1},{16,0},{17,19},{18,2},{19,17},{4,20},{5,... | collective-permute-start | bytes 442376 | tf_op jit(solution)/shard_map/ppermute | solution.py:51
  22.4 0.5 %shard_map.88.refs_8_ = f32[384,128]{1,0:T(8,128)S(1)} custom-call(bf16[128,4096]{1,0:T(8,128)(2,1)S(1)} %get-tuple-element.14.refs_0_, bf16[128,4096]{1,0:T(8,128)(2,1)S(1)} %get-tuple-element.15.refs_1_, bf16[128,4096]{1,0:T(8,128)(2,1)S(1)} %get-tuple-element.16.refs_2_, bf16[128,4096]{1,0:T(8,128)(2,1)S(1)} %get-tuple-element.17.refs_3_, ...), custom_call_target="tpu_custom_call" | custom-call | flops 268435456 | bytes 65536 | tf_op jit(solution)/shard_map/pallas_call | solution.py:27
  23.0 0.8 %collective-permute-done.8.refs_6_ = bf16[144,512]{1,0:T(8,128)(2,1)S(1)} collective-permute-done((bf16[144,512]{1,0:T(8,128)(2,1)S(1)}, bf16[144,512]{1,0:T(8,128)(2,1)S(1)}, u32[]{:S(2)}, u32[]{:S(2)}) %collective-permute-start.8) | collective-permute-done | bytes 147488 | tf_op jit(solution)/shard_map/ppermute | solution.py:51
  23.8 0.6 %collective-permute-done.9.refs_7_ = bf16[144,512]{1,0:T(8,128)(2,1)S(1)} collective-permute-done((bf16[144,512]{1,0:T(8,128)(2,1)S(1)}, bf16[144,512]{1,0:T(8,128)(2,1)S(1)}, u32[]{:S(2)}, u32[]{:S(2)}) %collective-permute-start.9) | collective-permute-done | bytes 147488 | tf_op jit(solution)/shard_map/ppermute | solution.py:51
  24.4 0.5 %shard_map.89.refs_10_ = f32[384,128]{1,0:T(8,128)S(1)} custom-call(bf16[128,4096]{1,0:T(8,128)(2,1)S(1)} %get-tuple-element.14.refs_0_, bf16[128,4096]{1,0:T(8,128)(2,1)S(1)} %get-tuple-element.15.refs_1_, bf16[128,4096]{1,0:T(8,128)(2,1)S(1)} %get-tuple-element.16.refs_2_, bf16[128,4096]{1,0:T(8,128)(2,1)S(1)} %get-tuple-element.17.refs_3_, ...), custom_call_target="tpu_custom_call" | custom-call | flops 268435456 | bytes 65536 | tf_op jit(solution)/shard_map/pallas_call | solution.py:27
  24.9 1.3 %collective-permute-done.2.refs_6_ = bf16[144,512]{1,0:T(8,128)(2,1)S(1)} collective-permute-done((bf16[144,512]{1,0:T(8,128)(2,1)S(1)}, bf16[144,512]{1,0:T(8,128)(2,1)S(1)}, u32[]{:S(2)}, u32[]{:S(2)}) %collective-permute-start.2) | collective-permute-done | bytes 147488 | tf_op jit(solution)/shard_map/ppermute | solution.py:51
  26.2 0.0 collective-permute-done.3.refs_7_
  26.2 0.0 collective-permute-done.5.refs_9_
  26.2 0.8 %shard_map.90.mine = f32[384,128]{1,0:T(8,128)S(1)} custom-call(bf16[128,4096]{1,0:T(8,128)(2,1)S(1)} %get-tuple-element.14.refs_0_, bf16[128,4096]{1,0:T(8,128)(2,1)S(1)} %get-tuple-element.15.refs_1_, bf16[128,4096]{1,0:T(8,128)(2,1)S(1)} %get-tuple-element.16.refs_2_, bf16[128,4096]{1,0:T(8,128)(2,1)S(1)} %get-tuple-element.17.refs_3_, ...), custom_call_target="tpu_custom_call" | custom-call | flops 268435456 | bytes 65536 | tf_op jit(solution)/shard_map/pallas_call | solution.py:27
  27.1 0.1 collective-permute-start.10
  28.4 0.1 collective-permute-done.10.other
  28.6 0.5 %shard_map.91 = (f32[136,128]{1,0:T(8,128)S(1)}, f32[1,64,128]{2,1,0:T(8,128)S(1)}, f32[128,64]{1,0:T(8,128)S(1)}) custom-call(s32[1]{0:T(128)S(6)} %copy.9.len_tr, s32[1]{0:T(128)S(6)} %copy.10.len_te, f32[384,128]{1,0:T(8,128)S(1)} %shard_map.90.mine, f32[384,128]{1,0:T(8,128)S(1)} %collective-permute-done.10.other), custom_call_target="tpu_custom_call" | custom-call | bytes 65536 | tf_op jit(solution)/shard_map/pallas_call | solution.py:27
  29.1 1.6 %collective-permute-start.11 = (f32[136,128]{1,0:T(8,128)S(1)}, f32[136,128]{1,0:T(8,128)S(1)}, u32[]{:S(2)}, u32[]{:S(2)}) collective-permute-start(f32[136,128]{1,0:T(8,128)S(1)} %get-tuple-element.20), channel_id=1, source_target_pairs={{0,2},{1,9},{2,0},{3,11},{4,6},{5,13},{6,4},{7,15},{8,10},{9,1},{1... | collective-permute-start | bytes 208904 | tf_op jit(solution)/shard_map/ppermute | solution.py:51
  30.6 2.0 %collective-permute-start.14 = (f32[1,64,128]{2,1,0:T(8,128)S(1)}, f32[1,64,128]{2,1,0:T(8,128)S(1)}, u32[]{:S(2)}, u32[]{:S(2)}) collective-permute-start(f32[1,64,128]{2,1,0:T(8,128)S(1)} %get-tuple-element.22), channel_id=1, source_target_pairs={{0,8},{4,12},{8,0},{12,4},{1,9},{5,13},{9,1},{13,5},{2,10},{6,14},... | collective-permute-start | bytes 98312 | tf_op jit(solution)/shard_map/ppermute | solution.py:39
  32.7 0.8 %collective-permute-done.11 = f32[136,128]{1,0:T(8,128)S(1)} collective-permute-done((f32[136,128]{1,0:T(8,128)S(1)}, f32[136,128]{1,0:T(8,128)S(1)}, u32[]{:S(2)}, u32[]{:S(2)}) %collective-permute-start.11) | collective-permute-done | bytes 69664 | tf_op jit(solution)/shard_map/ppermute | solution.py:51
  33.4 1.1 %collective-permute-start.12 = (f32[136,128]{1,0:T(8,128)S(1)}, f32[136,128]{1,0:T(8,128)S(1)}, u32[]{:S(2)}, u32[]{:S(2)}) collective-permute-start(f32[136,128]{1,0:T(8,128)S(1)} %add.21), channel_id=1, source_target_pairs={{0,4},{1,3},{2,6},{3,1},{4,0},{5,7},{6,2},{7,5},{8,12},{9,11},{10,... | collective-permute-start | bytes 208904 | tf_op jit(solution)/shard_map/ppermute | solution.py:51
  34.5 1.0 %collective-permute-done.14 = f32[1,64,128]{2,1,0:T(8,128)S(1)} collective-permute-done((f32[1,64,128]{2,1,0:T(8,128)S(1)}, f32[1,64,128]{2,1,0:T(8,128)S(1)}, u32[]{:S(2)}, u32[]{:S(2)}) %collective-permute-start.14) | collective-permute-done | bytes 32800 | tf_op jit(solution)/shard_map/ppermute | solution.py:39
  35.5 0.9 %collective-permute-start.15 = (f32[2,64,128]{2,1,0:T(8,128)S(1)}, f32[2,64,128]{2,1,0:T(8,128)S(1)}, u32[]{:S(2)}, u32[]{:S(2)}) collective-permute-start(f32[2,64,128]{2,1,0:T(8,128)S(1)} %pad_maximum_fusion.2), channel_id=1, source_target_pairs={{0,4},{4,0},{8,12},{12,8},{1,5},{5,1},{9,13},{13,9},{2,6},{6,2},{1... | collective-permute-start | bytes 196616 | tf_op jit(solution)/shard_map/ppermute | solution.py:39
  36.4 1.4 %collective-permute-done.12 = f32[136,128]{1,0:T(8,128)S(1)} collective-permute-done((f32[136,128]{1,0:T(8,128)S(1)}, f32[136,128]{1,0:T(8,128)S(1)}, u32[]{:S(2)}, u32[]{:S(2)}) %collective-permute-start.12) | collective-permute-done | bytes 69664 | tf_op jit(solution)/shard_map/ppermute | solution.py:51
  37.8 2.1 %collective-permute-start.13 = (f32[136,128]{1,0:T(8,128)S(1)}, f32[136,128]{1,0:T(8,128)S(1)}, u32[]{:S(2)}, u32[]{:S(2)}) collective-permute-start(f32[136,128]{1,0:T(8,128)S(1)} %add.22), channel_id=1, source_target_pairs={{0,8},{1,5},{2,10},{3,7},{4,12},{5,1},{6,14},{7,3},{8,0},{9,13},{1... | collective-permute-start | bytes 208904 | tf_op jit(solution)/shard_map/ppermute | solution.py:51
  39.9 0.4 collective-permute-done.15
  40.4 1.2 %collective-permute-start.16 = (f32[4,64,128]{2,1,0:T(8,128)S(1)}, f32[4,64,128]{2,1,0:T(8,128)S(1)}, u32[]{:S(2)}, u32[]{:S(2)}) collective-permute-start(f32[4,64,128]{2,1,0:T(8,128)S(1)} %pad_maximum_fusion.1), channel_id=1, source_target_pairs={{0,2},{2,0},{1,3},{3,1},{4,6},{6,4},{5,7},{7,5},{8,10},{10,8},{9,1... | collective-permute-start | bytes 393224 | tf_op jit(solution)/shard_map/ppermute | solution.py:39
  41.5 2.3 %collective-permute-done.13 = f32[136,128]{1,0:T(8,128)S(1)} collective-permute-done((f32[136,128]{1,0:T(8,128)S(1)}, f32[136,128]{1,0:T(8,128)S(1)}, u32[]{:S(2)}, u32[]{:S(2)}) %collective-permute-start.13) | collective-permute-done | bytes 69664 | tf_op jit(solution)/shard_map/ppermute | solution.py:51
  43.9 2.5 %shard_map.92.side_ref = f32[64,128]{1,0:T(8,128)S(1)} custom-call(f32[136,128]{1,0:T(8,128)S(1)} %add.23.fac_ref, f32[128,64]{1,0:T(8,128)S(1)} %get-tuple-element.21.gtr_ref), custom_call_target="tpu_custom_call" | custom-call | flops 4294967296 | bytes 65536 | tf_op jit(solution)/shard_map/pallas_call | solution.py:27
  46.3 0.0 collective-permute-done.16
  46.4 0.6 %shard_map.93 = f32[1,8]{1,0:T(1,128)} custom-call(f32[64,128]{1,0:T(8,128)S(1)} %shard_map.92.side_ref, f32[8,64,128]{2,1,0:T(8,128)S(1)} %pad_maximum_fusion.gte_ref), custom_call_target="tpu_custom_call" | custom-call | bytes 65536 | tf_op jit(solution)/shard_map/pallas_call | solution.py:27
  (12 shorter events, 0.1 us)
Async XLA Ops:
  0.9 9.3 %collective-permute-start.6 = (bf16[48,512]{1,0:T(8,128)(2,1)S(1)}, bf16[48,512]{1,0:T(8,128)(2,1)S(1)}, u32[]{:S(2)}, u32[]{:S(2)}) collective-permute-start(bf16[48,512]{1,0:T(8,128)(2,1)S(1)} %get-tuple-element.25.refs_0_), channel_id=1, source_target_pairs={{0,8},{4,12},{8,0},{12,4},{1,9},{5,13},{9,1},{13,5},{2,10},{6,14},... | collective-permute-start | bytes 147464 | tf_op jit(solution)/shard_map/ppermute | solution.py:39
  5.0 8.5 %collective-permute-start = (bf16[48,512]{1,0:T(8,128)(2,1)S(1)}, bf16[48,512]{1,0:T(8,128)(2,1)S(1)}, u32[]{:S(2)}, u32[]{:S(2)}) collective-permute-start(bf16[48,512]{1,0:T(8,128)(2,1)S(1)} %get-tuple-element.26.refs_0_), channel_id=1, source_target_pairs={{0,8},{4,12},{8,0},{12,4},{1,9},{5,13},{9,1},{13,5},{2,10},{6,14},... | collective-permute-start | bytes 147464 | tf_op jit(solution)/shard_map/ppermute | solution.py:39
  5.1 9.8 %collective-permute-start.4 = (bf16[48,1024]{1,0:T(8,128)(2,1)S(1)}, bf16[48,1024]{1,0:T(8,128)(2,1)S(1)}, u32[]{:S(2)}, u32[]{:S(2)}) collective-permute-start(bf16[48,1024]{1,0:T(8,128)(2,1)S(1)} %get-tuple-element.23.refs_0_), channel_id=1, source_target_pairs={{0,8},{4,12},{8,0},{12,4},{1,9},{5,13},{9,1},{13,5},{2,10},{6,14},... | collective-permute-start | bytes 294920 | tf_op jit(solution)/shard_map/ppermute | solution.py:39
  10.3 6.7 %collective-permute-start.7 = (bf16[96,512]{1,0:T(8,128)(2,1)S(1)}, bf16[96,512]{1,0:T(8,128)(2,1)S(1)}, u32[]{:S(2)}, u32[]{:S(2)}) collective-permute-start(bf16[96,512]{1,0:T(8,128)(2,1)S(1)} %shard_map.86), channel_id=1, source_target_pairs={{0,4},{4,0},{8,12},{12,8},{1,5},{5,1},{9,13},{13,9},{2,6},{6,2},{1... | collective-permute-start | bytes 294920 | tf_op jit(solution)/shard_map/ppermute | solution.py:39
  13.5 6.6 %collective-permute-start.1 = (bf16[96,512]{1,0:T(8,128)(2,1)S(1)}, bf16[96,512]{1,0:T(8,128)(2,1)S(1)}, u32[]{:S(2)}, u32[]{:S(2)}) collective-permute-start(bf16[96,512]{1,0:T(8,128)(2,1)S(1)} %shard_map.83), channel_id=1, source_target_pairs={{0,4},{4,0},{8,12},{12,8},{1,5},{5,1},{9,13},{13,9},{2,6},{6,2},{1... | collective-permute-start | bytes 294920 | tf_op jit(solution)/shard_map/ppermute | solution.py:39
  14.9 11.4 %collective-permute-start.5 = (bf16[96,1024]{1,0:T(8,128)(2,1)S(1)}, bf16[96,1024]{1,0:T(8,128)(2,1)S(1)}, u32[]{:S(2)}, u32[]{:S(2)}) collective-permute-start(bf16[96,1024]{1,0:T(8,128)(2,1)S(1)} %shard_map.85), channel_id=1, source_target_pairs={{0,4},{4,0},{8,12},{12,8},{1,5},{5,1},{9,13},{13,9},{2,6},{6,2},{1... | collective-permute-start | bytes 589832 | tf_op jit(solution)/shard_map/ppermute | solution.py:39
  17.0 6.7 %collective-permute-start.8 = (bf16[144,512]{1,0:T(8,128)(2,1)S(1)}, bf16[144,512]{1,0:T(8,128)(2,1)S(1)}, u32[]{:S(2)}, u32[]{:S(2)}) collective-permute-start(bf16[144,512]{1,0:T(8,128)(2,1)S(1)} %shard_map.87.refs_6_), channel_id=1, source_target_pairs={{0,2},{1,17},{2,0},{3,19},{16,18},{17,1},{18,16},{19,3},{4,6},{5,2... | collective-permute-start | bytes 442376 | tf_op jit(solution)/shard_map/ppermute | solution.py:51
  18.6 5.8 %collective-permute-start.9 = (bf16[144,512]{1,0:T(8,128)(2,1)S(1)}, bf16[144,512]{1,0:T(8,128)(2,1)S(1)}, u32[]{:S(2)}, u32[]{:S(2)}) collective-permute-start(bf16[144,512]{1,0:T(8,128)(2,1)S(1)} %shard_map.87.refs_6_), channel_id=1, source_target_pairs={{0,16},{1,3},{2,18},{3,1},{16,0},{17,19},{18,2},{19,17},{4,20},{5,... | collective-permute-start | bytes 442376 | tf_op jit(solution)/shard_map/ppermute | solution.py:51
  20.1 6.1 %collective-permute-start.2 = (bf16[144,512]{1,0:T(8,128)(2,1)S(1)}, bf16[144,512]{1,0:T(8,128)(2,1)S(1)}, u32[]{:S(2)}, u32[]{:S(2)}) collective-permute-start(bf16[144,512]{1,0:T(8,128)(2,1)S(1)} %shard_map.84.refs_7_), channel_id=1, source_target_pairs={{0,2},{1,17},{2,0},{3,19},{16,18},{17,1},{18,16},{19,3},{4,6},{5,2... | collective-permute-start | bytes 442376 | tf_op jit(solution)/shard_map/ppermute | solution.py:51
  20.9 5.3 %collective-permute-start.3 = (bf16[144,512]{1,0:T(8,128)(2,1)S(1)}, bf16[144,512]{1,0:T(8,128)(2,1)S(1)}, u32[]{:S(2)}, u32[]{:S(2)}) collective-permute-start(bf16[144,512]{1,0:T(8,128)(2,1)S(1)} %shard_map.84.refs_7_), channel_id=1, source_target_pairs={{0,16},{1,3},{2,18},{3,1},{16,0},{17,19},{18,2},{19,17},{4,20},{5,... | collective-permute-start | bytes 442376 | tf_op jit(solution)/shard_map/ppermute | solution.py:51
  27.1 1.5 %collective-permute-start.10 = (f32[384,128]{1,0:T(8,128)S(1)}, f32[384,128]{1,0:T(8,128)S(1)}, u32[]{:S(2)}, u32[]{:S(2)}) collective-permute-start(f32[384,128]{1,0:T(8,128)S(1)} %shard_map.90.mine), channel_id=1, source_target_pairs={{0,1},{1,0},{2,3},{3,2},{4,5},{5,4},{6,7},{7,6},{8,9},{9,8},{10,11... | collective-permute-start | bytes 589832 | tf_op jit(solution)/shard_map/ppermute | solution.py:39
  29.1 4.4 %collective-permute-start.11 = (f32[136,128]{1,0:T(8,128)S(1)}, f32[136,128]{1,0:T(8,128)S(1)}, u32[]{:S(2)}, u32[]{:S(2)}) collective-permute-start(f32[136,128]{1,0:T(8,128)S(1)} %get-tuple-element.20), channel_id=1, source_target_pairs={{0,2},{1,9},{2,0},{3,11},{4,6},{5,13},{6,4},{7,15},{8,10},{9,1},{1... | collective-permute-start | bytes 208904 | tf_op jit(solution)/shard_map/ppermute | solution.py:51
  30.6 4.9 %collective-permute-start.14 = (f32[1,64,128]{2,1,0:T(8,128)S(1)}, f32[1,64,128]{2,1,0:T(8,128)S(1)}, u32[]{:S(2)}, u32[]{:S(2)}) collective-permute-start(f32[1,64,128]{2,1,0:T(8,128)S(1)} %get-tuple-element.22), channel_id=1, source_target_pairs={{0,8},{4,12},{8,0},{12,4},{1,9},{5,13},{9,1},{13,5},{2,10},{6,14},... | collective-permute-start | bytes 98312 | tf_op jit(solution)/shard_map/ppermute | solution.py:39
  33.4 4.4 %collective-permute-start.12 = (f32[136,128]{1,0:T(8,128)S(1)}, f32[136,128]{1,0:T(8,128)S(1)}, u32[]{:S(2)}, u32[]{:S(2)}) collective-permute-start(f32[136,128]{1,0:T(8,128)S(1)} %add.21), channel_id=1, source_target_pairs={{0,4},{1,3},{2,6},{3,1},{4,0},{5,7},{6,2},{7,5},{8,12},{9,11},{10,... | collective-permute-start | bytes 208904 | tf_op jit(solution)/shard_map/ppermute | solution.py:51
  35.5 4.9 %collective-permute-start.15 = (f32[2,64,128]{2,1,0:T(8,128)S(1)}, f32[2,64,128]{2,1,0:T(8,128)S(1)}, u32[]{:S(2)}, u32[]{:S(2)}) collective-permute-start(f32[2,64,128]{2,1,0:T(8,128)S(1)} %pad_maximum_fusion.2), channel_id=1, source_target_pairs={{0,4},{4,0},{8,12},{12,8},{1,5},{5,1},{9,13},{13,9},{2,6},{6,2},{1... | collective-permute-start | bytes 196616 | tf_op jit(solution)/shard_map/ppermute | solution.py:39
  37.8 6.0 %collective-permute-start.13 = (f32[136,128]{1,0:T(8,128)S(1)}, f32[136,128]{1,0:T(8,128)S(1)}, u32[]{:S(2)}, u32[]{:S(2)}) collective-permute-start(f32[136,128]{1,0:T(8,128)S(1)} %add.22), channel_id=1, source_target_pairs={{0,8},{1,5},{2,10},{3,7},{4,12},{5,1},{6,14},{7,3},{8,0},{9,13},{1... | collective-permute-start | bytes 208904 | tf_op jit(solution)/shard_map/ppermute | solution.py:51
  40.4 6.0 %collective-permute-start.16 = (f32[4,64,128]{2,1,0:T(8,128)S(1)}, f32[4,64,128]{2,1,0:T(8,128)S(1)}, u32[]{:S(2)}, u32[]{:S(2)}) collective-permute-start(f32[4,64,128]{2,1,0:T(8,128)S(1)} %pad_maximum_fusion.1), channel_id=1, source_target_pairs={{0,2},{2,0},{1,3},{3,1},{4,6},{6,4},{5,7},{7,5},{8,10},{10,8},{9,1... | collective-permute-start | bytes 393224 | tf_op jit(solution)/shard_map/ppermute | solution.py:39

commit v18 on v17

--- a/solution.py
+++ b/solution.py
@@ -248,28 +248,33 @@
     return result
 
 
-def side_kernel(fac_ref, gtr_ref, out_ref):
+def side_kernel(fac_ref, other_ref, gtr_ref, out_ref):
     ki = fac_ref.shape[1]
     half = ki // 2
-    top = fac_ref[:half, :]
-    low = fac_ref[half:ki, :]
+    total = jnp.where(lax.axis_index("mp") == 1, fac_ref[...], other_ref[...])
+    top = total[:half]
+    low = total[half:ki]
     c_in = jnp.concatenate(
         [top, jnp.concatenate([top[:, half:].T, low[:, :half]], axis=1)], axis=0
     )
-    count = fac_ref[ki : ki + 1, :1]
+    count = total[ki : ki + 1, :1]
     inv_in, inv_out = inverses([c_in, wide(low[:, half:], half)])
     side = mm3(mm3(inv_in, right(gtr_ref[...])), right(inv_out)) * (count * count)
     out_ref[:, :half] = side[:half, :half]
     out_ref[:, half:] = side[half:, :half]
 
 
-def scores_kernel(order, n_blk, side_ref, gte_ref, out_ref):
+def scores_kernel(order, n_blk, side_ref, gte_ref, other_ref, out_ref):
     z = lax.axis_index("dp")
     b = lax.axis_index("blk")
     lane = lax.broadcasted_iota(jnp.int32, out_ref.shape, 1)
     row = jnp.zeros(out_ref.shape, jnp.float32)
     side = side_ref[...]
-    sums = [jnp.sum(side * gte_ref[p], axis=0, keepdims=True) for p in range(len(order))]
+    own = lax.axis_index("mp") == 0
+    sums = [
+        jnp.sum(side * jnp.where(own, gte_ref[p], other_ref[p]), axis=0, keepdims=True)
+        for p in range(len(order))
+    ]
     values = jnp.sum(jnp.concatenate(sums, axis=0), axis=1, keepdims=True)
     for p, (dz, db) in enumerate(order):
         row = jnp.where(lane == (z ^ dz) * n_blk + (b ^ db), values[p : p + 1, :], row)
@@ -372,29 +377,29 @@
         [smem(), smem(), vmem(), vmem()],
         (train_lengths, test_lengths, part, other),
     )
-    order = [(0, 0)]
-    for axis, count in (("dp", n_dp), ("blk", n_blk)):
-        for k in bits(count):
-            gte = jnp.concatenate([gte, swap(gte, axis, count, k)], axis=0)
-            order += [(dz ^ k, db) if axis == "dp" else (dz, db ^ k) for dz, db in order]
     steps_z = [(k, 0) for k in bits(n_dp)]
     steps_x = [(0, k) for k in bits(n_blk)]
-    first = steps_x + steps_z[::-1]
-    second = steps_z[:1] + steps_x + steps_z[1:]
-    for step0, step1 in zip(first, second):
-        fac = fac + mixed(fac, ("dp", "blk"), (n_dp, n_blk), step0, step1)
+    axes, counts, stay = ("dp", "blk"), (n_dp, n_blk), (0, 0)
+    order = [(0, 0)]
+    for step in steps_z + steps_x:
+        gte = jnp.concatenate([gte, mixed(gte, axes, counts, step, stay)], axis=0)
+        order += [(dz ^ step[0], db ^ step[1]) for dz, db in order]
+    for step in steps_x + steps_z:
+        fac = fac + mixed(fac, axes, counts, stay, step)
+    fac_other = swap(fac, "mp", 2, 1)
+    gte_other = swap(gte, "mp", 2, 1)
     side = call(
         side_kernel,
         jax.ShapeDtypeStruct((ki // 2, ki), jnp.float32),
-        [vmem()] * 2,
-        (fac, gtr),
+        [vmem()] * 3,
+        (fac, fac_other, gtr),
         flops=4 << 30,
     )
     return call(
         functools.partial(scores_kernel, order, n_blk),
         jax.ShapeDtypeStruct((1, n_dp * n_blk), jnp.float32),
-        [vmem()] * 2,
-        (side, gte),
+        [vmem()] * 3,
+        (side, gte, gte_other),
     )
 
 

time: 47.2 us -> 52.4 us (1.11)
  starting transfers between devices: 23.9 us -> 28.4 us
    ppermute x7 -> x10, starting transfers between devices: 10.1 us -> 17.5 us  [mixed(): return lax.ppermute(x, (*axes, 'mp'), pairs)]
    ppermute x10 -> x9, starting transfers between devices: 13.8 us -> 10.9 us  [swap(): return lax.ppermute(x, axis, [(i, i ^ k) for i in range(count)])]
    ppermute x7 -> x10, waiting for transfers between devices: 7.26 us -> 9.03 us  [mixed(): return lax.ppermute(x, (*axes, 'mp'), pairs)]
    ppermute x10 -> x9, waiting for transfers between devices: 5.64 us -> 4.27 us  [swap(): return lax.ppermute(x, axis, [(i, i ^ k) for i in range(count)])]
  transfers between devices with their start and end apart: 17 -> 19, of which waited for: 12 -> 10; matrix products, arithmetic and copies ran while one was open for 0% -> 0% of each run, Pallas kernels for 13% -> 11%
where the time goes in v18:
time: 52.4 us; the launch traced here: 52.1 us
  starting transfers between devices  28.4 us (54%)
  waiting for transfers between devices  13.3 us (25%)
  Pallas kernels  7.86 us (15%)
  between operations  1.53 us (3%)
  other arithmetic  0.94 us (2%)
    ppermute x10, starting transfers between devices, mixed(): return lax.ppermute(x, (*axes, 'mp'), pairs)  17.5 us
    ppermute x9, starting transfers between devices, swap(): return lax.ppermute(x, axis, [(i, i ^ k) for i in range(count)])  10.9 us
    ppermute x10, waiting for transfers between devices, mixed(): return lax.ppermute(x, (*axes, 'mp'), pairs)  9.03 us
    pallas_call x12, Pallas kernels, call(): pl.pallas_call(kernel, out_shape=out_shape, in_specs=in_specs, out_specs=...  7.86 us
    ppermute x9, waiting for transfers between devices, swap(): return lax.ppermute(x, axis, [(i, i ^ k) for i in range(count)])  4.27 us
  transfers between devices with their start and end apart: 19, of which 10 were waited for; matrix products, arithmetic and copies ran while one was open for 0% of the time, Pallas kernels for 11%

profile of v18, /device:TPU:0, one launch (start us, length us, event | category | flops | bytes accessed | tf_op | source)
XLA Modules:
  0.0 52.1 jit_solution(17157819532510647360)
XLA Ops:
  0.0 0.9 %fusion = (bf16[48,1024]{1,0:T(8,128)(2,1)S(1)}, bf16[48,1024]{1,0:T(8,128)(2,1)S(1)}) fusion(s32[]{:T(128)S(6)} %select_n.7, bf16[32,4096]{1,0:T(8,128)(2,1)} %bitcast.6, bf16[16,4096]{1,0:T(8,128)(2,1)} %bitcast.12, s32[]{:T(128)S(6)} %select_n.6), kind=kLoop, calls=%fused_computation.5 | loop fusion | flops 393216 | bytes 589832 | tf_op jit(solution)/shard_map/concatenate | solution.py:297
  0.9 4.1 %collective-permute-start.6 = (bf16[48,512]{1,0:T(8,128)(2,1)S(1)}, bf16[48,512]{1,0:T(8,128)(2,1)S(1)}, u32[]{:S(2)}, u32[]{:S(2)}) collective-permute-start(bf16[48,512]{1,0:T(8,128)(2,1)S(1)} %get-tuple-element.25.refs_0_), channel_id=1, source_target_pairs={{0,8},{4,12},{8,0},{12,4},{1,9},{5,13},{9,1},{13,5},{2,10},{6,14},... | collective-permute-start | bytes 147464 | tf_op jit(solution)/shard_map/ppermute | solution.py:39
  5.0 0.1 collective-permute-start
  5.1 2.8 %collective-permute-start.4 = (bf16[48,1024]{1,0:T(8,128)(2,1)S(1)}, bf16[48,1024]{1,0:T(8,128)(2,1)S(1)}, u32[]{:S(2)}, u32[]{:S(2)}) collective-permute-start(bf16[48,1024]{1,0:T(8,128)(2,1)S(1)} %get-tuple-element.23.refs_0_), channel_id=1, source_target_pairs={{0,8},{4,12},{8,0},{12,4},{1,9},{5,13},{9,1},{13,5},{2,10},{6,14},... | collective-permute-start | bytes 294920 | tf_op jit(solution)/shard_map/ppermute | solution.py:39
  7.9 2.3 %shard_map.82 = (bf16[128,4096]{1,0:T(8,128)(2,1)S(1)}, bf16[128,4096]{1,0:T(8,128)(2,1)S(1)}, bf16[128,4096]{1,0:T(8,128)(2,1)S(1)}, bf16[128,4096]{1,0:T(8,128...) custom-call(bf16[128,4096]{1,0:T(8,128)(2,1)} %bitcast.8, bf16[128,4096]{1,0:T(8,128)(2,1)} %bitcast.9, ...), custom_call_target="tpu_custom_call" | custom-call | flops 1073741824 | bytes 65536 | tf_op jit(solution)/shard_map/pallas_call | solution.py:27
  10.3 0.0 collective-permute-done.6.refs_1_.refs_0_
  10.3 1.6 %collective-permute-start.7 = (bf16[96,512]{1,0:T(8,128)(2,1)S(1)}, bf16[96,512]{1,0:T(8,128)(2,1)S(1)}, u32[]{:S(2)}, u32[]{:S(2)}) collective-permute-start(bf16[96,512]{1,0:T(8,128)(2,1)S(1)} %shard_map.86), channel_id=1, source_target_pairs={{0,4},{4,0},{8,12},{12,8},{1,5},{5,1},{9,13},{13,9},{2,6},{6,2},{1... | collective-permute-start | bytes 294920 | tf_op jit(solution)/shard_map/ppermute | solution.py:39
  11.9 1.6 %collective-permute-done.refs_1_.refs_0_ = bf16[48,512]{1,0:T(8,128)(2,1)S(1)} collective-permute-done((bf16[48,512]{1,0:T(8,128)(2,1)S(1)}, bf16[48,512]{1,0:T(8,128)(2,1)S(1)}, u32[]{:S(2)}, u32[]{:S(2)}) %collective-permute-start) | collective-permute-done | bytes 49184 | tf_op jit(solution)/shard_map/ppermute | solution.py:39
  13.5 0.1 collective-permute-start.1
  13.6 1.2 %collective-permute-done.4.refs_1_.refs_8_ = bf16[48,1024]{1,0:T(8,128)(2,1)S(1)} collective-permute-done((bf16[48,1024]{1,0:T(8,128)(2,1)S(1)}, bf16[48,1024]{1,0:T(8,128)(2,1)S(1)}, u32[]{:S(2)}, u32[]{:S(2)}) %collective-permute-start.4) | collective-permute-done | bytes 98336 | tf_op jit(solution)/shard_map/ppermute | solution.py:39
  14.9 0.9 %collective-permute-start.5 = (bf16[96,1024]{1,0:T(8,128)(2,1)S(1)}, bf16[96,1024]{1,0:T(8,128)(2,1)S(1)}, u32[]{:S(2)}, u32[]{:S(2)}) collective-permute-start(bf16[96,1024]{1,0:T(8,128)(2,1)S(1)} %shard_map.85), channel_id=1, source_target_pairs={{0,4},{4,0},{8,12},{12,8},{1,5},{5,1},{9,13},{13,9},{2,6},{6,2},{1... | collective-permute-start | bytes 589832 | tf_op jit(solution)/shard_map/ppermute | solution.py:39
  15.7 1.3 %collective-permute-done.7.refs_1_ = bf16[96,512]{1,0:T(8,128)(2,1)S(1)} collective-permute-done((bf16[96,512]{1,0:T(8,128)(2,1)S(1)}, bf16[96,512]{1,0:T(8,128)(2,1)S(1)}, u32[]{:S(2)}, u32[]{:S(2)}) %collective-permute-start.7) | collective-permute-done | bytes 98336 | tf_op jit(solution)/shard_map/ppermute | solution.py:39
  17.0 1.6 %collective-permute-start.8 = (bf16[144,512]{1,0:T(8,128)(2,1)S(1)}, bf16[144,512]{1,0:T(8,128)(2,1)S(1)}, u32[]{:S(2)}, u32[]{:S(2)}) collective-permute-start(bf16[144,512]{1,0:T(8,128)(2,1)S(1)} %shard_map.87.refs_6_), channel_id=1, source_target_pairs={{0,2},{1,17},{2,0},{3,19},{16,18},{17,1},{18,16},{19,3},{4,6},{5,2... | collective-permute-start | bytes 442376 | tf_op jit(solution)/shard_map/ppermute | solution.py:51
  18.6 1.5 %collective-permute-start.9 = (bf16[144,512]{1,0:T(8,128)(2,1)S(1)}, bf16[144,512]{1,0:T(8,128)(2,1)S(1)}, u32[]{:S(2)}, u32[]{:S(2)}) collective-permute-start(bf16[144,512]{1,0:T(8,128)(2,1)S(1)} %shard_map.87.refs_6_), channel_id=1, source_target_pairs={{0,16},{1,3},{2,18},{3,1},{16,0},{17,19},{18,2},{19,17},{4,20},{5,... | collective-permute-start | bytes 442376 | tf_op jit(solution)/shard_map/ppermute | solution.py:51
  20.1 0.0 collective-permute-done.1.refs_1_
  20.1 0.8 %collective-permute-start.2 = (bf16[144,512]{1,0:T(8,128)(2,1)S(1)}, bf16[144,512]{1,0:T(8,128)(2,1)S(1)}, u32[]{:S(2)}, u32[]{:S(2)}) collective-permute-start(bf16[144,512]{1,0:T(8,128)(2,1)S(1)} %shard_map.84.refs_7_), channel_id=1, source_target_pairs={{0,2},{1,17},{2,0},{3,19},{16,18},{17,1},{18,16},{19,3},{4,6},{5,2... | collective-permute-start | bytes 442376 | tf_op jit(solution)/shard_map/ppermute | solution.py:51
  20.9 1.5 %collective-permute-start.3 = (bf16[144,512]{1,0:T(8,128)(2,1)S(1)}, bf16[144,512]{1,0:T(8,128)(2,1)S(1)}, u32[]{:S(2)}, u32[]{:S(2)}) collective-permute-start(bf16[144,512]{1,0:T(8,128)(2,1)S(1)} %shard_map.84.refs_7_), channel_id=1, source_target_pairs={{0,16},{1,3},{2,18},{3,1},{16,0},{17,19},{18,2},{19,17},{4,20},{5,... | collective-permute-start | bytes 442376 | tf_op jit(solution)/shard_map/ppermute | solution.py:51
  22.4 0.5 %shard_map.88.refs_8_ = f32[384,128]{1,0:T(8,128)S(1)} custom-call(bf16[128,4096]{1,0:T(8,128)(2,1)S(1)} %get-tuple-element.14.refs_0_, bf16[128,4096]{1,0:T(8,128)(2,1)S(1)} %get-tuple-element.15.refs_1_, bf16[128,4096]{1,0:T(8,128)(2,1)S(1)} %get-tuple-element.16.refs_2_, bf16[128,4096]{1,0:T(8,128)(2,1)S(1)} %get-tuple-element.17.refs_3_, ...), custom_call_target="tpu_custom_call" | custom-call | flops 268435456 | bytes 65536 | tf_op jit(solution)/shard_map/pallas_call | solution.py:27
  23.0 0.8 %collective-permute-done.8.refs_6_ = bf16[144,512]{1,0:T(8,128)(2,1)S(1)} collective-permute-done((bf16[144,512]{1,0:T(8,128)(2,1)S(1)}, bf16[144,512]{1,0:T(8,128)(2,1)S(1)}, u32[]{:S(2)}, u32[]{:S(2)}) %collective-permute-start.8) | collective-permute-done | bytes 147488 | tf_op jit(solution)/shard_map/ppermute | solution.py:51
  23.8 0.6 %collective-permute-done.9.refs_7_ = bf16[144,512]{1,0:T(8,128)(2,1)S(1)} collective-permute-done((bf16[144,512]{1,0:T(8,128)(2,1)S(1)}, bf16[144,512]{1,0:T(8,128)(2,1)S(1)}, u32[]{:S(2)}, u32[]{:S(2)}) %collective-permute-start.9) | collective-permute-done | bytes 147488 | tf_op jit(solution)/shard_map/ppermute | solution.py:51
  24.4 0.5 %shard_map.89.refs_10_ = f32[384,128]{1,0:T(8,128)S(1)} custom-call(bf16[128,4096]{1,0:T(8,128)(2,1)S(1)} %get-tuple-element.14.refs_0_, bf16[128,4096]{1,0:T(8,128)(2,1)S(1)} %get-tuple-element.15.refs_1_, bf16[128,4096]{1,0:T(8,128)(2,1)S(1)} %get-tuple-element.16.refs_2_, bf16[128,4096]{1,0:T(8,128)(2,1)S(1)} %get-tuple-element.17.refs_3_, ...), custom_call_target="tpu_custom_call" | custom-call | flops 268435456 | bytes 65536 | tf_op jit(solution)/shard_map/pallas_call | solution.py:27
  24.9 1.3 %collective-permute-done.2.refs_6_ = bf16[144,512]{1,0:T(8,128)(2,1)S(1)} collective-permute-done((bf16[144,512]{1,0:T(8,128)(2,1)S(1)}, bf16[144,512]{1,0:T(8,128)(2,1)S(1)}, u32[]{:S(2)}, u32[]{:S(2)}) %collective-permute-start.2) | collective-permute-done | bytes 147488 | tf_op jit(solution)/shard_map/ppermute | solution.py:51
  26.2 0.0 collective-permute-done.3.refs_7_
  26.2 0.0 collective-permute-done.5.refs_9_
  26.2 0.8 %shard_map.90.mine = f32[384,128]{1,0:T(8,128)S(1)} custom-call(bf16[128,4096]{1,0:T(8,128)(2,1)S(1)} %get-tuple-element.14.refs_0_, bf16[128,4096]{1,0:T(8,128)(2,1)S(1)} %get-tuple-element.15.refs_1_, bf16[128,4096]{1,0:T(8,128)(2,1)S(1)} %get-tuple-element.16.refs_2_, bf16[128,4096]{1,0:T(8,128)(2,1)S(1)} %get-tuple-element.17.refs_3_, ...), custom_call_target="tpu_custom_call" | custom-call | flops 268435456 | bytes 65536 | tf_op jit(solution)/shard_map/pallas_call | solution.py:27
  27.1 0.1 collective-permute-start.10
  28.4 0.1 collective-permute-done.10.other
  28.6 0.5 shard_map.91
  29.1 4.0 %collective-permute-start.15 = (f32[1,64,128]{2,1,0:T(8,128)S(1)}, f32[1,64,128]{2,1,0:T(8,128)S(1)}, u32[]{:S(2)}, u32[]{:S(2)}) collective-permute-start(f32[1,64,128]{2,1,0:T(8,128)S(1)} %get-tuple-element.22), channel_id=1, source_target_pairs={{0,8},{1,1},{2,10},{3,3},{4,12},{5,5},{6,14},{7,7},{8,0},{9,9},{10... | collective-permute-start | bytes 98312 | tf_op jit(solution)/shard_map/ppermute | solution.py:51
  33.0 0.7 %collective-permute-start.11 = (f32[136,128]{1,0:T(8,128)S(1)}, f32[136,128]{1,0:T(8,128)S(1)}, u32[]{:S(2)}, u32[]{:S(2)}) collective-permute-start(f32[136,128]{1,0:T(8,128)S(1)} %get-tuple-element.20), channel_id=1, source_target_pairs={{0,0},{1,3},{2,2},{3,1},{4,4},{5,7},{6,6},{7,5},{8,8},{9,11},{10,1... | collective-permute-start | bytes 208904 | tf_op jit(solution)/shard_map/ppermute | solution.py:51
  33.7 2.1 %collective-permute-done.15 = f32[1,64,128]{2,1,0:T(8,128)S(1)} collective-permute-done((f32[1,64,128]{2,1,0:T(8,128)S(1)}, f32[1,64,128]{2,1,0:T(8,128)S(1)}, u32[]{:S(2)}, u32[]{:S(2)}) %collective-permute-start.15) | collective-permute-done | bytes 32800 | tf_op jit(solution)/shard_map/ppermute | solution.py:51
  35.8 2.8 %collective-permute-start.16 = (f32[2,64,128]{2,1,0:T(8,128)S(1)}, f32[2,64,128]{2,1,0:T(8,128)S(1)}, u32[]{:S(2)}, u32[]{:S(2)}) collective-permute-start(f32[2,64,128]{2,1,0:T(8,128)S(1)} %pad_maximum_fusion.1), channel_id=1, source_target_pairs={{0,4},{1,1},{2,6},{3,3},{4,0},{5,5},{6,2},{7,7},{8,12},{9,9},{10,1... | collective-permute-start | bytes 196616 | tf_op jit(solution)/shard_map/ppermute | solution.py:51
  38.6 0.0 collective-permute-done.11
  38.6 0.7 %collective-permute-start.12 = (f32[136,128]{1,0:T(8,128)S(1)}, f32[136,128]{1,0:T(8,128)S(1)}, u32[]{:S(2)}, u32[]{:S(2)}) collective-permute-start(f32[136,128]{1,0:T(8,128)S(1)} %add.21), channel_id=1, source_target_pairs={{0,0},{1,9},{2,2},{3,11},{4,4},{5,13},{6,6},{7,15},{8,8},{9,1},{10... | collective-permute-start | bytes 208904 | tf_op jit(solution)/shard_map/ppermute | solution.py:51
  39.3 2.7 %collective-permute-done.16 = f32[2,64,128]{2,1,0:T(8,128)S(1)} collective-permute-done((f32[2,64,128]{2,1,0:T(8,128)S(1)}, f32[2,64,128]{2,1,0:T(8,128)S(1)}, u32[]{:S(2)}, u32[]{:S(2)}) %collective-permute-start.16) | collective-permute-done | bytes 65568 | tf_op jit(solution)/shard_map/ppermute | solution.py:51
  42.0 3.4 %collective-permute-start.17 = (f32[4,64,128]{2,1,0:T(8,128)S(1)}, f32[4,64,128]{2,1,0:T(8,128)S(1)}, u32[]{:S(2)}, u32[]{:S(2)}) collective-permute-start(f32[4,64,128]{2,1,0:T(8,128)S(1)} %pad_maximum_fusion), channel_id=1, source_target_pairs={{0,2},{1,1},{2,0},{3,3},{4,6},{5,5},{6,4},{7,7},{8,10},{9,9},{10,8... | collective-permute-start | bytes 393224 | tf_op jit(solution)/shard_map/ppermute | solution.py:51
  45.4 0.0 collective-permute-done.12
  45.4 0.7 %collective-permute-start.13 = (f32[136,128]{1,0:T(8,128)S(1)}, f32[136,128]{1,0:T(8,128)S(1)}, u32[]{:S(2)}, u32[]{:S(2)}) collective-permute-start(f32[136,128]{1,0:T(8,128)S(1)} %add.22), channel_id=1, source_target_pairs={{0,0},{1,5},{2,2},{3,7},{4,4},{5,1},{6,6},{7,3},{8,8},{9,13},{10,1... | collective-permute-start | bytes 208904 | tf_op jit(solution)/shard_map/ppermute | solution.py:51
  46.1 0.0 collective-permute-done.13
  46.2 1.1 %collective-permute-start.14 = (f32[136,128]{1,0:T(8,128)S(1)}, f32[136,128]{1,0:T(8,128)S(1)}, u32[]{:S(2)}, u32[]{:S(2)}) collective-permute-start(f32[136,128]{1,0:T(8,128)S(1)} %add.23.fac_ref), channel_id=1, source_target_pairs={{0,1},{1,0},{2,3},{3,2},{4,5},{5,4},{6,7},{7,6},{8,9},{9,8},{10,11... | collective-permute-start | bytes 208904 | tf_op jit(solution)/shard_map/ppermute | solution.py:39
  47.3 1.5 %collective-permute-done.17 = f32[4,64,128]{2,1,0:T(8,128)S(1)} collective-permute-done((f32[4,64,128]{2,1,0:T(8,128)S(1)}, f32[4,64,128]{2,1,0:T(8,128)S(1)}, u32[]{:S(2)}, u32[]{:S(2)}) %collective-permute-start.17) | collective-permute-done | bytes 131104 | tf_op jit(solution)/shard_map/ppermute | solution.py:51
  48.9 0.1 collective-permute-start.18
  49.0 0.0 collective-permute-done.14.other_ref
  49.0 2.5 %shard_map.92.side_ref = f32[64,128]{1,0:T(8,128)S(1)} custom-call(f32[136,128]{1,0:T(8,128)S(1)} %add.23.fac_ref, f32[136,128]{1,0:T(8,128)S(1)} %collective-permute-done.14.other_ref, f32[128,64]{1,0:T(8,128)S(1)} %get-tuple-element.21.gtr_ref), custom_call_target="tpu_custom_call" | custom-call | flops 4294967296 | bytes 65536 | tf_op jit(solution)/shard_map/pallas_call | solution.py:27
  51.4 0.0 collective-permute-done.18.other_ref
  51.4 0.7 %shard_map.93 = f32[1,8]{1,0:T(1,128)} custom-call(f32[64,128]{1,0:T(8,128)S(1)} %shard_map.92.side_ref, f32[8,64,128]{2,1,0:T(8,128)S(1)} %constant_dynamic-update-slice_fusion.gte_ref, f32[8,64,128]{2,1,0:T(8,128)S(1)} %collective-permute-done.18.other_ref), custom_call_target="tpu_custom_call" | custom-call | bytes 65536 | tf_op jit(solution)/shard_map/pallas_call | solution.py:27
  (15 shorter events, 0.1 us)
Async XLA Ops:
  0.9 9.3 %collective-permute-start.6 = (bf16[48,512]{1,0:T(8,128)(2,1)S(1)}, bf16[48,512]{1,0:T(8,128)(2,1)S(1)}, u32[]{:S(2)}, u32[]{:S(2)}) collective-permute-start(bf16[48,512]{1,0:T(8,128)(2,1)S(1)} %get-tuple-element.25.refs_0_), channel_id=1, source_target_pairs={{0,8},{4,12},{8,0},{12,4},{1,9},{5,13},{9,1},{13,5},{2,10},{6,14},... | collective-permute-start | bytes 147464 | tf_op jit(solution)/shard_map/ppermute | solution.py:39
  5.0 8.5 %collective-permute-start = (bf16[48,512]{1,0:T(8,128)(2,1)S(1)}, bf16[48,512]{1,0:T(8,128)(2,1)S(1)}, u32[]{:S(2)}, u32[]{:S(2)}) collective-permute-start(bf16[48,512]{1,0:T(8,128)(2,1)S(1)} %get-tuple-element.26.refs_0_), channel_id=1, source_target_pairs={{0,8},{4,12},{8,0},{12,4},{1,9},{5,13},{9,1},{13,5},{2,10},{6,14},... | collective-permute-start | bytes 147464 | tf_op jit(solution)/shard_map/ppermute | solution.py:39
  5.1 9.8 %collective-permute-start.4 = (bf16[48,1024]{1,0:T(8,128)(2,1)S(1)}, bf16[48,1024]{1,0:T(8,128)(2,1)S(1)}, u32[]{:S(2)}, u32[]{:S(2)}) collective-permute-start(bf16[48,1024]{1,0:T(8,128)(2,1)S(1)} %get-tuple-element.23.refs_0_), channel_id=1, source_target_pairs={{0,8},{4,12},{8,0},{12,4},{1,9},{5,13},{9,1},{13,5},{2,10},{6,14},... | collective-permute-start | bytes 294920 | tf_op jit(solution)/shard_map/ppermute | solution.py:39
  10.3 6.7 %collective-permute-start.7 = (bf16[96,512]{1,0:T(8,128)(2,1)S(1)}, bf16[96,512]{1,0:T(8,128)(2,1)S(1)}, u32[]{:S(2)}, u32[]{:S(2)}) collective-permute-start(bf16[96,512]{1,0:T(8,128)(2,1)S(1)} %shard_map.86), channel_id=1, source_target_pairs={{0,4},{4,0},{8,12},{12,8},{1,5},{5,1},{9,13},{13,9},{2,6},{6,2},{1... | collective-permute-start | bytes 294920 | tf_op jit(solution)/shard_map/ppermute | solution.py:39
  13.5 6.6 %collective-permute-start.1 = (bf16[96,512]{1,0:T(8,128)(2,1)S(1)}, bf16[96,512]{1,0:T(8,128)(2,1)S(1)}, u32[]{:S(2)}, u32[]{:S(2)}) collective-permute-start(bf16[96,512]{1,0:T(8,128)(2,1)S(1)} %shard_map.83), channel_id=1, source_target_pairs={{0,4},{4,0},{8,12},{12,8},{1,5},{5,1},{9,13},{13,9},{2,6},{6,2},{1... | collective-permute-start | bytes 294920 | tf_op jit(solution)/shard_map/ppermute | solution.py:39
  14.9 11.4 %collective-permute-start.5 = (bf16[96,1024]{1,0:T(8,128)(2,1)S(1)}, bf16[96,1024]{1,0:T(8,128)(2,1)S(1)}, u32[]{:S(2)}, u32[]{:S(2)}) collective-permute-start(bf16[96,1024]{1,0:T(8,128)(2,1)S(1)} %shard_map.85), channel_id=1, source_target_pairs={{0,4},{4,0},{8,12},{12,8},{1,5},{5,1},{9,13},{13,9},{2,6},{6,2},{1... | collective-permute-start | bytes 589832 | tf_op jit(solution)/shard_map/ppermute | solution.py:39
  17.0 6.7 %collective-permute-start.8 = (bf16[144,512]{1,0:T(8,128)(2,1)S(1)}, bf16[144,512]{1,0:T(8,128)(2,1)S(1)}, u32[]{:S(2)}, u32[]{:S(2)}) collective-permute-start(bf16[144,512]{1,0:T(8,128)(2,1)S(1)} %shard_map.87.refs_6_), channel_id=1, source_target_pairs={{0,2},{1,17},{2,0},{3,19},{16,18},{17,1},{18,16},{19,3},{4,6},{5,2... | collective-permute-start | bytes 442376 | tf_op jit(solution)/shard_map/ppermute | solution.py:51
  18.6 5.8 %collective-permute-start.9 = (bf16[144,512]{1,0:T(8,128)(2,1)S(1)}, bf16[144,512]{1,0:T(8,128)(2,1)S(1)}, u32[]{:S(2)}, u32[]{:S(2)}) collective-permute-start(bf16[144,512]{1,0:T(8,128)(2,1)S(1)} %shard_map.87.refs_6_), channel_id=1, source_target_pairs={{0,16},{1,3},{2,18},{3,1},{16,0},{17,19},{18,2},{19,17},{4,20},{5,... | collective-permute-start | bytes 442376 | tf_op jit(solution)/shard_map/ppermute | solution.py:51
  20.1 6.1 %collective-permute-start.2 = (bf16[144,512]{1,0:T(8,128)(2,1)S(1)}, bf16[144,512]{1,0:T(8,128)(2,1)S(1)}, u32[]{:S(2)}, u32[]{:S(2)}) collective-permute-start(bf16[144,512]{1,0:T(8,128)(2,1)S(1)} %shard_map.84.refs_7_), channel_id=1, source_target_pairs={{0,2},{1,17},{2,0},{3,19},{16,18},{17,1},{18,16},{19,3},{4,6},{5,2... | collective-permute-start | bytes 442376 | tf_op jit(solution)/shard_map/ppermute | solution.py:51
  20.9 5.3 %collective-permute-start.3 = (bf16[144,512]{1,0:T(8,128)(2,1)S(1)}, bf16[144,512]{1,0:T(8,128)(2,1)S(1)}, u32[]{:S(2)}, u32[]{:S(2)}) collective-permute-start(bf16[144,512]{1,0:T(8,128)(2,1)S(1)} %shard_map.84.refs_7_), channel_id=1, source_target_pairs={{0,16},{1,3},{2,18},{3,1},{16,0},{17,19},{18,2},{19,17},{4,20},{5,... | collective-permute-start | bytes 442376 | tf_op jit(solution)/shard_map/ppermute | solution.py:51
  27.1 1.5 %collective-permute-start.10 = (f32[384,128]{1,0:T(8,128)S(1)}, f32[384,128]{1,0:T(8,128)S(1)}, u32[]{:S(2)}, u32[]{:S(2)}) collective-permute-start(f32[384,128]{1,0:T(8,128)S(1)} %shard_map.90.mine), channel_id=1, source_target_pairs={{0,1},{1,0},{2,3},{3,2},{4,5},{5,4},{6,7},{7,6},{8,9},{9,8},{10,11... | collective-permute-start | bytes 589832 | tf_op jit(solution)/shard_map/ppermute | solution.py:39
  29.1 6.7 %collective-permute-start.15 = (f32[1,64,128]{2,1,0:T(8,128)S(1)}, f32[1,64,128]{2,1,0:T(8,128)S(1)}, u32[]{:S(2)}, u32[]{:S(2)}) collective-permute-start(f32[1,64,128]{2,1,0:T(8,128)S(1)} %get-tuple-element.22), channel_id=1, source_target_pairs={{0,8},{1,1},{2,10},{3,3},{4,12},{5,5},{6,14},{7,7},{8,0},{9,9},{10... | collective-permute-start | bytes 98312 | tf_op jit(solution)/shard_map/ppermute | solution.py:51
  33.0 5.6 %collective-permute-start.11 = (f32[136,128]{1,0:T(8,128)S(1)}, f32[136,128]{1,0:T(8,128)S(1)}, u32[]{:S(2)}, u32[]{:S(2)}) collective-permute-start(f32[136,128]{1,0:T(8,128)S(1)} %get-tuple-element.20), channel_id=1, source_target_pairs={{0,0},{1,3},{2,2},{3,1},{4,4},{5,7},{6,6},{7,5},{8,8},{9,11},{10,1... | collective-permute-start | bytes 208904 | tf_op jit(solution)/shard_map/ppermute | solution.py:51
  35.8 6.2 %collective-permute-start.16 = (f32[2,64,128]{2,1,0:T(8,128)S(1)}, f32[2,64,128]{2,1,0:T(8,128)S(1)}, u32[]{:S(2)}, u32[]{:S(2)}) collective-permute-start(f32[2,64,128]{2,1,0:T(8,128)S(1)} %pad_maximum_fusion.1), channel_id=1, source_target_pairs={{0,4},{1,1},{2,6},{3,3},{4,0},{5,5},{6,2},{7,7},{8,12},{9,9},{10,1... | collective-permute-start | bytes 196616 | tf_op jit(solution)/shard_map/ppermute | solution.py:51
  38.6 6.8 %collective-permute-start.12 = (f32[136,128]{1,0:T(8,128)S(1)}, f32[136,128]{1,0:T(8,128)S(1)}, u32[]{:S(2)}, u32[]{:S(2)}) collective-permute-start(f32[136,128]{1,0:T(8,128)S(1)} %add.21), channel_id=1, source_target_pairs={{0,0},{1,9},{2,2},{3,11},{4,4},{5,13},{6,6},{7,15},{8,8},{9,1},{10... | collective-permute-start | bytes 208904 | tf_op jit(solution)/shard_map/ppermute | solution.py:51
  42.0 6.9 %collective-permute-start.17 = (f32[4,64,128]{2,1,0:T(8,128)S(1)}, f32[4,64,128]{2,1,0:T(8,128)S(1)}, u32[]{:S(2)}, u32[]{:S(2)}) collective-permute-start(f32[4,64,128]{2,1,0:T(8,128)S(1)} %pad_maximum_fusion), channel_id=1, source_target_pairs={{0,2},{1,1},{2,0},{3,3},{4,6},{5,5},{6,4},{7,7},{8,10},{9,9},{10,8... | collective-permute-start | bytes 393224 | tf_op jit(solution)/shard_map/ppermute | solution.py:51
  45.4 0.7 %collective-permute-start.13 = (f32[136,128]{1,0:T(8,128)S(1)}, f32[136,128]{1,0:T(8,128)S(1)}, u32[]{:S(2)}, u32[]{:S(2)}) collective-permute-start(f32[136,128]{1,0:T(8,128)S(1)} %add.22), channel_id=1, source_target_pairs={{0,0},{1,5},{2,2},{3,7},{4,4},{5,1},{6,6},{7,3},{8,8},{9,13},{10,1... | collective-permute-start | bytes 208904 | tf_op jit(solution)/shard_map/ppermute | solution.py:51
  46.2 2.8 %collective-permute-start.14 = (f32[136,128]{1,0:T(8,128)S(1)}, f32[136,128]{1,0:T(8,128)S(1)}, u32[]{:S(2)}, u32[]{:S(2)}) collective-permute-start(f32[136,128]{1,0:T(8,128)S(1)} %add.23.fac_ref), channel_id=1, source_target_pairs={{0,1},{1,0},{2,3},{3,2},{4,5},{5,4},{6,7},{7,6},{8,9},{9,8},{10,11... | collective-permute-start | bytes 208904 | tf_op jit(solution)/shard_map/ppermute | solution.py:39
  48.9 2.6 %collective-permute-start.18 = (f32[8,64,128]{2,1,0:T(8,128)S(1)}, f32[8,64,128]{2,1,0:T(8,128)S(1)}, u32[]{:S(2)}, u32[]{:S(2)}) collective-permute-start(f32[8,64,128]{2,1,0:T(8,128)S(1)} %constant_dynamic-update-slice_fusion.gte_ref), channel_id=1, source_target_pairs={{0,1},{1,0},{2,3},{3,2},{4,5},{5,4},{6,7},{7,6},{8,9},{9,8},{10,11... | collective-permute-start | bytes 786440 | tf_op jit(solution)/shard_map/ppermute | solution.py:39

commit v19 on v17

--- a/solution.py
+++ b/solution.py
@@ -308,7 +308,7 @@
     near_a = swap(both_a, "dp", n_dp, 1)
     both_b = stack((halves[1], far[1]))
     near_b = swap(both_b, "dp", n_dp, 1)
-    za = stack((far[0], near_a))
+    za = stack((far[0], near_a), far_op)
     along_x, along_y = (0, 1), (1, 0)
     xa = mixed(za, PLANE, (n_groups, n_blk), along_x, along_y)
     ya = mixed(za, PLANE, (n_groups, n_blk), along_y, along_x)
@@ -326,7 +326,7 @@
             out_shape,
             [vmem()] * len(args),
             args,
-            flops=1 << 28,
+            flops=1 << 30,
             scratch_shapes=[
                 pltpu.VMEM((ki, total), jnp.bfloat16),
                 pltpu.VMEM((ko, total), jnp.bfloat16),

time: 47.2 us -> 47.9 us (1.015)
  starting transfers between devices: 23.9 us -> 24.9 us
    ppermute x10, starting transfers between devices: 13.8 us -> 14.5 us  [swap(): return lax.ppermute(x, axis, [(i, i ^ k) for i in range(count)])]
    ppermute x7, waiting for transfers between devices: 7.26 us -> 6.59 us  [mixed(): return lax.ppermute(x, (*axes, 'mp'), pairs)]
  transfers between devices with their start and end apart: 17 -> 17, of which waited for: 12 -> 10; matrix products, arithmetic and copies ran while one was open for 0% -> 0% of each run, Pallas kernels for 13% -> 12%
where the time goes in v19:
time: 47.9 us; the launch traced here: 47.7 us
  starting transfers between devices  24.9 us (52%)
  waiting for transfers between devices  12.6 us (26%)
  Pallas kernels  7.82 us (16%)
  between operations  1.43 us (3%)
  other arithmetic  0.95 us (2%)
    ppermute x10, starting transfers between devices, swap(): return lax.ppermute(x, axis, [(i, i ^ k) for i in range(count)])  14.5 us
    ppermute x7, starting transfers between devices, mixed(): return lax.ppermute(x, (*axes, 'mp'), pairs)  10.4 us
    pallas_call x12, Pallas kernels, call(): pl.pallas_call(kernel, out_shape=out_shape, in_specs=in_specs, out_specs=...  7.82 us
    ppermute x7, waiting for transfers between devices, mixed(): return lax.ppermute(x, (*axes, 'mp'), pairs)  6.59 us
    ppermute x10, waiting for transfers between devices, swap(): return lax.ppermute(x, axis, [(i, i ^ k) for i in range(count)])  5.96 us
  transfers between devices with their start and end apart: 17, of which 10 were waited for; matrix products, arithmetic and copies ran while one was open for 0% of the time, Pallas kernels for 12%

profile of v19, /device:TPU:0, one launch (start us, length us, event | category | flops | bytes accessed | tf_op | source)
XLA Modules:
  0.0 47.7 jit_solution(7249559160927702798)
XLA Ops:
  0.0 0.9 %fusion = (bf16[48,1024]{1,0:T(8,128)(2,1)S(1)}, bf16[48,1024]{1,0:T(8,128)(2,1)S(1)}) fusion(s32[]{:T(128)S(6)} %select_n.7, bf16[32,4096]{1,0:T(8,128)(2,1)} %bitcast.6, bf16[16,4096]{1,0:T(8,128)(2,1)} %bitcast.12, s32[]{:T(128)S(6)} %select_n.6), kind=kLoop, calls=%fused_computation.6 | loop fusion | flops 393216 | bytes 589832 | tf_op jit(solution)/shard_map/concatenate | solution.py:292
  0.9 4.1 %collective-permute-start.6 = (bf16[48,512]{1,0:T(8,128)(2,1)S(1)}, bf16[48,512]{1,0:T(8,128)(2,1)S(1)}, u32[]{:S(2)}, u32[]{:S(2)}) collective-permute-start(bf16[48,512]{1,0:T(8,128)(2,1)S(1)} %get-tuple-element.25.refs_0_), channel_id=1, source_target_pairs={{0,8},{4,12},{8,0},{12,4},{1,9},{5,13},{9,1},{13,5},{2,10},{6,14},... | collective-permute-start | bytes 147464 | tf_op jit(solution)/shard_map/ppermute | solution.py:39
  5.0 0.1 collective-permute-start.4
  5.1 2.8 %collective-permute-start = (bf16[48,512]{1,0:T(8,128)(2,1)S(1)}, bf16[48,512]{1,0:T(8,128)(2,1)S(1)}, u32[]{:S(2)}, u32[]{:S(2)}) collective-permute-start(bf16[48,512]{1,0:T(8,128)(2,1)S(1)} %get-tuple-element.26.refs_0_), channel_id=1, source_target_pairs={{0,8},{4,12},{8,0},{12,4},{1,9},{5,13},{9,1},{13,5},{2,10},{6,14},... | collective-permute-start | bytes 147464 | tf_op jit(solution)/shard_map/ppermute | solution.py:39
  7.9 2.3 %shard_map.82 = (bf16[128,4096]{1,0:T(8,128)(2,1)S(1)}, bf16[128,4096]{1,0:T(8,128)(2,1)S(1)}, bf16[128,4096]{1,0:T(8,128)(2,1)S(1)}, bf16[128,4096]{1,0:T(8,128...) custom-call(bf16[128,4096]{1,0:T(8,128)(2,1)} %bitcast.8, bf16[128,4096]{1,0:T(8,128)(2,1)} %bitcast.9, ...), custom_call_target="tpu_custom_call" | custom-call | flops 1073741824 | bytes 65536 | tf_op jit(solution)/shard_map/pallas_call | solution.py:27
  10.3 0.0 collective-permute-done.6.refs_1_.refs_0_
  10.3 1.6 %collective-permute-start.7 = (bf16[96,512]{1,0:T(8,128)(2,1)S(1)}, bf16[96,512]{1,0:T(8,128)(2,1)S(1)}, u32[]{:S(2)}, u32[]{:S(2)}) collective-permute-start(bf16[96,512]{1,0:T(8,128)(2,1)S(1)} %shard_map.86), channel_id=1, source_target_pairs={{0,4},{4,0},{8,12},{12,8},{1,5},{5,1},{9,13},{13,9},{2,6},{6,2},{1... | collective-permute-start | bytes 294920 | tf_op jit(solution)/shard_map/ppermute | solution.py:39
  11.9 2.9 %collective-permute-done.refs_1_.refs_0_ = bf16[48,512]{1,0:T(8,128)(2,1)S(1)} collective-permute-done((bf16[48,512]{1,0:T(8,128)(2,1)S(1)}, bf16[48,512]{1,0:T(8,128)(2,1)S(1)}, u32[]{:S(2)}, u32[]{:S(2)}) %collective-permute-start) | collective-permute-done | bytes 49184 | tf_op jit(solution)/shard_map/ppermute | solution.py:39
  14.9 0.1 collective-permute-start.1
  14.9 0.0 collective-permute-done.4.refs_1_.refs_2_.refs_8_
  14.9 2.0 %collective-permute-done.7.refs_1_ = bf16[96,512]{1,0:T(8,128)(2,1)S(1)} collective-permute-done((bf16[96,512]{1,0:T(8,128)(2,1)S(1)}, bf16[96,512]{1,0:T(8,128)(2,1)S(1)}, u32[]{:S(2)}, u32[]{:S(2)}) %collective-permute-start.7) | collective-permute-done | bytes 98336 | tf_op jit(solution)/shard_map/ppermute | solution.py:39
  17.0 1.6 %collective-permute-start.8 = (bf16[144,512]{1,0:T(8,128)(2,1)S(1)}, bf16[144,512]{1,0:T(8,128)(2,1)S(1)}, u32[]{:S(2)}, u32[]{:S(2)}) collective-permute-start(bf16[144,512]{1,0:T(8,128)(2,1)S(1)} %shard_map.87.refs_6_), channel_id=1, source_target_pairs={{0,2},{1,17},{2,0},{3,19},{16,18},{17,1},{18,16},{19,3},{4,6},{5,2... | collective-permute-start | bytes 442376 | tf_op jit(solution)/shard_map/ppermute | solution.py:51
  18.5 1.5 %collective-permute-start.9 = (bf16[144,512]{1,0:T(8,128)(2,1)S(1)}, bf16[144,512]{1,0:T(8,128)(2,1)S(1)}, u32[]{:S(2)}, u32[]{:S(2)}) collective-permute-start(bf16[144,512]{1,0:T(8,128)(2,1)S(1)} %shard_map.87.refs_6_), channel_id=1, source_target_pairs={{0,16},{1,3},{2,18},{3,1},{16,0},{17,19},{18,2},{19,17},{4,20},{5,... | collective-permute-start | bytes 442376 | tf_op jit(solution)/shard_map/ppermute | solution.py:51
  20.1 0.1 collective-permute-start.5
  20.1 0.0 collective-permute-done.1.refs_1_
  20.2 1.0 %collective-permute-start.2 = (bf16[144,512]{1,0:T(8,128)(2,1)S(1)}, bf16[144,512]{1,0:T(8,128)(2,1)S(1)}, u32[]{:S(2)}, u32[]{:S(2)}) collective-permute-start(bf16[144,512]{1,0:T(8,128)(2,1)S(1)} %shard_map.84.refs_7_), channel_id=1, source_target_pairs={{0,2},{1,17},{2,0},{3,19},{16,18},{17,1},{18,16},{19,3},{4,6},{5,2... | collective-permute-start | bytes 442376 | tf_op jit(solution)/shard_map/ppermute | solution.py:51
  21.1 1.5 %collective-permute-start.3 = (bf16[144,512]{1,0:T(8,128)(2,1)S(1)}, bf16[144,512]{1,0:T(8,128)(2,1)S(1)}, u32[]{:S(2)}, u32[]{:S(2)}) collective-permute-start(bf16[144,512]{1,0:T(8,128)(2,1)S(1)} %shard_map.84.refs_7_), channel_id=1, source_target_pairs={{0,16},{1,3},{2,18},{3,1},{16,0},{17,19},{18,2},{19,17},{4,20},{5,... | collective-permute-start | bytes 442376 | tf_op jit(solution)/shard_map/ppermute | solution.py:51
  22.6 0.5 %shard_map.88.refs_8_ = f32[384,128]{1,0:T(8,128)S(1)} custom-call(bf16[128,4096]{1,0:T(8,128)(2,1)S(1)} %get-tuple-element.14.refs_0_, bf16[128,4096]{1,0:T(8,128)(2,1)S(1)} %get-tuple-element.15.refs_1_, bf16[128,4096]{1,0:T(8,128)(2,1)S(1)} %get-tuple-element.16.refs_2_, bf16[128,4096]{1,0:T(8,128)(2,1)S(1)} %get-tuple-element.17.refs_3_, ...), custom_call_target="tpu_custom_call" | custom-call | flops 1073741824 | bytes 65536 | tf_op jit(solution)/shard_map/pallas_call | solution.py:27
  23.2 0.4 collective-permute-done.8.refs_6_
  23.5 1.6 %collective-permute-done.9.refs_7_ = bf16[144,512]{1,0:T(8,128)(2,1)S(1)} collective-permute-done((bf16[144,512]{1,0:T(8,128)(2,1)S(1)}, bf16[144,512]{1,0:T(8,128)(2,1)S(1)}, u32[]{:S(2)}, u32[]{:S(2)}) %collective-permute-start.9) | collective-permute-done | bytes 147488 | tf_op jit(solution)/shard_map/ppermute | solution.py:51
  25.1 0.5 %shard_map.89.refs_10_ = f32[384,128]{1,0:T(8,128)S(1)} custom-call(bf16[128,4096]{1,0:T(8,128)(2,1)S(1)} %get-tuple-element.14.refs_0_, bf16[128,4096]{1,0:T(8,128)(2,1)S(1)} %get-tuple-element.15.refs_1_, bf16[128,4096]{1,0:T(8,128)(2,1)S(1)} %get-tuple-element.16.refs_2_, bf16[128,4096]{1,0:T(8,128)(2,1)S(1)} %get-tuple-element.17.refs_3_, ...), custom_call_target="tpu_custom_call" | custom-call | flops 1073741824 | bytes 65536 | tf_op jit(solution)/shard_map/pallas_call | solution.py:27
  25.7 1.2 %collective-permute-done.2.refs_6_ = bf16[144,512]{1,0:T(8,128)(2,1)S(1)} collective-permute-done((bf16[144,512]{1,0:T(8,128)(2,1)S(1)}, bf16[144,512]{1,0:T(8,128)(2,1)S(1)}, u32[]{:S(2)}, u32[]{:S(2)}) %collective-permute-start.2) | collective-permute-done | bytes 147488 | tf_op jit(solution)/shard_map/ppermute | solution.py:51
  26.9 0.0 collective-permute-done.3.refs_7_
  26.9 0.0 collective-permute-done.5.refs_9_
  26.9 0.8 %shard_map.90.mine = f32[384,128]{1,0:T(8,128)S(1)} custom-call(bf16[128,4096]{1,0:T(8,128)(2,1)S(1)} %get-tuple-element.14.refs_0_, bf16[128,4096]{1,0:T(8,128)(2,1)S(1)} %get-tuple-element.15.refs_1_, bf16[128,4096]{1,0:T(8,128)(2,1)S(1)} %get-tuple-element.16.refs_2_, bf16[128,4096]{1,0:T(8,128)(2,1)S(1)} %get-tuple-element.17.refs_3_, ...), custom_call_target="tpu_custom_call" | custom-call | flops 1073741824 | bytes 65536 | tf_op jit(solution)/shard_map/pallas_call | solution.py:27
  27.7 0.1 collective-permute-start.10
  29.1 0.1 collective-permute-done.10.other
  29.2 0.5 shard_map.91
  29.7 1.4 %collective-permute-start.11 = (f32[136,128]{1,0:T(8,128)S(1)}, f32[136,128]{1,0:T(8,128)S(1)}, u32[]{:S(2)}, u32[]{:S(2)}) collective-permute-start(f32[136,128]{1,0:T(8,128)S(1)} %get-tuple-element.20), channel_id=1, source_target_pairs={{0,2},{1,9},{2,0},{3,11},{4,6},{5,13},{6,4},{7,15},{8,10},{9,1},{1... | collective-permute-start | bytes 208904 | tf_op jit(solution)/shard_map/ppermute | solution.py:51
  31.1 2.6 %collective-permute-start.14 = (f32[1,64,128]{2,1,0:T(8,128)S(1)}, f32[1,64,128]{2,1,0:T(8,128)S(1)}, u32[]{:S(2)}, u32[]{:S(2)}) collective-permute-start(f32[1,64,128]{2,1,0:T(8,128)S(1)} %get-tuple-element.22), channel_id=1, source_target_pairs={{0,8},{4,12},{8,0},{12,4},{1,9},{5,13},{9,1},{13,5},{2,10},{6,14},... | collective-permute-start | bytes 98312 | tf_op jit(solution)/shard_map/ppermute | solution.py:39
  33.6 0.5 collective-permute-done.11
  34.1 1.1 %collective-permute-start.12 = (f32[136,128]{1,0:T(8,128)S(1)}, f32[136,128]{1,0:T(8,128)S(1)}, u32[]{:S(2)}, u32[]{:S(2)}) collective-permute-start(f32[136,128]{1,0:T(8,128)S(1)} %add.21), channel_id=1, source_target_pairs={{0,4},{1,3},{2,6},{3,1},{4,0},{5,7},{6,2},{7,5},{8,12},{9,11},{10,... | collective-permute-start | bytes 208904 | tf_op jit(solution)/shard_map/ppermute | solution.py:51
  35.2 0.9 %collective-permute-done.14 = f32[1,64,128]{2,1,0:T(8,128)S(1)} collective-permute-done((f32[1,64,128]{2,1,0:T(8,128)S(1)}, f32[1,64,128]{2,1,0:T(8,128)S(1)}, u32[]{:S(2)}, u32[]{:S(2)}) %collective-permute-start.14) | collective-permute-done | bytes 32800 | tf_op jit(solution)/shard_map/ppermute | solution.py:39
  36.1 1.3 %collective-permute-start.15 = (f32[2,64,128]{2,1,0:T(8,128)S(1)}, f32[2,64,128]{2,1,0:T(8,128)S(1)}, u32[]{:S(2)}, u32[]{:S(2)}) collective-permute-start(f32[2,64,128]{2,1,0:T(8,128)S(1)} %pad_maximum_fusion.2), channel_id=1, source_target_pairs={{0,4},{4,0},{8,12},{12,8},{1,5},{5,1},{9,13},{13,9},{2,6},{6,2},{1... | collective-permute-start | bytes 196616 | tf_op jit(solution)/shard_map/ppermute | solution.py:39
  37.4 1.1 %collective-permute-done.12 = f32[136,128]{1,0:T(8,128)S(1)} collective-permute-done((f32[136,128]{1,0:T(8,128)S(1)}, f32[136,128]{1,0:T(8,128)S(1)}, u32[]{:S(2)}, u32[]{:S(2)}) %collective-permute-start.12) | collective-permute-done | bytes 69664 | tf_op jit(solution)/shard_map/ppermute | solution.py:51
  38.5 2.4 %collective-permute-start.13 = (f32[136,128]{1,0:T(8,128)S(1)}, f32[136,128]{1,0:T(8,128)S(1)}, u32[]{:S(2)}, u32[]{:S(2)}) collective-permute-start(f32[136,128]{1,0:T(8,128)S(1)} %add.22), channel_id=1, source_target_pairs={{0,8},{1,5},{2,10},{3,7},{4,12},{5,1},{6,14},{7,3},{8,0},{9,13},{1... | collective-permute-start | bytes 208904 | tf_op jit(solution)/shard_map/ppermute | solution.py:51
  40.9 0.0 collective-permute-done.15
  40.9 1.7 %collective-permute-start.16 = (f32[4,64,128]{2,1,0:T(8,128)S(1)}, f32[4,64,128]{2,1,0:T(8,128)S(1)}, u32[]{:S(2)}, u32[]{:S(2)}) collective-permute-start(f32[4,64,128]{2,1,0:T(8,128)S(1)} %pad_maximum_fusion.1), channel_id=1, source_target_pairs={{0,2},{2,0},{1,3},{3,1},{4,6},{6,4},{5,7},{7,5},{8,10},{10,8},{9,1... | collective-permute-start | bytes 393224 | tf_op jit(solution)/shard_map/ppermute | solution.py:39
  42.7 1.8 %collective-permute-done.13 = f32[136,128]{1,0:T(8,128)S(1)} collective-permute-done((f32[136,128]{1,0:T(8,128)S(1)}, f32[136,128]{1,0:T(8,128)S(1)}, u32[]{:S(2)}, u32[]{:S(2)}) %collective-permute-start.13) | collective-permute-done | bytes 69664 | tf_op jit(solution)/shard_map/ppermute | solution.py:51
  44.5 2.5 %shard_map.92.side_ref = f32[64,128]{1,0:T(8,128)S(1)} custom-call(f32[136,128]{1,0:T(8,128)S(1)} %add.23.fac_ref, f32[128,64]{1,0:T(8,128)S(1)} %get-tuple-element.21.gtr_ref), custom_call_target="tpu_custom_call" | custom-call | flops 4294967296 | bytes 65536 | tf_op jit(solution)/shard_map/pallas_call | solution.py:27
  47.0 0.0 collective-permute-done.16
  47.0 0.6 %shard_map.93 = f32[1,8]{1,0:T(1,128)} custom-call(f32[64,128]{1,0:T(8,128)S(1)} %shard_map.92.side_ref, f32[8,64,128]{2,1,0:T(8,128)S(1)} %pad_maximum_fusion.gte_ref), custom_call_target="tpu_custom_call" | custom-call | bytes 65536 | tf_op jit(solution)/shard_map/pallas_call | solution.py:27
  (12 shorter events, 0.1 us)
Async XLA Ops:
  0.9 9.3 %collective-permute-start.6 = (bf16[48,512]{1,0:T(8,128)(2,1)S(1)}, bf16[48,512]{1,0:T(8,128)(2,1)S(1)}, u32[]{:S(2)}, u32[]{:S(2)}) collective-permute-start(bf16[48,512]{1,0:T(8,128)(2,1)S(1)} %get-tuple-element.25.refs_0_), channel_id=1, source_target_pairs={{0,8},{4,12},{8,0},{12,4},{1,9},{5,13},{9,1},{13,5},{2,10},{6,14},... | collective-permute-start | bytes 147464 | tf_op jit(solution)/shard_map/ppermute | solution.py:39
  5.0 9.9 %collective-permute-start.4 = (bf16[48,1024]{1,0:T(8,128)(2,1)S(1)}, bf16[48,1024]{1,0:T(8,128)(2,1)S(1)}, u32[]{:S(2)}, u32[]{:S(2)}) collective-permute-start(bf16[48,1024]{1,0:T(8,128)(2,1)S(1)} %get-tuple-element.23.refs_0_), channel_id=1, source_target_pairs={{0,8},{4,12},{8,0},{12,4},{1,9},{5,13},{9,1},{13,5},{2,10},{6,14},... | collective-permute-start | bytes 294920 | tf_op jit(solution)/shard_map/ppermute | solution.py:39
  5.1 9.8 %collective-permute-start = (bf16[48,512]{1,0:T(8,128)(2,1)S(1)}, bf16[48,512]{1,0:T(8,128)(2,1)S(1)}, u32[]{:S(2)}, u32[]{:S(2)}) collective-permute-start(bf16[48,512]{1,0:T(8,128)(2,1)S(1)} %get-tuple-element.26.refs_0_), channel_id=1, source_target_pairs={{0,8},{4,12},{8,0},{12,4},{1,9},{5,13},{9,1},{13,5},{2,10},{6,14},... | collective-permute-start | bytes 147464 | tf_op jit(solution)/shard_map/ppermute | solution.py:39
  10.3 6.7 %collective-permute-start.7 = (bf16[96,512]{1,0:T(8,128)(2,1)S(1)}, bf16[96,512]{1,0:T(8,128)(2,1)S(1)}, u32[]{:S(2)}, u32[]{:S(2)}) collective-permute-start(bf16[96,512]{1,0:T(8,128)(2,1)S(1)} %shard_map.86), channel_id=1, source_target_pairs={{0,4},{4,0},{8,12},{12,8},{1,5},{5,1},{9,13},{13,9},{2,6},{6,2},{1... | collective-permute-start | bytes 294920 | tf_op jit(solution)/shard_map/ppermute | solution.py:39
  14.9 5.3 %collective-permute-start.1 = (bf16[96,512]{1,0:T(8,128)(2,1)S(1)}, bf16[96,512]{1,0:T(8,128)(2,1)S(1)}, u32[]{:S(2)}, u32[]{:S(2)}) collective-permute-start(bf16[96,512]{1,0:T(8,128)(2,1)S(1)} %shard_map.83), channel_id=1, source_target_pairs={{0,4},{4,0},{8,12},{12,8},{1,5},{5,1},{9,13},{13,9},{2,6},{6,2},{1... | collective-permute-start | bytes 294920 | tf_op jit(solution)/shard_map/ppermute | solution.py:39
  17.0 6.6 %collective-permute-start.8 = (bf16[144,512]{1,0:T(8,128)(2,1)S(1)}, bf16[144,512]{1,0:T(8,128)(2,1)S(1)}, u32[]{:S(2)}, u32[]{:S(2)}) collective-permute-start(bf16[144,512]{1,0:T(8,128)(2,1)S(1)} %shard_map.87.refs_6_), channel_id=1, source_target_pairs={{0,2},{1,17},{2,0},{3,19},{16,18},{17,1},{18,16},{19,3},{4,6},{5,2... | collective-permute-start | bytes 442376 | tf_op jit(solution)/shard_map/ppermute | solution.py:51
  18.5 6.6 %collective-permute-start.9 = (bf16[144,512]{1,0:T(8,128)(2,1)S(1)}, bf16[144,512]{1,0:T(8,128)(2,1)S(1)}, u32[]{:S(2)}, u32[]{:S(2)}) collective-permute-start(bf16[144,512]{1,0:T(8,128)(2,1)S(1)} %shard_map.87.refs_6_), channel_id=1, source_target_pairs={{0,16},{1,3},{2,18},{3,1},{16,0},{17,19},{18,2},{19,17},{4,20},{5,... | collective-permute-start | bytes 442376 | tf_op jit(solution)/shard_map/ppermute | solution.py:51
  20.1 6.9 %collective-permute-start.5 = (bf16[96,1024]{1,0:T(8,128)(2,1)S(1)}, bf16[96,1024]{1,0:T(8,128)(2,1)S(1)}, u32[]{:S(2)}, u32[]{:S(2)}) collective-permute-start(bf16[96,1024]{1,0:T(8,128)(2,1)S(1)} %shard_map.85), channel_id=1, source_target_pairs={{0,4},{4,0},{8,12},{12,8},{1,5},{5,1},{9,13},{13,9},{2,6},{6,2},{1... | collective-permute-start | bytes 589832 | tf_op jit(solution)/shard_map/ppermute | solution.py:39
  20.2 6.7 %collective-permute-start.2 = (bf16[144,512]{1,0:T(8,128)(2,1)S(1)}, bf16[144,512]{1,0:T(8,128)(2,1)S(1)}, u32[]{:S(2)}, u32[]{:S(2)}) collective-permute-start(bf16[144,512]{1,0:T(8,128)(2,1)S(1)} %shard_map.84.refs_7_), channel_id=1, source_target_pairs={{0,2},{1,17},{2,0},{3,19},{16,18},{17,1},{18,16},{19,3},{4,6},{5,2... | collective-permute-start | bytes 442376 | tf_op jit(solution)/shard_map/ppermute | solution.py:51
  21.1 5.8 %collective-permute-start.3 = (bf16[144,512]{1,0:T(8,128)(2,1)S(1)}, bf16[144,512]{1,0:T(8,128)(2,1)S(1)}, u32[]{:S(2)}, u32[]{:S(2)}) collective-permute-start(bf16[144,512]{1,0:T(8,128)(2,1)S(1)} %shard_map.84.refs_7_), channel_id=1, source_target_pairs={{0,16},{1,3},{2,18},{3,1},{16,0},{17,19},{18,2},{19,17},{4,20},{5,... | collective-permute-start | bytes 442376 | tf_op jit(solution)/shard_map/ppermute | solution.py:51
  27.7 1.5 %collective-permute-start.10 = (f32[384,128]{1,0:T(8,128)S(1)}, f32[384,128]{1,0:T(8,128)S(1)}, u32[]{:S(2)}, u32[]{:S(2)}) collective-permute-start(f32[384,128]{1,0:T(8,128)S(1)} %shard_map.90.mine), channel_id=1, source_target_pairs={{0,1},{1,0},{2,3},{3,2},{4,5},{5,4},{6,7},{7,6},{8,9},{9,8},{10,11... | collective-permute-start | bytes 589832 | tf_op jit(solution)/shard_map/ppermute | solution.py:39
  29.7 4.4 %collective-permute-start.11 = (f32[136,128]{1,0:T(8,128)S(1)}, f32[136,128]{1,0:T(8,128)S(1)}, u32[]{:S(2)}, u32[]{:S(2)}) collective-permute-start(f32[136,128]{1,0:T(8,128)S(1)} %get-tuple-element.20), channel_id=1, source_target_pairs={{0,2},{1,9},{2,0},{3,11},{4,6},{5,13},{6,4},{7,15},{8,10},{9,1},{1... | collective-permute-start | bytes 208904 | tf_op jit(solution)/shard_map/ppermute | solution.py:51
  31.1 5.0 %collective-permute-start.14 = (f32[1,64,128]{2,1,0:T(8,128)S(1)}, f32[1,64,128]{2,1,0:T(8,128)S(1)}, u32[]{:S(2)}, u32[]{:S(2)}) collective-permute-start(f32[1,64,128]{2,1,0:T(8,128)S(1)} %get-tuple-element.22), channel_id=1, source_target_pairs={{0,8},{4,12},{8,0},{12,4},{1,9},{5,13},{9,1},{13,5},{2,10},{6,14},... | collective-permute-start | bytes 98312 | tf_op jit(solution)/shard_map/ppermute | solution.py:39
  34.1 4.4 %collective-permute-start.12 = (f32[136,128]{1,0:T(8,128)S(1)}, f32[136,128]{1,0:T(8,128)S(1)}, u32[]{:S(2)}, u32[]{:S(2)}) collective-permute-start(f32[136,128]{1,0:T(8,128)S(1)} %add.21), channel_id=1, source_target_pairs={{0,4},{1,3},{2,6},{3,1},{4,0},{5,7},{6,2},{7,5},{8,12},{9,11},{10,... | collective-permute-start | bytes 208904 | tf_op jit(solution)/shard_map/ppermute | solution.py:51
  36.1 4.9 %collective-permute-start.15 = (f32[2,64,128]{2,1,0:T(8,128)S(1)}, f32[2,64,128]{2,1,0:T(8,128)S(1)}, u32[]{:S(2)}, u32[]{:S(2)}) collective-permute-start(f32[2,64,128]{2,1,0:T(8,128)S(1)} %pad_maximum_fusion.2), channel_id=1, source_target_pairs={{0,4},{4,0},{8,12},{12,8},{1,5},{5,1},{9,13},{13,9},{2,6},{6,2},{1... | collective-permute-start | bytes 196616 | tf_op jit(solution)/shard_map/ppermute | solution.py:39
  38.5 6.0 %collective-permute-start.13 = (f32[136,128]{1,0:T(8,128)S(1)}, f32[136,128]{1,0:T(8,128)S(1)}, u32[]{:S(2)}, u32[]{:S(2)}) collective-permute-start(f32[136,128]{1,0:T(8,128)S(1)} %add.22), channel_id=1, source_target_pairs={{0,8},{1,5},{2,10},{3,7},{4,12},{5,1},{6,14},{7,3},{8,0},{9,13},{1... | collective-permute-start | bytes 208904 | tf_op jit(solution)/shard_map/ppermute | solution.py:51
  40.9 6.1 %collective-permute-start.16 = (f32[4,64,128]{2,1,0:T(8,128)S(1)}, f32[4,64,128]{2,1,0:T(8,128)S(1)}, u32[]{:S(2)}, u32[]{:S(2)}) collective-permute-start(f32[4,64,128]{2,1,0:T(8,128)S(1)} %pad_maximum_fusion.1), channel_id=1, source_target_pairs={{0,2},{2,0},{1,3},{3,1},{4,6},{6,4},{5,7},{7,5},{8,10},{10,8},{9,1... | collective-permute-start | bytes 393224 | tf_op jit(solution)/shard_map/ppermute | solution.py:39

commit v20 on v17

--- a/solution.py
+++ b/solution.py
@@ -304,7 +304,7 @@
     halves = [mine[:, :part], mine[:, part:]]
     far = [swap(h, "dp", n_dp, 2) for h in halves]
     far_op = swap(opposite, "dp", n_dp, 2)
-    both_a = stack((halves[0], far[0]), w_out)
+    both_a = stack((halves[0], far[0]))
     near_a = swap(both_a, "dp", n_dp, 1)
     both_b = stack((halves[1], far[1]))
     near_b = swap(both_b, "dp", n_dp, 1)

time: 47.2 us -> 46.5 us (0.985)
  waiting for transfers between devices: 12.9 us -> 9.21 us
  starting transfers between devices: 23.9 us -> 26.8 us
    ppermute x7, waiting for transfers between devices: 7.26 us -> 3.72 us  [mixed(): return lax.ppermute(x, (*axes, 'mp'), pairs)]
    ppermute x10, starting transfers between devices: 13.8 us -> 16.6 us  [swap(): return lax.ppermute(x, axis, [(i, i ^ k) for i in range(count)])]
  transfers between devices with their start and end apart: 17 -> 17, of which waited for: 12 -> 9; matrix products, arithmetic and copies ran while one was open for 0% -> 0% of each run, Pallas kernels for 13% -> 13%
where the time goes in v20:
time: 46.5 us; the launch traced here: 46.3 us
  starting transfers between devices  26.8 us (58%)
  waiting for transfers between devices  9.21 us (20%)
  Pallas kernels  7.86 us (17%)
  between operations  1.42 us (3%)
  other arithmetic  0.95 us (2%)
    ppermute x10, starting transfers between devices, swap(): return lax.ppermute(x, axis, [(i, i ^ k) for i in range(count)])  16.6 us
    ppermute x7, starting transfers between devices, mixed(): return lax.ppermute(x, (*axes, 'mp'), pairs)  10.3 us
    pallas_call x12, Pallas kernels, call(): pl.pallas_call(kernel, out_shape=out_shape, in_specs=in_specs, out_specs=...  7.86 us
    ppermute x10, waiting for transfers between devices, swap(): return lax.ppermute(x, axis, [(i, i ^ k) for i in range(count)])  5.49 us
    ppermute x7, waiting for transfers between devices, mixed(): return lax.ppermute(x, (*axes, 'mp'), pairs)  3.72 us
  transfers between devices with their start and end apart: 17, of which 9 were waited for; matrix products, arithmetic and copies ran while one was open for 0% of the time, Pallas kernels for 13%

profile of v20, /device:TPU:0, one launch (start us, length us, event | category | flops | bytes accessed | tf_op | source)
XLA Modules:
  0.0 46.3 jit_solution(887163113780325015)
XLA Ops:
  0.0 0.9 %fusion = (bf16[48,1024]{1,0:T(8,128)(2,1)S(1)}, bf16[48,1024]{1,0:T(8,128)(2,1)S(1)}) fusion(s32[]{:T(128)S(6)} %select_n.7, bf16[32,4096]{1,0:T(8,128)(2,1)} %bitcast.6, bf16[16,4096]{1,0:T(8,128)(2,1)} %bitcast.12, s32[]{:T(128)S(6)} %select_n.6), kind=kLoop, calls=%fused_computation.6 | loop fusion | flops 393216 | bytes 589832 | tf_op jit(solution)/shard_map/concatenate | solution.py:292
  0.9 4.1 %collective-permute-start.6 = (bf16[48,512]{1,0:T(8,128)(2,1)S(1)}, bf16[48,512]{1,0:T(8,128)(2,1)S(1)}, u32[]{:S(2)}, u32[]{:S(2)}) collective-permute-start(bf16[48,512]{1,0:T(8,128)(2,1)S(1)} %get-tuple-element.25.refs_0_), channel_id=1, source_target_pairs={{0,8},{4,12},{8,0},{12,4},{1,9},{5,13},{9,1},{13,5},{2,10},{6,14},... | collective-permute-start | bytes 147464 | tf_op jit(solution)/shard_map/ppermute | solution.py:39
  5.0 0.1 collective-permute-start
  5.1 2.8 %collective-permute-start.4 = (bf16[48,1024]{1,0:T(8,128)(2,1)S(1)}, bf16[48,1024]{1,0:T(8,128)(2,1)S(1)}, u32[]{:S(2)}, u32[]{:S(2)}) collective-permute-start(bf16[48,1024]{1,0:T(8,128)(2,1)S(1)} %get-tuple-element.23.refs_0_), channel_id=1, source_target_pairs={{0,8},{4,12},{8,0},{12,4},{1,9},{5,13},{9,1},{13,5},{2,10},{6,14},... | collective-permute-start | bytes 294920 | tf_op jit(solution)/shard_map/ppermute | solution.py:39
  7.9 0.0 collective-permute-done.6.refs_1_.refs_0_
  8.0 2.8 %collective-permute-start.7 = (bf16[96,512]{1,0:T(8,128)(2,1)S(1)}, bf16[96,512]{1,0:T(8,128)(2,1)S(1)}, u32[]{:S(2)}, u32[]{:S(2)}) collective-permute-start(bf16[96,512]{1,0:T(8,128)(2,1)S(1)} %shard_map.86), channel_id=1, source_target_pairs={{0,4},{4,0},{8,12},{12,8},{1,5},{5,1},{9,13},{13,9},{2,6},{6,2},{1... | collective-permute-start | bytes 294920 | tf_op jit(solution)/shard_map/ppermute | solution.py:39
  10.7 2.8 %collective-permute-done.refs_1_.refs_0_ = bf16[48,512]{1,0:T(8,128)(2,1)S(1)} collective-permute-done((bf16[48,512]{1,0:T(8,128)(2,1)S(1)}, bf16[48,512]{1,0:T(8,128)(2,1)S(1)}, u32[]{:S(2)}, u32[]{:S(2)}) %collective-permute-start) | collective-permute-done | bytes 49184 | tf_op jit(solution)/shard_map/ppermute | solution.py:39
  13.5 0.1 collective-permute-start.1
  13.6 1.2 %collective-permute-done.4.refs_1_.refs_8_ = bf16[48,1024]{1,0:T(8,128)(2,1)S(1)} collective-permute-done((bf16[48,1024]{1,0:T(8,128)(2,1)S(1)}, bf16[48,1024]{1,0:T(8,128)(2,1)S(1)}, u32[]{:S(2)}, u32[]{:S(2)}) %collective-permute-start.4) | collective-permute-done | bytes 98336 | tf_op jit(solution)/shard_map/ppermute | solution.py:39
  14.9 0.9 %collective-permute-start.5 = (bf16[96,1024]{1,0:T(8,128)(2,1)S(1)}, bf16[96,1024]{1,0:T(8,128)(2,1)S(1)}, u32[]{:S(2)}, u32[]{:S(2)}) collective-permute-start(bf16[96,1024]{1,0:T(8,128)(2,1)S(1)} %shard_map.85), channel_id=1, source_target_pairs={{0,4},{4,0},{8,12},{12,8},{1,5},{5,1},{9,13},{13,9},{2,6},{6,2},{1... | collective-permute-start | bytes 589832 | tf_op jit(solution)/shard_map/ppermute | solution.py:39
  15.7 1.0 %collective-permute-done.7.refs_1_ = bf16[96,512]{1,0:T(8,128)(2,1)S(1)} collective-permute-done((bf16[96,512]{1,0:T(8,128)(2,1)S(1)}, bf16[96,512]{1,0:T(8,128)(2,1)S(1)}, u32[]{:S(2)}, u32[]{:S(2)}) %collective-permute-start.7) | collective-permute-done | bytes 98336 | tf_op jit(solution)/shard_map/ppermute | solution.py:39
  16.7 1.6 %collective-permute-start.8 = (bf16[144,512]{1,0:T(8,128)(2,1)S(1)}, bf16[144,512]{1,0:T(8,128)(2,1)S(1)}, u32[]{:S(2)}, u32[]{:S(2)}) collective-permute-start(bf16[144,512]{1,0:T(8,128)(2,1)S(1)} %shard_map.87.refs_6_), channel_id=1, source_target_pairs={{0,2},{1,17},{2,0},{3,19},{16,18},{17,1},{18,16},{19,3},{4,6},{5,2... | collective-permute-start | bytes 442376 | tf_op jit(solution)/shard_map/ppermute | solution.py:51
  18.3 1.5 %collective-permute-start.9 = (bf16[144,512]{1,0:T(8,128)(2,1)S(1)}, bf16[144,512]{1,0:T(8,128)(2,1)S(1)}, u32[]{:S(2)}, u32[]{:S(2)}) collective-permute-start(bf16[144,512]{1,0:T(8,128)(2,1)S(1)} %shard_map.87.refs_6_), channel_id=1, source_target_pairs={{0,16},{1,3},{2,18},{3,1},{16,0},{17,19},{18,2},{19,17},{4,20},{5,... | collective-permute-start | bytes 442376 | tf_op jit(solution)/shard_map/ppermute | solution.py:51
  19.8 0.0 collective-permute-done.1.refs_1_
  19.8 1.1 %collective-permute-start.2 = (bf16[144,512]{1,0:T(8,128)(2,1)S(1)}, bf16[144,512]{1,0:T(8,128)(2,1)S(1)}, u32[]{:S(2)}, u32[]{:S(2)}) collective-permute-start(bf16[144,512]{1,0:T(8,128)(2,1)S(1)} %shard_map.84.refs_7_), channel_id=1, source_target_pairs={{0,2},{1,17},{2,0},{3,19},{16,18},{17,1},{18,16},{19,3},{4,6},{5,2... | collective-permute-start | bytes 442376 | tf_op jit(solution)/shard_map/ppermute | solution.py:51
  20.9 1.5 %collective-permute-start.3 = (bf16[144,512]{1,0:T(8,128)(2,1)S(1)}, bf16[144,512]{1,0:T(8,128)(2,1)S(1)}, u32[]{:S(2)}, u32[]{:S(2)}) collective-permute-start(bf16[144,512]{1,0:T(8,128)(2,1)S(1)} %shard_map.84.refs_7_), channel_id=1, source_target_pairs={{0,16},{1,3},{2,18},{3,1},{16,0},{17,19},{18,2},{19,17},{4,20},{5,... | collective-permute-start | bytes 442376 | tf_op jit(solution)/shard_map/ppermute | solution.py:51
  22.4 2.3 %shard_map.82 = (bf16[128,4096]{1,0:T(8,128)(2,1)S(1)}, bf16[128,4096]{1,0:T(8,128)(2,1)S(1)}, bf16[128,4096]{1,0:T(8,128)(2,1)S(1)}, bf16[128,4096]{1,0:T(8,128...) custom-call(bf16[128,4096]{1,0:T(8,128)(2,1)} %bitcast.8, bf16[128,4096]{1,0:T(8,128)(2,1)} %bitcast.9, ...), custom_call_target="tpu_custom_call" | custom-call | flops 1073741824 | bytes 65536 | tf_op jit(solution)/shard_map/pallas_call | solution.py:27
  24.8 0.6 %shard_map.88.refs_8_ = f32[384,128]{1,0:T(8,128)S(1)} custom-call(bf16[128,4096]{1,0:T(8,128)(2,1)S(1)} %get-tuple-element.14.refs_0_, bf16[128,4096]{1,0:T(8,128)(2,1)S(1)} %get-tuple-element.15.refs_1_, bf16[128,4096]{1,0:T(8,128)(2,1)S(1)} %get-tuple-element.16.refs_2_, bf16[128,4096]{1,0:T(8,128)(2,1)S(1)} %get-tuple-element.17.refs_3_, ...), custom_call_target="tpu_custom_call" | custom-call | flops 268435456 | bytes 65536 | tf_op jit(solution)/shard_map/pallas_call | solution.py:27
  25.3 0.0 collective-permute-done.8.refs_6_
  25.3 0.0 collective-permute-done.9.refs_7_
  25.3 0.6 %shard_map.89.refs_10_ = f32[384,128]{1,0:T(8,128)S(1)} custom-call(bf16[128,4096]{1,0:T(8,128)(2,1)S(1)} %get-tuple-element.14.refs_0_, bf16[128,4096]{1,0:T(8,128)(2,1)S(1)} %get-tuple-element.15.refs_1_, bf16[128,4096]{1,0:T(8,128)(2,1)S(1)} %get-tuple-element.16.refs_2_, bf16[128,4096]{1,0:T(8,128)(2,1)S(1)} %get-tuple-element.17.refs_3_, ...), custom_call_target="tpu_custom_call" | custom-call | flops 268435456 | bytes 65536 | tf_op jit(solution)/shard_map/pallas_call | solution.py:27
  25.9 0.0 collective-permute-done.2.refs_6_
  25.9 0.2 collective-permute-done.3.refs_7_
  26.1 0.0 collective-permute-done.5.refs_9_
  26.1 0.8 %shard_map.90.mine = f32[384,128]{1,0:T(8,128)S(1)} custom-call(bf16[128,4096]{1,0:T(8,128)(2,1)S(1)} %get-tuple-element.14.refs_0_, bf16[128,4096]{1,0:T(8,128)(2,1)S(1)} %get-tuple-element.15.refs_1_, bf16[128,4096]{1,0:T(8,128)(2,1)S(1)} %get-tuple-element.16.refs_2_, bf16[128,4096]{1,0:T(8,128)(2,1)S(1)} %get-tuple-element.17.refs_3_, ...), custom_call_target="tpu_custom_call" | custom-call | flops 268435456 | bytes 65536 | tf_op jit(solution)/shard_map/pallas_call | solution.py:27
  26.9 0.1 collective-permute-start.10
  28.3 0.1 collective-permute-done.10.other
  28.4 0.5 %shard_map.91 = (f32[136,128]{1,0:T(8,128)S(1)}, f32[1,64,128]{2,1,0:T(8,128)S(1)}, f32[128,64]{1,0:T(8,128)S(1)}) custom-call(s32[1]{0:T(128)S(6)} %copy.9.len_tr, s32[1]{0:T(128)S(6)} %copy.10.len_te, f32[384,128]{1,0:T(8,128)S(1)} %shard_map.90.mine, f32[384,128]{1,0:T(8,128)S(1)} %collective-permute-done.10.other), custom_call_target="tpu_custom_call" | custom-call | bytes 65536 | tf_op jit(solution)/shard_map/pallas_call | solution.py:27
  28.9 1.1 %collective-permute-start.11 = (f32[136,128]{1,0:T(8,128)S(1)}, f32[136,128]{1,0:T(8,128)S(1)}, u32[]{:S(2)}, u32[]{:S(2)}) collective-permute-start(f32[136,128]{1,0:T(8,128)S(1)} %get-tuple-element.20), channel_id=1, source_target_pairs={{0,2},{1,9},{2,0},{3,11},{4,6},{5,13},{6,4},{7,15},{8,10},{9,1},{1... | collective-permute-start | bytes 208904 | tf_op jit(solution)/shard_map/ppermute | solution.py:51
  30.0 2.7 %collective-permute-start.14 = (f32[1,64,128]{2,1,0:T(8,128)S(1)}, f32[1,64,128]{2,1,0:T(8,128)S(1)}, u32[]{:S(2)}, u32[]{:S(2)}) collective-permute-start(f32[1,64,128]{2,1,0:T(8,128)S(1)} %get-tuple-element.22), channel_id=1, source_target_pairs={{0,8},{4,12},{8,0},{12,4},{1,9},{5,13},{9,1},{13,5},{2,10},{6,14},... | collective-permute-start | bytes 98312 | tf_op jit(solution)/shard_map/ppermute | solution.py:39
  32.7 0.6 %collective-permute-done.11 = f32[136,128]{1,0:T(8,128)S(1)} collective-permute-done((f32[136,128]{1,0:T(8,128)S(1)}, f32[136,128]{1,0:T(8,128)S(1)}, u32[]{:S(2)}, u32[]{:S(2)}) %collective-permute-start.11) | collective-permute-done | bytes 69664 | tf_op jit(solution)/shard_map/ppermute | solution.py:51
  33.3 1.2 %collective-permute-start.12 = (f32[136,128]{1,0:T(8,128)S(1)}, f32[136,128]{1,0:T(8,128)S(1)}, u32[]{:S(2)}, u32[]{:S(2)}) collective-permute-start(f32[136,128]{1,0:T(8,128)S(1)} %add.21), channel_id=1, source_target_pairs={{0,4},{1,3},{2,6},{3,1},{4,0},{5,7},{6,2},{7,5},{8,12},{9,11},{10,... | collective-permute-start | bytes 208904 | tf_op jit(solution)/shard_map/ppermute | solution.py:51
  34.5 0.3 collective-permute-done.14
  34.8 1.5 %collective-permute-start.15 = (f32[2,64,128]{2,1,0:T(8,128)S(1)}, f32[2,64,128]{2,1,0:T(8,128)S(1)}, u32[]{:S(2)}, u32[]{:S(2)}) collective-permute-start(f32[2,64,128]{2,1,0:T(8,128)S(1)} %pad_maximum_fusion.2), channel_id=1, source_target_pairs={{0,4},{4,0},{8,12},{12,8},{1,5},{5,1},{9,13},{13,9},{2,6},{6,2},{1... | collective-permute-start | bytes 196616 | tf_op jit(solution)/shard_map/ppermute | solution.py:39
  36.3 1.3 %collective-permute-done.12 = f32[136,128]{1,0:T(8,128)S(1)} collective-permute-done((f32[136,128]{1,0:T(8,128)S(1)}, f32[136,128]{1,0:T(8,128)S(1)}, u32[]{:S(2)}, u32[]{:S(2)}) %collective-permute-start.12) | collective-permute-done | bytes 69664 | tf_op jit(solution)/shard_map/ppermute | solution.py:51
  37.7 2.3 %collective-permute-start.13 = (f32[136,128]{1,0:T(8,128)S(1)}, f32[136,128]{1,0:T(8,128)S(1)}, u32[]{:S(2)}, u32[]{:S(2)}) collective-permute-start(f32[136,128]{1,0:T(8,128)S(1)} %add.22), channel_id=1, source_target_pairs={{0,8},{1,5},{2,10},{3,7},{4,12},{5,1},{6,14},{7,3},{8,0},{9,13},{1... | collective-permute-start | bytes 208904 | tf_op jit(solution)/shard_map/ppermute | solution.py:51
  39.9 0.0 collective-permute-done.15
  40.0 1.6 %collective-permute-start.16 = (f32[4,64,128]{2,1,0:T(8,128)S(1)}, f32[4,64,128]{2,1,0:T(8,128)S(1)}, u32[]{:S(2)}, u32[]{:S(2)}) collective-permute-start(f32[4,64,128]{2,1,0:T(8,128)S(1)} %pad_maximum_fusion.1), channel_id=1, source_target_pairs={{0,2},{2,0},{1,3},{3,1},{4,6},{6,4},{5,7},{7,5},{8,10},{10,8},{9,1... | collective-permute-start | bytes 393224 | tf_op jit(solution)/shard_map/ppermute | solution.py:39
  41.5 1.6 %collective-permute-done.13 = f32[136,128]{1,0:T(8,128)S(1)} collective-permute-done((f32[136,128]{1,0:T(8,128)S(1)}, f32[136,128]{1,0:T(8,128)S(1)}, u32[]{:S(2)}, u32[]{:S(2)}) %collective-permute-start.13) | collective-permute-done | bytes 69664 | tf_op jit(solution)/shard_map/ppermute | solution.py:51
  43.1 2.5 %shard_map.92.side_ref = f32[64,128]{1,0:T(8,128)S(1)} custom-call(f32[136,128]{1,0:T(8,128)S(1)} %add.23.fac_ref, f32[128,64]{1,0:T(8,128)S(1)} %get-tuple-element.21.gtr_ref), custom_call_target="tpu_custom_call" | custom-call | flops 4294967296 | bytes 65536 | tf_op jit(solution)/shard_map/pallas_call | solution.py:27
  45.6 0.0 collective-permute-done.16
  45.7 0.6 %shard_map.93 = f32[1,8]{1,0:T(1,128)} custom-call(f32[64,128]{1,0:T(8,128)S(1)} %shard_map.92.side_ref, f32[8,64,128]{2,1,0:T(8,128)S(1)} %pad_maximum_fusion.gte_ref), custom_call_target="tpu_custom_call" | custom-call | bytes 65536 | tf_op jit(solution)/shard_map/pallas_call | solution.py:27
  (12 shorter events, 0.1 us)
Async XLA Ops:
  0.9 7.0 %collective-permute-start.6 = (bf16[48,512]{1,0:T(8,128)(2,1)S(1)}, bf16[48,512]{1,0:T(8,128)(2,1)S(1)}, u32[]{:S(2)}, u32[]{:S(2)}) collective-permute-start(bf16[48,512]{1,0:T(8,128)(2,1)S(1)} %get-tuple-element.25.refs_0_), channel_id=1, source_target_pairs={{0,8},{4,12},{8,0},{12,4},{1,9},{5,13},{9,1},{13,5},{2,10},{6,14},... | collective-permute-start | bytes 147464 | tf_op jit(solution)/shard_map/ppermute | solution.py:39
  5.0 8.5 %collective-permute-start = (bf16[48,512]{1,0:T(8,128)(2,1)S(1)}, bf16[48,512]{1,0:T(8,128)(2,1)S(1)}, u32[]{:S(2)}, u32[]{:S(2)}) collective-permute-start(bf16[48,512]{1,0:T(8,128)(2,1)S(1)} %get-tuple-element.26.refs_0_), channel_id=1, source_target_pairs={{0,8},{4,12},{8,0},{12,4},{1,9},{5,13},{9,1},{13,5},{2,10},{6,14},... | collective-permute-start | bytes 147464 | tf_op jit(solution)/shard_map/ppermute | solution.py:39
  5.1 9.8 %collective-permute-start.4 = (bf16[48,1024]{1,0:T(8,128)(2,1)S(1)}, bf16[48,1024]{1,0:T(8,128)(2,1)S(1)}, u32[]{:S(2)}, u32[]{:S(2)}) collective-permute-start(bf16[48,1024]{1,0:T(8,128)(2,1)S(1)} %get-tuple-element.23.refs_0_), channel_id=1, source_target_pairs={{0,8},{4,12},{8,0},{12,4},{1,9},{5,13},{9,1},{13,5},{2,10},{6,14},... | collective-permute-start | bytes 294920 | tf_op jit(solution)/shard_map/ppermute | solution.py:39
  8.0 8.8 %collective-permute-start.7 = (bf16[96,512]{1,0:T(8,128)(2,1)S(1)}, bf16[96,512]{1,0:T(8,128)(2,1)S(1)}, u32[]{:S(2)}, u32[]{:S(2)}) collective-permute-start(bf16[96,512]{1,0:T(8,128)(2,1)S(1)} %shard_map.86), channel_id=1, source_target_pairs={{0,4},{4,0},{8,12},{12,8},{1,5},{5,1},{9,13},{13,9},{2,6},{6,2},{1... | collective-permute-start | bytes 294920 | tf_op jit(solution)/shard_map/ppermute | solution.py:39
  13.5 6.3 %collective-permute-start.1 = (bf16[96,512]{1,0:T(8,128)(2,1)S(1)}, bf16[96,512]{1,0:T(8,128)(2,1)S(1)}, u32[]{:S(2)}, u32[]{:S(2)}) collective-permute-start(bf16[96,512]{1,0:T(8,128)(2,1)S(1)} %shard_map.83), channel_id=1, source_target_pairs={{0,4},{4,0},{8,12},{12,8},{1,5},{5,1},{9,13},{13,9},{2,6},{6,2},{1... | collective-permute-start | bytes 294920 | tf_op jit(solution)/shard_map/ppermute | solution.py:39
  14.9 11.2 %collective-permute-start.5 = (bf16[96,1024]{1,0:T(8,128)(2,1)S(1)}, bf16[96,1024]{1,0:T(8,128)(2,1)S(1)}, u32[]{:S(2)}, u32[]{:S(2)}) collective-permute-start(bf16[96,1024]{1,0:T(8,128)(2,1)S(1)} %shard_map.85), channel_id=1, source_target_pairs={{0,4},{4,0},{8,12},{12,8},{1,5},{5,1},{9,13},{13,9},{2,6},{6,2},{1... | collective-permute-start | bytes 589832 | tf_op jit(solution)/shard_map/ppermute | solution.py:39
  16.7 8.6 %collective-permute-start.8 = (bf16[144,512]{1,0:T(8,128)(2,1)S(1)}, bf16[144,512]{1,0:T(8,128)(2,1)S(1)}, u32[]{:S(2)}, u32[]{:S(2)}) collective-permute-start(bf16[144,512]{1,0:T(8,128)(2,1)S(1)} %shard_map.87.refs_6_), channel_id=1, source_target_pairs={{0,2},{1,17},{2,0},{3,19},{16,18},{17,1},{18,16},{19,3},{4,6},{5,2... | collective-permute-start | bytes 442376 | tf_op jit(solution)/shard_map/ppermute | solution.py:51
  18.3 7.0 %collective-permute-start.9 = (bf16[144,512]{1,0:T(8,128)(2,1)S(1)}, bf16[144,512]{1,0:T(8,128)(2,1)S(1)}, u32[]{:S(2)}, u32[]{:S(2)}) collective-permute-start(bf16[144,512]{1,0:T(8,128)(2,1)S(1)} %shard_map.87.refs_6_), channel_id=1, source_target_pairs={{0,16},{1,3},{2,18},{3,1},{16,0},{17,19},{18,2},{19,17},{4,20},{5,... | collective-permute-start | bytes 442376 | tf_op jit(solution)/shard_map/ppermute | solution.py:51
  19.8 6.0 %collective-permute-start.2 = (bf16[144,512]{1,0:T(8,128)(2,1)S(1)}, bf16[144,512]{1,0:T(8,128)(2,1)S(1)}, u32[]{:S(2)}, u32[]{:S(2)}) collective-permute-start(bf16[144,512]{1,0:T(8,128)(2,1)S(1)} %shard_map.84.refs_7_), channel_id=1, source_target_pairs={{0,2},{1,17},{2,0},{3,19},{16,18},{17,1},{18,16},{19,3},{4,6},{5,2... | collective-permute-start | bytes 442376 | tf_op jit(solution)/shard_map/ppermute | solution.py:51
  20.9 5.1 %collective-permute-start.3 = (bf16[144,512]{1,0:T(8,128)(2,1)S(1)}, bf16[144,512]{1,0:T(8,128)(2,1)S(1)}, u32[]{:S(2)}, u32[]{:S(2)}) collective-permute-start(bf16[144,512]{1,0:T(8,128)(2,1)S(1)} %shard_map.84.refs_7_), channel_id=1, source_target_pairs={{0,16},{1,3},{2,18},{3,1},{16,0},{17,19},{18,2},{19,17},{4,20},{5,... | collective-permute-start | bytes 442376 | tf_op jit(solution)/shard_map/ppermute | solution.py:51
  26.9 1.5 %collective-permute-start.10 = (f32[384,128]{1,0:T(8,128)S(1)}, f32[384,128]{1,0:T(8,128)S(1)}, u32[]{:S(2)}, u32[]{:S(2)}) collective-permute-start(f32[384,128]{1,0:T(8,128)S(1)} %shard_map.90.mine), channel_id=1, source_target_pairs={{0,1},{1,0},{2,3},{3,2},{4,5},{5,4},{6,7},{7,6},{8,9},{9,8},{10,11... | collective-permute-start | bytes 589832 | tf_op jit(solution)/shard_map/ppermute | solution.py:39
  28.9 4.4 %collective-permute-start.11 = (f32[136,128]{1,0:T(8,128)S(1)}, f32[136,128]{1,0:T(8,128)S(1)}, u32[]{:S(2)}, u32[]{:S(2)}) collective-permute-start(f32[136,128]{1,0:T(8,128)S(1)} %get-tuple-element.20), channel_id=1, source_target_pairs={{0,2},{1,9},{2,0},{3,11},{4,6},{5,13},{6,4},{7,15},{8,10},{9,1},{1... | collective-permute-start | bytes 208904 | tf_op jit(solution)/shard_map/ppermute | solution.py:51
  30.0 4.8 %collective-permute-start.14 = (f32[1,64,128]{2,1,0:T(8,128)S(1)}, f32[1,64,128]{2,1,0:T(8,128)S(1)}, u32[]{:S(2)}, u32[]{:S(2)}) collective-permute-start(f32[1,64,128]{2,1,0:T(8,128)S(1)} %get-tuple-element.22), channel_id=1, source_target_pairs={{0,8},{4,12},{8,0},{12,4},{1,9},{5,13},{9,1},{13,5},{2,10},{6,14},... | collective-permute-start | bytes 98312 | tf_op jit(solution)/shard_map/ppermute | solution.py:39
  33.3 4.4 %collective-permute-start.12 = (f32[136,128]{1,0:T(8,128)S(1)}, f32[136,128]{1,0:T(8,128)S(1)}, u32[]{:S(2)}, u32[]{:S(2)}) collective-permute-start(f32[136,128]{1,0:T(8,128)S(1)} %add.21), channel_id=1, source_target_pairs={{0,4},{1,3},{2,6},{3,1},{4,0},{5,7},{6,2},{7,5},{8,12},{9,11},{10,... | collective-permute-start | bytes 208904 | tf_op jit(solution)/shard_map/ppermute | solution.py:51
  34.8 5.2 %collective-permute-start.15 = (f32[2,64,128]{2,1,0:T(8,128)S(1)}, f32[2,64,128]{2,1,0:T(8,128)S(1)}, u32[]{:S(2)}, u32[]{:S(2)}) collective-permute-start(f32[2,64,128]{2,1,0:T(8,128)S(1)} %pad_maximum_fusion.2), channel_id=1, source_target_pairs={{0,4},{4,0},{8,12},{12,8},{1,5},{5,1},{9,13},{13,9},{2,6},{6,2},{1... | collective-permute-start | bytes 196616 | tf_op jit(solution)/shard_map/ppermute | solution.py:39
  37.7 5.5 %collective-permute-start.13 = (f32[136,128]{1,0:T(8,128)S(1)}, f32[136,128]{1,0:T(8,128)S(1)}, u32[]{:S(2)}, u32[]{:S(2)}) collective-permute-start(f32[136,128]{1,0:T(8,128)S(1)} %add.22), channel_id=1, source_target_pairs={{0,8},{1,5},{2,10},{3,7},{4,12},{5,1},{6,14},{7,3},{8,0},{9,13},{1... | collective-permute-start | bytes 208904 | tf_op jit(solution)/shard_map/ppermute | solution.py:51
  40.0 5.7 %collective-permute-start.16 = (f32[4,64,128]{2,1,0:T(8,128)S(1)}, f32[4,64,128]{2,1,0:T(8,128)S(1)}, u32[]{:S(2)}, u32[]{:S(2)}) collective-permute-start(f32[4,64,128]{2,1,0:T(8,128)S(1)} %pad_maximum_fusion.1), channel_id=1, source_target_pairs={{0,2},{2,0},{1,3},{3,1},{4,6},{6,4},{5,7},{7,5},{8,10},{10,8},{9,1... | collective-permute-start | bytes 393224 | tf_op jit(solution)/shard_map/ppermute | solution.py:39

commit v21 on v20

--- a/solution.py
+++ b/solution.py
@@ -144,6 +144,12 @@
     store_products(xs, gs, acc_ref, out_ref)
 
 
+def with_corner(x, value):
+    row = lax.broadcasted_iota(jnp.int32, x.shape, 0)
+    col = lax.broadcasted_iota(jnp.int32, x.shape, 1)
+    return jnp.where((row == 1) & (col == 0), value, x)
+
+
 def moments_kernel(len_tr, len_te, mine, other, fac_ref, gte_ref, gtr_ref):
     tokens = mine.shape[0] // 3
     ki = mine.shape[1]
@@ -165,12 +171,11 @@
         preferred_element_type=jnp.float32,
     )
     c_in = products[:, :ki]
-    c_out = dot(g_tr, g_tr)
+    c_out = with_corner(dot(g_tr, g_tr), n_tr.astype(jnp.float32))
     half = ki // 2
     fac_ref[:half, :] = c_in[:half, :]
     fac_ref[half:ki, :half] = c_in[half:, half:]
     fac_ref[half:ki, half:] = c_out
-    fac_ref[ki:, :] = jnp.full((8, ki), n_tr.astype(jnp.float32))
     grad_tr = products[:, ki:] / n_tr.astype(jnp.float32)
     grad_te = dot(x_te, g_te) / n_te.astype(jnp.float32)
     gtr_ref[...] = grad_tr
@@ -256,8 +261,10 @@
     c_in = jnp.concatenate(
         [top, jnp.concatenate([top[:, half:].T, low[:, :half]], axis=1)], axis=0
     )
-    count = fac_ref[ki : ki + 1, :1]
-    inv_in, inv_out = inverses([c_in, wide(low[:, half:], half)])
+    c_out = low[:, half:]
+    count = c_out[1:2, :1]
+    c_out = with_corner(c_out, c_out[:1, 1:2])
+    inv_in, inv_out = inverses([c_in, wide(c_out, half)])
     side = mm3(mm3(inv_in, right(gtr_ref[...])), right(inv_out)) * (count * count)
     out_ref[:, :half] = side[:half, :half]
     out_ref[:, half:] = side[half:, :half]
@@ -365,7 +372,7 @@
     fac, gte, gtr = call(
         moments_kernel,
         (
-            jax.ShapeDtypeStruct((ki + 8, ki), jnp.float32),
+            jax.ShapeDtypeStruct((ki, ki), jnp.float32),
             jax.ShapeDtypeStruct((1, ki // 2, ki), jnp.float32),
             jax.ShapeDtypeStruct((ki, ko), jnp.float32),
         ),

time: 46.5 us -> 46.2 us (level)
  no operation moved by 1% of the time
where the time goes in v21:
time: 46.2 us; the launch traced here: 46 us
  starting transfers between devices  26.9 us (58%)
  waiting for transfers between devices  8.84 us (19%)
  Pallas kernels  7.93 us (17%)
  between operations  1.41 us (3%)
  other arithmetic  0.95 us (2%)
    ppermute x10, starting transfers between devices, swap(): return lax.ppermute(x, axis, [(i, i ^ k) for i in range(count)])  16.6 us
    ppermute x7, starting transfers between devices, mixed(): return lax.ppermute(x, (*axes, 'mp'), pairs)  10.3 us
    pallas_call x12, Pallas kernels, call(): pl.pallas_call(kernel, out_shape=out_shape, in_specs=in_specs, out_specs=...  7.93 us
    ppermute x10, waiting for transfers between devices, swap(): return lax.ppermute(x, axis, [(i, i ^ k) for i in range(count)])  5.49 us
    ppermute x7, waiting for transfers between devices, mixed(): return lax.ppermute(x, (*axes, 'mp'), pairs)  3.35 us
  transfers between devices with their start and end apart: 17, of which 9 were waited for; matrix products, arithmetic and copies ran while one was open for 0% of the time, Pallas kernels for 13%

profile of v21, /device:TPU:0, one launch (start us, length us, event | category | flops | bytes accessed | tf_op | source)
XLA Modules:
  0.0 46.0 jit_solution(10866037543487062682)
XLA Ops:
  0.0 0.9 %fusion = (bf16[48,1024]{1,0:T(8,128)(2,1)S(1)}, bf16[48,1024]{1,0:T(8,128)(2,1)S(1)}) fusion(s32[]{:T(128)S(6)} %select_n.7, bf16[32,4096]{1,0:T(8,128)(2,1)} %bitcast.6, bf16[16,4096]{1,0:T(8,128)(2,1)} %bitcast.12, s32[]{:T(128)S(6)} %select_n.6), kind=kLoop, calls=%fused_computation.6 | loop fusion | flops 393216 | bytes 589832 | tf_op jit(solution)/shard_map/concatenate | solution.py:299
  0.9 4.1 %collective-permute-start.6 = (bf16[48,512]{1,0:T(8,128)(2,1)S(1)}, bf16[48,512]{1,0:T(8,128)(2,1)S(1)}, u32[]{:S(2)}, u32[]{:S(2)}) collective-permute-start(bf16[48,512]{1,0:T(8,128)(2,1)S(1)} %get-tuple-element.25.refs_0_), channel_id=1, source_target_pairs={{0,8},{4,12},{8,0},{12,4},{1,9},{5,13},{9,1},{13,5},{2,10},{6,14},... | collective-permute-start | bytes 147464 | tf_op jit(solution)/shard_map/ppermute | solution.py:39
  5.0 0.1 collective-permute-start
  5.1 2.8 %collective-permute-start.4 = (bf16[48,1024]{1,0:T(8,128)(2,1)S(1)}, bf16[48,1024]{1,0:T(8,128)(2,1)S(1)}, u32[]{:S(2)}, u32[]{:S(2)}) collective-permute-start(bf16[48,1024]{1,0:T(8,128)(2,1)S(1)} %get-tuple-element.23.refs_0_), channel_id=1, source_target_pairs={{0,8},{4,12},{8,0},{12,4},{1,9},{5,13},{9,1},{13,5},{2,10},{6,14},... | collective-permute-start | bytes 294920 | tf_op jit(solution)/shard_map/ppermute | solution.py:39
  7.9 0.0 collective-permute-done.6.refs_1_.refs_0_
  8.0 2.8 %collective-permute-start.7 = (bf16[96,512]{1,0:T(8,128)(2,1)S(1)}, bf16[96,512]{1,0:T(8,128)(2,1)S(1)}, u32[]{:S(2)}, u32[]{:S(2)}) collective-permute-start(bf16[96,512]{1,0:T(8,128)(2,1)S(1)} %shard_map.86), channel_id=1, source_target_pairs={{0,4},{4,0},{8,12},{12,8},{1,5},{5,1},{9,13},{13,9},{2,6},{6,2},{1... | collective-permute-start | bytes 294920 | tf_op jit(solution)/shard_map/ppermute | solution.py:39
  10.7 2.8 %collective-permute-done.refs_1_.refs_0_ = bf16[48,512]{1,0:T(8,128)(2,1)S(1)} collective-permute-done((bf16[48,512]{1,0:T(8,128)(2,1)S(1)}, bf16[48,512]{1,0:T(8,128)(2,1)S(1)}, u32[]{:S(2)}, u32[]{:S(2)}) %collective-permute-start) | collective-permute-done | bytes 49184 | tf_op jit(solution)/shard_map/ppermute | solution.py:39
  13.5 0.1 collective-permute-start.1
  13.6 1.2 %collective-permute-done.4.refs_1_.refs_8_ = bf16[48,1024]{1,0:T(8,128)(2,1)S(1)} collective-permute-done((bf16[48,1024]{1,0:T(8,128)(2,1)S(1)}, bf16[48,1024]{1,0:T(8,128)(2,1)S(1)}, u32[]{:S(2)}, u32[]{:S(2)}) %collective-permute-start.4) | collective-permute-done | bytes 98336 | tf_op jit(solution)/shard_map/ppermute | solution.py:39
  14.9 0.9 %collective-permute-start.5 = (bf16[96,1024]{1,0:T(8,128)(2,1)S(1)}, bf16[96,1024]{1,0:T(8,128)(2,1)S(1)}, u32[]{:S(2)}, u32[]{:S(2)}) collective-permute-start(bf16[96,1024]{1,0:T(8,128)(2,1)S(1)} %shard_map.85), channel_id=1, source_target_pairs={{0,4},{4,0},{8,12},{12,8},{1,5},{5,1},{9,13},{13,9},{2,6},{6,2},{1... | collective-permute-start | bytes 589832 | tf_op jit(solution)/shard_map/ppermute | solution.py:39
  15.7 1.0 %collective-permute-done.7.refs_1_ = bf16[96,512]{1,0:T(8,128)(2,1)S(1)} collective-permute-done((bf16[96,512]{1,0:T(8,128)(2,1)S(1)}, bf16[96,512]{1,0:T(8,128)(2,1)S(1)}, u32[]{:S(2)}, u32[]{:S(2)}) %collective-permute-start.7) | collective-permute-done | bytes 98336 | tf_op jit(solution)/shard_map/ppermute | solution.py:39
  16.7 1.6 %collective-permute-start.8 = (bf16[144,512]{1,0:T(8,128)(2,1)S(1)}, bf16[144,512]{1,0:T(8,128)(2,1)S(1)}, u32[]{:S(2)}, u32[]{:S(2)}) collective-permute-start(bf16[144,512]{1,0:T(8,128)(2,1)S(1)} %shard_map.87.refs_6_), channel_id=1, source_target_pairs={{0,2},{1,17},{2,0},{3,19},{16,18},{17,1},{18,16},{19,3},{4,6},{5,2... | collective-permute-start | bytes 442376 | tf_op jit(solution)/shard_map/ppermute | solution.py:51
  18.3 1.5 %collective-permute-start.9 = (bf16[144,512]{1,0:T(8,128)(2,1)S(1)}, bf16[144,512]{1,0:T(8,128)(2,1)S(1)}, u32[]{:S(2)}, u32[]{:S(2)}) collective-permute-start(bf16[144,512]{1,0:T(8,128)(2,1)S(1)} %shard_map.87.refs_6_), channel_id=1, source_target_pairs={{0,16},{1,3},{2,18},{3,1},{16,0},{17,19},{18,2},{19,17},{4,20},{5,... | collective-permute-start | bytes 442376 | tf_op jit(solution)/shard_map/ppermute | solution.py:51
  19.8 0.0 collective-permute-done.1.refs_1_
  19.8 1.1 %collective-permute-start.2 = (bf16[144,512]{1,0:T(8,128)(2,1)S(1)}, bf16[144,512]{1,0:T(8,128)(2,1)S(1)}, u32[]{:S(2)}, u32[]{:S(2)}) collective-permute-start(bf16[144,512]{1,0:T(8,128)(2,1)S(1)} %shard_map.84.refs_7_), channel_id=1, source_target_pairs={{0,2},{1,17},{2,0},{3,19},{16,18},{17,1},{18,16},{19,3},{4,6},{5,2... | collective-permute-start | bytes 442376 | tf_op jit(solution)/shard_map/ppermute | solution.py:51
  20.9 1.5 %collective-permute-start.3 = (bf16[144,512]{1,0:T(8,128)(2,1)S(1)}, bf16[144,512]{1,0:T(8,128)(2,1)S(1)}, u32[]{:S(2)}, u32[]{:S(2)}) collective-permute-start(bf16[144,512]{1,0:T(8,128)(2,1)S(1)} %shard_map.84.refs_7_), channel_id=1, source_target_pairs={{0,16},{1,3},{2,18},{3,1},{16,0},{17,19},{18,2},{19,17},{4,20},{5,... | collective-permute-start | bytes 442376 | tf_op jit(solution)/shard_map/ppermute | solution.py:51
  22.4 2.3 %shard_map.82 = (bf16[128,4096]{1,0:T(8,128)(2,1)S(1)}, bf16[128,4096]{1,0:T(8,128)(2,1)S(1)}, bf16[128,4096]{1,0:T(8,128)(2,1)S(1)}, bf16[128,4096]{1,0:T(8,128...) custom-call(bf16[128,4096]{1,0:T(8,128)(2,1)} %bitcast.8, bf16[128,4096]{1,0:T(8,128)(2,1)} %bitcast.9, ...), custom_call_target="tpu_custom_call" | custom-call | flops 1073741824 | bytes 65536 | tf_op jit(solution)/shard_map/pallas_call | solution.py:27
  24.8 0.6 %shard_map.88.refs_8_ = f32[384,128]{1,0:T(8,128)S(1)} custom-call(bf16[128,4096]{1,0:T(8,128)(2,1)S(1)} %get-tuple-element.14.refs_0_, bf16[128,4096]{1,0:T(8,128)(2,1)S(1)} %get-tuple-element.15.refs_1_, bf16[128,4096]{1,0:T(8,128)(2,1)S(1)} %get-tuple-element.16.refs_2_, bf16[128,4096]{1,0:T(8,128)(2,1)S(1)} %get-tuple-element.17.refs_3_, ...), custom_call_target="tpu_custom_call" | custom-call | flops 268435456 | bytes 65536 | tf_op jit(solution)/shard_map/pallas_call | solution.py:27
  25.3 0.0 collective-permute-done.8.refs_6_
  25.3 0.0 collective-permute-done.9.refs_7_
  25.3 0.6 %shard_map.89.refs_10_ = f32[384,128]{1,0:T(8,128)S(1)} custom-call(bf16[128,4096]{1,0:T(8,128)(2,1)S(1)} %get-tuple-element.14.refs_0_, bf16[128,4096]{1,0:T(8,128)(2,1)S(1)} %get-tuple-element.15.refs_1_, bf16[128,4096]{1,0:T(8,128)(2,1)S(1)} %get-tuple-element.16.refs_2_, bf16[128,4096]{1,0:T(8,128)(2,1)S(1)} %get-tuple-element.17.refs_3_, ...), custom_call_target="tpu_custom_call" | custom-call | flops 268435456 | bytes 65536 | tf_op jit(solution)/shard_map/pallas_call | solution.py:27
  25.9 0.0 collective-permute-done.2.refs_6_
  25.9 0.2 collective-permute-done.3.refs_7_
  26.1 0.0 collective-permute-done.5.refs_9_
  26.1 0.8 %shard_map.90.mine = f32[384,128]{1,0:T(8,128)S(1)} custom-call(bf16[128,4096]{1,0:T(8,128)(2,1)S(1)} %get-tuple-element.14.refs_0_, bf16[128,4096]{1,0:T(8,128)(2,1)S(1)} %get-tuple-element.15.refs_1_, bf16[128,4096]{1,0:T(8,128)(2,1)S(1)} %get-tuple-element.16.refs_2_, bf16[128,4096]{1,0:T(8,128)(2,1)S(1)} %get-tuple-element.17.refs_3_, ...), custom_call_target="tpu_custom_call" | custom-call | flops 268435456 | bytes 65536 | tf_op jit(solution)/shard_map/pallas_call | solution.py:27
  26.9 0.1 collective-permute-start.10
  28.3 0.1 collective-permute-done.10.other
  28.4 0.5 %shard_map.91 = (f32[128,128]{1,0:T(8,128)S(1)}, f32[1,64,128]{2,1,0:T(8,128)S(1)}, f32[128,64]{1,0:T(8,128)S(1)}) custom-call(s32[1]{0:T(128)S(6)} %copy.9.len_tr, s32[1]{0:T(128)S(6)} %copy.10.len_te, f32[384,128]{1,0:T(8,128)S(1)} %shard_map.90.mine, f32[384,128]{1,0:T(8,128)S(1)} %collective-permute-done.10.other), custom_call_target="tpu_custom_call" | custom-call | bytes 65536 | tf_op jit(solution)/shard_map/pallas_call | solution.py:27
  28.9 1.1 %collective-permute-start.11 = (f32[128,128]{1,0:T(8,128)S(1)}, f32[128,128]{1,0:T(8,128)S(1)}, u32[]{:S(2)}, u32[]{:S(2)}) collective-permute-start(f32[128,128]{1,0:T(8,128)S(1)} %get-tuple-element.20), channel_id=1, source_target_pairs={{0,2},{1,9},{2,0},{3,11},{4,6},{5,13},{6,4},{7,15},{8,10},{9,1},{1... | collective-permute-start | bytes 196616 | tf_op jit(solution)/shard_map/ppermute | solution.py:51
  30.0 2.7 %collective-permute-start.14 = (f32[1,64,128]{2,1,0:T(8,128)S(1)}, f32[1,64,128]{2,1,0:T(8,128)S(1)}, u32[]{:S(2)}, u32[]{:S(2)}) collective-permute-start(f32[1,64,128]{2,1,0:T(8,128)S(1)} %get-tuple-element.22), channel_id=1, source_target_pairs={{0,8},{4,12},{8,0},{12,4},{1,9},{5,13},{9,1},{13,5},{2,10},{6,14},... | collective-permute-start | bytes 98312 | tf_op jit(solution)/shard_map/ppermute | solution.py:39
  32.7 0.6 %collective-permute-done.11 = f32[128,128]{1,0:T(8,128)S(1)} collective-permute-done((f32[128,128]{1,0:T(8,128)S(1)}, f32[128,128]{1,0:T(8,128)S(1)}, u32[]{:S(2)}, u32[]{:S(2)}) %collective-permute-start.11) | collective-permute-done | bytes 65568 | tf_op jit(solution)/shard_map/ppermute | solution.py:51
  33.2 1.3 %collective-permute-start.12 = (f32[128,128]{1,0:T(8,128)S(1)}, f32[128,128]{1,0:T(8,128)S(1)}, u32[]{:S(2)}, u32[]{:S(2)}) collective-permute-start(f32[128,128]{1,0:T(8,128)S(1)} %add.21), channel_id=1, source_target_pairs={{0,4},{1,3},{2,6},{3,1},{4,0},{5,7},{6,2},{7,5},{8,12},{9,11},{10,... | collective-permute-start | bytes 196616 | tf_op jit(solution)/shard_map/ppermute | solution.py:51
  34.5 0.3 collective-permute-done.14
  34.8 1.5 %collective-permute-start.15 = (f32[2,64,128]{2,1,0:T(8,128)S(1)}, f32[2,64,128]{2,1,0:T(8,128)S(1)}, u32[]{:S(2)}, u32[]{:S(2)}) collective-permute-start(f32[2,64,128]{2,1,0:T(8,128)S(1)} %pad_maximum_fusion.2), channel_id=1, source_target_pairs={{0,4},{4,0},{8,12},{12,8},{1,5},{5,1},{9,13},{13,9},{2,6},{6,2},{1... | collective-permute-start | bytes 196616 | tf_op jit(solution)/shard_map/ppermute | solution.py:39
  36.3 1.2 %collective-permute-done.12 = f32[128,128]{1,0:T(8,128)S(1)} collective-permute-done((f32[128,128]{1,0:T(8,128)S(1)}, f32[128,128]{1,0:T(8,128)S(1)}, u32[]{:S(2)}, u32[]{:S(2)}) %collective-permute-start.12) | collective-permute-done | bytes 65568 | tf_op jit(solution)/shard_map/ppermute | solution.py:51
  37.6 2.3 %collective-permute-start.13 = (f32[128,128]{1,0:T(8,128)S(1)}, f32[128,128]{1,0:T(8,128)S(1)}, u32[]{:S(2)}, u32[]{:S(2)}) collective-permute-start(f32[128,128]{1,0:T(8,128)S(1)} %add.22), channel_id=1, source_target_pairs={{0,8},{1,5},{2,10},{3,7},{4,12},{5,1},{6,14},{7,3},{8,0},{9,13},{1... | collective-permute-start | bytes 196616 | tf_op jit(solution)/shard_map/ppermute | solution.py:51
  39.9 0.0 collective-permute-done.15
  39.9 1.6 %collective-permute-start.16 = (f32[4,64,128]{2,1,0:T(8,128)S(1)}, f32[4,64,128]{2,1,0:T(8,128)S(1)}, u32[]{:S(2)}, u32[]{:S(2)}) collective-permute-start(f32[4,64,128]{2,1,0:T(8,128)S(1)} %pad_maximum_fusion.1), channel_id=1, source_target_pairs={{0,2},{2,0},{1,3},{3,1},{4,6},{6,4},{5,7},{7,5},{8,10},{10,8},{9,1... | collective-permute-start | bytes 393224 | tf_op jit(solution)/shard_map/ppermute | solution.py:39
  41.4 1.4 %collective-permute-done.13 = f32[128,128]{1,0:T(8,128)S(1)} collective-permute-done((f32[128,128]{1,0:T(8,128)S(1)}, f32[128,128]{1,0:T(8,128)S(1)}, u32[]{:S(2)}, u32[]{:S(2)}) %collective-permute-start.13) | collective-permute-done | bytes 65568 | tf_op jit(solution)/shard_map/ppermute | solution.py:51
  42.8 2.5 %shard_map.92.side_ref = f32[64,128]{1,0:T(8,128)S(1)} custom-call(f32[128,128]{1,0:T(8,128)S(1)} %add.23.fac_ref, f32[128,64]{1,0:T(8,128)S(1)} %get-tuple-element.21.gtr_ref), custom_call_target="tpu_custom_call" | custom-call | flops 4294967296 | bytes 65536 | tf_op jit(solution)/shard_map/pallas_call | solution.py:27
  45.4 0.0 collective-permute-done.16
  45.4 0.6 %shard_map.93 = f32[1,8]{1,0:T(1,128)} custom-call(f32[64,128]{1,0:T(8,128)S(1)} %shard_map.92.side_ref, f32[8,64,128]{2,1,0:T(8,128)S(1)} %pad_maximum_fusion.gte_ref), custom_call_target="tpu_custom_call" | custom-call | bytes 65536 | tf_op jit(solution)/shard_map/pallas_call | solution.py:27
  (12 shorter events, 0.1 us)
Async XLA Ops:
  0.9 7.0 %collective-permute-start.6 = (bf16[48,512]{1,0:T(8,128)(2,1)S(1)}, bf16[48,512]{1,0:T(8,128)(2,1)S(1)}, u32[]{:S(2)}, u32[]{:S(2)}) collective-permute-start(bf16[48,512]{1,0:T(8,128)(2,1)S(1)} %get-tuple-element.25.refs_0_), channel_id=1, source_target_pairs={{0,8},{4,12},{8,0},{12,4},{1,9},{5,13},{9,1},{13,5},{2,10},{6,14},... | collective-permute-start | bytes 147464 | tf_op jit(solution)/shard_map/ppermute | solution.py:39
  5.0 8.5 %collective-permute-start = (bf16[48,512]{1,0:T(8,128)(2,1)S(1)}, bf16[48,512]{1,0:T(8,128)(2,1)S(1)}, u32[]{:S(2)}, u32[]{:S(2)}) collective-permute-start(bf16[48,512]{1,0:T(8,128)(2,1)S(1)} %get-tuple-element.26.refs_0_), channel_id=1, source_target_pairs={{0,8},{4,12},{8,0},{12,4},{1,9},{5,13},{9,1},{13,5},{2,10},{6,14},... | collective-permute-start | bytes 147464 | tf_op jit(solution)/shard_map/ppermute | solution.py:39
  5.1 9.8 %collective-permute-start.4 = (bf16[48,1024]{1,0:T(8,128)(2,1)S(1)}, bf16[48,1024]{1,0:T(8,128)(2,1)S(1)}, u32[]{:S(2)}, u32[]{:S(2)}) collective-permute-start(bf16[48,1024]{1,0:T(8,128)(2,1)S(1)} %get-tuple-element.23.refs_0_), channel_id=1, source_target_pairs={{0,8},{4,12},{8,0},{12,4},{1,9},{5,13},{9,1},{13,5},{2,10},{6,14},... | collective-permute-start | bytes 294920 | tf_op jit(solution)/shard_map/ppermute | solution.py:39
  8.0 8.8 %collective-permute-start.7 = (bf16[96,512]{1,0:T(8,128)(2,1)S(1)}, bf16[96,512]{1,0:T(8,128)(2,1)S(1)}, u32[]{:S(2)}, u32[]{:S(2)}) collective-permute-start(bf16[96,512]{1,0:T(8,128)(2,1)S(1)} %shard_map.86), channel_id=1, source_target_pairs={{0,4},{4,0},{8,12},{12,8},{1,5},{5,1},{9,13},{13,9},{2,6},{6,2},{1... | collective-permute-start | bytes 294920 | tf_op jit(solution)/shard_map/ppermute | solution.py:39
  13.5 6.3 %collective-permute-start.1 = (bf16[96,512]{1,0:T(8,128)(2,1)S(1)}, bf16[96,512]{1,0:T(8,128)(2,1)S(1)}, u32[]{:S(2)}, u32[]{:S(2)}) collective-permute-start(bf16[96,512]{1,0:T(8,128)(2,1)S(1)} %shard_map.83), channel_id=1, source_target_pairs={{0,4},{4,0},{8,12},{12,8},{1,5},{5,1},{9,13},{13,9},{2,6},{6,2},{1... | collective-permute-start | bytes 294920 | tf_op jit(solution)/shard_map/ppermute | solution.py:39
  14.9 11.2 %collective-permute-start.5 = (bf16[96,1024]{1,0:T(8,128)(2,1)S(1)}, bf16[96,1024]{1,0:T(8,128)(2,1)S(1)}, u32[]{:S(2)}, u32[]{:S(2)}) collective-permute-start(bf16[96,1024]{1,0:T(8,128)(2,1)S(1)} %shard_map.85), channel_id=1, source_target_pairs={{0,4},{4,0},{8,12},{12,8},{1,5},{5,1},{9,13},{13,9},{2,6},{6,2},{1... | collective-permute-start | bytes 589832 | tf_op jit(solution)/shard_map/ppermute | solution.py:39
  16.7 8.6 %collective-permute-start.8 = (bf16[144,512]{1,0:T(8,128)(2,1)S(1)}, bf16[144,512]{1,0:T(8,128)(2,1)S(1)}, u32[]{:S(2)}, u32[]{:S(2)}) collective-permute-start(bf16[144,512]{1,0:T(8,128)(2,1)S(1)} %shard_map.87.refs_6_), channel_id=1, source_target_pairs={{0,2},{1,17},{2,0},{3,19},{16,18},{17,1},{18,16},{19,3},{4,6},{5,2... | collective-permute-start | bytes 442376 | tf_op jit(solution)/shard_map/ppermute | solution.py:51
  18.3 7.0 %collective-permute-start.9 = (bf16[144,512]{1,0:T(8,128)(2,1)S(1)}, bf16[144,512]{1,0:T(8,128)(2,1)S(1)}, u32[]{:S(2)}, u32[]{:S(2)}) collective-permute-start(bf16[144,512]{1,0:T(8,128)(2,1)S(1)} %shard_map.87.refs_6_), channel_id=1, source_target_pairs={{0,16},{1,3},{2,18},{3,1},{16,0},{17,19},{18,2},{19,17},{4,20},{5,... | collective-permute-start | bytes 442376 | tf_op jit(solution)/shard_map/ppermute | solution.py:51
  19.8 6.0 %collective-permute-start.2 = (bf16[144,512]{1,0:T(8,128)(2,1)S(1)}, bf16[144,512]{1,0:T(8,128)(2,1)S(1)}, u32[]{:S(2)}, u32[]{:S(2)}) collective-permute-start(bf16[144,512]{1,0:T(8,128)(2,1)S(1)} %shard_map.84.refs_7_), channel_id=1, source_target_pairs={{0,2},{1,17},{2,0},{3,19},{16,18},{17,1},{18,16},{19,3},{4,6},{5,2... | collective-permute-start | bytes 442376 | tf_op jit(solution)/shard_map/ppermute | solution.py:51
  20.9 5.1 %collective-permute-start.3 = (bf16[144,512]{1,0:T(8,128)(2,1)S(1)}, bf16[144,512]{1,0:T(8,128)(2,1)S(1)}, u32[]{:S(2)}, u32[]{:S(2)}) collective-permute-start(bf16[144,512]{1,0:T(8,128)(2,1)S(1)} %shard_map.84.refs_7_), channel_id=1, source_target_pairs={{0,16},{1,3},{2,18},{3,1},{16,0},{17,19},{18,2},{19,17},{4,20},{5,... | collective-permute-start | bytes 442376 | tf_op jit(solution)/shard_map/ppermute | solution.py:51
  26.9 1.5 %collective-permute-start.10 = (f32[384,128]{1,0:T(8,128)S(1)}, f32[384,128]{1,0:T(8,128)S(1)}, u32[]{:S(2)}, u32[]{:S(2)}) collective-permute-start(f32[384,128]{1,0:T(8,128)S(1)} %shard_map.90.mine), channel_id=1, source_target_pairs={{0,1},{1,0},{2,3},{3,2},{4,5},{5,4},{6,7},{7,6},{8,9},{9,8},{10,11... | collective-permute-start | bytes 589832 | tf_op jit(solution)/shard_map/ppermute | solution.py:39
  28.9 4.3 %collective-permute-start.11 = (f32[128,128]{1,0:T(8,128)S(1)}, f32[128,128]{1,0:T(8,128)S(1)}, u32[]{:S(2)}, u32[]{:S(2)}) collective-permute-start(f32[128,128]{1,0:T(8,128)S(1)} %get-tuple-element.20), channel_id=1, source_target_pairs={{0,2},{1,9},{2,0},{3,11},{4,6},{5,13},{6,4},{7,15},{8,10},{9,1},{1... | collective-permute-start | bytes 196616 | tf_op jit(solution)/shard_map/ppermute | solution.py:51
  30.0 4.8 %collective-permute-start.14 = (f32[1,64,128]{2,1,0:T(8,128)S(1)}, f32[1,64,128]{2,1,0:T(8,128)S(1)}, u32[]{:S(2)}, u32[]{:S(2)}) collective-permute-start(f32[1,64,128]{2,1,0:T(8,128)S(1)} %get-tuple-element.22), channel_id=1, source_target_pairs={{0,8},{4,12},{8,0},{12,4},{1,9},{5,13},{9,1},{13,5},{2,10},{6,14},... | collective-permute-start | bytes 98312 | tf_op jit(solution)/shard_map/ppermute | solution.py:39
  33.2 4.3 %collective-permute-start.12 = (f32[128,128]{1,0:T(8,128)S(1)}, f32[128,128]{1,0:T(8,128)S(1)}, u32[]{:S(2)}, u32[]{:S(2)}) collective-permute-start(f32[128,128]{1,0:T(8,128)S(1)} %add.21), channel_id=1, source_target_pairs={{0,4},{1,3},{2,6},{3,1},{4,0},{5,7},{6,2},{7,5},{8,12},{9,11},{10,... | collective-permute-start | bytes 196616 | tf_op jit(solution)/shard_map/ppermute | solution.py:51
  34.8 5.1 %collective-permute-start.15 = (f32[2,64,128]{2,1,0:T(8,128)S(1)}, f32[2,64,128]{2,1,0:T(8,128)S(1)}, u32[]{:S(2)}, u32[]{:S(2)}) collective-permute-start(f32[2,64,128]{2,1,0:T(8,128)S(1)} %pad_maximum_fusion.2), channel_id=1, source_target_pairs={{0,4},{4,0},{8,12},{12,8},{1,5},{5,1},{9,13},{13,9},{2,6},{6,2},{1... | collective-permute-start | bytes 196616 | tf_op jit(solution)/shard_map/ppermute | solution.py:39
  37.6 5.2 %collective-permute-start.13 = (f32[128,128]{1,0:T(8,128)S(1)}, f32[128,128]{1,0:T(8,128)S(1)}, u32[]{:S(2)}, u32[]{:S(2)}) collective-permute-start(f32[128,128]{1,0:T(8,128)S(1)} %add.22), channel_id=1, source_target_pairs={{0,8},{1,5},{2,10},{3,7},{4,12},{5,1},{6,14},{7,3},{8,0},{9,13},{1... | collective-permute-start | bytes 196616 | tf_op jit(solution)/shard_map/ppermute | solution.py:51
  39.9 5.5 %collective-permute-start.16 = (f32[4,64,128]{2,1,0:T(8,128)S(1)}, f32[4,64,128]{2,1,0:T(8,128)S(1)}, u32[]{:S(2)}, u32[]{:S(2)}) collective-permute-start(f32[4,64,128]{2,1,0:T(8,128)S(1)} %pad_maximum_fusion.1), channel_id=1, source_target_pairs={{0,2},{2,0},{1,3},{3,1},{4,6},{6,4},{5,7},{7,5},{8,10},{10,8},{9,1... | collective-permute-start | bytes 393224 | tf_op jit(solution)/shard_map/ppermute | solution.py:39

commit v22 on v21

--- a/solution.py
+++ b/solution.py
@@ -344,9 +344,15 @@
         return tuple((p, i * shard, k) for i, k in enumerate((2, 1, 3)))
 
     acc = accumulate(
-        ((0, 0, part, stacked(0)), (0, part, part, stacked(1))), (za, zb), None)
-    acc = accumulate(
-        ((1, 0, part, stacked(0)), (2, 0, part, stacked(1))), (xa, ya), acc)
+        (
+            (0, 0, part, stacked(0)),
+            (0, part, part, stacked(1)),
+            (1, 0, part, stacked(2)),
+            (2, 0, part, stacked(3)),
+        ),
+        (za, zb, xa, ya),
+        None,
+    )
     return accumulate(
         (
             (1, part, part, stacked(0)),

time: 46.2 us -> 46.2 us (level)
    pallas_call x12 -> x11, Pallas kernels: 7.93 us -> 7.66 us  [call(): pl.pallas_call(kernel, out_shape=out_shape, in_specs=in_specs, out_specs=...]
  transfers between devices with their start and end apart: 17 -> 17, of which waited for: 9 -> 9; matrix products, arithmetic and copies ran while one was open for 0% -> 0% of each run, Pallas kernels for 13% -> 12%
where the time goes in v22:
time: 46.2 us; the launch traced here: 46 us
  starting transfers between devices  26.9 us (58%)
  waiting for transfers between devices  9.11 us (20%)
  Pallas kernels  7.66 us (17%)
  between operations  1.42 us (3%)
  other arithmetic  0.95 us (2%)
    ppermute x10, starting transfers between devices, swap(): return lax.ppermute(x, axis, [(i, i ^ k) for i in range(count)])  16.6 us
    ppermute x7, starting transfers between devices, mixed(): return lax.ppermute(x, (*axes, 'mp'), pairs)  10.3 us
    pallas_call x11, Pallas kernels, call(): pl.pallas_call(kernel, out_shape=out_shape, in_specs=in_specs, out_specs=...  7.66 us
    ppermute x10, waiting for transfers between devices, swap(): return lax.ppermute(x, axis, [(i, i ^ k) for i in range(count)])  5.49 us
    ppermute x7, waiting for transfers between devices, mixed(): return lax.ppermute(x, (*axes, 'mp'), pairs)  3.62 us
  transfers between devices with their start and end apart: 17, of which 9 were waited for; matrix products, arithmetic and copies ran while one was open for 0% of the time, Pallas kernels for 12%

profile of v22, /device:TPU:0, one launch (start us, length us, event | category | flops | bytes accessed | tf_op | source)
XLA Modules:
  0.0 46.0 jit_solution(7506593460635268708)
XLA Ops:
  0.0 0.9 %fusion = (bf16[48,1024]{1,0:T(8,128)(2,1)S(1)}, bf16[48,1024]{1,0:T(8,128)(2,1)S(1)}) fusion(s32[]{:T(128)S(6)} %select_n.7, bf16[32,4096]{1,0:T(8,128)(2,1)} %bitcast.6, bf16[16,4096]{1,0:T(8,128)(2,1)} %bitcast.12, s32[]{:T(128)S(6)} %select_n.6), kind=kLoop, calls=%fused_computation.6 | loop fusion | flops 393216 | bytes 589832 | tf_op jit(solution)/shard_map/concatenate | solution.py:299
  0.9 4.1 %collective-permute-start.6 = (bf16[48,512]{1,0:T(8,128)(2,1)S(1)}, bf16[48,512]{1,0:T(8,128)(2,1)S(1)}, u32[]{:S(2)}, u32[]{:S(2)}) collective-permute-start(bf16[48,512]{1,0:T(8,128)(2,1)S(1)} %get-tuple-element.25.refs_0_), channel_id=1, source_target_pairs={{0,8},{4,12},{8,0},{12,4},{1,9},{5,13},{9,1},{13,5},{2,10},{6,14},... | collective-permute-start | bytes 147464 | tf_op jit(solution)/shard_map/ppermute | solution.py:39
  5.0 0.1 collective-permute-start
  5.1 2.8 %collective-permute-start.4 = (bf16[48,1024]{1,0:T(8,128)(2,1)S(1)}, bf16[48,1024]{1,0:T(8,128)(2,1)S(1)}, u32[]{:S(2)}, u32[]{:S(2)}) collective-permute-start(bf16[48,1024]{1,0:T(8,128)(2,1)S(1)} %get-tuple-element.23.refs_0_), channel_id=1, source_target_pairs={{0,8},{4,12},{8,0},{12,4},{1,9},{5,13},{9,1},{13,5},{2,10},{6,14},... | collective-permute-start | bytes 294920 | tf_op jit(solution)/shard_map/ppermute | solution.py:39
  7.9 0.0 collective-permute-done.6.refs_1_.refs_0_
  8.0 2.8 %collective-permute-start.7 = (bf16[96,512]{1,0:T(8,128)(2,1)S(1)}, bf16[96,512]{1,0:T(8,128)(2,1)S(1)}, u32[]{:S(2)}, u32[]{:S(2)}) collective-permute-start(bf16[96,512]{1,0:T(8,128)(2,1)S(1)} %shard_map.86), channel_id=1, source_target_pairs={{0,4},{4,0},{8,12},{12,8},{1,5},{5,1},{9,13},{13,9},{2,6},{6,2},{1... | collective-permute-start | bytes 294920 | tf_op jit(solution)/shard_map/ppermute | solution.py:39
  10.7 2.8 %collective-permute-done.refs_1_.refs_0_ = bf16[48,512]{1,0:T(8,128)(2,1)S(1)} collective-permute-done((bf16[48,512]{1,0:T(8,128)(2,1)S(1)}, bf16[48,512]{1,0:T(8,128)(2,1)S(1)}, u32[]{:S(2)}, u32[]{:S(2)}) %collective-permute-start) | collective-permute-done | bytes 49184 | tf_op jit(solution)/shard_map/ppermute | solution.py:39
  13.5 0.1 collective-permute-start.1
  13.6 1.2 %collective-permute-done.4.refs_1_.refs_8_ = bf16[48,1024]{1,0:T(8,128)(2,1)S(1)} collective-permute-done((bf16[48,1024]{1,0:T(8,128)(2,1)S(1)}, bf16[48,1024]{1,0:T(8,128)(2,1)S(1)}, u32[]{:S(2)}, u32[]{:S(2)}) %collective-permute-start.4) | collective-permute-done | bytes 98336 | tf_op jit(solution)/shard_map/ppermute | solution.py:39
  14.9 0.9 %collective-permute-start.5 = (bf16[96,1024]{1,0:T(8,128)(2,1)S(1)}, bf16[96,1024]{1,0:T(8,128)(2,1)S(1)}, u32[]{:S(2)}, u32[]{:S(2)}) collective-permute-start(bf16[96,1024]{1,0:T(8,128)(2,1)S(1)} %shard_map.85), channel_id=1, source_target_pairs={{0,4},{4,0},{8,12},{12,8},{1,5},{5,1},{9,13},{13,9},{2,6},{6,2},{1... | collective-permute-start | bytes 589832 | tf_op jit(solution)/shard_map/ppermute | solution.py:39
  15.7 1.0 %collective-permute-done.7.refs_1_ = bf16[96,512]{1,0:T(8,128)(2,1)S(1)} collective-permute-done((bf16[96,512]{1,0:T(8,128)(2,1)S(1)}, bf16[96,512]{1,0:T(8,128)(2,1)S(1)}, u32[]{:S(2)}, u32[]{:S(2)}) %collective-permute-start.7) | collective-permute-done | bytes 98336 | tf_op jit(solution)/shard_map/ppermute | solution.py:39
  16.7 1.6 %collective-permute-start.8 = (bf16[144,512]{1,0:T(8,128)(2,1)S(1)}, bf16[144,512]{1,0:T(8,128)(2,1)S(1)}, u32[]{:S(2)}, u32[]{:S(2)}) collective-permute-start(bf16[144,512]{1,0:T(8,128)(2,1)S(1)} %shard_map.87.refs_6_), channel_id=1, source_target_pairs={{0,2},{1,17},{2,0},{3,19},{16,18},{17,1},{18,16},{19,3},{4,6},{5,2... | collective-permute-start | bytes 442376 | tf_op jit(solution)/shard_map/ppermute | solution.py:51
  18.3 1.5 %collective-permute-start.9 = (bf16[144,512]{1,0:T(8,128)(2,1)S(1)}, bf16[144,512]{1,0:T(8,128)(2,1)S(1)}, u32[]{:S(2)}, u32[]{:S(2)}) collective-permute-start(bf16[144,512]{1,0:T(8,128)(2,1)S(1)} %shard_map.87.refs_6_), channel_id=1, source_target_pairs={{0,16},{1,3},{2,18},{3,1},{16,0},{17,19},{18,2},{19,17},{4,20},{5,... | collective-permute-start | bytes 442376 | tf_op jit(solution)/shard_map/ppermute | solution.py:51
  19.8 0.0 collective-permute-done.1.refs_1_
  19.8 1.1 %collective-permute-start.2 = (bf16[144,512]{1,0:T(8,128)(2,1)S(1)}, bf16[144,512]{1,0:T(8,128)(2,1)S(1)}, u32[]{:S(2)}, u32[]{:S(2)}) collective-permute-start(bf16[144,512]{1,0:T(8,128)(2,1)S(1)} %shard_map.84.refs_7_), channel_id=1, source_target_pairs={{0,2},{1,17},{2,0},{3,19},{16,18},{17,1},{18,16},{19,3},{4,6},{5,2... | collective-permute-start | bytes 442376 | tf_op jit(solution)/shard_map/ppermute | solution.py:51
  20.9 1.5 %collective-permute-start.3 = (bf16[144,512]{1,0:T(8,128)(2,1)S(1)}, bf16[144,512]{1,0:T(8,128)(2,1)S(1)}, u32[]{:S(2)}, u32[]{:S(2)}) collective-permute-start(bf16[144,512]{1,0:T(8,128)(2,1)S(1)} %shard_map.84.refs_7_), channel_id=1, source_target_pairs={{0,16},{1,3},{2,18},{3,1},{16,0},{17,19},{18,2},{19,17},{4,20},{5,... | collective-permute-start | bytes 442376 | tf_op jit(solution)/shard_map/ppermute | solution.py:51
  22.4 2.3 %shard_map.82 = (bf16[128,4096]{1,0:T(8,128)(2,1)S(1)}, bf16[128,4096]{1,0:T(8,128)(2,1)S(1)}, bf16[128,4096]{1,0:T(8,128)(2,1)S(1)}, bf16[128,4096]{1,0:T(8,128...) custom-call(bf16[128,4096]{1,0:T(8,128)(2,1)} %bitcast.8, bf16[128,4096]{1,0:T(8,128)(2,1)} %bitcast.9, ...), custom_call_target="tpu_custom_call" | custom-call | flops 1073741824 | bytes 65536 | tf_op jit(solution)/shard_map/pallas_call | solution.py:27
  24.8 0.0 collective-permute-done.8.refs_8_
  24.8 0.0 collective-permute-done.9.refs_9_
  24.8 0.8 %shard_map.88.refs_10_ = f32[384,128]{1,0:T(8,128)S(1)} custom-call(bf16[128,4096]{1,0:T(8,128)(2,1)S(1)} %get-tuple-element.14.refs_0_, bf16[128,4096]{1,0:T(8,128)(2,1)S(1)} %get-tuple-element.15.refs_1_, bf16[128,4096]{1,0:T(8,128)(2,1)S(1)} %get-tuple-element.16.refs_2_, bf16[128,4096]{1,0:T(8,128)(2,1)S(1)} %get-tuple-element.17.refs_3_, ...), custom_call_target="tpu_custom_call" | custom-call | flops 268435456 | bytes 65536 | tf_op jit(solution)/shard_map/pallas_call | solution.py:27
  25.6 0.0 collective-permute-done.2.refs_6_
  25.6 0.4 collective-permute-done.3.refs_7_
  26.1 0.0 collective-permute-done.5.refs_9_
  26.1 0.8 %shard_map.89.mine = f32[384,128]{1,0:T(8,128)S(1)} custom-call(bf16[128,4096]{1,0:T(8,128)(2,1)S(1)} %get-tuple-element.14.refs_0_, bf16[128,4096]{1,0:T(8,128)(2,1)S(1)} %get-tuple-element.15.refs_1_, bf16[128,4096]{1,0:T(8,128)(2,1)S(1)} %get-tuple-element.16.refs_2_, bf16[128,4096]{1,0:T(8,128)(2,1)S(1)} %get-tuple-element.17.refs_3_, ...), custom_call_target="tpu_custom_call" | custom-call | flops 268435456 | bytes 65536 | tf_op jit(solution)/shard_map/pallas_call | solution.py:27
  26.9 0.1 collective-permute-start.10
  28.3 0.1 collective-permute-done.10.other
  28.4 0.5 %shard_map.90 = (f32[128,128]{1,0:T(8,128)S(1)}, f32[1,64,128]{2,1,0:T(8,128)S(1)}, f32[128,64]{1,0:T(8,128)S(1)}) custom-call(s32[1]{0:T(128)S(6)} %copy.9.len_tr, s32[1]{0:T(128)S(6)} %copy.10.len_te, f32[384,128]{1,0:T(8,128)S(1)} %shard_map.89.mine, f32[384,128]{1,0:T(8,128)S(1)} %collective-permute-done.10.other), custom_call_target="tpu_custom_call" | custom-call | bytes 65536 | tf_op jit(solution)/shard_map/pallas_call | solution.py:27
  28.9 1.1 %collective-permute-start.11 = (f32[128,128]{1,0:T(8,128)S(1)}, f32[128,128]{1,0:T(8,128)S(1)}, u32[]{:S(2)}, u32[]{:S(2)}) collective-permute-start(f32[128,128]{1,0:T(8,128)S(1)} %get-tuple-element.20), channel_id=1, source_target_pairs={{0,2},{1,9},{2,0},{3,11},{4,6},{5,13},{6,4},{7,15},{8,10},{9,1},{1... | collective-permute-start | bytes 196616 | tf_op jit(solution)/shard_map/ppermute | solution.py:51
  30.0 2.7 %collective-permute-start.14 = (f32[1,64,128]{2,1,0:T(8,128)S(1)}, f32[1,64,128]{2,1,0:T(8,128)S(1)}, u32[]{:S(2)}, u32[]{:S(2)}) collective-permute-start(f32[1,64,128]{2,1,0:T(8,128)S(1)} %get-tuple-element.22), channel_id=1, source_target_pairs={{0,8},{4,12},{8,0},{12,4},{1,9},{5,13},{9,1},{13,5},{2,10},{6,14},... | collective-permute-start | bytes 98312 | tf_op jit(solution)/shard_map/ppermute | solution.py:39
  32.7 0.6 %collective-permute-done.11 = f32[128,128]{1,0:T(8,128)S(1)} collective-permute-done((f32[128,128]{1,0:T(8,128)S(1)}, f32[128,128]{1,0:T(8,128)S(1)}, u32[]{:S(2)}, u32[]{:S(2)}) %collective-permute-start.11) | collective-permute-done | bytes 65568 | tf_op jit(solution)/shard_map/ppermute | solution.py:51
  33.2 1.3 %collective-permute-start.12 = (f32[128,128]{1,0:T(8,128)S(1)}, f32[128,128]{1,0:T(8,128)S(1)}, u32[]{:S(2)}, u32[]{:S(2)}) collective-permute-start(f32[128,128]{1,0:T(8,128)S(1)} %add.21), channel_id=1, source_target_pairs={{0,4},{1,3},{2,6},{3,1},{4,0},{5,7},{6,2},{7,5},{8,12},{9,11},{10,... | collective-permute-start | bytes 196616 | tf_op jit(solution)/shard_map/ppermute | solution.py:51
  34.5 0.3 collective-permute-done.14
  34.8 1.5 %collective-permute-start.15 = (f32[2,64,128]{2,1,0:T(8,128)S(1)}, f32[2,64,128]{2,1,0:T(8,128)S(1)}, u32[]{:S(2)}, u32[]{:S(2)}) collective-permute-start(f32[2,64,128]{2,1,0:T(8,128)S(1)} %pad_maximum_fusion.2), channel_id=1, source_target_pairs={{0,4},{4,0},{8,12},{12,8},{1,5},{5,1},{9,13},{13,9},{2,6},{6,2},{1... | collective-permute-start | bytes 196616 | tf_op jit(solution)/shard_map/ppermute | solution.py:39
  36.3 1.2 %collective-permute-done.12 = f32[128,128]{1,0:T(8,128)S(1)} collective-permute-done((f32[128,128]{1,0:T(8,128)S(1)}, f32[128,128]{1,0:T(8,128)S(1)}, u32[]{:S(2)}, u32[]{:S(2)}) %collective-permute-start.12) | collective-permute-done | bytes 65568 | tf_op jit(solution)/shard_map/ppermute | solution.py:51
  37.6 2.3 %collective-permute-start.13 = (f32[128,128]{1,0:T(8,128)S(1)}, f32[128,128]{1,0:T(8,128)S(1)}, u32[]{:S(2)}, u32[]{:S(2)}) collective-permute-start(f32[128,128]{1,0:T(8,128)S(1)} %add.22), channel_id=1, source_target_pairs={{0,8},{1,5},{2,10},{3,7},{4,12},{5,1},{6,14},{7,3},{8,0},{9,13},{1... | collective-permute-start | bytes 196616 | tf_op jit(solution)/shard_map/ppermute | solution.py:51
  39.9 0.0 collective-permute-done.15
  39.9 1.6 %collective-permute-start.16 = (f32[4,64,128]{2,1,0:T(8,128)S(1)}, f32[4,64,128]{2,1,0:T(8,128)S(1)}, u32[]{:S(2)}, u32[]{:S(2)}) collective-permute-start(f32[4,64,128]{2,1,0:T(8,128)S(1)} %pad_maximum_fusion.1), channel_id=1, source_target_pairs={{0,2},{2,0},{1,3},{3,1},{4,6},{6,4},{5,7},{7,5},{8,10},{10,8},{9,1... | collective-permute-start | bytes 393224 | tf_op jit(solution)/shard_map/ppermute | solution.py:39
  41.4 1.4 %collective-permute-done.13 = f32[128,128]{1,0:T(8,128)S(1)} collective-permute-done((f32[128,128]{1,0:T(8,128)S(1)}, f32[128,128]{1,0:T(8,128)S(1)}, u32[]{:S(2)}, u32[]{:S(2)}) %collective-permute-start.13) | collective-permute-done | bytes 65568 | tf_op jit(solution)/shard_map/ppermute | solution.py:51
  42.8 2.5 %shard_map.91.side_ref = f32[64,128]{1,0:T(8,128)S(1)} custom-call(f32[128,128]{1,0:T(8,128)S(1)} %add.23.fac_ref, f32[128,64]{1,0:T(8,128)S(1)} %get-tuple-element.21.gtr_ref), custom_call_target="tpu_custom_call" | custom-call | flops 4294967296 | bytes 65536 | tf_op jit(solution)/shard_map/pallas_call | solution.py:27
  45.4 0.0 collective-permute-done.16
  45.4 0.6 %shard_map.92 = f32[1,8]{1,0:T(1,128)} custom-call(f32[64,128]{1,0:T(8,128)S(1)} %shard_map.91.side_ref, f32[8,64,128]{2,1,0:T(8,128)S(1)} %pad_maximum_fusion.gte_ref), custom_call_target="tpu_custom_call" | custom-call | bytes 65536 | tf_op jit(solution)/shard_map/pallas_call | solution.py:27
  (12 shorter events, 0.1 us)
Async XLA Ops:
  0.9 7.0 %collective-permute-start.6 = (bf16[48,512]{1,0:T(8,128)(2,1)S(1)}, bf16[48,512]{1,0:T(8,128)(2,1)S(1)}, u32[]{:S(2)}, u32[]{:S(2)}) collective-permute-start(bf16[48,512]{1,0:T(8,128)(2,1)S(1)} %get-tuple-element.25.refs_0_), channel_id=1, source_target_pairs={{0,8},{4,12},{8,0},{12,4},{1,9},{5,13},{9,1},{13,5},{2,10},{6,14},... | collective-permute-start | bytes 147464 | tf_op jit(solution)/shard_map/ppermute | solution.py:39
  5.0 8.5 %collective-permute-start = (bf16[48,512]{1,0:T(8,128)(2,1)S(1)}, bf16[48,512]{1,0:T(8,128)(2,1)S(1)}, u32[]{:S(2)}, u32[]{:S(2)}) collective-permute-start(bf16[48,512]{1,0:T(8,128)(2,1)S(1)} %get-tuple-element.26.refs_0_), channel_id=1, source_target_pairs={{0,8},{4,12},{8,0},{12,4},{1,9},{5,13},{9,1},{13,5},{2,10},{6,14},... | collective-permute-start | bytes 147464 | tf_op jit(solution)/shard_map/ppermute | solution.py:39
  5.1 9.8 %collective-permute-start.4 = (bf16[48,1024]{1,0:T(8,128)(2,1)S(1)}, bf16[48,1024]{1,0:T(8,128)(2,1)S(1)}, u32[]{:S(2)}, u32[]{:S(2)}) collective-permute-start(bf16[48,1024]{1,0:T(8,128)(2,1)S(1)} %get-tuple-element.23.refs_0_), channel_id=1, source_target_pairs={{0,8},{4,12},{8,0},{12,4},{1,9},{5,13},{9,1},{13,5},{2,10},{6,14},... | collective-permute-start | bytes 294920 | tf_op jit(solution)/shard_map/ppermute | solution.py:39
  8.0 8.8 %collective-permute-start.7 = (bf16[96,512]{1,0:T(8,128)(2,1)S(1)}, bf16[96,512]{1,0:T(8,128)(2,1)S(1)}, u32[]{:S(2)}, u32[]{:S(2)}) collective-permute-start(bf16[96,512]{1,0:T(8,128)(2,1)S(1)} %shard_map.86), channel_id=1, source_target_pairs={{0,4},{4,0},{8,12},{12,8},{1,5},{5,1},{9,13},{13,9},{2,6},{6,2},{1... | collective-permute-start | bytes 294920 | tf_op jit(solution)/shard_map/ppermute | solution.py:39
  13.5 6.3 %collective-permute-start.1 = (bf16[96,512]{1,0:T(8,128)(2,1)S(1)}, bf16[96,512]{1,0:T(8,128)(2,1)S(1)}, u32[]{:S(2)}, u32[]{:S(2)}) collective-permute-start(bf16[96,512]{1,0:T(8,128)(2,1)S(1)} %shard_map.83), channel_id=1, source_target_pairs={{0,4},{4,0},{8,12},{12,8},{1,5},{5,1},{9,13},{13,9},{2,6},{6,2},{1... | collective-permute-start | bytes 294920 | tf_op jit(solution)/shard_map/ppermute | solution.py:39
  14.9 11.2 %collective-permute-start.5 = (bf16[96,1024]{1,0:T(8,128)(2,1)S(1)}, bf16[96,1024]{1,0:T(8,128)(2,1)S(1)}, u32[]{:S(2)}, u32[]{:S(2)}) collective-permute-start(bf16[96,1024]{1,0:T(8,128)(2,1)S(1)} %shard_map.85), channel_id=1, source_target_pairs={{0,4},{4,0},{8,12},{12,8},{1,5},{5,1},{9,13},{13,9},{2,6},{6,2},{1... | collective-permute-start | bytes 589832 | tf_op jit(solution)/shard_map/ppermute | solution.py:39
  16.7 8.0 %collective-permute-start.8 = (bf16[144,512]{1,0:T(8,128)(2,1)S(1)}, bf16[144,512]{1,0:T(8,128)(2,1)S(1)}, u32[]{:S(2)}, u32[]{:S(2)}) collective-permute-start(bf16[144,512]{1,0:T(8,128)(2,1)S(1)} %shard_map.87.refs_6_), channel_id=1, source_target_pairs={{0,2},{1,17},{2,0},{3,19},{16,18},{17,1},{18,16},{19,3},{4,6},{5,2... | collective-permute-start | bytes 442376 | tf_op jit(solution)/shard_map/ppermute | solution.py:51
  18.3 6.5 %collective-permute-start.9 = (bf16[144,512]{1,0:T(8,128)(2,1)S(1)}, bf16[144,512]{1,0:T(8,128)(2,1)S(1)}, u32[]{:S(2)}, u32[]{:S(2)}) collective-permute-start(bf16[144,512]{1,0:T(8,128)(2,1)S(1)} %shard_map.87.refs_6_), channel_id=1, source_target_pairs={{0,16},{1,3},{2,18},{3,1},{16,0},{17,19},{18,2},{19,17},{4,20},{5,... | collective-permute-start | bytes 442376 | tf_op jit(solution)/shard_map/ppermute | solution.py:51
  19.8 5.8 %collective-permute-start.2 = (bf16[144,512]{1,0:T(8,128)(2,1)S(1)}, bf16[144,512]{1,0:T(8,128)(2,1)S(1)}, u32[]{:S(2)}, u32[]{:S(2)}) collective-permute-start(bf16[144,512]{1,0:T(8,128)(2,1)S(1)} %shard_map.84.refs_7_), channel_id=1, source_target_pairs={{0,2},{1,17},{2,0},{3,19},{16,18},{17,1},{18,16},{19,3},{4,6},{5,2... | collective-permute-start | bytes 442376 | tf_op jit(solution)/shard_map/ppermute | solution.py:51
  20.9 5.1 %collective-permute-start.3 = (bf16[144,512]{1,0:T(8,128)(2,1)S(1)}, bf16[144,512]{1,0:T(8,128)(2,1)S(1)}, u32[]{:S(2)}, u32[]{:S(2)}) collective-permute-start(bf16[144,512]{1,0:T(8,128)(2,1)S(1)} %shard_map.84.refs_7_), channel_id=1, source_target_pairs={{0,16},{1,3},{2,18},{3,1},{16,0},{17,19},{18,2},{19,17},{4,20},{5,... | collective-permute-start | bytes 442376 | tf_op jit(solution)/shard_map/ppermute | solution.py:51
  26.9 1.5 %collective-permute-start.10 = (f32[384,128]{1,0:T(8,128)S(1)}, f32[384,128]{1,0:T(8,128)S(1)}, u32[]{:S(2)}, u32[]{:S(2)}) collective-permute-start(f32[384,128]{1,0:T(8,128)S(1)} %shard_map.89.mine), channel_id=1, source_target_pairs={{0,1},{1,0},{2,3},{3,2},{4,5},{5,4},{6,7},{7,6},{8,9},{9,8},{10,11... | collective-permute-start | bytes 589832 | tf_op jit(solution)/shard_map/ppermute | solution.py:39
  28.9 4.3 %collective-permute-start.11 = (f32[128,128]{1,0:T(8,128)S(1)}, f32[128,128]{1,0:T(8,128)S(1)}, u32[]{:S(2)}, u32[]{:S(2)}) collective-permute-start(f32[128,128]{1,0:T(8,128)S(1)} %get-tuple-element.20), channel_id=1, source_target_pairs={{0,2},{1,9},{2,0},{3,11},{4,6},{5,13},{6,4},{7,15},{8,10},{9,1},{1... | collective-permute-start | bytes 196616 | tf_op jit(solution)/shard_map/ppermute | solution.py:51
  30.0 4.8 %collective-permute-start.14 = (f32[1,64,128]{2,1,0:T(8,128)S(1)}, f32[1,64,128]{2,1,0:T(8,128)S(1)}, u32[]{:S(2)}, u32[]{:S(2)}) collective-permute-start(f32[1,64,128]{2,1,0:T(8,128)S(1)} %get-tuple-element.22), channel_id=1, source_target_pairs={{0,8},{4,12},{8,0},{12,4},{1,9},{5,13},{9,1},{13,5},{2,10},{6,14},... | collective-permute-start | bytes 98312 | tf_op jit(solution)/shard_map/ppermute | solution.py:39
  33.2 4.3 %collective-permute-start.12 = (f32[128,128]{1,0:T(8,128)S(1)}, f32[128,128]{1,0:T(8,128)S(1)}, u32[]{:S(2)}, u32[]{:S(2)}) collective-permute-start(f32[128,128]{1,0:T(8,128)S(1)} %add.21), channel_id=1, source_target_pairs={{0,4},{1,3},{2,6},{3,1},{4,0},{5,7},{6,2},{7,5},{8,12},{9,11},{10,... | collective-permute-start | bytes 196616 | tf_op jit(solution)/shard_map/ppermute | solution.py:51
  34.8 5.1 %collective-permute-start.15 = (f32[2,64,128]{2,1,0:T(8,128)S(1)}, f32[2,64,128]{2,1,0:T(8,128)S(1)}, u32[]{:S(2)}, u32[]{:S(2)}) collective-permute-start(f32[2,64,128]{2,1,0:T(8,128)S(1)} %pad_maximum_fusion.2), channel_id=1, source_target_pairs={{0,4},{4,0},{8,12},{12,8},{1,5},{5,1},{9,13},{13,9},{2,6},{6,2},{1... | collective-permute-start | bytes 196616 | tf_op jit(solution)/shard_map/ppermute | solution.py:39
  37.6 5.2 %collective-permute-start.13 = (f32[128,128]{1,0:T(8,128)S(1)}, f32[128,128]{1,0:T(8,128)S(1)}, u32[]{:S(2)}, u32[]{:S(2)}) collective-permute-start(f32[128,128]{1,0:T(8,128)S(1)} %add.22), channel_id=1, source_target_pairs={{0,8},{1,5},{2,10},{3,7},{4,12},{5,1},{6,14},{7,3},{8,0},{9,13},{1... | collective-permute-start | bytes 196616 | tf_op jit(solution)/shard_map/ppermute | solution.py:51
  39.9 5.5 %collective-permute-start.16 = (f32[4,64,128]{2,1,0:T(8,128)S(1)}, f32[4,64,128]{2,1,0:T(8,128)S(1)}, u32[]{:S(2)}, u32[]{:S(2)}) collective-permute-start(f32[4,64,128]{2,1,0:T(8,128)S(1)} %pad_maximum_fusion.1), channel_id=1, source_target_pairs={{0,2},{2,0},{1,3},{3,1},{4,6},{6,4},{5,7},{7,5},{8,10},{10,8},{9,1... | collective-permute-start | bytes 393224 | tf_op jit(solution)/shard_map/ppermute | solution.py:39
